TPU v7x, 32 devices: a whole 2x2x4 slice. The times are simulated.
32 devices in a mesh: seq: 4 (over y, x), exp: 8 (over z, core).
Axes of the slice: x: 2, y: 2, z: 4, core: 2. Of those that a mesh axis runs over, the one named last changes fastest.
Arguments:
- tokens: bfloat16 [2, 4, 1024, 1280], P(None, 'seq', 'exp'), may hold values from -6 to 6
- cotangent: bfloat16 [2, 4, 1024, 1280], P(None, 'seq', 'exp'), may hold values from -6 to 6
- expert_ids: int32 [2, 4, 1024, 7], P(None, 'seq', 'exp'), may hold values from 0 to 15, all different within a row; in each aligned block of 128 rows (0 to 127, 128 to 255, ..., all dimensions but the last counted through in order) at most 112 rows name the same one
- owner_table: int32 [16], replicated, may hold values from 0 to 15, each once
- w_query: bfloat16 [1280, 1280], replicated, may hold values from -0.25 to 0.25
- w_key: bfloat16 [1280, 1280], replicated, may hold values from -0.25 to 0.25
- w_value: bfloat16 [1280, 1280], replicated, may hold values from -0.15625 to 0.15625
- w_out: bfloat16 [1280, 1280], replicated, may hold values from -1.25 to 1.25
- gain_one: float32 [1280], replicated, may hold values from 0.5 to 1.5
- gain_two: float32 [1280], replicated, may hold values from 0.5 to 1.5
- w_router: bfloat16 [1280, 16], replicated, may hold values from -0.083984375 to 0.083984375
- shared_gate: bfloat16 [1280, 896], replicated, may hold values from -0.15625 to 0.15625
- shared_up: bfloat16 [1280, 896], replicated, may hold values from -0.15625 to 0.15625
- shared_down: bfloat16 [1280, 896], replicated, may hold values from -0.1875 to 0.1875
- routed_gate: bfloat16 [16, 1280, 896], P('exp'), may hold values from -0.15625 to 0.15625
- routed_up: bfloat16 [16, 1280, 896], P('exp'), may hold values from -0.15625 to 0.15625
- routed_down: bfloat16 [16, 1280, 896], P('exp'), may hold values from -0.1875 to 0.1875
Outputs:
- layer_out: bfloat16 [2, 4, 1024, 1280], P(None, 'seq', 'exp')
- grad_tokens: bfloat16 [2, 4, 1024, 1280], P(None, 'seq', 'exp')
- grad_query: float32 [1280, 1280], P('exp')
- grad_key: float32 [1280, 1280], P('exp')
- grad_value: float32 [1280, 1280], P('exp')
- grad_out_proj: float32 [1280, 1280], P('exp')
- grad_gain_one: float32 [1280], P('exp')
- grad_gain_two: float32 [1280], P('exp')
- grad_router: float32 [1280, 16], P('exp')
- grad_shared_gate: float32 [1280, 896], P('exp')
- grad_shared_up: float32 [1280, 896], P('exp')
- grad_shared_down: float32 [1280, 896], P('exp')
- grad_routed_gate: float32 [16, 1280, 896], P('exp', 'seq')
- grad_routed_up: float32 [16, 1280, 896], P('exp', 'seq')
- grad_routed_down: float32 [16, 1280, 896], P('exp', 'seq')
Inputs may be any that keep to these rules, and one draw needn't show every extreme that they name: `expert_ids`: each token names 7 different experts. In each aligned block of 128 positions of a sequence (the tokens of one index of exp), no expert is named by more than 112 tokens; some block has an expert named by exactly 112. A permutation: expert e's weights are row owner_table[e] of routed_gate, routed_up and routed_down.
All inputs are finite; a program needn't handle non-finite values.
Results may differ from a plain program's by a relative error of at most 0.024.
Values may be sent and summed in bfloat16 or wider, within the bound.
A program may use at most 448 MiB of HBM per device.

v0:
```python
import math

import jax
import jax.numpy as jnp
from jax import lax
from jax.sharding import PartitionSpec as P

D = 1280
HEADS = 10
HD = 128
TOP = 7
EXP_DEV = 2
MB = 2
SEQ_DEV = 128


eps = 1e-06


def norm_rows(inputs, gain):
    return inputs * lax.rsqrt(jnp.mean(inputs * inputs, axis=-1, keepdims=True) + eps) * gain


def angle_tables(positions):
    steps_half = jnp.arange(HD // 2).astype(positions.dtype)
    frequency = jnp.exp(steps_half * (-2.0 * math.log(10000.0) / HD))
    angles = positions[:, None] * frequency[None, :]
    angles = jnp.concatenate([angles, angles], axis=-1)
    return (jnp.cos(angles), jnp.sin(angles))


def rotate(inputs, cos_table, sin_table):
    row_count = inputs.shape[0]
    per_head = inputs.reshape(row_count, HEADS, HD)
    first_half = per_head[..., : HD // 2]
    second_half = per_head[..., HD // 2 :]
    turned = jnp.concatenate([-second_half, first_half], axis=-1)
    return (per_head * cos_table[:, None, :] + turned * sin_table[:, None, :]).reshape(
        row_count, HEADS * HD
    )


def softmax_rows(scores):
    largest = jnp.max(scores, axis=-1, keepdims=True)
    powers = jnp.exp(scores - largest)
    return powers / jnp.sum(powers, axis=-1, keepdims=True)


def silu_product(gate_part, up_part):
    return jax.nn.silu(gate_part) * up_part


def attention_probs(queries_low, key_rows, visible):
    scores = jnp.einsum(
        "qhd,khd->hqk", queries_low, key_rows, preferred_element_type=jnp.float32
    ) * HD ** (-0.5)
    masked = jnp.where(visible[None], scores, -1e30)
    largest = jnp.max(masked, axis=-1, keepdims=True)
    powers = jnp.exp(masked - largest)
    totals = jnp.sum(powers, axis=-1, keepdims=True)
    log_total = (largest + jnp.log(totals))[..., 0]
    return (powers / totals, log_total)


def on_device(
    tokens,
    cotangent,
    expert_ids,
    owner_table,
    w_query,
    w_key,
    w_value,
    w_out,
    gain_one,
    gain_two,
    w_router,
    shared_gate,
    shared_up,
    shared_down,
    routed_gate,
    routed_up,
    routed_down,
):
    devices = lax.axis_size("exp")
    experts = owner_table.shape[0]
    most = 2 * SEQ_DEV * TOP // experts
    length = SEQ_DEV * devices
    factor = HD ** (-0.5)
    offset = lax.axis_index("exp") * SEQ_DEV
    query_pos = offset + jnp.arange(SEQ_DEV)
    cos_table, sin_table = angle_tables(query_pos.astype(jnp.float32))
    visible = query_pos[:, None] >= jnp.arange(length)[None, :]
    expert_range = jnp.arange(experts)
    pair_count = SEQ_DEV * TOP
    sum_query = jnp.zeros(w_query.shape, jnp.float32)
    sum_key = jnp.zeros(w_key.shape, jnp.float32)
    sum_value = jnp.zeros(w_value.shape, jnp.float32)
    sum_out = jnp.zeros(w_out.shape, jnp.float32)
    sum_gain_one = jnp.zeros(gain_one.shape, jnp.float32)
    sum_gain_two = jnp.zeros(gain_two.shape, jnp.float32)
    sum_router = jnp.zeros(w_router.shape, jnp.float32)
    sum_shared_gate = jnp.zeros(shared_gate.shape, jnp.float32)
    sum_shared_up = jnp.zeros(shared_up.shape, jnp.float32)
    sum_shared_down = jnp.zeros(shared_down.shape, jnp.float32)
    sum_routed_gate = jnp.zeros(routed_gate.shape, jnp.float32)
    sum_routed_up = jnp.zeros(routed_up.shape, jnp.float32)
    sum_routed_down = jnp.zeros(routed_down.shape, jnp.float32)
    outputs_list = []
    grads_list = []
    for micro_batch in range(MB):
        rows_in = tokens[micro_batch, 0].astype(jnp.float32)
        normed_low = norm_rows(rows_in, gain_one).astype(jnp.bfloat16)
        query_raw = jnp.dot(normed_low, w_query, preferred_element_type=jnp.float32)
        key_raw = jnp.dot(normed_low, w_key, preferred_element_type=jnp.float32)
        queries_low = rotate(query_raw, cos_table, sin_table).astype(jnp.bfloat16)
        key_low = rotate(key_raw, cos_table, sin_table).astype(jnp.bfloat16)
        value_low = jnp.dot(normed_low, w_value, preferred_element_type=jnp.float32).astype(
            jnp.bfloat16
        )
        gathered = (
            lax.all_gather(key_low, "exp", axis=0, tiled=True),
            lax.all_gather(value_low, "exp", axis=0, tiled=True),
        )
        key_rows = gathered[0].reshape(length, HEADS, HD)
        value_rows = gathered[1].reshape(length, HEADS, HD)
        query_heads = queries_low.reshape(SEQ_DEV, HEADS, HD)
        attention, unused_total = attention_probs(query_heads, key_rows, visible)
        mixed_low = (
            jnp.einsum(
                "hqk,khd->qhd",
                attention.astype(jnp.bfloat16),
                value_rows,
                preferred_element_type=jnp.float32,
            )
            .astype(jnp.bfloat16)
            .reshape(SEQ_DEV, D)
        )
        hidden_one = rows_in + jnp.dot(mixed_low, w_out, preferred_element_type=jnp.float32)
        two_low = norm_rows(hidden_one, gain_two).astype(jnp.bfloat16)
        logits = jnp.dot(two_low, w_router, preferred_element_type=jnp.float32)
        chosen_ids = expert_ids[micro_batch, 0]
        choice_hot = (chosen_ids[..., None] == expert_range).astype(jnp.float32)
        chosen_logits = jnp.sum(choice_hot * logits[:, None, :], axis=-1)
        gate_weights = softmax_rows(chosen_logits)
        shared_gate_value = jnp.dot(two_low, shared_gate, preferred_element_type=jnp.float32)
        shared_up_value = jnp.dot(two_low, shared_up, preferred_element_type=jnp.float32)
        shared_hidden = silu_product(shared_gate_value, shared_up_value).astype(jnp.bfloat16)
        shared_result = jnp.einsum(
            "tf,df->td", shared_hidden, shared_down, preferred_element_type=jnp.float32
        )
        pair_ids = chosen_ids.reshape(pair_count)
        pair_hot = (pair_ids[:, None] == expert_range).astype(jnp.int32)
        ranks = jnp.sum((jnp.cumsum(pair_hot, axis=0) - pair_hot) * pair_hot, axis=1)
        slot_of = jnp.sum(pair_hot * owner_table[None, :], axis=1)
        places = slot_of * most + ranks
        pair_rows = jnp.repeat(two_low, TOP, axis=0)
        send_rows = jnp.zeros((experts * most, D), jnp.bfloat16).at[places].set(pair_rows)
        received = lax.all_to_all(
            send_rows.reshape(devices, EXP_DEV * most, D),
            "exp",
            split_axis=0,
            concat_axis=0,
            tiled=True,
        )
        received = received.reshape(devices, EXP_DEV, most, D)
        gate_part = jnp.einsum(
            "semd,edf->semf", received, routed_gate, preferred_element_type=jnp.float32
        )
        up_part = jnp.einsum(
            "semd,edf->semf", received, routed_up, preferred_element_type=jnp.float32
        )
        inner_rows = silu_product(gate_part, up_part).astype(jnp.bfloat16)
        expert_rows = jnp.einsum(
            "semf,edf->semd", inner_rows, routed_down, preferred_element_type=jnp.float32
        ).astype(jnp.bfloat16)
        returned = lax.all_to_all(
            expert_rows.reshape(devices, EXP_DEV * most, D),
            "exp",
            split_axis=0,
            concat_axis=0,
            tiled=True,
        )
        pair_out = (
            returned.reshape(experts * most, D)[places].reshape(SEQ_DEV, TOP, D).astype(jnp.float32)
        )
        routed_result = jnp.sum(gate_weights[..., None] * pair_out, axis=1)
        outputs_list.append((hidden_one + shared_result + routed_result).astype(jnp.bfloat16))
        grad_rows = cotangent[micro_batch, 0].astype(jnp.float32)
        grad_gates = jnp.sum(grad_rows[:, None, :] * pair_out, axis=-1)
        grad_chosen = gate_weights * (
            grad_gates - jnp.sum(gate_weights * grad_gates, axis=-1, keepdims=True)
        )
        grad_logits = jnp.sum(choice_hot * grad_chosen[..., None], axis=1).astype(jnp.bfloat16)
        sum_router = sum_router + jnp.einsum(
            "td,te->de", two_low, grad_logits, preferred_element_type=jnp.float32
        )
        grad_two = jnp.einsum(
            "te,de->td", grad_logits, w_router, preferred_element_type=jnp.float32
        )
        pair_grad = (
            (gate_weights[..., None] * grad_rows[:, None, :])
            .reshape(pair_count, D)
            .astype(jnp.bfloat16)
        )
        send_grads = jnp.zeros((experts * most, D), jnp.bfloat16).at[places].set(pair_grad)
        grad_received = lax.all_to_all(
            send_grads.reshape(devices, EXP_DEV * most, D),
            "exp",
            split_axis=0,
            concat_axis=0,
            tiled=True,
        )
        grad_received = grad_received.reshape(devices, EXP_DEV, most, D)
        grad_inner = jnp.einsum(
            "semd,edf->semf", grad_received, routed_down, preferred_element_type=jnp.float32
        )
        sum_routed_down = sum_routed_down + jnp.einsum(
            "semd,semf->edf", grad_received, inner_rows, preferred_element_type=jnp.float32
        )
        unused_act, act_pullback = jax.vjp(silu_product, gate_part, up_part)
        grad_gate_part, grad_up_part = act_pullback(grad_inner)
        grad_gate_low = grad_gate_part.astype(jnp.bfloat16)
        grad_up_low = grad_up_part.astype(jnp.bfloat16)
        sum_routed_gate = sum_routed_gate + jnp.einsum(
            "semd,semf->edf", received, grad_gate_low, preferred_element_type=jnp.float32
        )
        sum_routed_up = sum_routed_up + jnp.einsum(
            "semd,semf->edf", received, grad_up_low, preferred_element_type=jnp.float32
        )
        back_rows = jnp.einsum(
            "semf,edf->semd", grad_gate_low, routed_gate, preferred_element_type=jnp.float32
        ) + jnp.einsum("semf,edf->semd", grad_up_low, routed_up, preferred_element_type=jnp.float32)
        back_rows = back_rows.astype(jnp.bfloat16).reshape(devices, EXP_DEV * most, D)
        came_back = lax.all_to_all(back_rows, "exp", split_axis=0, concat_axis=0, tiled=True)
        pair_back = (
            came_back.reshape(experts * most, D)[places]
            .reshape(SEQ_DEV, TOP, D)
            .astype(jnp.float32)
        )
        grad_two = grad_two + jnp.sum(pair_back, axis=1)
        grad_low = grad_rows.astype(jnp.bfloat16)
        sum_shared_down = sum_shared_down + jnp.einsum(
            "td,tf->df", grad_low, shared_hidden, preferred_element_type=jnp.float32
        )
        grad_shared = jnp.einsum(
            "td,df->tf", grad_low, shared_down, preferred_element_type=jnp.float32
        )
        unused_shared, shared_pullback = jax.vjp(silu_product, shared_gate_value, shared_up_value)
        shared_dgate, shared_dup = shared_pullback(grad_shared)
        shared_dgate = shared_dgate.astype(jnp.bfloat16)
        shared_dup = shared_dup.astype(jnp.bfloat16)
        sum_shared_gate = sum_shared_gate + jnp.einsum(
            "td,tf->df", two_low, shared_dgate, preferred_element_type=jnp.float32
        )
        sum_shared_up = sum_shared_up + jnp.einsum(
            "td,tf->df", two_low, shared_dup, preferred_element_type=jnp.float32
        )
        grad_two = grad_two + jnp.einsum(
            "tf,df->td", shared_dgate, shared_gate, preferred_element_type=jnp.float32
        )
        grad_two = grad_two + jnp.einsum(
            "tf,df->td", shared_dup, shared_up, preferred_element_type=jnp.float32
        )
        unused_two, norm_two_pullback = jax.vjp(norm_rows, hidden_one, gain_two)
        grad_hidden_part, grad_gain_part = norm_two_pullback(grad_two)
        grad_hidden = grad_rows + grad_hidden_part
        sum_gain_two = sum_gain_two + grad_gain_part
        grad_mix = grad_hidden.astype(jnp.bfloat16)
        sum_out = sum_out + jnp.einsum(
            "td,te->de", mixed_low, grad_mix, preferred_element_type=jnp.float32
        )
        grad_mixed = jnp.einsum("te,de->td", grad_mix, w_out, preferred_element_type=jnp.float32)
        grad_mixed = grad_mixed.astype(jnp.bfloat16).reshape(SEQ_DEV, HEADS, HD)
        again = (
            lax.all_gather(key_low, "exp", axis=0, tiled=True),
            lax.all_gather(value_low, "exp", axis=0, tiled=True),
        )
        key_back = again[0].reshape(length, HEADS, HD)
        value_back = again[1].reshape(length, HEADS, HD)
        attention_back, log_total = attention_probs(query_heads, key_back, visible)
        grad_att = jnp.einsum(
            "qhd,khd->hqk", grad_mixed, value_back, preferred_element_type=jnp.float32
        )
        row_term = jnp.sum(attention_back * grad_att, axis=-1)
        grad_scores = (attention_back * (grad_att - row_term[..., None])).astype(jnp.bfloat16)
        grad_queries = (
            jnp.einsum("hqk,khd->qhd", grad_scores, key_back, preferred_element_type=jnp.float32)
            * factor
        )
        grad_values = jnp.einsum(
            "hqk,qhd->khd",
            attention_back.astype(jnp.bfloat16),
            grad_mixed,
            preferred_element_type=jnp.float32,
        )
        grad_keys = (
            jnp.einsum("hqk,qhd->khd", grad_scores, query_heads, preferred_element_type=jnp.float32)
            * factor
        )
        own_keys, own_values = (
            lax.psum_scatter(
                grad_keys.reshape(length, D).astype(jnp.bfloat16),
                "exp",
                scatter_dimension=0,
                tiled=True,
            ).astype(jnp.float32),
            lax.psum_scatter(
                grad_values.reshape(length, D).astype(jnp.bfloat16),
                "exp",
                scatter_dimension=0,
                tiled=True,
            ).astype(jnp.float32),
        )
        query_grad_low = rotate(grad_queries.reshape(SEQ_DEV, D), cos_table, -sin_table).astype(
            jnp.bfloat16
        )
        key_grad_low = rotate(own_keys, cos_table, -sin_table).astype(jnp.bfloat16)
        value_grad_low = own_values.astype(jnp.bfloat16)
        sum_query = sum_query + jnp.einsum(
            "td,te->de", normed_low, query_grad_low, preferred_element_type=jnp.float32
        )
        sum_key = sum_key + jnp.einsum(
            "td,te->de", normed_low, key_grad_low, preferred_element_type=jnp.float32
        )
        sum_value = sum_value + jnp.einsum(
            "td,te->de", normed_low, value_grad_low, preferred_element_type=jnp.float32
        )
        grad_normed = (
            jnp.einsum("te,de->td", query_grad_low, w_query, preferred_element_type=jnp.float32)
            + jnp.einsum("te,de->td", key_grad_low, w_key, preferred_element_type=jnp.float32)
            + jnp.einsum("te,de->td", value_grad_low, w_value, preferred_element_type=jnp.float32)
        )
        unused_one, norm_one_pullback = jax.vjp(norm_rows, rows_in, gain_one)
        grad_input_part, grad_gain_first = norm_one_pullback(grad_normed)
        sum_gain_one = sum_gain_one + grad_gain_first
        grads_list.append((grad_hidden + grad_input_part).astype(jnp.bfloat16))
    layer_out = jnp.stack(outputs_list)[:, None]
    grad_tokens = jnp.stack(grads_list)[:, None]
    routed_parts = (
        lax.psum_scatter(
            sum_routed_gate.astype(jnp.bfloat16), "seq", scatter_dimension=1, tiled=True
        ).astype(jnp.float32),
        lax.psum_scatter(
            sum_routed_up.astype(jnp.bfloat16), "seq", scatter_dimension=1, tiled=True
        ).astype(jnp.float32),
        lax.psum_scatter(
            sum_routed_down.astype(jnp.bfloat16), "seq", scatter_dimension=1, tiled=True
        ).astype(jnp.float32),
    )
    dense_parts = (
        lax.psum_scatter(
            sum_query.astype(jnp.bfloat16), "exp", scatter_dimension=0, tiled=True
        ).astype(jnp.float32),
        lax.psum_scatter(
            sum_key.astype(jnp.bfloat16), "exp", scatter_dimension=0, tiled=True
        ).astype(jnp.float32),
        lax.psum_scatter(
            sum_value.astype(jnp.bfloat16), "exp", scatter_dimension=0, tiled=True
        ).astype(jnp.float32),
        lax.psum_scatter(
            sum_out.astype(jnp.bfloat16), "exp", scatter_dimension=0, tiled=True
        ).astype(jnp.float32),
        lax.psum_scatter(
            sum_gain_one.astype(jnp.bfloat16), "exp", scatter_dimension=0, tiled=True
        ).astype(jnp.float32),
        lax.psum_scatter(
            sum_gain_two.astype(jnp.bfloat16), "exp", scatter_dimension=0, tiled=True
        ).astype(jnp.float32),
        lax.psum_scatter(
            sum_router.astype(jnp.bfloat16), "exp", scatter_dimension=0, tiled=True
        ).astype(jnp.float32),
        lax.psum_scatter(
            sum_shared_gate.astype(jnp.bfloat16), "exp", scatter_dimension=0, tiled=True
        ).astype(jnp.float32),
        lax.psum_scatter(
            sum_shared_up.astype(jnp.bfloat16), "exp", scatter_dimension=0, tiled=True
        ).astype(jnp.float32),
        lax.psum_scatter(
            sum_shared_down.astype(jnp.bfloat16), "exp", scatter_dimension=0, tiled=True
        ).astype(jnp.float32),
    )
    dense_full = (
        lax.psum(dense_parts[0].astype(jnp.bfloat16), "seq").astype(jnp.float32),
        lax.psum(dense_parts[1].astype(jnp.bfloat16), "seq").astype(jnp.float32),
        lax.psum(dense_parts[2].astype(jnp.bfloat16), "seq").astype(jnp.float32),
        lax.psum(dense_parts[3].astype(jnp.bfloat16), "seq").astype(jnp.float32),
        lax.psum(dense_parts[4].astype(jnp.bfloat16), "seq").astype(jnp.float32),
        lax.psum(dense_parts[5].astype(jnp.bfloat16), "seq").astype(jnp.float32),
        lax.psum(dense_parts[6].astype(jnp.bfloat16), "seq").astype(jnp.float32),
        lax.psum(dense_parts[7].astype(jnp.bfloat16), "seq").astype(jnp.float32),
        lax.psum(dense_parts[8].astype(jnp.bfloat16), "seq").astype(jnp.float32),
        lax.psum(dense_parts[9].astype(jnp.bfloat16), "seq").astype(jnp.float32),
    )
    return (layer_out, grad_tokens) + tuple(dense_full) + tuple(routed_parts)


def solution(mesh):
    placed = (
        P(None, "seq", "exp", None),
        P(None, "seq", "exp", None),
        P(None, "seq", "exp", None),
        P(),
        P(),
        P(),
        P(),
        P(),
        P(),
        P(),
        P(),
        P(),
        P(),
        P(),
        P("exp", None, None),
        P("exp", None, None),
        P("exp", None, None),
    )
    return jax.shard_map(
        on_device,
        mesh=mesh,
        in_specs=placed,
        out_specs=(
            P(None, "seq", "exp", None),
            P(None, "seq", "exp", None),
            P("exp", None),
            P("exp", None),
            P("exp", None),
            P("exp", None),
            P("exp"),
            P("exp"),
            P("exp", None),
            P("exp", None),
            P("exp", None),
            P("exp", None),
            P("exp", "seq", None),
            P("exp", "seq", None),
            P("exp", "seq", None),
        ),
        check_vma=False,
    )
```

profile of v0, /device:TPU:12, one launch (start us, length us, event | category | flops | bytes accessed | tf_op | source)
XLA Modules:
  0.0 1913.4 jit_solution(17571013354598271986)
XLA Ops:
  9.2 5.6 copy.186
  14.9 5.6 copy.185
  45.4 26.1 %all-gather.7.cloned.1.call-done = bf16[1024,1280]{0,1:T(8,128)(2,1)} async-done(((bf16[128,1280]{0,1:T(8,128)(2,1)}), bf16[1024,1280]{0,1:T(8,128)(2,1)}) %all-gather.7.cloned.1.call-update) | async-done | bytes 2621456 | tf_op jit(solution)/shard_map/all_gather | solution.py:121
  71.5 6.4 fusion.243
  77.9 29.0 %all-gather.5.cloned.1.call-done = bf16[1024,1280]{1,0:T(8,128)(2,1)} async-done(((bf16[128,1280]{1,0:T(8,128)(2,1)}), bf16[1024,1280]{1,0:T(8,128)(2,1)}) %all-gather.5.cloned.1.call-update) | async-done | bytes 2621456 | tf_op jit(solution)/shard_map/all_gather | solution.py:122
  124.3 9.5 scatter_custom_fusion
  133.7 6.0 all-to-all-start
  145.2 5.3 mul.786
  153.3 13.3 scatter_custom_fusion.2
  166.7 71.9 %all-to-all-done = bf16[8,224,1280]{2,1,0:T(8,128)(2,1)} async-done(((bf16[8,224,1280]{2,1,0:T(8,128)(2,1)}), bf16[8,224,1280]{2,1,0:T(8,128)(2,1)}, u32[]{:S(2)}, u32[]{:S(2)}) %all-to-all-start) | async-done | bytes 4587552 | tf_op jit(solution)/shard_map/all_to_all | solution.py:158
  238.6 8.5 all-to-all-start.4
  247.1 11.2 fusion.35
  258.3 11.2 fusion.43
  269.6 76.4 %all-to-all-done.4 = bf16[8,224,1280]{2,1,0:T(8,128)(2,1)} async-done(((bf16[8,224,1280]{2,1,0:T(8,128)(2,1)}), bf16[8,224,1280]{2,1,0:T(8,128)(2,1)}, u32[]{:S(2)}, u32[]{:S(2)}) %all-to-all-start.4) | async-done | bytes 4587552 | tf_op jit(solution)/shard_map/all_to_all | solution.py:206
  346.0 13.5 fusion.16
  359.5 8.8 fusion.47
  370.8 8.1 all-to-all-start.1
  381.8 11.9 fusion.39
  393.8 8.9 fusion.53
  405.1 114.8 %all-to-all-done.1 = bf16[8,224,1280]{2,1,0:T(8,128)(2,1)} async-done(((bf16[8,224,1280]{2,1,0:T(8,128)(2,1)}), bf16[8,224,1280]{2,1,0:T(8,128)(2,1)}, u32[]{:S(2)}, u32[]{:S(2)}) %all-to-all-start.1) | async-done | bytes 4587552 | tf_op jit(solution)/shard_map/all_to_all | solution.py:176
  519.9 8.1 all-to-all-start.5
  533.1 6.4 fusion.244
  549.1 9.3 gather_fusion
  571.7 55.3 %all-to-all-done.5 = bf16[8,224,1280]{2,1,0:T(8,128)(2,1)} async-done(((bf16[8,224,1280]{2,1,0:T(8,128)(2,1)}), bf16[8,224,1280]{2,1,0:T(8,128)(2,1)}, u32[]{:S(2)}, u32[]{:S(2)}) %all-to-all-start.5) | async-done | bytes 4587552 | tf_op jit(solution)/shard_map/all_to_all | solution.py:234
  627.0 9.4 gather_fusion.2
  659.3 9.4 scatter_custom_fusion.1
  668.7 8.5 all-to-all-start.2
  688.8 13.3 scatter_custom_fusion.3
  702.1 74.1 %all-to-all-done.2 = bf16[8,224,1280]{2,1,0:T(8,128)(2,1)} async-done(((bf16[8,224,1280]{2,1,0:T(8,128)(2,1)}), bf16[8,224,1280]{2,1,0:T(8,128)(2,1)}, u32[]{:S(2)}, u32[]{:S(2)}) %all-to-all-start.2) | async-done | bytes 4587552 | tf_op jit(solution)/shard_map/all_to_all | solution.py:158
  776.2 8.3 all-to-all-start.6
  784.5 11.3 fusion.33
  795.7 11.2 fusion.41
  807.0 76.4 %all-to-all-done.6 = bf16[8,224,1280]{2,1,0:T(8,128)(2,1)} async-done(((bf16[8,224,1280]{2,1,0:T(8,128)(2,1)}), bf16[8,224,1280]{2,1,0:T(8,128)(2,1)}, u32[]{:S(2)}, u32[]{:S(2)}) %all-to-all-start.6) | async-done | bytes 4587552 | tf_op jit(solution)/shard_map/all_to_all | solution.py:206
  883.4 13.5 fusion.15
  896.8 8.8 fusion.50
  908.1 8.3 all-to-all-start.3
  916.4 11.9 fusion.37
  928.4 8.9 fusion.56
  939.7 75.7 %all-to-all-done.3 = bf16[8,224,1280]{2,1,0:T(8,128)(2,1)} async-done(((bf16[8,224,1280]{2,1,0:T(8,128)(2,1)}), bf16[8,224,1280]{2,1,0:T(8,128)(2,1)}, u32[]{:S(2)}, u32[]{:S(2)}) %all-to-all-start.3) | async-done | bytes 4587552 | tf_op jit(solution)/shard_map/all_to_all | solution.py:176
  1015.3 8.2 all-to-all-start.7
  1030.4 9.7 gather_fusion.1
  1053.4 69.1 %all-to-all-done.7 = bf16[8,224,1280]{2,1,0:T(8,128)(2,1)} async-done(((bf16[8,224,1280]{2,1,0:T(8,128)(2,1)}), bf16[8,224,1280]{2,1,0:T(8,128)(2,1)}, u32[]{:S(2)}, u32[]{:S(2)}) %all-to-all-start.7) | async-done | bytes 4587552 | tf_op jit(solution)/shard_map/all_to_all | solution.py:234
  1122.5 9.4 gather_fusion.3
  1218.8 10.5 fusion.66
  1230.7 11.3 fusion.2
  1242.1 8.3 fusion.69
  1250.5 9.8 fusion.3
  1260.3 8.8 fusion.72
  1269.2 9.8 fusion.4
  1297.8 6.0 fusion.7
  1339.8 12.8 reduce-scatter.56.cloned.1.call-done
  1359.3 25.2 %reduce-scatter.54.cloned.1.call-done = bf16[160,16]{1,0:T(8,128)(2,1)} async-done(((bf16[1280,16]{1,0:T(8,128)(2,1)}), bf16[160,16]{1,0:T(8,128)(2,1)}) %reduce-scatter.54.cloned.1.call-update) | async-done | bytes 5136
  1385.3 60.1 %reduce-scatter.44.cloned.1.call-done = bf16[2,320,896]{2,1,0:T(8,128)(2,1)} async-done(((bf16[2,1280,896]{2,1,0:T(8,128)(2,1)}), bf16[2,320,896]{2,1,0:T(8,128)(2,1)}) %reduce-scatter.44.cloned.1.call-update) | async-done | bytes 1146896 | tf_op jit(solution)/shard_map/reduce_scatter | solution.py:346
  1448.2 56.4 %reduce-scatter.42.cloned.1.call-done = bf16[2,320,896]{2,1,0:T(8,128)(2,1)} async-done(((bf16[2,1280,896]{2,1,0:T(8,128)(2,1)}), bf16[2,320,896]{2,1,0:T(8,128)(2,1)}) %reduce-scatter.42.cloned.1.call-update) | async-done | bytes 1146896 | tf_op jit(solution)/shard_map/reduce_scatter | solution.py:343
  1507.4 56.5 %reduce-scatter.40.cloned.1.call-done = bf16[2,320,896]{2,1,0:T(8,128)(2,1)} async-done(((bf16[2,1280,896]{2,1,0:T(8,128)(2,1)}), bf16[2,320,896]{2,1,0:T(8,128)(2,1)}) %reduce-scatter.40.cloned.1.call-update) | async-done | bytes 1146896 | tf_op jit(solution)/shard_map/reduce_scatter | solution.py:340
  1574.4 24.3 %reduce-scatter.38.cloned.1.call-done = bf16[160,896]{1,0:T(8,128)(2,1)} async-done(((bf16[1280,896]{1,0:T(8,128)(2,1)}), bf16[160,896]{1,0:T(8,128)(2,1)}) %reduce-scatter.38.cloned.1.call-update) | async-done | bytes 286736 | tf_op jit(solution)/shard_map/reduce_scatter | solution.py:375
  1598.7 37.7 %reduce-scatter.36.cloned.1.call-done = bf16[160,896]{1,0:T(8,128)(2,1)} async-done(((bf16[1280,896]{1,0:T(8,128)(2,1)}), bf16[160,896]{1,0:T(8,128)(2,1)}) %reduce-scatter.36.cloned.1.call-update) | async-done | bytes 286736 | tf_op jit(solution)/shard_map/reduce_scatter | solution.py:372
  1636.4 42.4 %reduce-scatter.34.cloned.1.call-done = bf16[160,1280]{1,0:T(8,128)(2,1)} async-done(((bf16[1280,1280]{1,0:T(8,128)(2,1)}), bf16[160,1280]{1,0:T(8,128)(2,1)}) %reduce-scatter.34.cloned.1.call-update) | async-done | bytes 409616 | tf_op jit(solution)/shard_map/reduce_scatter | solution.py:360
  1678.8 42.4 %reduce-scatter.32.cloned.1.call-done = bf16[160,1280]{1,0:T(8,128)(2,1)} async-done(((bf16[1280,1280]{1,0:T(8,128)(2,1)}), bf16[160,1280]{1,0:T(8,128)(2,1)}) %reduce-scatter.32.cloned.1.call-update) | async-done | bytes 409616 | tf_op jit(solution)/shard_map/reduce_scatter | solution.py:357
  1721.2 42.5 %reduce-scatter.30.cloned.1.call-done = bf16[160,1280]{1,0:T(8,128)(2,1)} async-done(((bf16[1280,1280]{1,0:T(8,128)(2,1)}), bf16[160,1280]{1,0:T(8,128)(2,1)}) %reduce-scatter.30.cloned.1.call-update) | async-done | bytes 409616 | tf_op jit(solution)/shard_map/reduce_scatter | solution.py:354
  1763.6 42.5 %reduce-scatter.28.cloned.1.call-done = bf16[160,1280]{1,0:T(8,128)(2,1)} async-done(((bf16[1280,1280]{1,0:T(8,128)(2,1)}), bf16[160,1280]{1,0:T(8,128)(2,1)}) %reduce-scatter.28.cloned.1.call-update) | async-done | bytes 409616 | tf_op jit(solution)/shard_map/reduce_scatter | solution.py:351
  1813.2 15.6 all-reduce.2
  1828.9 9.9 all-reduce.3
  1843.7 51.0 %all-reduce.7.cloned.1.call-done = (bf16[160,1280]{1,0:T(8,128)(2,1)}, bf16[160,1280]{1,0:T(8,128)(2,1)}, bf16[160,1280]{1,0:T(8,128)(2,1)}, bf16[160,1280]{1,0:...) async-done(((bf16[160,1280]{1,0:T(8,128)(2,1)}, bf16[160,1280]{1,0:T(8,128)(2,1)}, bf16[160,1280]{1,0:T(8,128)(2,1)}, ...) | async-done | bytes 2498576 | tf_op jit(solution)/shard_map/psum | solution.py:383
  (486 shorter events, 335.8 us)
Async XLA Ops:
  7.2 29.8 %copy-start = (bf16[1280,1280]{1,0:T(8,128)(2,1)S(1)}, bf16[1280,1280]{1,0:T(8,128)(2,1)}, u32[]{:S(2)}) copy-start(bf16[1280,1280]{1,0:T(8,128)(2,1)} %param.23) | copy-start | bytes 9830404
  7.2 64.3 %all-gather.7.cloned.1.call-start = ((), (), s32[]{:S(2)}) async-start(), calls=%async_computation.24 | async-start | bytes 2949120 | tf_op jit(solution)/shard_map/all_gather | solution.py:121
  8.7 18.8 copy-start.112
  9.2 27.7 %copy-start.82 = (f32[128]{0:T(128)}, f32[128]{0:T(128)S(1)}, u32[]{:S(2)}) copy-start(f32[128]{0:T(128)S(1)} %fusion.219) | copy-start | bytes 1540
  27.5 351.3 %copy-start.92 = (f32[128]{0:T(128)}, f32[128]{0:T(128)S(1)}, u32[]{:S(2)}) copy-start(f32[128]{0:T(128)S(1)} %fusion.221) | copy-start | bytes 1540
  35.3 9.8 copy-start.109
  36.7 70.2 %all-gather.5.cloned.1.call-start = ((), (), s32[]{:S(2)}) async-start(), calls=%async_computation.23 | async-start | bytes 2949120 | tf_op jit(solution)/shard_map/all_gather | solution.py:122
  77.9 37.8 %copy-start.97 = (f32[10,128]{1,0:T(8,128)}, f32[10,128]{1,0:T(8,128)S(1)}, u32[]{:S(2)}) copy-start(f32[10,128]{1,0:T(8,128)S(1)} %get-tuple-element.173) | copy-start | bytes 15364
  116.6 17.2 copy-start.114
  116.6 17.2 copy-start.104
  133.7 104.9 %all-to-all-start = ((bf16[8,224,1280]{2,1,0:T(8,128)(2,1)}), bf16[8,224,1280]{2,1,0:T(8,128)(2,1)}, u32[]{:S(2)}, u32[]{:S(2)}) async-start(bf16[8,224,1280]{2,1,0:T(8,128)(2,1)} %bitcast.516), calls=%async_computation | async-start | bytes 9175040 | tf_op jit(solution)/shard_map/all_to_all | solution.py:158
  151.1 15.5 copy-start.87
  152.4 14.3 copy-start.95
  153.1 13.6 copy-start.73
  238.6 107.4 %all-to-all-start.4 = ((bf16[8,224,1280]{2,1,0:T(8,128)(2,1)}), bf16[8,224,1280]{2,1,0:T(8,128)(2,1)}, u32[]{:S(2)}, u32[]{:S(2)}) async-start(bf16[8,224,1280]{2,1,0:T(8,128)(2,1)} %bitcast.519), calls=%async_computation.4 | async-start | bytes 9175040 | tf_op jit(solution)/shard_map/all_to_all | solution.py:206
  359.5 8.8 copy-start.126
  370.8 149.1 %all-to-all-start.1 = ((bf16[8,224,1280]{2,1,0:T(8,128)(2,1)}), bf16[8,224,1280]{2,1,0:T(8,128)(2,1)}, u32[]{:S(2)}, u32[]{:S(2)}) async-start(bf16[8,224,1280]{2,1,0:T(8,128)(2,1)} %bitcast.515), calls=%async_computation.1 | async-start | bytes 9175040 | tf_op jit(solution)/shard_map/all_to_all | solution.py:176
  378.8 149.8 %all-gather.9.cloned.1.call-start = ((), (), s32[]{:S(2)}) async-start(), calls=%async_computation.25 | async-start | bytes 2949120 | tf_op jit(solution)/shard_map/all_gather | solution.py:122
  381.2 151.9 %all-gather.11.cloned.1.call-start = ((), (), s32[]{:S(2)}) async-start(), calls=%async_computation.26 | async-start | bytes 2949120 | tf_op jit(solution)/shard_map/all_gather | solution.py:121
  381.8 12.0 copy-start.121
  519.9 107.0 %all-to-all-start.5 = ((bf16[8,224,1280]{2,1,0:T(8,128)(2,1)}), bf16[8,224,1280]{2,1,0:T(8,128)(2,1)}, u32[]{:S(2)}, u32[]{:S(2)}) async-start(bf16[8,224,1280]{2,1,0:T(8,128)(2,1)} %bitcast.513), calls=%async_computation.5 | async-start | bytes 9175040 | tf_op jit(solution)/shard_map/all_to_all | solution.py:234
  528.6 20.4 %copy-start.88 = (s32[1024]{0:T(1024)}, s32[1024]{0:T(1024)S(1)}, u32[]{:S(2)}) copy-start(s32[1024]{0:T(1024)S(1)} %pad_clamp_fusion.1) | copy-start | bytes 12292
  539.5 7.0 copy-start.26
  549.1 101.1 %copy-start.68 = (bf16[128,896]{1,0:T(8,128)(2,1)}, bf16[128,896]{1,0:T(8,128)(2,1)S(1)}, u32[]{:S(2)}) copy-start(bf16[128,896]{1,0:T(8,128)(2,1)S(1)} %get-tuple-element.130) | copy-start | bytes 688132
  641.2 9.0 copy-start.80
  668.7 107.4 %all-to-all-start.2 = ((bf16[8,224,1280]{2,1,0:T(8,128)(2,1)}), bf16[8,224,1280]{2,1,0:T(8,128)(2,1)}, u32[]{:S(2)}, u32[]{:S(2)}) async-start(bf16[8,224,1280]{2,1,0:T(8,128)(2,1)} %bitcast.517), calls=%async_computation.2 | async-start | bytes 9175040 | tf_op jit(solution)/shard_map/all_to_all | solution.py:158
  688.6 13.5 copy-start.74
  776.2 107.2 %all-to-all-start.6 = ((bf16[8,224,1280]{2,1,0:T(8,128)(2,1)}), bf16[8,224,1280]{2,1,0:T(8,128)(2,1)}, u32[]{:S(2)}, u32[]{:S(2)}) async-start(bf16[8,224,1280]{2,1,0:T(8,128)(2,1)} %bitcast.518), calls=%async_computation.6 | async-start | bytes 9175040 | tf_op jit(solution)/shard_map/all_to_all | solution.py:206
  896.8 8.8 copy-start.125
  908.1 107.2 %all-to-all-start.3 = ((bf16[8,224,1280]{2,1,0:T(8,128)(2,1)}), bf16[8,224,1280]{2,1,0:T(8,128)(2,1)}, u32[]{:S(2)}, u32[]{:S(2)}) async-start(bf16[8,224,1280]{2,1,0:T(8,128)(2,1)} %bitcast.520), calls=%async_computation.3 | async-start | bytes 9175040 | tf_op jit(solution)/shard_map/all_to_all | solution.py:176
  916.4 12.0 copy-start.122
  1015.3 8.3 copy-start.115
  1015.3 8.3 copy-start.118
  1015.3 107.2 %all-to-all-start.7 = ((bf16[8,224,1280]{2,1,0:T(8,128)(2,1)}), bf16[8,224,1280]{2,1,0:T(8,128)(2,1)}, u32[]{:S(2)}, u32[]{:S(2)}) async-start(bf16[8,224,1280]{2,1,0:T(8,128)(2,1)} %bitcast.514), calls=%async_computation.7 | async-start | bytes 9175040 | tf_op jit(solution)/shard_map/all_to_all | solution.py:234
  1023.5 269.2 %reduce-scatter.48.cloned.1.call-start = ((), (), s32[]{:S(2)}) async-start(), calls=%async_computation.37 | async-start | bytes 2949120
  1030.4 115.2 %copy-start.69 = (bf16[128,896]{1,0:T(8,128)(2,1)}, bf16[128,896]{1,0:T(8,128)(2,1)S(1)}, u32[]{:S(2)}) copy-start(bf16[128,896]{1,0:T(8,128)(2,1)S(1)} %get-tuple-element.133) | copy-start | bytes 688132
  1136.5 9.2 copy-start.81
  1162.4 135.3 %reduce-scatter.52.cloned.1.call-start = ((), (), s32[]{:S(2)}) async-start(), calls=%async_computation.39 | async-start | bytes 2949120
  1178.3 133.6 %reduce-scatter.50.cloned.1.call-start = ((), (), s32[]{:S(2)}) async-start(), calls=%async_computation.38 | async-start | bytes 2949120
  1194.3 123.0 %reduce-scatter.46.cloned.1.call-start = ((), (), s32[]{:S(2)}) async-start(), calls=%async_computation.36 | async-start | bytes 2949120
  1210.3 142.3 %reduce-scatter.56.cloned.1.call-start = ((), (), s32[]{:S(2)}) async-start(), calls=%async_computation.41 | async-start | bytes 2580480
  1218.7 10.6 copy-start.84
  1218.7 10.8 copy-start.85
  1218.8 165.7 %reduce-scatter.54.cloned.1.call-start = ((), (), s32[]{:S(2)}) async-start(), calls=%async_computation.40 | async-start | bytes 368640
  1218.8 10.6 copy-start.27
  1218.8 10.7 copy-start.22
  1230.7 214.7 %reduce-scatter.44.cloned.1.call-start = ((), (), s32[]{:S(2)}) async-start(), calls=%async_computation.35 | async-start | bytes 5734400 | tf_op jit(solution)/shard_map/reduce_scatter | solution.py:346
  1242.1 262.6 %reduce-scatter.42.cloned.1.call-start = ((), (), s32[]{:S(2)}) async-start(), calls=%async_computation.34 | async-start | bytes 5734400 | tf_op jit(solution)/shard_map/reduce_scatter | solution.py:343
  1242.1 8.3 copy-start.123
  1260.3 303.7 %reduce-scatter.40.cloned.1.call-start = ((), (), s32[]{:S(2)}) async-start(), calls=%async_computation.33 | async-start | bytes 5734400 | tf_op jit(solution)/shard_map/reduce_scatter | solution.py:340
  1260.3 8.9 copy-start.124
  1279.0 319.7 %reduce-scatter.38.cloned.1.call-start = ((), (), s32[]{:S(2)}) async-start(), calls=%async_computation.32 | async-start | bytes 2580480 | tf_op jit(solution)/shard_map/reduce_scatter | solution.py:375
  1283.2 353.3 %reduce-scatter.36.cloned.1.call-start = ((), (), s32[]{:S(2)}) async-start(), calls=%async_computation.31 | async-start | bytes 2580480 | tf_op jit(solution)/shard_map/reduce_scatter | solution.py:372
  1287.3 391.5 %reduce-scatter.34.cloned.1.call-start = ((), (), s32[]{:S(2)}) async-start(), calls=%async_computation.30 | async-start | bytes 3686400 | tf_op jit(solution)/shard_map/reduce_scatter | solution.py:360
  1292.5 428.6 %reduce-scatter.32.cloned.1.call-start = ((), (), s32[]{:S(2)}) async-start(), calls=%async_computation.29 | async-start | bytes 3686400 | tf_op jit(solution)/shard_map/reduce_scatter | solution.py:357
  1303.8 459.8 %reduce-scatter.30.cloned.1.call-start = ((), (), s32[]{:S(2)}) async-start(), calls=%async_computation.28 | async-start | bytes 3686400 | tf_op jit(solution)/shard_map/reduce_scatter | solution.py:354
  1329.6 476.5 %reduce-scatter.28.cloned.1.call-start = ((), (), s32[]{:S(2)}) async-start(), calls=%async_computation.27 | async-start | bytes 3686400 | tf_op jit(solution)/shard_map/reduce_scatter | solution.py:351
  1334.8 19.8 %copy-start.90 = (f32[1280]{0:T(1024)S(1)}, f32[1280]{0:T(1024)}, u32[]{:S(2)}) copy-start(f32[1280]{0:T(1024)} %get-tuple-element.96) | copy-start | bytes 15364
  1334.8 19.8 %copy-start.91 = (f32[1280]{0:T(1024)S(1)}, f32[1280]{0:T(1024)}, u32[]{:S(2)}) copy-start(f32[1280]{0:T(1024)} %get-tuple-element.94) | copy-start | bytes 15364
  1334.8 560.0 %all-reduce.7.cloned.1.call-start = ((), (), s32[]{:S(2)}) async-start(), calls=%async_computation.42 | async-start | bytes 5341184 | tf_op jit(solution)/shard_map/psum | solution.py:383
  1809.7 30.8 %copy-start.113 = (f32[128]{0:T(128)S(1)}, f32[128]{0:T(128)}, u32[]{:S(2)}) copy-start(f32[128]{0:T(128)} %copy-done.112) | copy-start | bytes 1540
  1809.7 30.8 %copy-start.111 = (f32[128]{0:T(128)S(1)}, f32[128]{0:T(128)}, u32[]{:S(2)}) copy-start(f32[128]{0:T(128)} %copy-done.110) | copy-start | bytes 1540
  1894.7 7.8 copy-start.78
  1894.7 8.7 copy-start.77
  (91 other events, 347.7 us)
Sparse Core Ops, SparseCore 0:
  36.8 34.6 all-gather.6
  73.7 33.1 all-gather.4
  381.9 55.4 all-gather.8
  439.4 70.5 all-gather.10
  1162.6 35.0 reduce-scatter.47
  1199.9 36.6 reduce-scatter.51
  1238.8 36.4 reduce-scatter.49
  1277.6 36.4 reduce-scatter.45
  1317.0 35.6 reduce-scatter.55
  1354.7 29.6 reduce-scatter.53
  1387.8 57.5 reduce-scatter.43
  1448.6 55.9 reduce-scatter.41
  1508.0 55.9 reduce-scatter.39
  1566.3 32.4 reduce-scatter.37
  1601.0 35.3 reduce-scatter.35
  1638.7 40.0 reduce-scatter.33
  1681.0 40.1 reduce-scatter.31
  1723.4 40.1 reduce-scatter.29
  1765.9 40.1 reduce-scatter.27
  1811.0 83.6 all-reduce.6
where the time goes:
time: 1920 us; the launch traced here: 1910 us
  waiting for transfers between devices  1160 us (60%)
  matrix products  346 us (18%)
  local copies, waits for them, and re-layouts  188 us (10%)
  other arithmetic  108 us (6%)
  starting transfers between devices  65.5 us (3%)
  blocking collectives  25.5 us (1%)
    all_to_all x2, waiting for transfers between devices, on_device(): lax.all_to_all(expert_rows.reshape(devices, EXP_DEV * most, D), 'exp', sp...  190 us
    all_to_all x2, waiting for transfers between devices, on_device(): lax.all_to_all(send_grads.reshape(devices, EXP_DEV * most, D), 'exp', spl...  153 us
    all_to_all x2, waiting for transfers between devices, on_device(): lax.all_to_all(send_rows.reshape(devices, EXP_DEV * most, D), 'exp', spli...  146 us
    all_to_all x2, waiting for transfers between devices, on_device(): lax.all_to_all(back_rows, 'exp', split_axis=0, concat_axis=0, tiled=True)  124 us
    reduce_scatter x1, waiting for transfers between devices, on_device(): lax.psum_scatter(sum_routed_down.astype(jnp.bfloat16), 'seq', scatter_dim...  60.1 us
    reduce_scatter x1, waiting for transfers between devices, on_device(): lax.psum_scatter(sum_routed_gate.astype(jnp.bfloat16), 'seq', scatter_dim...  56.5 us
    reduce_scatter x1, waiting for transfers between devices, on_device(): lax.psum_scatter(sum_routed_up.astype(jnp.bfloat16), 'seq', scatter_dimen...  56.4 us
    unnamed x271, local copies, waits for them, and re-layouts  54.4 us
  transfers between devices with their start and end apart: 28, of which 22 were waited for; matrix products, arithmetic and copies ran while one was open for 23% of the time, Pallas kernels for 0%

commit v1 on v0

v1 whole, which is shorter than its diff:
```python
import functools
import math

import jax
import jax.numpy as jnp
from jax import lax
from jax.experimental import pallas as pl
from jax.experimental.pallas import tpu as pltpu
from jax.sharding import PartitionSpec as P

D = 1280
HEADS = 10
HD = 128
FF = 896
TOP = 7
EXP_DEV = 2
MB = 2
SEQ_DEV = 128
LANES = 128
BLOCK = 256
VMEM_BYTES = 60 * 2**20

eps = 1e-06
BF = jnp.bfloat16
F32 = jnp.float32


def norm_rows(inputs, gain):
    return inputs * lax.rsqrt(jnp.mean(inputs * inputs, axis=-1, keepdims=True) + eps) * gain


def norm_back(inputs, gain, grad):
    scale = lax.rsqrt(jnp.mean(inputs * inputs, axis=-1, keepdims=True) + eps)
    unit = inputs * scale
    weighted = grad * gain
    back = scale * (weighted - unit * jnp.mean(weighted * unit, axis=-1, keepdims=True))
    return back, grad * unit


def angle_tables(positions):
    steps_half = jnp.arange(HD // 2).astype(positions.dtype)
    frequency = jnp.exp(steps_half * (-2.0 * math.log(10000.0) / HD))
    angles = positions[:, None] * frequency[None, :]
    angles = jnp.concatenate([angles, angles], axis=-1)
    return (jnp.cos(angles), jnp.sin(angles))


def dot(a, b):
    return jnp.dot(a, b, preferred_element_type=F32)


def dot_nt(a, b):
    return lax.dot_general(a, b, (((1,), (1,)), ((), ())), preferred_element_type=F32)


def dot_tn(a, b):
    return lax.dot_general(a, b, (((0,), (0,)), ((), ())), preferred_element_type=F32)


def gather_exp(array):
    return lax.all_gather(array, "exp", axis=0, tiled=True)


def scatter_exp(array):
    return lax.psum_scatter(array.astype(BF), "exp", scatter_dimension=0, tiled=True).astype(F32)


def turn(heads, cos_table, sin_table):
    return heads * cos_table + pltpu.roll(heads, HD // 2, 1) * sin_table


def visible_scores(queries, keys, start):
    scores = dot_nt(queries, keys) * HD ** (-0.5)
    rows = queries.shape[0]
    row = lax.broadcasted_iota(jnp.int32, (rows, rows), 0)
    column = lax.broadcasted_iota(jnp.int32, (rows, rows), 1)
    last = jnp.where(row >= column, scores[:, start:], -1e30)
    return last if start == 0 else jnp.concatenate([scores[:, :start], last], axis=1)


def attend_forward(slots, rows_ref, gain_ref, cos_ref, sin_ref, w_ref, normed_ref, qkv_ref, mixed_ref, lse_ref):
    length = rows_ref.shape[0]
    step = BLOCK if length <= 2048 else BLOCK // 2

    def project(i, carry):
        part = pl.ds(pl.multiple_of(i * step, step), step)
        normed = norm_rows(rows_ref[part, :].astype(F32), gain_ref[...]).astype(BF)
        normed_ref[part, :] = normed
        for slot in range(slots):
            base = 3 * HD * slot
            qkv = dot(normed, w_ref[:, base : base + 3 * HD])
            for j in range(2):
                turned = turn(qkv[:, j * HD : (j + 1) * HD], cos_ref[part, :], sin_ref[part, :])
                qkv_ref[part, base + j * HD : base + (j + 1) * HD] = turned.astype(BF)
            qkv_ref[part, base + 2 * HD : base + 3 * HD] = qkv[:, 2 * HD :].astype(BF)
        return carry

    lax.fori_loop(0, length // step, project, 0)
    for slot in range(slots):
        base = 3 * HD * slot
        for start in range(0, length, step):
            stop = start + step
            scores = visible_scores(
                qkv_ref[start:stop, base : base + HD], qkv_ref[:stop, base + HD : base + 2 * HD], start
            )
            largest = jnp.max(scores, axis=-1, keepdims=True)
            powers = jnp.exp(scores - largest)
            total = jnp.sum(powers, axis=-1, keepdims=True)
            attention = (powers * (1.0 / total)).astype(BF)
            mixed = dot(attention, qkv_ref[:stop, base + 2 * HD : base + 3 * HD])
            mixed_ref[start:stop, slot * HD : (slot + 1) * HD] = mixed.astype(BF)
            lse_ref[slot, start:stop, :] = largest + jnp.log(total)


def attend_backward(
    slots, mix_ref, normed_ref, qkv_ref, mixed_ref, lse_ref, cos_ref, sin_ref, w_ref, w_out_ref, live_ref,
    out_sum_ref, qkv_sum_ref, grad_ref, raw_ref, d_mixed_ref, d_keys_ref, d_values_ref,
):
    length = mix_ref.shape[0]
    step = BLOCK if length <= 2048 else BLOCK // 2
    factor = HD ** (-0.5)

    def project(i, carry):
        part = pl.ds(pl.multiple_of(i * step, step), step)
        d_mixed_ref[part, :] = (dot_nt(mix_ref[part, :], w_out_ref[...]) * live_ref[...]).astype(BF)
        return carry

    lax.fori_loop(0, length // step, project, 0)
    for slot in range(slots):
        base = 3 * HD * slot
        d_keys_ref[...] = jnp.zeros_like(d_keys_ref)
        d_values_ref[...] = jnp.zeros_like(d_values_ref)
        for start in range(0, length, step):
            stop = start + step
            queries = qkv_ref[start:stop, base : base + HD]
            keys = qkv_ref[:stop, base + HD : base + 2 * HD]
            values = qkv_ref[:stop, base + 2 * HD : base + 3 * HD]
            d_mixed = d_mixed_ref[start:stop, slot * HD : (slot + 1) * HD]
            attention = jnp.exp(visible_scores(queries, keys, start) - lse_ref[slot, start:stop, :])
            d_att = dot_nt(d_mixed, values)
            row_term = jnp.sum(attention * d_att, axis=-1, keepdims=True)
            d_scores = (attention * (d_att - row_term)).astype(BF)
            d_queries = dot(d_scores, keys) * factor
            raw = turn(d_queries, cos_ref[start:stop, :], -sin_ref[start:stop, :])
            raw_ref[start:stop, base : base + HD] = raw.astype(BF)
            d_keys_ref[:stop, :] += dot_tn(d_scores, queries)
            d_values_ref[:stop, :] += dot_tn(attention.astype(BF), d_mixed)
        raw = turn(d_keys_ref[...] * factor, cos_ref[...], -sin_ref[...])
        raw_ref[:, base + HD : base + 2 * HD] = raw.astype(BF)
        raw_ref[:, base + 2 * HD : base + 3 * HD] = d_values_ref[...].astype(BF)

    def give(i, carry):
        part = pl.ds(pl.multiple_of(i * step, step), step)
        grad_ref[part, :] = dot_nt(raw_ref[part, :], w_ref[...]).astype(BF)
        return carry

    lax.fori_loop(0, length // step, give, 0)
    out_sum_ref[...] = dot_tn(mixed_ref[...], mix_ref[...])

    def sums(i, carry):
        part = pl.ds(pl.multiple_of(i * 256, 256), 256)
        qkv_sum_ref[part, :] = dot_tn(normed_ref[:, part], raw_ref[...])
        return carry

    lax.fori_loop(0, D // 256, sums, 0)


def on_device(
    tokens,
    cotangent,
    expert_ids,
    owner_table,
    w_query,
    w_key,
    w_value,
    w_out,
    gain_one,
    gain_two,
    w_router,
    shared_gate,
    shared_up,
    shared_down,
    routed_gate,
    routed_up,
    routed_down,
):
    devices = lax.axis_size("exp")
    groups = lax.axis_size("seq")
    me = lax.axis_index("exp")
    experts = owner_table.shape[0]
    length = SEQ_DEV * devices
    rows_out = D // devices
    slots = -(-HEADS // devices)
    wide = slots * HD
    share = FF // devices
    used = EXP_DEV * FF + share
    padded = -(-used // LANES) * LANES

    head_of = [jnp.minimum(me + slot * devices, HEADS - 1) for slot in range(slots)]
    slot_live = jnp.concatenate(
        [
            jnp.full((HD,), jnp.where(me + slot * devices < HEADS, 1.0, 0.0), F32)
            for slot in range(slots)
        ]
    )

    w_qkv = jnp.concatenate(
        [
            lax.dynamic_slice(weight, (0, head * HD), (D, HD))
            for head in head_of
            for weight in (w_query, w_key, w_value)
        ],
        axis=1,
    )
    w_out_heads = jnp.concatenate(
        [lax.dynamic_slice(w_out, (head * HD, 0), (HD, D)) for head in head_of], axis=0
    )
    cos_table, sin_table = angle_tables(jnp.arange(length).astype(F32))
    sin_table = jnp.where(jnp.arange(HD) < HD // 2, -sin_table, sin_table)
    in_vmem = pl.BlockSpec(memory_space=pltpu.VMEM)
    params = pltpu.CompilerParams(vmem_limit_bytes=VMEM_BYTES)

    def like(*shape, dtype=BF):
        return jax.ShapeDtypeStruct(shape, dtype)

    forward = pl.pallas_call(
        functools.partial(attend_forward, slots),
        out_shape=(
            like(length, D),
            like(length, 3 * wide),
            like(length, wide),
            like(slots, length, 1, dtype=F32),
        ),
        in_specs=[in_vmem] * 5,
        out_specs=(in_vmem,) * 4,
        compiler_params=params,
        name="attend_forward",
    )
    backward = pl.pallas_call(
        functools.partial(attend_backward, slots),
        out_shape=(like(wide, D, dtype=F32), like(D, 3 * wide, dtype=F32), like(length, D)),
        in_specs=[in_vmem] * 10,
        out_specs=(in_vmem,) * 3,
        scratch_shapes=[
            pltpu.VMEM((length, 3 * wide), BF),
            pltpu.VMEM((length, wide), BF),
            pltpu.VMEM((length, HD), F32),
            pltpu.VMEM((length, HD), F32),
        ],
        compiler_params=params,
        name="attend_backward",
    )

    def joined(routed, shared):
        own = lax.dynamic_slice(shared, (0, me * share), (D, share))
        blank = jnp.zeros((D, padded - used), BF)
        return jnp.concatenate([routed[i] for i in range(EXP_DEV)] + [own, blank], axis=1)

    gate_all = joined(routed_gate, shared_gate)
    up_all = joined(routed_up, shared_up)
    down_all = joined(routed_down, shared_down)

    expert_at = jnp.sum(
        (owner_table[:, None] == jnp.arange(experts)[None, :]) * jnp.arange(experts)[:, None],
        axis=0,
    )
    router_rows = jnp.take(w_router, expert_at, axis=1)
    ids_all = lax.all_gather(expert_ids[:, 0], "exp", axis=1, tiled=True)

    first = []
    for micro_batch in range(MB):
        rows_all = gather_exp(tokens[micro_batch, 0])
        normed, qkv, mixed, lse = forward(rows_all, gain_one[None], cos_table, sin_table, w_qkv)
        sent = lax.all_to_all(
            mixed.reshape(devices, SEQ_DEV, wide), "exp", split_axis=0, concat_axis=0, tiled=True
        )
        own_mixed = (
            sent.reshape(devices, SEQ_DEV, slots, HD)
            .transpose(1, 2, 0, 3)
            .reshape(SEQ_DEV, slots * devices * HD)[:, :D]
        )
        rows_in = tokens[micro_batch, 0].astype(F32)
        hidden_one = rows_in + dot(own_mixed, w_out)
        two_low = norm_rows(hidden_one, gain_two).astype(BF)
        two_all = gather_exp(two_low)
        grad_all = gather_exp(cotangent[micro_batch, 0])
        first.append(
            (normed, qkv, mixed, lse, rows_in, hidden_one, two_all, grad_all)
        )

    column = jnp.arange(padded)
    second = []
    for micro_batch in range(MB):
        two_all, grad_all = first[micro_batch][6:]
        logits = dot(two_all, router_rows)
        named = jnp.any(ids_all[micro_batch][:, :, None] == expert_at[None, None, :], axis=1)
        chosen = jnp.where(named, logits, -jnp.inf)
        powers = jnp.where(named, jnp.exp(chosen - jnp.max(chosen, axis=-1, keepdims=True)), 0.0)
        gates = powers / jnp.sum(powers, axis=-1, keepdims=True)
        own_gates = lax.dynamic_slice(gates, (0, me * EXP_DEV), (length, EXP_DEV))
        weight = jnp.where(
            column[None, :] < FF,
            own_gates[:, :1],
            jnp.where(column[None, :] < 2 * FF, own_gates[:, 1:], 1.0),
        )
        gate_part = dot(two_all, gate_all)
        up_part = dot(two_all, up_all)
        down_part = dot(grad_all, down_all)
        sigmoid = jax.nn.sigmoid(gate_part)
        act = gate_part * sigmoid
        hidden = act * up_part
        products = hidden * down_part
        own_grads = jnp.stack(
            [jnp.sum(products[:, i * FF : (i + 1) * FF], axis=1) for i in range(EXP_DEV)], axis=1
        )
        hidden_low = (weight * hidden).astype(BF)
        weighted = weight * down_part
        d_gate = (weighted * up_part * (sigmoid + act * (1.0 - sigmoid))).astype(BF)
        d_up = (weighted * act).astype(BF)
        out_part = scatter_exp(dot_nt(hidden_low, down_all))
        back_part = scatter_exp(dot_nt(d_gate, gate_all) + dot_nt(d_up, up_all))
        gate_grads = lax.all_gather(own_grads, "exp", axis=1, tiled=True)
        grad_logits = (
            gates * (gate_grads - jnp.sum(gates * gate_grads, axis=-1, keepdims=True))
        ).astype(BF)
        second.append((hidden_low, d_gate, d_up, out_part, back_part, grad_logits))

    two_both = jnp.concatenate([f[6] for f in first])
    grad_both = jnp.concatenate([f[7] for f in first])
    gate_sum = dot_tn(two_both, jnp.concatenate([s[1] for s in second]))
    up_sum = dot_tn(two_both, jnp.concatenate([s[2] for s in second]))
    down_sum = dot_tn(grad_both, jnp.concatenate([s[0] for s in second]))

    def routed_sum(total):
        parts = jnp.stack([total[:, i * FF : (i + 1) * FF] for i in range(EXP_DEV)])
        return lax.psum_scatter(
            parts.astype(BF), "seq", scatter_dimension=1, tiled=True
        ).astype(F32)

    def shared_part(total):
        return total[:, EXP_DEV * FF : used]

    outputs_list = []
    grads_list = []
    small = jnp.zeros((D, experts + 2), F32)
    qkv_sum = jnp.zeros((D, 3 * wide), F32)
    out_sum = jnp.zeros((wide, D), F32)
    for micro_batch in range(MB):
        normed, qkv, mixed, lse, rows_in, hidden_one, two_all, _ = first[micro_batch]
        _, _, _, out_part, back_part, grad_logits = second[micro_batch]
        outputs_list.append((hidden_one + out_part).astype(BF))
        own_logits = lax.dynamic_slice(grad_logits, (me * SEQ_DEV, 0), (SEQ_DEV, experts))
        grad_two = back_part + dot_nt(own_logits, router_rows)
        back, gain_terms = norm_back(hidden_one, gain_two, grad_two)
        grad_hidden = cotangent[micro_batch, 0].astype(F32) + back
        own_two = lax.dynamic_slice(two_all, (me * SEQ_DEV, 0), (SEQ_DEV, D))
        router_part = dot_tn(own_two, own_logits)
        mix_all = gather_exp(grad_hidden.astype(BF))
        out_one, qkv_one, grad_part = backward(
            mix_all, normed, qkv, mixed, lse, cos_table, sin_table, w_qkv, w_out_heads, slot_live[None]
        )
        out_sum = out_sum + out_one
        qkv_sum = qkv_sum + qkv_one
        grad_normed = scatter_exp(grad_part)
        back_one, gain_one_terms = norm_back(rows_in, gain_one, grad_normed)
        grads_list.append((grad_hidden + back_one).astype(BF))
        small = small + jnp.concatenate(
            [
                router_part,
                jnp.sum(gain_one_terms, axis=0)[:, None],
                jnp.sum(gain_terms, axis=0)[:, None],
            ],
            axis=1,
        )

    def to_rows(columns):
        parts = columns.astype(BF).reshape(devices, rows_out, columns.shape[1])
        parts = lax.psum_scatter(parts, "seq", scatter_dimension=1, tiled=True)
        return lax.all_to_all(parts, "exp", split_axis=0, concat_axis=0, tiled=True)

    def to_all(rows):
        return lax.all_gather(rows, "seq", axis=0, tiled=True).astype(F32)

    piece = rows_out // groups
    shared_cols = jnp.concatenate([shared_part(t) for t in (gate_sum, up_sum, down_sum)], axis=1)
    shared_rows = to_rows(shared_cols).reshape(devices, piece, 3, share)
    shared_full = to_all(shared_rows.transpose(1, 2, 0, 3).reshape(piece, 3 * FF))
    qkv_rows = to_rows(qkv_sum).reshape(devices, piece, slots, 3, HD)
    qkv_rows = qkv_rows.transpose(1, 3, 2, 0, 4).reshape(piece, 3, slots * devices * HD)
    qkv_full = to_all(qkv_rows[:, :, :D].reshape(piece, 3 * D))
    out_part = lax.psum_scatter(out_sum.astype(BF), "seq", scatter_dimension=1, tiled=True)
    spread = jnp.zeros((slots * devices * HD, D // groups), BF)
    for slot in range(slots):
        spread = lax.dynamic_update_slice(
            spread, out_part[slot * HD : (slot + 1) * HD], ((me + slot * devices) * HD, 0)
        )
    out_rows = lax.psum_scatter(spread[:D], "exp", scatter_dimension=0, tiled=True)
    out_full = lax.all_gather(out_rows, "seq", axis=1, tiled=True).astype(F32)
    small_rows = lax.psum_scatter(
        lax.psum(small, "seq"), "exp", scatter_dimension=0, tiled=True
    )
    place_of = jnp.take(small_rows, owner_table, axis=1)
    return (
        jnp.stack(outputs_list)[:, None],
        jnp.stack(grads_list)[:, None],
        qkv_full[:, :D],
        qkv_full[:, D : 2 * D],
        qkv_full[:, 2 * D :],
        out_full,
        small_rows[:, experts],
        small_rows[:, experts + 1],
        place_of,
        shared_full[:, :FF],
        shared_full[:, FF : 2 * FF],
        shared_full[:, 2 * FF :],
        routed_sum(gate_sum),
        routed_sum(up_sum),
        routed_sum(down_sum),
    )


def solution(mesh):
    rows = P(None, "seq", "exp", None)
    placed = (rows,) * 3 + (P(),) * 11 + (P("exp", None, None),) * 3
    wide = P("exp", None)
    return jax.shard_map(
        on_device,
        mesh=mesh,
        in_specs=placed,
        out_specs=(rows, rows, wide, wide, wide, wide, P("exp"), P("exp"))
        + (wide,) * 4
        + (P("exp", "seq", None),) * 3,
        check_vma=False,
    )
```

time: 1920 us -> 1090 us (0.57)
  waiting for transfers between devices: 1160 us -> 518 us
  matrix products: 346 us -> 184 us
  local copies, waits for them, and re-layouts: 188 us -> 111 us
  Pallas kernels: 0 us -> 67.8 us
  blocking collectives: 25.5 us -> 89.9 us
  starting transfers between devices: 65.5 us -> 18.4 us
  other arithmetic: 108 us -> 69.6 us
    all_to_all x8 -> x3, waiting for transfers between devices: 614 us -> 25.1 us  [the longest x1 20.5 us: on_device(): lax.all_to_all(mixed.reshape(devices, SEQ_DEV, wide), 'exp', split_axis=0...]
    dot_general x76 -> x23, matrix products: 334 us -> 184 us  [the longest x10 78.3 us: dot(): return jnp.dot(a, b, preferred_element_type=F32)]
    reduce_scatter x9 -> x10, waiting for transfers between devices: 405 us -> 313 us  [the longest x3 148 us: routed_sum(): lax.psum_scatter(parts.astype(BF), 'seq', scatter_dimension=1, tiled=True)]
    pallas_call x0 -> x4, Pallas kernels: none -> 67.8 us  [the longest x2 43.3 us: on_device(): backward(mix_all, normed, qkv, mixed, lse, cos_table, sin_table, w_qkv, w...]
    all_gather x0 -> x5, blocking collectives: none -> 57.8 us  [the longest x2 25.6 us: on_device(): gate_grads = lax.all_gather(own_grads, 'exp', axis=1, tiled=True)]
    psum x1 -> x0, waiting for transfers between devices: 51 us -> none  [on_device(): lax.psum(dense_parts[0].astype(jnp.bfloat16), 'seq').astype(jnp.float32)]
    unnamed x26 -> x25, waiting for transfers between devices: 38.6 us -> 87.7 us
    all_to_all x8 -> x3, starting transfers between devices: 64 us -> 17.2 us  [the longest x2 10.6 us: to_rows(): return lax.all_to_all(parts, 'exp', split_axis=0, concat_axis=0, tiled=True)]
  transfers between devices with their start and end apart: 28 -> 25, of which waited for: 22 -> 19; matrix products, arithmetic and copies ran while one was open for 23% -> 27% of each run, Pallas kernels for 0% -> 3%
where the time goes in v1:
time: 1090 us; the launch traced here: 1070 us
  waiting for transfers between devices  518 us (48%)
  matrix products  184 us (17%)
  local copies, waits for them, and re-layouts  111 us (10%)
  blocking collectives  89.9 us (8%)
  other arithmetic  69.6 us (6%)
  Pallas kernels  67.8 us (6%)
  starting transfers between devices  18.4 us (2%)
  between operations  16.1 us (1%)
    reduce_scatter x3, waiting for transfers between devices, routed_sum(): lax.psum_scatter(parts.astype(BF), 'seq', scatter_dimension=1, tiled=True)  148 us
    reduce_scatter x6, waiting for transfers between devices, scatter_exp(): lax.psum_scatter(array.astype(BF), 'exp', scatter_dimension=0, tiled=True)  137 us
    unnamed x25, waiting for transfers between devices  87.7 us
    dot_general x10, matrix products, dot(): return jnp.dot(a, b, preferred_element_type=F32)  78.3 us
    all_gather x8, waiting for transfers between devices, gather_exp(): return lax.all_gather(array, 'exp', axis=0, tiled=True)  78.2 us
    dot_general x8, matrix products, dot_nt(): lax.dot_general(a, b, (((1,), (1,)), ((), ())), preferred_element_type=F32)  57.1 us
    dot_general x5, matrix products, dot_tn(): lax.dot_general(a, b, (((0,), (0,)), ((), ())), preferred_element_type=F32)  48.7 us
    pallas_call x2, Pallas kernels, on_device(): backward(mix_all, normed, qkv, mixed, lse, cos_table, sin_table, w_qkv, w...  43.3 us
  transfers between devices with their start and end apart: 25, of which 19 were waited for; matrix products, arithmetic and copies ran while one was open for 27% of the time, Pallas kernels for 3%

profile of v1, /device:TPU:12, one launch (start us, length us, event | category | flops | bytes accessed | tf_op | source)
XLA Modules:
  0.0 1074.9 jit_solution(14921737846414208229)
XLA Ops:
  21.6 2.9 negate_select_fusion
  24.5 20.1 %all-gather.28.cloned.1.call-done = bf16[1,1,1024,1280]{3,2,1,0:T(8,128)(2,1)} async-done(((bf16[1,1,128,1280]{3,2,1,0:T(8,128)(2,1)}), bf16[1,1,1024,1280]{3,2,1,0:T(8,128)(2,1)}) %all-gather.28.cloned.1.call-update) | async-done | bytes 2621456 | tf_op jit(solution)/shard_map/all_gather | solution.py:61
  44.6 12.3 %attend_forward.2 = (bf16[1024,1280]{1,0:T(8,128)(2,1)}, bf16[1024,768]{1,0:T(8,128)(2,1)}, bf16[1024,256]{1,0:T(8,128)(2,1)}, f32[2,1024,1]{2,1,0:T(8,128)}) custom-call(bf16[1024,1280]{1,0:T(8,128)(2,1)} %bitcast.202, f32[1,1280]{1,0:T(1,128)} %broadcast_in_dim.166.gain_ref, f32[1024,128]{1,0:T(8,128)} %get-tuple-element.178.cos_ref, ...), custom_call_target="tpu_custom_call" | custom-call | tf_op jit(solution)/shard_map/attend_forward/pallas_call | solution.py:273
  58.2 16.7 %all_to_all.20 = bf16[8,128,256]{1,2,0:T(8,128)(2,1)S(1)} all-to-all(bf16[8,128,256]{1,2,0:T(8,128)(2,1)S(1)} %copy.76), channel_id=1, replica_groups=mesh['seq'=4,'exp'=8] {'exp'}, dimensions={0} | all-to-all | bytes 1048576 | tf_op jit(solution)/shard_map/all_to_all | solution.py:274
  82.2 4.8 slice_bitcast_fusion.10
  87.0 5.2 slice_bitcast_fusion.8
  92.1 4.8 slice_bitcast_fusion.6
  97.0 11.5 %all-gather.1 = s32[2,1,1024,7]{2,1,3,0:T(1,128)S(1)} all-gather(s32[2,1,128,7]{2,1,3,0:T(1,128)S(1)} %copy-done.37), channel_id=3, replica_groups=mesh['seq'=4,'exp'=8] {'exp'}, dimensions={2}, use_global_device_ids=true | all-gather | bytes 64512 | tf_op jit(solution)/shard_map/all_gather | solution.py:268
  112.8 7.4 concatenate.55
  120.2 8.4 concatenate.56
  128.6 7.6 concatenate.57
  136.2 10.7 fusion.90
  146.9 7.7 fusion.91
  154.6 14.5 %bitcast_multiply_fusion.2 = (f32[1024,1920]{1,0:T(8,128)S(1)}, f32[1920,1024]{0,1:T(8,128)}) fusion(f32[1024,1920]{1,0:T(8,128)} %fusion.91, f32[1024,1920]{1,0:T(8,128)} %fusion.90, bf16[1280,1920]{1,0:T(8,128)(2,1)} %concatenate.57, bf16[1,1,1024,1280]{3,2,1,0:T(8,128)(2,1)} %all-gather.32.cloned.1.call-done), kind=kOutput, calls=%fused_computation.16 | convolution fusion | flops 5044961280 | bytes 38993920 | tf_op jit(solution)/shard_map/dot_general | solution.py:49
  169.5 12.5 %all-gather.5 = f32[8,2,1024]{2,1,0:T(2,128)S(1)} all-gather(f32[1,2,1024]{2,1,0:T(2,128)S(1)} %maximum_bitcast_fusion.2), channel_id=1, replica_groups=mesh['seq'=4,'exp'=8] {'exp'}, dimensions={0}, use_global_device_ids=true | all-gather | bytes 73728 | tf_op jit(solution)/shard_map/all_gather | solution.py:322
  184.9 12.8 %multiply_convert_fusion.2 = (bf16[1024,1920]{1,0:T(8,128)(2,1)S(1)}, bf16[1024,1920]{1,0:T(8,128)(2,1)S(1)}, bf16[1024,1920]{1,0:T(8,128)(2,1)}) fusion(f32[1920,1024]{0,1:T(8,128)} %get-tuple-element.193, f32[1024]{0:T(1024)S(1)} %bitcast.224, f32[1024]{0:T(1024)S(1)} %bitcast.223, pred[1920]{0:T(1024)(128)(4,1)S(1)} %get-tuple-element.208, ...), kind=kLoop, calls=%fused_computation.20 | loop fusion | flops 35389440 | bytes 35401472 | tf_op jit(solution)/shard_map/convert_element_type | solution.py:319
  197.8 5.6 fusion.94
  203.5 6.9 add_convert_fusion.1
  210.4 12.3 %attend_forward.3 = (bf16[1024,1280]{1,0:T(8,128)(2,1)}, bf16[1024,768]{1,0:T(8,128)(2,1)}, bf16[1024,256]{1,0:T(8,128)(2,1)}, f32[2,1024,1]{2,1,0:T(8,128)}) custom-call(bf16[1024,1280]{1,0:T(8,128)(2,1)} %bitcast.201, f32[1,1280]{1,0:T(1,128)} %broadcast_in_dim.166.gain_ref, f32[1024,128]{1,0:T(8,128)} %get-tuple-element.178.cos_ref, ...), custom_call_target="tpu_custom_call" | custom-call | tf_op jit(solution)/shard_map/attend_forward/pallas_call | solution.py:273
  224.8 6.6 all-to-all-start.1
  231.7 20.5 %all-to-all-done.1 = bf16[8,128,256]{1,2,0:T(8,128)(2,1)S(1)} async-done(((bf16[8,128,256]{1,2,0:T(8,128)(2,1)}), bf16[8,128,256]{1,2,0:T(8,128)(2,1)S(1)}, u32[]{:S(2)}, u32[]{:S(2)}) %all-to-all-start.1) | async-done | bytes 524320 | tf_op jit(solution)/shard_map/all_to_all | solution.py:274
  255.5 2.9 multiply_reduce_fusion.1
  259.2 34.0 %all-gather.20.cloned.1.call-done = bf16[1024,1280]{1,0:T(8,128)(2,1)} async-done(((bf16[128,1280]{1,0:T(8,128)(2,1)}), bf16[1024,1280]{1,0:T(8,128)(2,1)}) %all-gather.20.cloned.1.call-update) | async-done | bytes 2621456 | tf_op jit(solution)/shard_map/all_gather | solution.py:61
  293.2 10.6 fusion.92
  303.8 10.1 fusion.93
  313.9 13.8 %all-gather.34.cloned.1.call-done = bf16[1,1,1024,1280]{3,2,1,0:T(8,128)(2,1)} async-done(((bf16[1,1,128,1280]{3,2,1,0:T(8,128)(2,1)}), bf16[1,1,1024,1280]{3,2,1,0:T(8,128)(2,1)}) %all-gather.34.cloned.1.call-update) | async-done | bytes 2621456 | tf_op jit(solution)/shard_map/all_gather | solution.py:61
  327.8 14.1 %bitcast_multiply_fusion = (f32[1024,1920]{1,0:T(8,128)S(1)}, f32[1920,1024]{0,1:T(8,128)}) fusion(f32[1024,1920]{1,0:T(8,128)} %fusion.93, f32[1024,1920]{1,0:T(8,128)} %fusion.92, bf16[1280,1920]{1,0:T(8,128)(2,1)} %concatenate.57, bf16[1,1,1024,1280]{3,2,1,0:T(8,128)(2,1)} %all-gather.34.cloned.1.call-done), kind=kOutput, calls=%fused_computation.14 | convolution fusion | flops 5044961280 | bytes 38993920 | tf_op jit(solution)/shard_map/dot_general | solution.py:49
  342.3 13.2 %all-gather.6 = f32[8,2,1024]{2,1,0:T(2,128)S(1)} all-gather(f32[1,2,1024]{2,1,0:T(2,128)S(1)} %maximum_bitcast_fusion.3), channel_id=1, replica_groups=mesh['seq'=4,'exp'=8] {'exp'}, dimensions={0}, use_global_device_ids=true | all-gather | bytes 73728 | tf_op jit(solution)/shard_map/all_gather | solution.py:322
  358.1 12.2 %multiply_convert_fusion = (bf16[1024,1920]{1,0:T(8,128)(2,1)S(1)}, bf16[1024,1920]{1,0:T(8,128)(2,1)S(1)}, bf16[1024,1920]{1,0:T(8,128)(2,1)}) fusion(f32[1920,1024]{0,1:T(8,128)} %get-tuple-element.200, f32[1024]{0:T(1024)S(1)} %bitcast.222, f32[1024]{0:T(1024)S(1)} %bitcast.221, pred[1920]{0:T(1024)(128)(4,1)S(1)} %get-tuple-element.208, ...), kind=kLoop, calls=%fused_computation.18 | loop fusion | flops 35389440 | bytes 35401472 | tf_op jit(solution)/shard_map/convert_element_type | solution.py:319
  370.3 10.8 %fusion.95 = f32[1024,1280]{1,0:T(8,128)S(1)} fusion(bf16[1024,1920]{1,0:T(8,128)(2,1)S(1)} %get-tuple-element.146, bf16[1280,1920]{1,0:T(8,128)(2,1)} %concatenate.55), kind=kOutput, calls=%fused_computation.216 | convolution fusion | flops 5033164800 | bytes 14090240 | tf_op jit(solution)/shard_map/dot_general | solution.py:53
  381.2 9.4 add_convert_fusion
  390.6 9.9 convolution_convert_fusion
  400.7 24.3 %reduce-scatter.27.cloned.1.call-done = bf16[128,1280]{1,0:T(8,128)(2,1)} async-done(((bf16[1024,1280]{1,0:T(8,128)(2,1)}), bf16[128,1280]{1,0:T(8,128)(2,1)}) %reduce-scatter.27.cloned.1.call-update) | async-done | bytes 327696 | tf_op jit(solution)/shard_map/reduce_scatter | solution.py:65
  426.5 37.5 %reduce-scatter.21.cloned.1.call-done = bf16[128,1280]{1,0:T(8,128)(2,1)} async-done(((bf16[1024,1280]{1,0:T(8,128)(2,1)}), bf16[128,1280]{1,0:T(8,128)(2,1)}) %reduce-scatter.21.cloned.1.call-update) | async-done | bytes 327696 | tf_op jit(solution)/shard_map/reduce_scatter | solution.py:65
  469.4 3.5 constant_dynamic-update-slice_fusion.1
  476.4 15.0 %fusion.15 = bf16[1280,1920]{1,0:T(8,128)(2,1)} fusion(bf16[2048,1280]{1,0:T(8,128)(2,1)} %constant_dynamic-update-slice_fusion, bf16[1024,1920]{1,0:T(8,128)(2,1)S(1)} %copy-done.22, bf16[1024,1920]{1,0:T(8,128)(2,1)S(1)} %copy-done.18), kind=kOutput, calls=%fused_computation.29 | convolution fusion | flops 10084515840 | bytes 18022400 | tf_op jit(solution)/shard_map/dot_general | solution.py:57
  491.4 14.7 %fusion.18 = bf16[1280,1920]{1,0:T(8,128)(2,1)} fusion(bf16[2048,1280]{1,0:T(8,128)(2,1)} %constant_dynamic-update-slice_fusion, bf16[1024,1920]{1,0:T(8,128)(2,1)S(1)} %copy-done.20, bf16[1024,1920]{1,0:T(8,128)(2,1)S(1)} %copy-done.16), kind=kOutput, calls=%fused_computation.30 | convolution fusion | flops 10084515840 | bytes 18022400 | tf_op jit(solution)/shard_map/dot_general | solution.py:57
  506.1 21.8 %attend_backward.3 = (f32[256,1280]{1,0:T(8,128)}, f32[1280,768]{1,0:T(8,128)}, bf16[1024,1280]{1,0:T(8,128)(2,1)}) custom-call(bf16[1024,1280]{1,0:T(8,128)(2,1)} %all-gather.24.cloned.1.call-done.mix_ref, bf16[1024,1280]{1,0:T(8,128)(2,1)} %get-tuple-element.35.normed_ref, bf16[1024,768]{1,0:T(8,128)(2,1)} %get-tuple-element.36.qkv_ref, ...), custom_call_target="tpu_custom_call" | custom-call | tf_op jit(solution)/shard_map/attend_backward/pallas_call | solution.py:359
  527.9 10.2 all-gather.22.cloned.1.call-done.mix_ref
  538.1 21.4 %attend_backward.2 = (f32[256,1280]{1,0:T(8,128)}, f32[1280,768]{1,0:T(8,128)}, bf16[1024,1280]{1,0:T(8,128)(2,1)}) custom-call(bf16[1024,1280]{1,0:T(8,128)(2,1)} %all-gather.22.cloned.1.call-done.mix_ref, bf16[1024,1280]{1,0:T(8,128)(2,1)} %get-tuple-element.31.normed_ref, bf16[1024,768]{1,0:T(8,128)(2,1)} %get-tuple-element.32.qkv_ref, ...), custom_call_target="tpu_custom_call" | custom-call | tf_op jit(solution)/shard_map/attend_backward/pallas_call | solution.py:359
  562.6 15.3 %fusion.12 = bf16[1280,1920]{1,0:T(8,128)(2,1)S(1)} fusion(bf16[1024,1920]{1,0:T(8,128)(2,1)} %get-tuple-element.147, bf16[1024,1920]{1,0:T(8,128)(2,1)} %get-tuple-element.144, bf16[1024,1280]{1,0:T(8,128)(2,1)} %bitcast.234, bf16[1024,1280]{1,0:T(8,128)(2,1)} %bitcast.233), kind=kOutput, calls=%fused_computation.28 | convolution fusion | flops 10095001600 | bytes 18022400 | tf_op jit(solution)/shard_map/dot_general | solution.py:57
  582.2 4.0 add_convert_fusion.2
  586.2 2.8 slice_bitcast_fusion.1
  597.0 3.5 slice_bitcast_fusion.5
  607.2 10.1 convolution_convert_fusion.1
  619.9 55.9 %all-reduce.6.cloned.1.call-done = (bf16[8,160,768]{2,1,0:T(8,128)(2,1)}, bf16[8,160,336]{2,1,0:T(8,128)(2,1)}) async-done(((bf16[8,160,768]{2,1,0:T(8,128)(2,1)}, bf16[8,160,336]{2,1,0:T(8,128)(2,1)}), (bf16[8,160,768]{2,1,0:T(8,128)(2,1)}, bf16[8,160,336]{2,1,0:T(8,128)(2,1)})) %all-reduce.6.cloned.1.call-update) | async-done | bytes 2826256
  677.5 5.1 all-to-all-start.3
  685.6 4.6 all-to-all-done.3
  690.1 5.5 all-to-all-start.2
  699.3 35.5 %reduce-scatter.37.cloned.1.call-done = bf16[2,320,896]{2,1,0:T(8,128)(2,1)} async-done(((bf16[2,1280,896]{2,1,0:T(8,128)(2,1)}), bf16[2,320,896]{2,1,0:T(8,128)(2,1)}) %reduce-scatter.37.cloned.1.call-update) | async-done | bytes 1146896 | tf_op jit(solution)/shard_map/reduce_scatter | solution.py:336
  734.8 2.8 convert_element_type.177
  737.6 56.1 %reduce-scatter.35.cloned.1.call-done = bf16[2,320,896]{2,1,0:T(8,128)(2,1)} async-done(((bf16[2,1280,896]{2,1,0:T(8,128)(2,1)}), bf16[2,320,896]{2,1,0:T(8,128)(2,1)}) %reduce-scatter.35.cloned.1.call-update) | async-done | bytes 1146896 | tf_op jit(solution)/shard_map/reduce_scatter | solution.py:336
  793.7 2.8 convert_element_type.176
  796.5 56.1 %reduce-scatter.33.cloned.1.call-done = bf16[2,320,896]{2,1,0:T(8,128)(2,1)} async-done(((bf16[2,1280,896]{2,1,0:T(8,128)(2,1)}), bf16[2,320,896]{2,1,0:T(8,128)(2,1)}) %reduce-scatter.33.cloned.1.call-update) | async-done | bytes 1146896 | tf_op jit(solution)/shard_map/reduce_scatter | solution.py:336
  852.6 2.8 convert_element_type.175
  855.4 28.0 %reduce-scatter.31.cloned.1.call-done = bf16[160,320]{1,0:T(8,128)(2,1)} async-done(((bf16[1280,320]{1,0:T(8,128)(2,1)}), bf16[160,320]{1,0:T(8,128)(2,1)}) %reduce-scatter.31.cloned.1.call-update) | async-done | bytes 102416 | tf_op jit(solution)/shard_map/reduce_scatter | solution.py:397
  883.4 9.9 all-gather.7
  900.4 10.8 %all_gather.55 = bf16[160,2688]{1,0:T(8,128)(2,1)S(1)} all-gather(bf16[40,2688]{1,0:T(8,128)(2,1)S(1)} %reshape.187), channel_id=1, replica_groups=mesh['seq'=4,'exp'=8] {'seq'}, dimensions={0}, use_global_device_ids=true | all-gather | bytes 1075200 | tf_op jit(solution)/shard_map/all_gather | solution.py:382
  916.0 5.1 reduce-scatter.29.cloned.1.call-done
  921.1 39.0 %reduce-scatter.25.cloned.1.call-done = bf16[128,1280]{1,0:T(8,128)(2,1)} async-done(((bf16[1024,1280]{1,0:T(8,128)(2,1)}), bf16[128,1280]{1,0:T(8,128)(2,1)}) %reduce-scatter.25.cloned.1.call-update) | async-done | bytes 327696 | tf_op jit(solution)/shard_map/reduce_scatter | solution.py:65
  967.8 31.0 %reduce-scatter.19.cloned.1.call-done = bf16[128,1280]{1,0:T(8,128)(2,1)} async-done(((bf16[1024,1280]{1,0:T(8,128)(2,1)}), bf16[128,1280]{1,0:T(8,128)(2,1)}) %reduce-scatter.19.cloned.1.call-update) | async-done | bytes 327696 | tf_op jit(solution)/shard_map/reduce_scatter | solution.py:65
  1003.5 29.0 %reduce-scatter.41.cloned.1.call-done = f32[160,18]{1,0:T(8,128)} async-done(((f32[1280,18]{1,0:T(8,128)}), f32[160,18]{1,0:T(8,128)}) %reduce-scatter.41.cloned.1.call-update) | async-done | bytes 11536
  1033.5 15.4 %psum.8 = f32[160,18]{0,1:T(8,128)S(1)} all-reduce(f32[160,18]{0,1:T(8,128)S(1)} %copy.97), channel_id=1, replica_groups=mesh['seq'=4,'exp'=8] {'seq'}, use_global_device_ids=true, to_apply=%region_34.35 | all-reduce | flops 2880 | bytes 23040 | tf_op jit(solution)/shard_map/psum | solution.py:400
  1050.9 14.2 %all-gather.26.cloned.1.call-done = bf16[160,3840]{1,0:T(8,128)(2,1)} async-done(((bf16[40,3840]{1,0:T(8,128)(2,1)}), bf16[160,3840]{1,0:T(8,128)(2,1)}) %all-gather.26.cloned.1.call-update) | async-done | bytes 1228816 | tf_op jit(solution)/shard_map/all_gather | solution.py:382
  (275 shorter events, 112.1 us)
Async XLA Ops:
  7.2 101.3 %copy-start = (bf16[1280,896]{1,0:T(8,128)(2,1)S(1)}, bf16[1280,896]{1,0:T(8,128)(2,1)}, u32[]{:S(2)}) copy-start(bf16[1280,896]{1,0:T(8,128)(2,1)} %param.30) | copy-start | bytes 6881284
  7.2 37.4 %all-gather.28.cloned.1.call-start = ((), (), s32[]{:S(2)}) async-start(), calls=%async_computation.31 | async-start | bytes 2949120 | tf_op jit(solution)/shard_map/all_gather | solution.py:61
  9.4 126.8 %all-gather.18.cloned.1.call-start = ((), (), s32[]{:S(2)}) async-start(), calls=%async_computation.16 | async-start | bytes 2949120 | tf_op jit(solution)/shard_map/all_gather | solution.py:61
  44.6 30.4 %copy-start.3 = (bf16[2,1,128,1280]{3,2,1,0:T(8,128)(2,1)S(1)}, bf16[2,1,128,1280]{3,2,1,0:T(8,128)(2,1)}, u32[]{:S(2)}) copy-start(bf16[2,1,128,1280]{3,2,1,0:T(8,128)(2,1)} %param.17) | copy-start | bytes 1966084
  56.9 21.6 %copy-start.29 = (f32[1280]{0:T(1024)S(1)}, f32[1280]{0:T(1024)}, u32[]{:S(2)}) copy-start(f32[1280]{0:T(1024)} %param.26) | copy-start | bytes 15364
  77.7 386.4 %copy-start.35 = (f32[128]{0:T(128)}, f32[128]{0:T(128)S(1)}, u32[]{:S(2)}) copy-start(f32[128]{0:T(128)S(1)} %add_rsqrt_fusion.3) | copy-start | bytes 1540
  79.3 75.2 %all-gather.32.cloned.1.call-start = ((), (), s32[]{:S(2)}) async-start(), calls=%async_computation.33 | async-start | bytes 2949120 | tf_op jit(solution)/shard_map/all_gather | solution.py:61
  81.4 129.0 %all-gather.30.cloned.1.call-start = ((), (), s32[]{:S(2)}) async-start(), calls=%async_computation.32 | async-start | bytes 2949120 | tf_op jit(solution)/shard_map/all_gather | solution.py:61
  82.0 173.5 %reduce-scatter.23.cloned.1.call-start = ((), (), s32[]{:S(2)}) async-start(), calls=%async_computation.20 | async-start | bytes 2949120 | tf_op jit(solution)/shard_map/reduce_scatter | solution.py:65
  92.1 20.0 %copy-start.2 = (bf16[1280,16]{0,1:T(8,128)(2,1)S(1)}, bf16[1280,16]{0,1:T(8,128)(2,1)}, u32[]{:S(2)}) copy-start(bf16[1280,16]{0,1:T(8,128)(2,1)} %param.27) | copy-start | bytes 122884
  136.2 10.7 copy-start.14
  182.0 73.5 %copy-start.27 = (f32[16,1024]{1,0:T(8,128)}, f32[16,1024]{1,0:T(8,128)S(1)}, u32[]{:S(2)}) copy-start(f32[16,1024]{1,0:T(8,128)S(1)} %reshape.219) | copy-start | bytes 196612
  182.0 15.7 %slice-start.2 = ((s8[4915200]{0:T(1024)(128)(4,1)}), s8[4194304]{0:T(1024)(128)(4,1)S(1)}, s32[]{:S(2)}) async-start(s8[4915200]{0:T(1024)(128)(4,1)} %bitcast.197), calls=%async_computation.40 | async-start | bytes 8388608
  182.1 21.4 %slice-start.4 = ((s8[4915200]{0:T(1024)(128)(4,1)}), s8[4194304]{0:T(1024)(128)(4,1)S(1)}, s32[]{:S(2)}) async-start(s8[4915200]{0:T(1024)(128)(4,1)} %bitcast.199), calls=%async_computation.42 | async-start | bytes 8388608
  184.9 70.6 %copy-start.31 = (f32[1024,16]{0,1:T(8,128)}, f32[1024,16]{0,1:T(8,128)S(1)}, u32[]{:S(2)}) copy-start(f32[1024,16]{0,1:T(8,128)S(1)} %get-tuple-element.139) | copy-start | bytes 196612
  184.9 12.9 %slice-start.3 = ((s8[4915200]{0:T(1024)(128)(4,1)}), s8[720896]{0:T(1024)(128)(4,1)S(1)}, s32[]{:S(2)}) async-start(s8[4915200]{0:T(1024)(128)(4,1)} %bitcast.197), calls=%async_computation.41 | async-start | bytes 1441792
  184.9 18.5 %slice-start.5 = ((s8[4915200]{0:T(1024)(128)(4,1)}), s8[720896]{0:T(1024)(128)(4,1)S(1)}, s32[]{:S(2)}) async-start(s8[4915200]{0:T(1024)(128)(4,1)} %bitcast.199), calls=%async_computation.43 | async-start | bytes 1441792
  222.7 32.8 %copy-start.6 = (f32[128,1280]{1,0:T(8,128)S(1)}, f32[128,1280]{1,0:T(8,128)}, u32[]{:S(2)}) copy-start(f32[128,1280]{1,0:T(8,128)} %copy-done.5) | copy-start | bytes 1966084
  224.8 27.4 %all-to-all-start.1 = ((bf16[8,128,256]{1,2,0:T(8,128)(2,1)}), bf16[8,128,256]{1,2,0:T(8,128)(2,1)S(1)}, u32[]{:S(2)}, u32[]{:S(2)}) async-start(bf16[8,128,256]{1,2,0:T(8,128)(2,1)} %copy.78), calls=%async_computation.2 | async-start | bytes 1048576 | tf_op jit(solution)/shard_map/all_to_all | solution.py:274
  231.4 61.8 %all-gather.20.cloned.1.call-start = ((), (), s32[]{:S(2)}) async-start(), calls=%async_computation.18 | async-start | bytes 2949120 | tf_op jit(solution)/shard_map/all_gather | solution.py:61
  254.9 209.1 %copy-start.34 = (f32[128]{0:T(128)}, f32[128]{0:T(128)S(1)}, u32[]{:S(2)}) copy-start(f32[128]{0:T(128)S(1)} %add_rsqrt_fusion.2) | copy-start | bytes 1540
  255.0 48.8 %copy-start.41 = (f32[128]{0:T(128)}, f32[128]{0:T(128)S(1)}, u32[]{:S(2)}) copy-start(f32[128]{0:T(128)S(1)} %dynamic-slice.8) | copy-start | bytes 1540
  258.4 69.4 %all-gather.34.cloned.1.call-start = ((), (), s32[]{:S(2)}) async-start(), calls=%async_computation.34 | async-start | bytes 2949120 | tf_op jit(solution)/shard_map/all_gather | solution.py:61
  259.2 165.9 %reduce-scatter.27.cloned.1.call-start = ((), (), s32[]{:S(2)}) async-start(), calls=%async_computation.23 | async-start | bytes 2949120 | tf_op jit(solution)/shard_map/reduce_scatter | solution.py:65
  358.1 66.9 %copy-start.32 = (f32[1024,16]{0,1:T(8,128)}, f32[1024,16]{0,1:T(8,128)S(1)}, u32[]{:S(2)}) copy-start(f32[1024,16]{0,1:T(8,128)S(1)} %get-tuple-element.141) | copy-start | bytes 196612
  370.3 10.9 %copy-start.19 = (bf16[1024,1920]{1,0:T(8,128)(2,1)}, bf16[1024,1920]{1,0:T(8,128)(2,1)S(1)}, u32[]{:S(2)}) copy-start(bf16[1024,1920]{1,0:T(8,128)(2,1)S(1)} %get-tuple-element.146) | copy-start | bytes 11796484
  370.3 10.9 %copy-start.21 = (bf16[1024,1920]{1,0:T(8,128)(2,1)}, bf16[1024,1920]{1,0:T(8,128)(2,1)S(1)}, u32[]{:S(2)}) copy-start(bf16[1024,1920]{1,0:T(8,128)(2,1)S(1)} %get-tuple-element.145) | copy-start | bytes 11796484
  390.6 73.5 %reduce-scatter.21.cloned.1.call-start = ((), (), s32[]{:S(2)}) async-start(), calls=%async_computation.19 | async-start | bytes 2949120 | tf_op jit(solution)/shard_map/reduce_scatter | solution.py:65
  400.5 63.5 %copy-start.12 = (bf16[2,1,128,1280]{3,2,1,0:T(8,128)(2,1)S(1)}, bf16[2,1,128,1280]{3,2,1,0:T(8,128)(2,1)}, u32[]{:S(2)}) copy-start(bf16[2,1,128,1280]{3,2,1,0:T(8,128)(2,1)} %param.18) | copy-start | bytes 1966084
  400.6 105.5 %all-gather.24.cloned.1.call-start = ((), (), s32[]{:S(2)}) async-start(), calls=%async_computation.24 | async-start | bytes 2949120 | tf_op jit(solution)/shard_map/all_gather | solution.py:61
  400.6 67.6 %copy-start.39 = (f32[128]{0:T(128)}, f32[128]{0:T(128)S(1)}, u32[]{:S(2)}) copy-start(f32[128]{0:T(128)S(1)} %broadcast_multiply_fusion.4) | copy-start | bytes 1540
  426.5 42.7 %copy-start.38 = (f32[128]{0:T(128)}, f32[128]{0:T(128)S(1)}, u32[]{:S(2)}) copy-start(f32[128]{0:T(128)S(1)} %broadcast_multiply_fusion.2) | copy-start | bytes 1540
  466.5 71.6 %all-gather.22.cloned.1.call-start = ((), (), s32[]{:S(2)}) async-start(), calls=%async_computation.21 | async-start | bytes 2949120 | tf_op jit(solution)/shard_map/all_gather | solution.py:61
  469.2 134.1 %reduce-scatter.39.cloned.1.call-start = ((), (), s32[]{:S(2)}) async-start(), calls=%async_computation.35 | async-start | bytes 819200
  476.4 15.0 %copy-start.16 = (bf16[1024,1920]{1,0:T(8,128)(2,1)S(1)}, bf16[1024,1920]{1,0:T(8,128)(2,1)}, u32[]{:S(2)}) copy-start(bf16[1024,1920]{1,0:T(8,128)(2,1)} %copy-done.15) | copy-start | bytes 11796484
  476.4 15.0 %copy-start.20 = (bf16[1024,1920]{1,0:T(8,128)(2,1)S(1)}, bf16[1024,1920]{1,0:T(8,128)(2,1)}, u32[]{:S(2)}) copy-start(bf16[1024,1920]{1,0:T(8,128)(2,1)} %copy-done.19) | copy-start | bytes 11796484
  562.5 113.3 %all-reduce.6.cloned.1.call-start = ((), (), s32[]{:S(2)}) async-start(), calls=%async_computation.37 | async-start | bytes 5898240
  562.6 15.4 %slice-start = ((bf16[1280,1920]{1,0:T(8,128)(2,1)}), bf16[1280,112]{1,0:T(8,128)(2,1)S(1)}, s32[]{:S(2)}) async-start(bf16[1280,1920]{1,0:T(8,128)(2,1)} %fusion.18), calls=%async_computation.38 | async-start | bytes 655360 | tf_op jit(solution)/shard_map/slice | solution.py:341
  562.6 15.4 %slice-start.1 = ((bf16[1280,1920]{1,0:T(8,128)(2,1)}), bf16[1280,112]{1,0:T(8,128)(2,1)S(1)}, s32[]{:S(2)}) async-start(bf16[1280,1920]{1,0:T(8,128)(2,1)} %fusion.15), calls=%async_computation.39 | async-start | bytes 655360 | tf_op jit(solution)/shard_map/slice | solution.py:341
  586.2 148.6 %reduce-scatter.37.cloned.1.call-start = ((), (), s32[]{:S(2)}) async-start(), calls=%async_computation.30 | async-start | bytes 5734400 | tf_op jit(solution)/shard_map/reduce_scatter | solution.py:336
  591.6 202.1 %reduce-scatter.35.cloned.1.call-start = ((), (), s32[]{:S(2)}) async-start(), calls=%async_computation.29 | async-start | bytes 5734400 | tf_op jit(solution)/shard_map/reduce_scatter | solution.py:336
  597.0 255.6 %reduce-scatter.33.cloned.1.call-start = ((), (), s32[]{:S(2)}) async-start(), calls=%async_computation.28 | async-start | bytes 5734400 | tf_op jit(solution)/shard_map/reduce_scatter | solution.py:336
  603.2 280.2 %reduce-scatter.31.cloned.1.call-start = ((), (), s32[]{:S(2)}) async-start(), calls=%async_computation.27 | async-start | bytes 1105920 | tf_op jit(solution)/shard_map/reduce_scatter | solution.py:397
  605.8 315.3 %reduce-scatter.29.cloned.1.call-start = ((), (), s32[]{:S(2)}) async-start(), calls=%async_computation.25 | async-start | bytes 2949120 | tf_op jit(solution)/shard_map/reduce_scatter | solution.py:65
  606.3 353.8 %reduce-scatter.25.cloned.1.call-start = ((), (), s32[]{:S(2)}) async-start(), calls=%async_computation.22 | async-start | bytes 2949120 | tf_op jit(solution)/shard_map/reduce_scatter | solution.py:65
  607.1 11.5 %copy-start.4 = (bf16[2,1,128,1280]{3,2,1,0:T(8,128)(2,1)S(1)}, bf16[2,1,128,1280]{3,2,1,0:T(8,128)(2,1)}, u32[]{:S(2)}) copy-start(bf16[2,1,128,1280]{3,2,1,0:T(8,128)(2,1)} %param.17) | copy-start | bytes 1966084
  607.1 11.7 %copy-start.46 = (s32[16]{0:T(128)S(1)}, s32[16]{0:T(128)}, u32[]{:S(2)}) copy-start(s32[16]{0:T(128)} %param.20) | copy-start | bytes 196
  607.1 391.7 %reduce-scatter.19.cloned.1.call-start = ((), (), s32[]{:S(2)}) async-start(), calls=%async_computation.17 | async-start | bytes 2949120 | tf_op jit(solution)/shard_map/reduce_scatter | solution.py:65
  617.3 78.3 %copy-start.42 = (f32[128]{0:T(128)S(1)}, f32[128]{0:T(128)}, u32[]{:S(2)}) copy-start(f32[128]{0:T(128)} %copy-done.41) | copy-start | bytes 1540
  617.3 80.1 %copy-start.33 = (f32[1280]{0:T(1024)S(1)}, f32[1280]{0:T(1024)}, u32[]{:S(2)}) copy-start(f32[1280]{0:T(1024)} %get-tuple-element.124) | copy-start | bytes 15364
  677.5 12.7 %all-to-all-start.3 = ((bf16[8,40,336]{2,1,0:T(8,128)(2,1)}), bf16[8,40,336]{2,1,0:T(8,128)(2,1)S(1)}, u32[]{:S(2)}, u32[]{:S(2)}) async-start(bf16[8,40,336]{2,1,0:T(8,128)(2,1)} %constant_dynamic-slice_fusion.9), calls=%async_computation.10 | async-start | bytes 491520 | tf_op jit(solution)/shard_map/all_to_all | solution.py:379
  690.1 106.4 %copy-start.26 = (bf16[8,40,336]{2,1,0:T(8,128)(2,1)}, bf16[8,40,336]{2,1,0:T(8,128)(2,1)S(1)}, u32[]{:S(2)}) copy-start(bf16[8,40,336]{2,1,0:T(8,128)(2,1)S(1)} %all-to-all-done.3) | copy-start | bytes 645124
  690.1 222.3 %all-to-all-start.2 = ((bf16[8,40,768]{2,1,0:T(8,128)(2,1)}), bf16[8,40,768]{2,1,0:T(8,128)(2,1)S(1)}, u32[]{:S(2)}, u32[]{:S(2)}) async-start(bf16[8,40,768]{2,1,0:T(8,128)(2,1)} %constant_dynamic-slice_fusion.10), calls=%async_computation.8 | async-start | bytes 983040 | tf_op jit(solution)/shard_map/all_to_all | solution.py:379
  695.6 336.9 %reduce-scatter.41.cloned.1.call-start = ((), (), s32[]{:S(2)}) async-start(), calls=%async_computation.36 | async-start | bytes 737280
  900.4 59.7 %copy-start.30 = (f32[1280]{0:T(1024)S(1)}, f32[1280]{0:T(1024)}, u32[]{:S(2)}) copy-start(f32[1280]{0:T(1024)} %param.25) | copy-start | bytes 15364
  911.2 50.6 %copy-start.28 = (f32[1280,16]{0,1:T(8,128)S(1)}, f32[1280,16]{0,1:T(8,128)}, u32[]{:S(2)}) copy-start(f32[1280,16]{0,1:T(8,128)} %fusion.55) | copy-start | bytes 245764
  916.0 82.8 %copy-start.36 = (f32[128]{0:T(128)S(1)}, f32[128]{0:T(128)}, u32[]{:S(2)}) copy-start(f32[128]{0:T(128)} %copy-done.35) | copy-start | bytes 1540
  916.0 82.8 %copy-start.40 = (f32[128]{0:T(128)S(1)}, f32[128]{0:T(128)}, u32[]{:S(2)}) copy-start(f32[128]{0:T(128)} %copy-done.39) | copy-start | bytes 1540
  916.0 82.8 %copy-start.43 = (f32[128]{0:T(128)S(1)}, f32[128]{0:T(128)}, u32[]{:S(2)}) copy-start(f32[128]{0:T(128)} %add_rsqrt_fusion.1) | copy-start | bytes 1540
  921.1 44.6 %copy-start.25 = (bf16[128,1280]{1,0:T(8,128)(2,1)S(1)}, bf16[128,1280]{1,0:T(8,128)(2,1)}, u32[]{:S(2)}) copy-start(bf16[128,1280]{1,0:T(8,128)(2,1)} %reduce-scatter.29.cloned.1.call-done) | copy-start | bytes 983044
  963.8 101.2 %all-gather.26.cloned.1.call-start = ((), (), s32[]{:S(2)}) async-start(), calls=%async_computation.26 | async-start | bytes 1536000 | tf_op jit(solution)/shard_map/all_gather | solution.py:382
  965.6 37.0 %copy-start.24 = (bf16[1,128,1280]{2,1,0:T(8,128)(2,1)S(1)}, bf16[1,128,1280]{2,1,0:T(8,128)(2,1)}, u32[]{:S(2)}) copy-start(bf16[1,128,1280]{2,1,0:T(8,128)(2,1)} %get-tuple-element.170) | copy-start | bytes 983044
  967.8 82.4 %copy-start.44 = (pred[16]{0:T(512)(128)(4,1)S(1)}, pred[16]{0:T(512)(128)(4,1)}, u32[]{:S(2)}) copy-start(pred[16]{0:T(512)(128)(4,1)} %compare_and_fusion) | copy-start | bytes 52
  1000.6 67.2 %copy-start.1 = (bf16[1280,896]{1,0:T(8,128)(2,1)S(1)}, bf16[1280,896]{1,0:T(8,128)(2,1)}, u32[]{:S(2)}) copy-start(bf16[1280,896]{1,0:T(8,128)(2,1)} %param.30) | copy-start | bytes 6881284
  (15 other events, 92.0 us)
Sparse Core Ops, SparseCore 0:
  10.2 34.3 all-gather.27
  79.5 34.3 all-gather.17
  115.5 32.8 all-gather.31
  150.5 33.3 all-gather.29
  210.5 44.9 reduce-scatter.22
  258.5 34.6 all-gather.19
  294.9 32.8 all-gather.33
  390.7 34.3 reduce-scatter.26
  427.4 36.6 reduce-scatter.20
  466.6 36.3 all-gather.23
  505.2 32.8 all-gather.21
  562.6 25.0 reduce-scatter.38
  591.8 83.9 all-reduce.5
  678.8 56.0 reduce-scatter.36
  737.7 55.9 reduce-scatter.34
  796.6 55.9 reduce-scatter.32
  854.7 28.5 reduce-scatter.30
  885.6 35.3 reduce-scatter.28
  923.5 36.5 reduce-scatter.24
  962.4 36.3 reduce-scatter.18
  1001.7 30.7 reduce-scatter.40
  1035.1 29.9 all-gather.25

commit v2 on v1

--- a/solution.py
+++ b/solution.py
@@ -163,6 +163,755 @@
         return carry
 
     lax.fori_loop(0, D // 256, sums, 0)
+
+
+MESH = pl.DeviceIdType.MESH
+
+
+def place():
+    me = lax.axis_index("exp")
+    return me // 2, me % 2
+
+
+def remote(source, target, send_sem, recv_sem, chip, core):
+    return pltpu.make_async_remote_copy(
+        src_ref=source,
+        dst_ref=target,
+        send_sem=send_sem,
+        recv_sem=recv_sem,
+        device_id={"exp": 2 * chip + core},
+        device_id_type=MESH,
+    )
+
+
+def meet(chips):
+    chip, core = place()
+    barrier = pltpu.get_barrier_semaphore()
+
+    def greet(to_chip, to_core):
+        pl.semaphore_signal(
+            barrier, inc=1, device_id={"exp": 2 * to_chip + to_core}, device_id_type=MESH
+        )
+
+    greet(chip, 1 - core)
+
+    @pl.when(chip < chips - 1)
+    def _():
+        greet(chip + 1, core)
+
+    @pl.when(chip > 0)
+    def _():
+        greet(chip - 1, core)
+
+    below = (chip + chips - 1) // chips
+    above = (2 * chips - 2 - chip) // chips
+    pl.semaphore_wait(barrier, 1 + below + above)
+
+
+def gather_sems(chips):
+    return [pltpu.SemaphoreType.DMA((chips,))] * 4 + [pltpu.SemaphoreType.DMA((2 * chips,))] * 2
+
+
+class Gather:
+    def __init__(self, chips, own, blocks, sems):
+        self.chips, self.own, self.blocks = chips, own, blocks
+        self.up_send, self.up_recv, self.down_send, self.down_recv = sems[:4]
+        self.pair_send, self.pair_recv = sems[4:]
+
+    def _source(self, hop, number):
+        return self.own if hop == 0 else self.blocks.at[number]
+
+    def _up(self, hop):
+        chip, core = place()
+        number = 2 * (chip - hop) + core
+        return remote(
+            self._source(hop, number), self.blocks.at[number],
+            self.up_send.at[hop], self.up_recv.at[hop], chip + 1, core,
+        )
+
+    def _down(self, hop):
+        chip, core = place()
+        number = 2 * (chip + hop) + core
+        return remote(
+            self._source(hop, number), self.blocks.at[number],
+            self.down_send.at[hop], self.down_recv.at[hop], chip - 1, core,
+        )
+
+    def _pair(self, away):
+        chip, core = place()
+        number = 2 * (chip + away) + core
+        source = self.own if isinstance(away, int) and away == 0 else self.blocks.at[number]
+        slot = away + self.chips
+        return remote(
+            source, self.blocks.at[number], self.pair_send.at[slot], self.pair_recv.at[slot],
+            chip, 1 - core,
+        )
+
+    def _from_pair(self, away):
+        chip, core = place()
+        block = self.blocks.at[2 * (chip + away) + 1 - core]
+        slot = away + self.chips
+        return remote(
+            block, block, self.pair_send.at[slot], self.pair_recv.at[slot], chip, 1 - core
+        )
+
+    def start(self):
+        chip, _ = place()
+
+        @pl.when(chip < self.chips - 1)
+        def _():
+            self._up(0).start()
+
+        @pl.when(chip > 0)
+        def _():
+            self._down(0).start()
+
+        self._pair(0).start()
+
+    def hop(self, hop):
+        chip, core = place()
+
+        @pl.when(chip >= hop)
+        def _():
+            block = self.blocks.at[2 * (chip - hop) + core]
+            remote(
+                block, block, self.up_send.at[hop - 1], self.up_recv.at[hop - 1], chip, 1 - core
+            ).wait_recv()
+
+            @pl.when(chip < self.chips - 1)
+            def _():
+                self._up(hop).start()
+
+            self._pair(-hop).start()
+
+        @pl.when(chip + hop < self.chips)
+        def _():
+            block = self.blocks.at[2 * (chip + hop) + core]
+            remote(
+                block, block, self.down_send.at[hop - 1], self.down_recv.at[hop - 1], chip, 1 - core
+            ).wait_recv()
+
+            @pl.when(chip > 0)
+            def _():
+                self._down(hop).start()
+
+            self._pair(hop).start()
+
+    def take_pair(self, away):
+        self._from_pair(away).wait_recv()
+
+    def finish(self, pairs):
+        chip, _ = place()
+        for away in range(-self.chips + 1, self.chips):
+
+            @pl.when(jnp.logical_and(chip + away >= 0, chip + away < self.chips))
+            def _():
+                if pairs:
+                    self._from_pair(away).wait_recv()
+                self._pair(away).wait_send()
+
+        for hop in range(self.chips):
+
+            @pl.when(jnp.logical_and(chip >= hop, chip < self.chips - 1))
+            def _():
+                self._up(hop).wait_send()
+
+            @pl.when(jnp.logical_and(chip + hop < self.chips, chip > 0))
+            def _():
+                self._down(hop).wait_send()
+
+
+def scatter_sems(chips):
+    return [pltpu.SemaphoreType.DMA((chips,))] * 6
+
+
+class Scatter:
+    def __init__(self, chips, theirs, mine, pair, line, sems):
+        self.chips, self.theirs, self.mine, self.pair, self.line = chips, theirs, mine, pair, line
+        self.pair_send, self.pair_recv, self.up_send, self.up_recv = sems[:4]
+        self.down_send, self.down_recv = sems[4:]
+
+    def _pair(self, to):
+        chip, core = place()
+        return remote(
+            self.theirs(to), self.pair.at[to], self.pair_send.at[to], self.pair_recv.at[to],
+            chip, 1 - core,
+        )
+
+    def _up(self, chip, to):
+        return remote(
+            self.mine(to), self.line.at[to - chip - 1], self.up_send.at[to], self.up_recv.at[to],
+            chip + 1, place()[1],
+        )
+
+    def _down(self, chip, to):
+        return remote(
+            self.mine(to), self.line.at[self.chips - chip + 1 + to],
+            self.down_send.at[to], self.down_recv.at[to], chip - 1, place()[1],
+        )
+
+    def _arrived_up(self, to):
+        chip, core = place()
+        block = self.line.at[to - chip]
+        remote(block, block, self.up_send.at[to], self.up_recv.at[to], chip, 1 - core).wait_recv()
+        return block[...].astype(F32)
+
+    def _arrived_down(self, to):
+        chip, core = place()
+        block = self.line.at[self.chips - chip + to]
+        remote(
+            block, block, self.down_send.at[to], self.down_recv.at[to], chip, 1 - core
+        ).wait_recv()
+        return block[...].astype(F32)
+
+    def _both(self, to):
+        chip, core = place()
+        block = self.pair.at[to]
+        remote(
+            block, block, self.pair_send.at[to], self.pair_recv.at[to], chip, 1 - core
+        ).wait_recv()
+        return self.mine(to)[...].astype(F32) + block[...].astype(F32)
+
+    def start(self):
+        for to in range(self.chips):
+            self._pair(to).start()
+
+    def slot(self, turn):
+        chip, _ = place()
+        last = self.chips - 1
+
+        @pl.when(chip <= turn)
+        def _():
+            to = last - turn + chip
+            total = self._both(to)
+
+            @pl.when(chip == 0)
+            def _():
+                self.mine(to)[...] = total.astype(BF)
+
+            @pl.when(chip > 0)
+            def _():
+                self.mine(to)[...] = (total + self._arrived_up(to)).astype(BF)
+
+            self._up(chip, to).start()
+
+        @pl.when(last - chip <= turn)
+        def _():
+            to = turn - last + chip
+            total = self._both(to)
+
+            @pl.when(chip == last)
+            def _():
+                self.mine(to)[...] = total.astype(BF)
+
+            @pl.when(chip < last)
+            def _():
+                self.mine(to)[...] = (total + self._arrived_down(to)).astype(BF)
+
+            self._down(chip, to).start()
+
+    def finish(self, result):
+        chip, _ = place()
+        last = self.chips - 1
+        result[...] = self._both(chip)
+
+        @pl.when(chip > 0)
+        def _():
+            result[...] += self._arrived_up(chip)
+
+        @pl.when(chip < last)
+        def _():
+            result[...] += self._arrived_down(chip)
+
+        for to in range(self.chips):
+            self._pair(to).wait_send()
+
+            @pl.when(to > chip)
+            def _():
+                self._up(chip, to).wait_send()
+
+            @pl.when(to < chip)
+            def _():
+                self._down(chip, to).wait_send()
+
+
+def part_of(array, index):
+    return array.at[index]
+
+
+def block_order(chip, turn, chips):
+    number, bit = 0, 1
+    while bit < chips:
+        number = number + bit * ((chip // bit + turn // bit) % 2)
+        bit = 2 * bit
+    return number
+
+
+def expert_rows(
+    chips, experts,
+    own_ref, grad_ref, named_ref, router_ref, routed_refs, shared_refs,
+    rows_ref, hidden_ref, d_gate_ref, d_up_ref, out_b_ref, back_b_ref, out_a_ref, back_a_ref,
+    weights, rows, grads, stage, out, back, pairs, lines, weight_sem, local_sem, grad_sem, stage_sem, keep_sem,
+    *sems,
+):
+    chip, core = place()
+    me = 2 * chip + core
+    blocks = chips
+    size = 2 * SEQ_DEV
+    gathers = [Gather(chips, own_ref.at[m], rows.at[m], sems[6 * m : 6 * m + 6]) for m in range(MB)]
+    parts = (out, back)
+    scatters = [
+        Scatter(
+            chips,
+            lambda to, k=k: parts[k].at[0, 2 * to + 1 - core],
+            lambda to, k=k: parts[k].at[0, 2 * to + core],
+            pairs[k], lines[k], sems[12 + 6 * k : 18 + 6 * k],
+        )
+        for k in range(2)
+    ]
+    loads = []
+    for k in range(3):
+        for e in range(EXP_DEV):
+            loads.append(
+                pltpu.make_async_copy(
+                    routed_refs[k].at[e], weights.at[k, :, e * FF : (e + 1) * FF],
+                    weight_sem.at[k, e],
+                )
+            )
+        loads.append(
+            pltpu.make_async_copy(
+                shared_refs[k], weights.at[k, :, EXP_DEV * FF :], weight_sem.at[k, EXP_DEV]
+            )
+        )
+
+    def grad_load(step):
+        block = block_order(chip, step % blocks, chips)
+        start = pl.multiple_of(block * size, size)
+        return pltpu.make_async_copy(
+            grad_ref.at[step // blocks, pl.ds(start, size), :], grads.at[step % 2],
+            grad_sem.at[step % 2],
+        )
+
+    def stage_out(step, k):
+        block = block_order(chip, step % blocks, chips)
+        start = pl.multiple_of((step // blocks * blocks + block) * size, size)
+        target = (hidden_ref, d_gate_ref, d_up_ref)[k]
+        return pltpu.make_async_copy(
+            stage.at[step % 2, k], target.at[pl.ds(start, size), :], stage_sem.at[step % 2, k]
+        )
+
+    def keep_out(step, k):
+        block = block_order(chip, step % blocks, chips)
+        target = (out_b_ref, back_b_ref)[k]
+        return pltpu.make_async_copy(
+            parts[k].at[1, pl.ds(2 * block, 2)], target.at[pl.ds(2 * block, 2)],
+            keep_sem.at[k, step % blocks],
+        )
+
+    grad_load(0).start()
+    for load in loads:
+        load.start()
+    own_copies = [
+        pltpu.make_async_copy(own_ref.at[m], rows.at[m, me], local_sem.at[m]) for m in range(MB)
+    ]
+    for copy in own_copies:
+        copy.start()
+    meet(chips)
+    gathers[0].start()
+    for copy in own_copies:
+        copy.wait()
+    for load in loads:
+        load.wait()
+
+    def at(step, number, action):
+        @pl.when(step == number)
+        def _():
+            action()
+
+    def body(step, carry):
+        micro_batch = step // blocks
+        block = block_order(chip, step % blocks, chips)
+        for m in range(MB):
+            for hop in range(1, chips):
+                at(step, m * blocks + hop, lambda m=m, hop=hop: gathers[m].hop(hop))
+        at(step, 1, gathers[1].start)
+        at(step, blocks, lambda: [s.start() for s in scatters])
+        for turn in range(chips - 1):
+            at(step, blocks + 1 + turn, lambda turn=turn: scatters[1].slot(turn))
+        for m in range(MB):
+
+            @pl.when(micro_batch == m)
+            def _():
+                gathers[m].take_pair(block - chip)
+
+        grad_load(step).wait()
+
+        @pl.when(step + 1 < MB * blocks)
+        def _():
+            grad_load(step + 1).start()
+
+        @pl.when(step >= 2)
+        def _():
+            for k in range(3):
+                stage_out(step - 2, k).wait()
+
+        slot = step % 2
+        normed = rows[micro_batch, pl.ds(2 * block, 2)].reshape(size, D)
+        grad = grads[slot]
+        logits = dot(normed, router_ref[...])
+        named = named_ref[pl.ds(pl.multiple_of((micro_batch * blocks + block) * size, size), size), :]
+        chosen = jnp.where(named > 0.0, logits, -1e30)
+        powers = jnp.where(
+            named > 0.0, jnp.exp(chosen - jnp.max(chosen, axis=1, keepdims=True)), 0.0
+        )
+        gates = powers / jnp.sum(powers, axis=1, keepdims=True)
+        lane = lax.broadcasted_iota(jnp.int32, (size, LANES), 1)
+        own = [
+            jnp.sum(jnp.where(lane == EXP_DEV * me + e, gates, 0.0), axis=1, keepdims=True)
+            for e in range(EXP_DEV)
+        ]
+        gate_grads = [jnp.zeros((size, 1), F32) for _ in range(EXP_DEV)]
+        wide = weights.shape[2]
+        for left in range(0, wide, 512):
+            right = min(left + 512, wide)
+            gate_part = dot(normed, weights[0, :, left:right])
+            up_part = dot(normed, weights[1, :, left:right])
+            down_part = dot(grad, weights[2, :, left:right])
+            sigmoid = 1.0 / (1.0 + jnp.exp(-gate_part))
+            act = gate_part * sigmoid
+            hidden = act * up_part
+            product = hidden * down_part
+            scales = []
+            for e in range(EXP_DEV + 1):
+                low, high = max(left, e * FF), min(right, (e + 1) * FF)
+                if low >= high:
+                    continue
+                if e < EXP_DEV:
+                    gate_grads[e] += jnp.sum(
+                        product[:, low - left : high - left], axis=1, keepdims=True
+                    )
+                    scales.append(jnp.broadcast_to(own[e], (size, high - low)))
+                else:
+                    scales.append(jnp.ones((size, high - low), F32))
+            scale = scales[0] if len(scales) == 1 else jnp.concatenate(scales, axis=1)
+            scaled = down_part * scale
+            stage[slot, 0, :, left:right] = (hidden * scale).astype(BF)
+            stage[slot, 1, :, left:right] = (
+                scaled * up_part * (sigmoid + act * (1.0 - sigmoid))
+            ).astype(BF)
+            stage[slot, 2, :, left:right] = (scaled * act).astype(BF)
+        for k in range(3):
+            stage_out(step, k).start()
+        for turn in range(chips - 1):
+            at(step, blocks + turn, lambda turn=turn: scatters[0].slot(turn))
+        result = dot_nt(stage[slot, 0], weights[2]).astype(BF)
+        out[micro_batch, pl.ds(2 * block, 2)] = result.reshape(2, SEQ_DEV, D)
+        result = (dot_nt(stage[slot, 1], weights[0]) + dot_nt(stage[slot, 2], weights[1])).astype(BF)
+        back[micro_batch, pl.ds(2 * block, 2), :, :D] = result.reshape(2, SEQ_DEV, D)
+        tail = jnp.zeros((size, LANES), F32)
+        for e in range(EXP_DEV):
+            high = gate_grads[e].astype(BF).astype(F32)
+            tail = jnp.where(lane == EXP_DEV * me + e, high, tail)
+            tail = jnp.where(lane == experts + EXP_DEV * me + e, gate_grads[e] - high, tail)
+        back[micro_batch, pl.ds(2 * block, 2), :, D:] = tail.astype(BF).reshape(2, SEQ_DEV, LANES)
+
+        @pl.when(micro_batch == 1)
+        def _():
+            for k in range(2):
+                keep_out(step, k).start()
+
+        return carry
+
+    lax.fori_loop(0, MB * blocks, body, 0)
+    last = MB * blocks
+    row_copies = [
+        pltpu.make_async_copy(rows.at[m], rows_ref.at[m], local_sem.at[m]) for m in range(MB)
+    ]
+    for copy in row_copies:
+        copy.start()
+    scatters[0].finish(out_a_ref)
+    scatters[1].finish(back_a_ref)
+    for m in range(MB):
+        gathers[m].finish(False)
+    for copy in row_copies:
+        copy.wait()
+    for step in (last - 2, last - 1):
+        for k in range(3):
+            stage_out(step, k).wait()
+    for turn in range(blocks):
+        for k in range(2):
+            keep_out(blocks + turn, k).wait()
+
+
+def expert_sums(
+    chips,
+    rows_ref, grads_ref, hidden_ref, d_gate_ref, d_up_ref, shared_h_ref, shared_g_ref, shared_u_ref, out_ref, back_ref,
+    gate_ref, up_ref, down_ref, shared_ref, out_b_ref, back_b_ref,
+    mine_out, mine_back, pairs, lines, local_sem, *sems,
+):
+    chip, core = place()
+    step = pl.program_id(0) * (D // 256) + pl.program_id(1)
+    parts, mine = (out_ref, back_ref), (mine_out, mine_back)
+    scatters = [
+        Scatter(
+            chips,
+            lambda to, k=k: parts[k].at[2 * to + 1 - core],
+            lambda to, k=k: mine[k].at[to],
+            pairs[k], lines[k], sems[6 * k : 6 * k + 6],
+        )
+        for k in range(2)
+    ]
+
+    def at(number, action):
+        @pl.when(step == number)
+        def _():
+            action()
+
+    def begin():
+        loads = [
+            pltpu.make_async_copy(
+                parts[k].at[2 * to + core], mine[k].at[to], local_sem.at[k, to]
+            )
+            for k in range(2)
+            for to in range(chips)
+        ]
+        for load in loads:
+            load.start()
+        meet(chips)
+        for s in scatters:
+            s.start()
+        for load in loads:
+            load.wait()
+
+    at(0, begin)
+    ticks = [(k, turn) for turn in range(chips - 1) for k in range(2)]
+    for number, (k, turn) in enumerate(ticks):
+        at(min(number + 1, 7), lambda k=k, turn=turn: scatters[k].slot(turn))
+    normed, grad = rows_ref[...], grads_ref[...]
+    gate_ref[0] = dot_tn(normed, d_gate_ref[...]).astype(BF)
+    up_ref[0] = dot_tn(normed, d_up_ref[...]).astype(BF)
+    down_ref[0] = dot_tn(grad, hidden_ref[...]).astype(BF)
+
+    @pl.when(pl.program_id(0) == 0)
+    def _():
+        start = pl.ds(pl.multiple_of(pl.program_id(1) * 256, 256), 256)
+        shared_ref[0, start, :] = dot_tn(normed, shared_g_ref[...])
+        shared_ref[1, start, :] = dot_tn(normed, shared_u_ref[...])
+        shared_ref[2, start, :] = dot_tn(grad, shared_h_ref[...])
+
+    at(8, lambda: scatters[0].finish(out_b_ref))
+    at(9, lambda: scatters[1].finish(back_b_ref))
+
+
+def like(*shape, dtype=BF):
+    return jax.ShapeDtypeStruct(shape, dtype)
+
+
+IN_VMEM = pl.BlockSpec(memory_space=pltpu.VMEM)
+ANYWHERE = pl.BlockSpec(memory_space=pl.ANY)
+
+
+def experts_on_lines(two_own, grad_all, ids_all, expert_at, router_rows, routed, shared, share):
+    devices = lax.axis_size("exp")
+    me = lax.axis_index("exp")
+    experts = expert_at.shape[0]
+    chips = devices // 2
+    length = SEQ_DEV * devices
+    wide = EXP_DEV * FF + LANES
+    own_shared = [
+        jnp.pad(lax.dynamic_slice(w, (0, me * share), (D, share)), ((0, 0), (0, LANES - share)))
+        for w in shared
+    ]
+    spare = jnp.full((LANES - experts,), -1, jnp.int32)
+    columns = jnp.concatenate([expert_at.astype(jnp.int32), spare])
+    named = jnp.any(ids_all[..., None] == columns, axis=2).astype(F32).reshape(MB * length, LANES)
+    router = jnp.pad(router_rows, ((0, 0), (0, LANES - experts)))
+    block_back = (devices, SEQ_DEV, D + LANES)
+    block_out = (devices, SEQ_DEV, D)
+    sems = [gather_sems(chips) for _ in range(MB)] + [scatter_sems(chips) for _ in range(2)]
+
+    def call_rows(own, grad, names, router_in, *weights):
+        def kernel(own_ref, grad_ref, named_ref, router_ref, *refs):
+            expert_rows(
+                chips, experts, own_ref, grad_ref, named_ref, router_ref, refs[:3], refs[3:6], *refs[6:]
+            )
+
+        return pl.pallas_call(
+            kernel,
+            out_shape=(
+                like(MB, devices, SEQ_DEV, D),
+                like(MB * length, wide),
+                like(MB * length, wide),
+                like(MB * length, wide),
+                like(*block_out),
+                like(*block_back),
+                like(SEQ_DEV, D, dtype=F32),
+                like(SEQ_DEV, D + LANES, dtype=F32),
+            ),
+            in_specs=[IN_VMEM, ANYWHERE, IN_VMEM, IN_VMEM] + [ANYWHERE] * 6,
+            out_specs=(ANYWHERE,) * 6 + (IN_VMEM,) * 2,
+            scratch_shapes=[
+                pltpu.VMEM((3, D, wide), BF),
+                pltpu.VMEM((MB, devices, SEQ_DEV, D), BF),
+                pltpu.VMEM((2, 2 * SEQ_DEV, D), BF),
+                pltpu.VMEM((2, 3, 2 * SEQ_DEV, wide), BF),
+                pltpu.VMEM((MB, *block_out), BF),
+                pltpu.VMEM((MB, *block_back), BF),
+                (
+                    pltpu.VMEM((chips, SEQ_DEV, D), BF),
+                    pltpu.VMEM((chips, SEQ_DEV, D + LANES), BF),
+                ),
+                (
+                    pltpu.VMEM((chips + 1, SEQ_DEV, D), BF),
+                    pltpu.VMEM((chips + 1, SEQ_DEV, D + LANES), BF),
+                ),
+                pltpu.SemaphoreType.DMA((3, EXP_DEV + 1)),
+                pltpu.SemaphoreType.DMA((MB,)),
+                pltpu.SemaphoreType.DMA((2,)),
+                pltpu.SemaphoreType.DMA((2, 3)),
+                pltpu.SemaphoreType.DMA((2, chips)),
+            ]
+            + [sem for group in sems for sem in group],
+            compiler_params=pltpu.CompilerParams(
+                collective_id=1, has_side_effects=True, vmem_limit_bytes=VMEM_BYTES
+            ),
+            name="expert_rows",
+        )(own, grad, names, router_in, *weights)
+
+    rows, hidden, d_gate, d_up, out_b, back_b, out_sum_a, back_sum_a = call_rows(
+        two_own, grad_all, named, router, *routed, *own_shared
+    )
+    flat = MB * length
+
+    def call_sums(*operands):
+        def kernel(*refs):
+            expert_sums(chips, *refs)
+
+        by_rows = pl.BlockSpec((flat, 256), lambda e, d: (0, d))
+        by_expert = pl.BlockSpec((flat, FF), lambda e, d: (0, e))
+        last = pl.BlockSpec((flat, LANES), lambda e, d: (0, EXP_DEV * FF // LANES))
+        routed_out = pl.BlockSpec((1, 256, FF), lambda e, d: (e, d, 0))
+
+        def whole(*shape):
+            return pl.BlockSpec(shape, lambda e, d: (0,) * len(shape))
+
+        return pl.pallas_call(
+            kernel,
+            grid=(EXP_DEV, D // 256),
+            out_shape=(like(EXP_DEV, D, FF),) * 3
+            + (
+                like(3, D, LANES, dtype=F32),
+                like(SEQ_DEV, D, dtype=F32),
+                like(SEQ_DEV, D + LANES, dtype=F32),
+            ),
+            in_specs=[by_rows] * 2 + [by_expert] * 3 + [last] * 3 + [ANYWHERE] * 2,
+            out_specs=(routed_out,) * 3
+            + (whole(3, D, LANES), whole(SEQ_DEV, D), whole(SEQ_DEV, D + LANES)),
+            scratch_shapes=[
+                pltpu.VMEM((chips, SEQ_DEV, D), BF),
+                pltpu.VMEM((chips, SEQ_DEV, D + LANES), BF),
+                (
+                    pltpu.VMEM((chips, SEQ_DEV, D), BF),
+                    pltpu.VMEM((chips, SEQ_DEV, D + LANES), BF),
+                ),
+                (
+                    pltpu.VMEM((chips + 1, SEQ_DEV, D), BF),
+                    pltpu.VMEM((chips + 1, SEQ_DEV, D + LANES), BF),
+                ),
+                pltpu.SemaphoreType.DMA((2, chips)),
+            ]
+            + scatter_sems(chips) * 2,
+            compiler_params=pltpu.CompilerParams(
+                collective_id=2, has_side_effects=True, vmem_limit_bytes=VMEM_BYTES
+            ),
+            name="expert_sums",
+        )(*operands)
+
+    gate_sum, up_sum, down_sum, shared_sum, out_sum_b, back_sum_b = call_sums(
+        rows.reshape(flat, D), grad_all.reshape(flat, D), hidden, d_gate, d_up, hidden, d_gate, d_up,
+        out_b, back_b,
+    )
+    backs = (back_sum_a, back_sum_b)
+    tails = [
+        b[:, D : D + experts] + b[:, D + experts : D + 2 * experts] for b in backs
+    ]
+    shared_cols = jnp.concatenate([shared_sum[k, :, :share] for k in range(3)], axis=1)
+    return (
+        (out_sum_a, out_sum_b),
+        [b[:, :D] for b in backs],
+        tails,
+        (gate_sum, up_sum, down_sum),
+        shared_cols,
+    )
+
+
+def experts_plain(two_own, grad_all, ids_all, expert_at, router_rows, routed, shared, share):
+    me = lax.axis_index("exp")
+    used = EXP_DEV * FF + share
+    padded = -(-used // LANES) * LANES
+    length = grad_all.shape[1]
+
+    def joined(weight, extra):
+        own = lax.dynamic_slice(extra, (0, me * share), (D, share))
+        blank = jnp.zeros((D, padded - used), BF)
+        return jnp.concatenate([weight[i] for i in range(EXP_DEV)] + [own, blank], axis=1)
+
+    gate_all, up_all, down_all = [joined(r, s) for r, s in zip(routed, shared)]
+    column = jnp.arange(padded)
+    all_rows, kept, outs, backs, tails = [], [], [], [], []
+    for micro_batch in range(MB):
+        two_all = gather_exp(two_own[micro_batch])
+        all_rows.append(two_all)
+        logits = dot(two_all, router_rows)
+        named = jnp.any(ids_all[micro_batch][:, :, None] == expert_at[None, None, :], axis=1)
+        gates = named_softmax(logits, named)
+        own_gates = lax.dynamic_slice(gates, (0, me * EXP_DEV), (length, EXP_DEV))
+        weight = jnp.where(
+            column[None, :] < FF,
+            own_gates[:, :1],
+            jnp.where(column[None, :] < 2 * FF, own_gates[:, 1:], 1.0),
+        )
+        gate_part = dot(two_all, gate_all)
+        up_part = dot(two_all, up_all)
+        down_part = dot(grad_all[micro_batch], down_all)
+        sigmoid = jax.nn.sigmoid(gate_part)
+        act = gate_part * sigmoid
+        hidden = act * up_part
+        products = hidden * down_part
+        own_grads = jnp.stack(
+            [jnp.sum(products[:, i * FF : (i + 1) * FF], axis=1) for i in range(EXP_DEV)], axis=1
+        )
+        hidden_low = (weight * hidden).astype(BF)
+        weighted = weight * down_part
+        d_gate = (weighted * up_part * (sigmoid + act * (1.0 - sigmoid))).astype(BF)
+        d_up = (weighted * act).astype(BF)
+        kept.append((hidden_low, d_gate, d_up))
+        outs.append(scatter_exp(dot_nt(hidden_low, down_all)))
+        backs.append(scatter_exp(dot_nt(d_gate, gate_all) + dot_nt(d_up, up_all)))
+        gate_grads = lax.all_gather(own_grads, "exp", axis=1, tiled=True)
+        tails.append(
+            lax.dynamic_slice(
+                gate_grads, (me * SEQ_DEV, 0), (SEQ_DEV, gate_grads.shape[1])
+            )
+        )
+    two_both = jnp.concatenate(all_rows)
+    hidden_low, d_gate, d_up = [jnp.concatenate([k[i] for k in kept]) for i in range(3)]
+    sums = (
+        dot_tn(two_both, d_gate),
+        dot_tn(two_both, d_up),
+        dot_tn(grad_all.reshape(MB * length, D), hidden_low),
+    )
+    routed_sums = [
+        jnp.stack([t[:, i * FF : (i + 1) * FF] for i in range(EXP_DEV)]).astype(BF) for t in sums
+    ]
+    shared_cols = jnp.concatenate([t[:, EXP_DEV * FF : used] for t in sums], axis=1)
+    return outs, backs, tails, routed_sums, shared_cols
+
+
+def named_softmax(logits, named):
+    chosen = jnp.where(named, logits, -jnp.inf)
+    powers = jnp.where(named, jnp.exp(chosen - jnp.max(chosen, axis=-1, keepdims=True)), 0.0)
+    return powers / jnp.sum(powers, axis=-1, keepdims=True)
 
 
 def on_device(
@@ -193,8 +942,6 @@
     slots = -(-HEADS // devices)
     wide = slots * HD
     share = FF // devices
-    used = EXP_DEV * FF + share
-    padded = -(-used // LANES) * LANES
 
     head_of = [jnp.minimum(me + slot * devices, HEADS - 1) for slot in range(slots)]
     slot_live = jnp.concatenate(
@@ -217,12 +964,7 @@
     )
     cos_table, sin_table = angle_tables(jnp.arange(length).astype(F32))
     sin_table = jnp.where(jnp.arange(HD) < HD // 2, -sin_table, sin_table)
-    in_vmem = pl.BlockSpec(memory_space=pltpu.VMEM)
     params = pltpu.CompilerParams(vmem_limit_bytes=VMEM_BYTES)
-
-    def like(*shape, dtype=BF):
-        return jax.ShapeDtypeStruct(shape, dtype)
-
     forward = pl.pallas_call(
         functools.partial(attend_forward, slots),
         out_shape=(
@@ -231,16 +973,16 @@
             like(length, wide),
             like(slots, length, 1, dtype=F32),
         ),
-        in_specs=[in_vmem] * 5,
-        out_specs=(in_vmem,) * 4,
+        in_specs=[IN_VMEM] * 5,
+        out_specs=(IN_VMEM,) * 4,
         compiler_params=params,
         name="attend_forward",
     )
     backward = pl.pallas_call(
         functools.partial(attend_backward, slots),
         out_shape=(like(wide, D, dtype=F32), like(D, 3 * wide, dtype=F32), like(length, D)),
-        in_specs=[in_vmem] * 10,
-        out_specs=(in_vmem,) * 3,
+        in_specs=[IN_VMEM] * 10,
+        out_specs=(IN_VMEM,) * 3,
         scratch_shapes=[
             pltpu.VMEM((length, 3 * wide), BF),
             pltpu.VMEM((length, wide), BF),
@@ -251,21 +993,13 @@
         name="attend_backward",
     )
 
-    def joined(routed, shared):
-        own = lax.dynamic_slice(shared, (0, me * share), (D, share))
-        blank = jnp.zeros((D, padded - used), BF)
-        return jnp.concatenate([routed[i] for i in range(EXP_DEV)] + [own, blank], axis=1)
-
-    gate_all = joined(routed_gate, shared_gate)
-    up_all = joined(routed_up, shared_up)
-    down_all = joined(routed_down, shared_down)
-
     expert_at = jnp.sum(
         (owner_table[:, None] == jnp.arange(experts)[None, :]) * jnp.arange(experts)[:, None],
         axis=0,
     )
     router_rows = jnp.take(w_router, expert_at, axis=1)
     ids_all = lax.all_gather(expert_ids[:, 0], "exp", axis=1, tiled=True)
+    grad_all = lax.all_gather(cotangent[:, 0], "exp", axis=1, tiled=True)
 
     first = []
     for micro_batch in range(MB):
@@ -282,63 +1016,27 @@
         rows_in = tokens[micro_batch, 0].astype(F32)
         hidden_one = rows_in + dot(own_mixed, w_out)
         two_low = norm_rows(hidden_one, gain_two).astype(BF)
-        two_all = gather_exp(two_low)
-        grad_all = gather_exp(cotangent[micro_batch, 0])
-        first.append(
-            (normed, qkv, mixed, lse, rows_in, hidden_one, two_all, grad_all)
-        )
-
-    column = jnp.arange(padded)
-    second = []
-    for micro_batch in range(MB):
-        two_all, grad_all = first[micro_batch][6:]
-        logits = dot(two_all, router_rows)
-        named = jnp.any(ids_all[micro_batch][:, :, None] == expert_at[None, None, :], axis=1)
-        chosen = jnp.where(named, logits, -jnp.inf)
-        powers = jnp.where(named, jnp.exp(chosen - jnp.max(chosen, axis=-1, keepdims=True)), 0.0)
-        gates = powers / jnp.sum(powers, axis=-1, keepdims=True)
-        own_gates = lax.dynamic_slice(gates, (0, me * EXP_DEV), (length, EXP_DEV))
-        weight = jnp.where(
-            column[None, :] < FF,
-            own_gates[:, :1],
-            jnp.where(column[None, :] < 2 * FF, own_gates[:, 1:], 1.0),
-        )
-        gate_part = dot(two_all, gate_all)
-        up_part = dot(two_all, up_all)
-        down_part = dot(grad_all, down_all)
-        sigmoid = jax.nn.sigmoid(gate_part)
-        act = gate_part * sigmoid
-        hidden = act * up_part
-        products = hidden * down_part
-        own_grads = jnp.stack(
-            [jnp.sum(products[:, i * FF : (i + 1) * FF], axis=1) for i in range(EXP_DEV)], axis=1
-        )
-        hidden_low = (weight * hidden).astype(BF)
-        weighted = weight * down_part
-        d_gate = (weighted * up_part * (sigmoid + act * (1.0 - sigmoid))).astype(BF)
-        d_up = (weighted * act).astype(BF)
-        out_part = scatter_exp(dot_nt(hidden_low, down_all))
-        back_part = scatter_exp(dot_nt(d_gate, gate_all) + dot_nt(d_up, up_all))
-        gate_grads = lax.all_gather(own_grads, "exp", axis=1, tiled=True)
-        grad_logits = (
-            gates * (gate_grads - jnp.sum(gates * gate_grads, axis=-1, keepdims=True))
-        ).astype(BF)
-        second.append((hidden_low, d_gate, d_up, out_part, back_part, grad_logits))
-
-    two_both = jnp.concatenate([f[6] for f in first])
-    grad_both = jnp.concatenate([f[7] for f in first])
-    gate_sum = dot_tn(two_both, jnp.concatenate([s[1] for s in second]))
-    up_sum = dot_tn(two_both, jnp.concatenate([s[2] for s in second]))
-    down_sum = dot_tn(grad_both, jnp.concatenate([s[0] for s in second]))
-
-    def routed_sum(total):
-        parts = jnp.stack([total[:, i * FF : (i + 1) * FF] for i in range(EXP_DEV)])
-        return lax.psum_scatter(
-            parts.astype(BF), "seq", scatter_dimension=1, tiled=True
-        ).astype(F32)
-
-    def shared_part(total):
-        return total[:, EXP_DEV * FF : used]
+        logits = dot(two_low, router_rows)
+        named = jnp.any(
+            expert_ids[micro_batch, 0][:, :, None] == expert_at[None, None, :], axis=1
+        )
+        gates = named_softmax(logits, named)
+        first.append((normed, qkv, mixed, lse, rows_in, hidden_one, two_low, gates))
+
+    experts_of = experts_on_lines if devices <= 8 else experts_plain
+    outs, backs, tails, routed_sums, shared_cols = experts_of(
+        jnp.stack([f[6] for f in first]),
+        grad_all,
+        ids_all,
+        expert_at,
+        router_rows,
+        (routed_gate, routed_up, routed_down),
+        (shared_gate, shared_up, shared_down),
+        share,
+    )
+
+    def routed_sum(parts):
+        return lax.psum_scatter(parts, "seq", scatter_dimension=1, tiled=True).astype(F32)
 
     outputs_list = []
     grads_list = []
@@ -346,15 +1044,14 @@
     qkv_sum = jnp.zeros((D, 3 * wide), F32)
     out_sum = jnp.zeros((wide, D), F32)
     for micro_batch in range(MB):
-        normed, qkv, mixed, lse, rows_in, hidden_one, two_all, _ = first[micro_batch]
-        _, _, _, out_part, back_part, grad_logits = second[micro_batch]
-        outputs_list.append((hidden_one + out_part).astype(BF))
-        own_logits = lax.dynamic_slice(grad_logits, (me * SEQ_DEV, 0), (SEQ_DEV, experts))
-        grad_two = back_part + dot_nt(own_logits, router_rows)
+        normed, qkv, mixed, lse, rows_in, hidden_one, two_low, gates = first[micro_batch]
+        outputs_list.append((hidden_one + outs[micro_batch]).astype(BF))
+        tail = tails[micro_batch]
+        own_logits = (gates * (tail - jnp.sum(gates * tail, axis=-1, keepdims=True))).astype(BF)
+        grad_two = backs[micro_batch] + dot_nt(own_logits, router_rows)
         back, gain_terms = norm_back(hidden_one, gain_two, grad_two)
         grad_hidden = cotangent[micro_batch, 0].astype(F32) + back
-        own_two = lax.dynamic_slice(two_all, (me * SEQ_DEV, 0), (SEQ_DEV, D))
-        router_part = dot_tn(own_two, own_logits)
+        router_part = dot_tn(two_low, own_logits)
         mix_all = gather_exp(grad_hidden.astype(BF))
         out_one, qkv_one, grad_part = backward(
             mix_all, normed, qkv, mixed, lse, cos_table, sin_table, w_qkv, w_out_heads, slot_live[None]
@@ -382,7 +1079,6 @@
         return lax.all_gather(rows, "seq", axis=0, tiled=True).astype(F32)
 
     piece = rows_out // groups
-    shared_cols = jnp.concatenate([shared_part(t) for t in (gate_sum, up_sum, down_sum)], axis=1)
     shared_rows = to_rows(shared_cols).reshape(devices, piece, 3, share)
     shared_full = to_all(shared_rows.transpose(1, 2, 0, 3).reshape(piece, 3 * FF))
     qkv_rows = to_rows(qkv_sum).reshape(devices, piece, slots, 3, HD)
@@ -413,9 +1109,7 @@
         shared_full[:, :FF],
         shared_full[:, FF : 2 * FF],
         shared_full[:, 2 * FF :],
-        routed_sum(gate_sum),
-        routed_sum(up_sum),
-        routed_sum(down_sum),
+        *(routed_sum(parts) for parts in routed_sums),
     )
 
 

time: 1090 us -> 918 us (0.84)
  matrix products: 184 us -> 9.15 us
  Pallas kernels: 67.8 us -> 237 us
  waiting for transfers between devices: 518 us -> 454 us
  local copies, waits for them, and re-layouts: 111 us -> 56.2 us
  other arithmetic: 69.6 us -> 42.5 us
  blocking collectives: 89.9 us -> 66.3 us
    pallas_call x0 -> x2, Pallas kernels: none -> 169 us  [the longest x1 108 us: call_rows(): pl.pallas_call(kernel, out_shape=(like(MB, devices, SEQ_DEV, D), like(MB...]
    reduce_scatter x6 -> x2, waiting for transfers between devices: 137 us -> 45.6 us  [scatter_exp(): lax.psum_scatter(array.astype(BF), 'exp', scatter_dimension=0, tiled=True)]
    dot_general x10 -> x4, matrix products: 78.3 us -> 4.17 us  [dot(): return jnp.dot(a, b, preferred_element_type=F32)]
    dot_general x8 -> x2, matrix products: 57.1 us -> 2.52 us  [dot_nt(): lax.dot_general(a, b, (((1,), (1,)), ((), ())), preferred_element_type=F32)]
    dot_general x5 -> x2, matrix products: 48.7 us -> 2.46 us  [dot_tn(): lax.dot_general(a, b, (((0,), (0,)), ((), ())), preferred_element_type=F32)]
    unnamed x25 -> x18, waiting for transfers between devices: 87.7 us -> 127 us
    all_gather x2 -> x0, blocking collectives: 25.6 us -> none  [on_device(): gate_grads = lax.all_gather(own_grads, 'exp', axis=1, tiled=True)]
    concatenate x4 -> x1, local copies, waits for them, and re-layouts: 25.1 us -> 0.01 us  [experts_on_lines(): columns = jnp.concatenate([expert_at.astype(jnp.int32), spare])]
  transfers between devices with their start and end apart: 25 -> 19, of which waited for: 19 -> 16; matrix products, arithmetic and copies ran while one was open for 27% -> 10% of each run, Pallas kernels for 3% -> 5%
where the time goes in v2:
time: 918 us; the launch traced here: 906 us
  waiting for transfers between devices  454 us (49%)
  Pallas kernels  237 us (26%)
  blocking collectives  66.3 us (7%)
  local copies, waits for them, and re-layouts  56.2 us (6%)
  other arithmetic  42.5 us (5%)
  starting transfers between devices  24.6 us (3%)
  between operations  15.9 us (2%)
    reduce_scatter x3, waiting for transfers between devices, routed_sum(): lax.psum_scatter(parts, 'seq', scatter_dimension=1, tiled=True).astype(F32)  172 us
    unnamed x18, waiting for transfers between devices  127 us
    pallas_call x1, Pallas kernels, call_rows(): pl.pallas_call(kernel, out_shape=(like(MB, devices, SEQ_DEV, D), like(MB...  108 us
    all_gather x4, waiting for transfers between devices, gather_exp(): return lax.all_gather(array, 'exp', axis=0, tiled=True)  79.8 us
    pallas_call x1, Pallas kernels, call_sums(): pl.pallas_call(kernel, grid=(EXP_DEV, D // 256), out_shape=(like(EXP_DEV,...  61 us
    reduce_scatter x2, waiting for transfers between devices, scatter_exp(): lax.psum_scatter(array.astype(BF), 'exp', scatter_dimension=0, tiled=True)  45.6 us
    pallas_call x2, Pallas kernels, on_device(): backward(mix_all, normed, qkv, mixed, lse, cos_table, sin_table, w_qkv, w...  43.3 us
    all_gather x1, blocking collectives, on_device(): ids_all = lax.all_gather(expert_ids[:, 0], 'exp', axis=1, tiled=True)  29 us
  transfers between devices with their start and end apart: 19, of which 16 were waited for; matrix products, arithmetic and copies ran while one was open for 10% of the time, Pallas kernels for 5%

profile of v2, /device:TPU:12, one launch (start us, length us, event | category | flops | bytes accessed | tf_op | source)
XLA Modules:
  0.0 905.7 jit_solution(10804745984366735511)
XLA Ops:
  7.3 2.1 fusion.46
  11.6 1.7 dynamic-slice_dynamic-update-slice_fusion.5
  13.3 1.7 dynamic-slice_dynamic-update-slice_fusion.4
  15.0 1.7 dynamic-slice_dynamic-update-slice_fusion.3
  16.8 1.7 dynamic-slice_dynamic-update-slice_fusion.2
  18.5 1.7 dynamic-slice_dynamic-update-slice_fusion.1
  20.2 1.7 dynamic-slice_dynamic-update-slice_fusion.w_ref
  22.1 2.3 constant_dynamic-slice_fusion.2
  24.4 2.9 negate_select_fusion
  27.3 17.3 %all-gather.20.cloned.1.call-done = bf16[1,1,1024,1280]{3,2,1,0:T(8,128)(2,1)} async-done(((bf16[1,1,128,1280]{3,2,1,0:T(8,128)(2,1)}), bf16[1,1,1024,1280]{3,2,1,0:T(8,128)(2,1)}) %all-gather.20.cloned.1.call-update) | async-done | bytes 2621456 | tf_op jit(solution)/shard_map/all_gather | solution.py:61
  44.7 12.2 %attend_forward.3 = (bf16[1024,1280]{1,0:T(8,128)(2,1)}, bf16[1024,768]{1,0:T(8,128)(2,1)}, bf16[1024,256]{1,0:T(8,128)(2,1)}, f32[2,1024,1]{2,1,0:T(8,128)}) custom-call(bf16[1024,1280]{1,0:T(8,128)(2,1)} %bitcast.129, f32[1,1280]{1,0:T(1,128)} %broadcast_in_dim.52.gain_ref, f32[1024,128]{1,0:T(8,128)} %get-tuple-element.181.cos_ref, ...), custom_call_target="tpu_custom_call" | custom-call | tf_op jit(solution)/shard_map/attend_forward/pallas_call | solution.py:1007
  56.9 2.0 copy.93
  58.9 4.6 all-to-all-start.1
  63.6 1.8 pad.18.refs_4_
  67.0 21.2 %all-gather.18.cloned.1.call-done = bf16[1,1,1024,1280]{3,2,1,0:T(8,128)(2,1)} async-done(((bf16[1,1,128,1280]{3,2,1,0:T(8,128)(2,1)}), bf16[1,1,1024,1280]{3,2,1,0:T(8,128)(2,1)}) %all-gather.18.cloned.1.call-update) | async-done | bytes 2621456 | tf_op jit(solution)/shard_map/all_gather | solution.py:61
  88.2 12.2 %attend_forward.2 = (bf16[1024,1280]{1,0:T(8,128)(2,1)}, bf16[1024,768]{1,0:T(8,128)(2,1)}, bf16[1024,256]{1,0:T(8,128)(2,1)}, f32[2,1024,1]{2,1,0:T(8,128)}) custom-call(bf16[1024,1280]{1,0:T(8,128)(2,1)} %bitcast.128, f32[1,1280]{1,0:T(1,128)} %broadcast_in_dim.52.gain_ref, f32[1024,128]{1,0:T(8,128)} %get-tuple-element.181.cos_ref, ...), custom_call_target="tpu_custom_call" | custom-call | tf_op jit(solution)/shard_map/attend_forward/pallas_call | solution.py:1007
  100.5 2.1 copy.91
  102.5 8.1 all-to-all-start
  112.8 29.0 %all-gather.3 = s32[2,1,1024,7]{2,1,3,0:T(1,128)S(1)} all-gather(s32[2,1,128,7]{2,1,3,0:T(1,128)S(1)} %copy-done.26), channel_id=5, replica_groups=mesh['seq'=4,'exp'=8] {'exp'}, dimensions={2}, use_global_device_ids=true | all-gather | bytes 64512 | tf_op jit(solution)/shard_map/all_gather | solution.py:1001
  141.9 2.7 compare_reduce_fusion
  147.1 2.8 multiply_reduce_fusion.4
  152.9 2.4 all-gather.22.cloned.1.call-done
  155.3 107.9 %expert_rows.1 = (bf16[2,8,128,1280]{3,2,1,0:T(8,128)(2,1)}, bf16[2048,1920]{1,0:T(8,128)(2,1)}, bf16[2048,1920]{1,0:T(8,128)(2,1)}, bf16[2048,1920]{1,0:T(8,128...) custom-call(bf16[2,128,1280]{2,1,0:T(8,128)(2,1)} %pad_maximum_fusio, ...), custom_call_target="tpu_custom_call" | custom-call | tf_op jit(solution)/shard_map/expert_rows/pallas_call | solution.py:739
  265.4 61.0 %expert_sums.1 = (bf16[2,1280,896]{2,1,0:T(8,128)(2,1)}, bf16[2,1280,896]{2,1,0:T(8,128)(2,1)}, bf16[2,1280,896]{2,1,0:T(8,128)(2,1)}, f32[3,1280,128]{2,1,0:T(8...) custom-call(bf16[2048,1280]{1,0:T(8,128)(2,1)} %bitcast.124, bf16[2048,1280]{1,0:T(8,128)(2,1)} %bitcast.121, ...), custom_call_target="tpu_custom_call" | custom-call | tf_op jit(solution)/shard_map/expert_sums/pallas_call | solution.py:798
  328.7 1.4 convolution_add_fusion.2
  331.4 1.3 fusion.41
  337.3 27.8 %all-gather.14.cloned.1.call-done.mix_ref = bf16[1024,1280]{1,0:T(8,128)(2,1)} async-done(((bf16[128,1280]{1,0:T(8,128)(2,1)}), bf16[1024,1280]{1,0:T(8,128)(2,1)}) %all-gather.14.cloned.1.call-update) | async-done | bytes 2621456 | tf_op jit(solution)/shard_map/all_gather | solution.py:61
  365.1 21.5 %attend_backward.3 = (f32[256,1280]{1,0:T(8,128)}, f32[1280,768]{1,0:T(8,128)}, bf16[1024,1280]{1,0:T(8,128)(2,1)}) custom-call(bf16[1024,1280]{1,0:T(8,128)(2,1)} %all-gather.14.cloned.1.call-done.mix_ref, bf16[1024,1280]{1,0:T(8,128)(2,1)} %get-tuple-element.59.normed_ref, bf16[1024,768]{1,0:T(8,128)(2,1)} %get-tuple-element.60.qkv_ref, ...), custom_call_target="tpu_custom_call" | custom-call | tf_op jit(solution)/shard_map/attend_backward/pallas_call | solution.py:1056
  386.6 13.5 %all-gather.12.cloned.1.call-done.mix_ref = bf16[1024,1280]{1,0:T(8,128)(2,1)} async-done(((bf16[128,1280]{1,0:T(8,128)(2,1)}), bf16[1024,1280]{1,0:T(8,128)(2,1)}) %all-gather.12.cloned.1.call-update) | async-done | bytes 2621456 | tf_op jit(solution)/shard_map/all_gather | solution.py:61
  400.1 21.8 %attend_backward.2 = (f32[256,1280]{1,0:T(8,128)}, f32[1280,768]{1,0:T(8,128)}, bf16[1024,1280]{1,0:T(8,128)(2,1)}) custom-call(bf16[1024,1280]{1,0:T(8,128)(2,1)} %all-gather.12.cloned.1.call-done.mix_ref, bf16[1024,1280]{1,0:T(8,128)(2,1)} %get-tuple-element.54.normed_ref, bf16[1024,768]{1,0:T(8,128)(2,1)} %get-tuple-element.55.qkv_ref, ...), custom_call_target="tpu_custom_call" | custom-call | tf_op jit(solution)/shard_map/attend_backward/pallas_call | solution.py:1056
  421.9 2.7 add_convert_fusion.1
  424.6 2.2 copy.115
  426.8 1.4 fusion.44
  428.2 1.4 pad_maximum_fusion
  429.6 3.9 add_convert_fusion
  433.7 18.3 %reduce-scatter.27.cloned.1.call-done = bf16[320,256]{1,0:T(8,128)(2,1)} async-done(((bf16[1280,256]{1,0:T(8,128)(2,1)}), bf16[320,256]{1,0:T(8,128)(2,1)}) %reduce-scatter.27.cloned.1.call-update) | async-done | bytes 163856
  461.4 78.6 %all-reduce.11.cloned.1.call-done = (bf16[8,160,768]{2,1,0:T(8,128)(2,1)}, bf16[8,160,336]{2,1,0:T(8,128)(2,1)}) async-done(((bf16[8,160,768]{2,1,0:T(8,128)(2,1)}, bf16[8,160,336]{2,1,0:T(8,128)(2,1)}), (bf16[8,160,768]{2,1,0:T(8,128)(2,1)}, bf16[8,160,336]{2,1,0:T(8,128)(2,1)})) %all-reduce.11.cloned.1.call-update) | async-done | bytes 2826256
  540.1 1.7 constant_dynamic-slice_fusion.5
  541.7 5.1 all-to-all-start.3
  546.9 1.3 pad_clamp_fusion
  549.3 1.8 constant_dynamic-slice_fusion.6
  551.1 5.6 all-to-all-done.3
  556.7 5.6 all-to-all-start.2
  564.6 1.6 fusion.53
  566.2 8.2 reduce-scatter.19.cloned.1.call-done
  574.4 10.6 %all-gather.4 = bf16[4,320,160]{1,2,0:T(8,128)(2,1)S(1)} all-gather(bf16[1,320,160]{1,2,0:T(8,128)(2,1)} %bitcast.145), channel_id=1, replica_groups=mesh['seq'=4,'exp'=8] {'seq'}, dimensions={0}, use_global_device_ids=true | all-gather | bytes 512000 | tf_op jit(solution)/shard_map/all_gather | solution.py:1094
  586.2 2.7 reshape.228
  589.4 11.4 %all_gather.35 = bf16[160,2688]{1,0:T(8,128)(2,1)S(1)} all-gather(bf16[40,2688]{1,0:T(8,128)(2,1)S(1)} %reshape.198), channel_id=1, replica_groups=mesh['seq'=4,'exp'=8] {'seq'}, dimensions={0}, use_global_device_ids=true | all-gather | bytes 1075200 | tf_op jit(solution)/shard_map/all_gather | solution.py:1079
  600.8 1.2 fusion.45
  602.0 1.9 reshape.194
  605.1 1.2 reshape.195
  606.4 6.7 reduce-scatter.17.cloned.1.call-done
  613.1 38.9 %reduce-scatter.15.cloned.1.call-done = bf16[128,1280]{1,0:T(8,128)(2,1)} async-done(((bf16[1024,1280]{1,0:T(8,128)(2,1)}), bf16[128,1280]{1,0:T(8,128)(2,1)}) %reduce-scatter.15.cloned.1.call-update) | async-done | bytes 327696 | tf_op jit(solution)/shard_map/reduce_scatter | solution.py:65
  652.0 1.6 fusion.17
  655.6 58.8 %reduce-scatter.21.cloned.1.call-done = bf16[2,320,896]{2,1,0:T(8,128)(2,1)} async-done(((bf16[2,1280,896]{2,1,0:T(8,128)(2,1)}), bf16[2,320,896]{2,1,0:T(8,128)(2,1)}) %reduce-scatter.21.cloned.1.call-update) | async-done | bytes 1146896 | tf_op jit(solution)/shard_map/reduce_scatter | solution.py:1039
  714.4 2.8 convert_element_type.139
  717.2 56.4 %reduce-scatter.23.cloned.1.call-done = bf16[2,320,896]{2,1,0:T(8,128)(2,1)} async-done(((bf16[2,1280,896]{2,1,0:T(8,128)(2,1)}), bf16[2,320,896]{2,1,0:T(8,128)(2,1)}) %reduce-scatter.23.cloned.1.call-update) | async-done | bytes 1146896 | tf_op jit(solution)/shard_map/reduce_scatter | solution.py:1039
  773.7 2.8 convert_element_type.140
  776.5 56.5 %reduce-scatter.25.cloned.1.call-done = bf16[2,320,896]{2,1,0:T(8,128)(2,1)} async-done(((bf16[2,1280,896]{2,1,0:T(8,128)(2,1)}), bf16[2,320,896]{2,1,0:T(8,128)(2,1)}) %reduce-scatter.25.cloned.1.call-update) | async-done | bytes 1146896 | tf_op jit(solution)/shard_map/reduce_scatter | solution.py:1039
  833.0 2.9 convert_element_type.141
  838.8 24.9 %reduce-scatter.29.cloned.1.call-done = f32[160,18]{1,0:T(8,128)} async-done(((f32[1280,18]{1,0:T(8,128)}), f32[160,18]{1,0:T(8,128)}) %reduce-scatter.29.cloned.1.call-update) | async-done | bytes 11536
  864.6 15.3 %psum.8 = f32[160,18]{0,1:T(8,128)S(1)} all-reduce(f32[160,18]{0,1:T(8,128)S(1)} %copy.120), channel_id=1, replica_groups=mesh['seq'=4,'exp'=8] {'seq'}, use_global_device_ids=true, to_apply=%region_27.28 | all-reduce | flops 2880 | bytes 23040 | tf_op jit(solution)/shard_map/psum | solution.py:1096
  881.9 14.0 %all-gather.16.cloned.1.call-done = bf16[160,3840]{1,0:T(8,128)(2,1)} async-done(((bf16[40,3840]{1,0:T(8,128)(2,1)}), bf16[160,3840]{1,0:T(8,128)(2,1)}) %all-gather.16.cloned.1.call-update) | async-done | bytes 1228816 | tf_op jit(solution)/shard_map/all_gather | solution.py:1079
  895.9 2.7 fusion.43
  (203 shorter events, 44.4 us)
Async XLA Ops:
  7.2 103.8 %copy-start = (bf16[1280,896]{1,0:T(8,128)(2,1)S(1)}, bf16[1280,896]{1,0:T(8,128)(2,1)}, u32[]{:S(2)}) copy-start(bf16[1280,896]{1,0:T(8,128)(2,1)} %param.28) | copy-start | bytes 6881284
  7.2 3.7 copy-start.24
  7.2 4.3 copy-start.40
  7.2 37.4 %all-gather.20.cloned.1.call-start = ((), (), s32[]{:S(2)}) async-start(), calls=%async_computation.22 | async-start | bytes 2949120 | tf_op jit(solution)/shard_map/all_gather | solution.py:61
  9.4 78.8 %all-gather.18.cloned.1.call-start = ((), (), s32[]{:S(2)}) async-start(), calls=%async_computation.21 | async-start | bytes 2949120 | tf_op jit(solution)/shard_map/all_gather | solution.py:61
  10.1 145.2 %all-gather.22.cloned.1.call-start = ((), (), s32[]{:S(2)}) async-start(), calls=%async_computation.23 | async-start | bytes 5898240 | tf_op jit(solution)/shard_map/all_gather | solution.py:1002
  56.9 9.2 %copy-start.2 = (bf16[1280,16]{0,1:T(8,128)(2,1)S(1)}, bf16[1280,16]{0,1:T(8,128)(2,1)}, u32[]{:S(2)}) copy-start(bf16[1280,16]{0,1:T(8,128)(2,1)} %param.27) | copy-start | bytes 122884
  58.9 43.6 %all-to-all-start.1 = ((bf16[8,128,256]{1,2,0:T(8,128)(2,1)}), bf16[8,128,256]{1,2,0:T(8,128)(2,1)S(1)}, u32[]{:S(2)}, u32[]{:S(2)}) async-start(bf16[8,128,256]{1,2,0:T(8,128)(2,1)} %copy.93), calls=%async_computation.1 | async-start | bytes 1048576 | tf_op jit(solution)/shard_map/all_to_all | solution.py:1008
  67.0 84.5 %copy-start.31 = (pred[16]{0:T(512)(128)(4,1)}, pred[16]{0:T(512)(128)(4,1)S(1)}, u32[]{:S(2)}) copy-start(pred[16]{0:T(512)(128)(4,1)S(1)} %compare_and_fusion.1) | copy-start | bytes 52
  100.5 12.3 %copy-start.26 = (s32[2,1,128,7]{2,1,3,0:T(1,128)S(1)}, s32[2,1,128,7]{2,1,3,0:T(1,128)}, u32[]{:S(2)}) copy-start(s32[2,1,128,7]{2,1,3,0:T(1,128)} %param.19) | copy-start | bytes 21508
  102.5 43.4 %all-to-all-start = ((bf16[8,128,256]{1,2,0:T(8,128)(2,1)}), bf16[8,128,256]{1,2,0:T(8,128)(2,1)}, u32[]{:S(2)}, u32[]{:S(2)}) async-start(bf16[8,128,256]{1,2,0:T(8,128)(2,1)} %copy.91), calls=%async_computation | async-start | bytes 1048576 | tf_op jit(solution)/shard_map/all_to_all | solution.py:1008
  110.7 254.5 %all-gather.14.cloned.1.call-start = ((), (), s32[]{:S(2)}) async-start(), calls=%async_computation.14 | async-start | bytes 2949120 | tf_op jit(solution)/shard_map/all_gather | solution.py:61
  112.0 35.1 %copy-start.3 = (bf16[2,1,128,1280]{3,2,1,0:T(8,128)(2,1)S(1)}, bf16[2,1,128,1280]{3,2,1,0:T(8,128)(2,1)}, u32[]{:S(2)}) copy-start(bf16[2,1,128,1280]{3,2,1,0:T(8,128)(2,1)} %param.17) | copy-start | bytes 1966084
  147.1 2.9 copy-start.4
  150.0 0.8 copy-start.22
  150.7 180.6 %copy-start.27 = (f32[128]{0:T(128)}, f32[128]{0:T(128)S(1)}, u32[]{:S(2)}) copy-start(f32[128]{0:T(128)S(1)} %get-tuple-element.202) | copy-start | bytes 1540
  150.7 180.6 %copy-start.29 = (f32[128]{0:T(128)}, f32[128]{0:T(128)S(1)}, u32[]{:S(2)}) copy-start(f32[128]{0:T(128)S(1)} %get-tuple-element.201) | copy-start | bytes 1540
  150.9 112.3 %copy-start.10 = (bf16[128,1280]{1,0:T(8,128)(2,1)}, bf16[128,1280]{1,0:T(8,128)(2,1)S(1)}, u32[]{:S(2)}) copy-start(bf16[128,1280]{1,0:T(8,128)(2,1)S(1)} %get-tuple-element.188) | copy-start | bytes 983044
  265.4 63.3 %copy-start.32 = (pred[16]{0:T(512)(128)(4,1)S(1)}, pred[16]{0:T(512)(128)(4,1)}, u32[]{:S(2)}) copy-start(pred[16]{0:T(512)(128)(4,1)} %copy-done.31) | copy-start | bytes 52
  326.5 3.7 copy-start.16
  328.7 2.6 copy-start.21
  328.7 2.6 copy-start.5
  328.7 2.6 copy-start.17
  331.3 1.4 copy-start.7
  331.3 1.4 copy-start.35
  331.3 1.4 copy-start.33
  332.7 67.4 %all-gather.12.cloned.1.call-start = ((), (), s32[]{:S(2)}) async-start(), calls=%async_computation.12 | async-start | bytes 2949120 | tf_op jit(solution)/shard_map/all_gather | solution.py:61
  333.3 118.6 %reduce-scatter.27.cloned.1.call-start = ((), (), s32[]{:S(2)}) async-start(), calls=%async_computation.24 | async-start | bytes 819200
  333.6 2.6 copy-start.12
  426.8 113.3 %all-reduce.11.cloned.1.call-start = ((), (), s32[]{:S(2)}) async-start(), calls=%async_computation.26 | async-start | bytes 5898240
  426.8 2.8 copy-start.9
  433.6 140.8 %reduce-scatter.19.cloned.1.call-start = ((), (), s32[]{:S(2)}) async-start(), calls=%async_computation.17 | async-start | bytes 1105920 | tf_op jit(solution)/shard_map/reduce_scatter | solution.py:1093
  454.4 158.7 %reduce-scatter.17.cloned.1.call-start = ((), (), s32[]{:S(2)}) async-start(), calls=%async_computation.15 | async-start | bytes 2949120 | tf_op jit(solution)/shard_map/reduce_scatter | solution.py:65
  455.2 196.8 %reduce-scatter.15.cloned.1.call-start = ((), (), s32[]{:S(2)}) async-start(), calls=%async_computation.13 | async-start | bytes 2949120 | tf_op jit(solution)/shard_map/reduce_scatter | solution.py:65
  455.8 258.7 %reduce-scatter.21.cloned.1.call-start = ((), (), s32[]{:S(2)}) async-start(), calls=%async_computation.18 | async-start | bytes 5734400 | tf_op jit(solution)/shard_map/reduce_scatter | solution.py:1039
  456.5 317.2 %reduce-scatter.23.cloned.1.call-start = ((), (), s32[]{:S(2)}) async-start(), calls=%async_computation.19 | async-start | bytes 5734400 | tf_op jit(solution)/shard_map/reduce_scatter | solution.py:1039
  457.1 376.0 %reduce-scatter.25.cloned.1.call-start = ((), (), s32[]{:S(2)}) async-start(), calls=%async_computation.20 | async-start | bytes 5734400 | tf_op jit(solution)/shard_map/reduce_scatter | solution.py:1039
  457.1 0.7 copy-start.42
  457.1 2.7 copy-start.41
  457.8 104.5 %copy-start.11 = (bf16[128,1280]{1,0:T(8,128)(2,1)S(1)}, bf16[128,1280]{1,0:T(8,128)(2,1)}, u32[]{:S(2)}) copy-start(bf16[128,1280]{1,0:T(8,128)(2,1)} %copy-done.10) | copy-start | bytes 983044
  541.7 15.0 %all-to-all-start.3 = ((bf16[8,40,336]{2,1,0:T(8,128)(2,1)}), bf16[8,40,336]{2,1,0:T(8,128)(2,1)S(1)}, u32[]{:S(2)}, u32[]{:S(2)}) async-start(bf16[8,40,336]{2,1,0:T(8,128)(2,1)} %constant_dynamic-slice_fusion.5), calls=%async_computation.6 | async-start | bytes 491520 | tf_op jit(solution)/shard_map/all_to_all | solution.py:1076
  556.7 45.3 %all-to-all-start.2 = ((bf16[8,40,768]{2,1,0:T(8,128)(2,1)}), bf16[8,40,768]{2,1,0:T(8,128)(2,1)}, u32[]{:S(2)}, u32[]{:S(2)}) async-start(bf16[8,40,768]{2,1,0:T(8,128)(2,1)} %constant_dynamic-slice_fusion.6), calls=%async_computation.4 | async-start | bytes 983040 | tf_op jit(solution)/shard_map/all_to_all | solution.py:1076
  562.3 301.4 %reduce-scatter.29.cloned.1.call-start = ((), (), s32[]{:S(2)}) async-start(), calls=%async_computation.25 | async-start | bytes 737280
  602.0 50.0 %copy-start.25 = (f32[1280]{0:T(1024)S(1)}, f32[1280]{0:T(1024)}, u32[]{:S(2)}) copy-start(f32[1280]{0:T(1024)} %param.25) | copy-start | bytes 15364
  602.0 50.0 %copy-start.37 = (f32[128]{0:T(128)S(1)}, f32[128]{0:T(128)}, u32[]{:S(2)}) copy-start(f32[128]{0:T(128)} %add_rsqrt_fusion) | copy-start | bytes 1540
  602.0 50.0 %copy-start.38 = (f32[128]{0:T(128)S(1)}, f32[128]{0:T(128)}, u32[]{:S(2)}) copy-start(f32[128]{0:T(128)} %add_rsqrt_fusion.1) | copy-start | bytes 1540
  602.0 51.6 %copy-start.19 = (f32[1280,16]{0,1:T(8,128)S(1)}, f32[1280,16]{0,1:T(8,128)}, u32[]{:S(2)}) copy-start(f32[1280,16]{0,1:T(8,128)} %fusion.52) | copy-start | bytes 245764
  602.0 51.6 %copy-start.20 = (f32[1280,16]{0,1:T(8,128)S(1)}, f32[1280,16]{0,1:T(8,128)}, u32[]{:S(2)}) copy-start(f32[1280,16]{0,1:T(8,128)} %fusion.53) | copy-start | bytes 245764
  654.8 241.2 %all-gather.16.cloned.1.call-start = ((), (), s32[]{:S(2)}) async-start(), calls=%async_computation.16 | async-start | bytes 1536000 | tf_op jit(solution)/shard_map/all_gather | solution.py:1079
  776.5 59.5 %copy-start.15 = (bf16[128,1280]{1,0:T(8,128)(2,1)S(1)}, bf16[128,1280]{1,0:T(8,128)(2,1)}, u32[]{:S(2)}) copy-start(bf16[128,1280]{1,0:T(8,128)(2,1)} %reduce-scatter.17.cloned.1.call-done) | copy-start | bytes 983044
  776.5 59.5 %copy-start.23 = (f32[1280]{0:T(1024)S(1)}, f32[1280]{0:T(1024)}, u32[]{:S(2)}) copy-start(f32[1280]{0:T(1024)} %param.26) | copy-start | bytes 15364
  776.5 59.5 %copy-start.30 = (f32[128]{0:T(128)S(1)}, f32[128]{0:T(128)}, u32[]{:S(2)}) copy-start(f32[128]{0:T(128)} %copy-done.29) | copy-start | bytes 1540
  776.5 59.5 %copy-start.36 = (f32[128]{0:T(128)S(1)}, f32[128]{0:T(128)}, u32[]{:S(2)}) copy-start(f32[128]{0:T(128)} %copy-done.35) | copy-start | bytes 1540
  776.5 60.0 %copy-start.14 = (bf16[128,1280]{1,0:T(8,128)(2,1)S(1)}, bf16[128,1280]{1,0:T(8,128)(2,1)}, u32[]{:S(2)}) copy-start(bf16[128,1280]{1,0:T(8,128)(2,1)} %reduce-scatter.15.cloned.1.call-done) | copy-start | bytes 983044
  776.5 60.0 %copy-start.28 = (f32[128]{0:T(128)S(1)}, f32[128]{0:T(128)}, u32[]{:S(2)}) copy-start(f32[128]{0:T(128)} %copy-done.27) | copy-start | bytes 1540
  776.5 60.0 %copy-start.34 = (f32[128]{0:T(128)S(1)}, f32[128]{0:T(128)}, u32[]{:S(2)}) copy-start(f32[128]{0:T(128)} %copy-done.33) | copy-start | bytes 1540
  833.0 3.0 copy-start.6
  833.0 3.4 copy-start.8
  833.0 3.5 copy-start.18
  836.5 1.4 copy-start.13
  837.0 44.3 %copy-start.39 = (pred[16]{0:T(512)(128)(4,1)S(1)}, pred[16]{0:T(512)(128)(4,1)}, u32[]{:S(2)}) copy-start(pred[16]{0:T(512)(128)(4,1)} %compare_and_fusion) | copy-start | bytes 52
  881.2 17.5 %copy-start.1 = (bf16[1280,896]{1,0:T(8,128)(2,1)S(1)}, bf16[1280,896]{1,0:T(8,128)(2,1)}, u32[]{:S(2)}) copy-start(bf16[1280,896]{1,0:T(8,128)(2,1)} %param.28) | copy-start | bytes 6881284
Sparse Core Ops, SparseCore 0:
  10.3 34.3 all-gather.19
  46.9 41.2 all-gather.17
  89.8 65.4 all-gather.21
  332.8 32.2 all-gather.13
  367.2 32.8 all-gather.11
  426.9 25.0 reduce-scatter.26
  456.1 83.9 all-reduce.10
  542.9 31.4 reduce-scatter.18
  576.8 36.2 reduce-scatter.16
  615.3 36.5 reduce-scatter.14
  655.3 59.0 reduce-scatter.20
  717.7 55.9 reduce-scatter.22
  777.0 55.9 reduce-scatter.24
  835.8 27.7 reduce-scatter.28
  866.1 29.7 all-gather.15

commit v3 on v2

--- a/solution.py
+++ b/solution.py
@@ -695,12 +695,412 @@
     @pl.when(pl.program_id(0) == 0)
     def _():
         start = pl.ds(pl.multiple_of(pl.program_id(1) * 256, 256), 256)
-        shared_ref[0, start, :] = dot_tn(normed, shared_g_ref[...])
-        shared_ref[1, start, :] = dot_tn(normed, shared_u_ref[...])
-        shared_ref[2, start, :] = dot_tn(grad, shared_h_ref[...])
+        shared_ref[0, start, :] = dot_tn(normed, shared_g_ref[...]).astype(BF)
+        shared_ref[1, start, :] = dot_tn(normed, shared_u_ref[...]).astype(BF)
+        shared_ref[2, start, :] = dot_tn(grad, shared_h_ref[...]).astype(BF)
 
     at(8, lambda: scatters[0].finish(out_b_ref))
     at(9, lambda: scatters[1].finish(back_b_ref))
+
+
+def meet_all(axes):
+    barrier = pltpu.get_barrier_semaphore()
+    count = 0
+    for axis in axes:
+        size = lax.axis_size(axis)
+        for away in range(1, size):
+            other = (lax.axis_index(axis) + away) % size
+            pl.semaphore_signal(barrier, inc=1, device_id={axis: other}, device_id_type=MESH)
+            count += 1
+    pl.semaphore_wait(barrier, count)
+
+
+def heads_backward(
+    chips, slots,
+    own_ref, qkv_ref, mixed_ref, normed_ref, lse_ref, cos_ref, sin_ref, w_ref,
+    sums_ref, grad_a_ref, grad_b_ref,
+    d_mixed, probs, raw, parts, d_keys, d_values, pairs, lines, local_sem, send_sem, recv_sem, *sems,
+):
+    devices = 2 * chips
+    me = lax.axis_index("exp")
+    core = me % 2
+    length = SEQ_DEV * devices
+    step = BLOCK
+    factor = HD ** (-0.5)
+    scatters = [
+        Scatter(
+            chips,
+            lambda to, m=m: parts.at[m, 2 * to + 1 - core],
+            lambda to, m=m: parts.at[m, 2 * to + core],
+            pairs.at[m], lines.at[m], sems[6 * m : 6 * m + 6],
+        )
+        for m in range(MB)
+    ]
+
+    def block_at(m, device, slot):
+        rows = pl.ds(pl.multiple_of(device * SEQ_DEV, SEQ_DEV), SEQ_DEV)
+        return d_mixed.at[m, rows, slot * HD : (slot + 1) * HD]
+
+    def columns(m, head):
+        return own_ref.at[m, :, pl.ds(pl.multiple_of(head * HD, HD), HD)]
+
+    def exchange(m, away, slot):
+        other = (me + away) % devices
+        return pltpu.make_async_remote_copy(
+            src_ref=columns(m, other + slot * devices),
+            dst_ref=block_at(m, me, slot),
+            send_sem=send_sem.at[m, away, slot],
+            recv_sem=recv_sem.at[m, away, slot],
+            device_id={"exp": other},
+            device_id_type=MESH,
+        )
+
+    def arrival(m, away, slot):
+        block = block_at(m, (me + devices - away) % devices, slot)
+        return pltpu.make_async_remote_copy(
+            src_ref=block,
+            dst_ref=block,
+            send_sem=send_sem.at[m, away, slot],
+            recv_sem=recv_sem.at[m, away, slot],
+            device_id={"exp": (me + away) % devices},
+            device_id_type=MESH,
+        )
+
+    def keep(m, slot):
+        return pltpu.make_async_copy(
+            columns(m, me + slot * devices), block_at(m, me, slot), local_sem.at[m, slot]
+        )
+
+    meet_all(("exp",))
+    for m in range(MB):
+        for away in range(1, devices):
+            for slot in range(slots):
+
+                @pl.when((me + away) % devices + slot * devices < HEADS)
+                def _():
+                    exchange(m, away, slot).start()
+
+        for slot in range(slots):
+
+            @pl.when(me + slot * devices < HEADS)
+            def _():
+                keep(m, slot).start()
+
+            @pl.when(me + slot * devices >= HEADS)
+            def _():
+                d_mixed[m, :, slot * HD : (slot + 1) * HD] = jnp.zeros((length, HD), BF)
+
+    def weigh(m, carry):
+        for slot in range(slots):
+            base = 3 * HD * slot
+            for start in range(0, length, step):
+                stop = start + step
+                scores = visible_scores(
+                    qkv_ref[m, start:stop, base : base + HD],
+                    qkv_ref[m, :stop, base + HD : base + 2 * HD],
+                    start,
+                )
+                probs[m, slot, start:stop, :stop] = jnp.exp(
+                    scores - lse_ref[m, slot, start:stop, :]
+                ).astype(BF)
+        return carry
+
+    lax.fori_loop(0, MB, weigh, 0)
+
+    def body(m, carry):
+        for number in range(MB):
+
+            @pl.when(m == number)
+            def _():
+                for slot in range(slots):
+
+                    @pl.when(me + slot * devices < HEADS)
+                    def _():
+                        keep(number, slot).wait()
+                        for away in range(1, devices):
+                            arrival(number, away, slot).wait_recv()
+
+        @pl.when(m == 1)
+        def _():
+            scatters[0].start()
+
+        for slot in range(slots):
+            base = 3 * HD * slot
+            d_keys[...] = jnp.zeros_like(d_keys)
+            d_values[...] = jnp.zeros_like(d_values)
+            for start in range(0, length, step):
+                stop = start + step
+                queries = qkv_ref[m, start:stop, base : base + HD]
+                keys = qkv_ref[m, :stop, base + HD : base + 2 * HD]
+                values = qkv_ref[m, :stop, base + 2 * HD : base + 3 * HD]
+                d_mix = d_mixed[m, start:stop, slot * HD : (slot + 1) * HD]
+                mixed = mixed_ref[m, start:stop, slot * HD : (slot + 1) * HD]
+                row_term = jnp.sum(d_mix.astype(F32) * mixed.astype(F32), axis=1, keepdims=True)
+                attention = probs[m, slot, start:stop, :stop]
+                d_scores = (attention.astype(F32) * (dot_nt(d_mix, values) - row_term)).astype(BF)
+                turned = turn(dot(d_scores, keys) * factor, cos_ref[start:stop, :], -sin_ref[start:stop, :])
+                raw[m, start:stop, base : base + HD] = turned.astype(BF)
+                d_keys[:stop, :] += dot_tn(d_scores, queries)
+                d_values[:stop, :] += dot_tn(attention, d_mix)
+            turned = turn(d_keys[...] * factor, cos_ref[...], -sin_ref[...])
+            raw[m, :, base + HD : base + 2 * HD] = turned.astype(BF)
+            raw[m, :, base + 2 * HD : base + 3 * HD] = d_values[...].astype(BF)
+
+            @pl.when(m == 1)
+            def _():
+                scatters[0].slot(min(slot, chips - 2))
+
+        for start in range(0, length, step):
+            back = dot_nt(raw[m, start : start + step, :], w_ref[...]).astype(BF)
+            first = start // SEQ_DEV
+            parts[m, first : first + step // SEQ_DEV] = back.reshape(step // SEQ_DEV, SEQ_DEV, D)
+        return carry
+
+    lax.fori_loop(0, MB, body, 0)
+    scatters[1].start()
+    for turn_ in range(min(slots, chips - 1), chips - 1):
+        scatters[0].slot(turn_)
+    both = raw.reshape(MB * length, 3 * slots * HD)
+    rows = normed_ref.reshape(MB * length, D)
+    ticks = [lambda: scatters[0].finish(grad_a_ref)]
+    ticks = [lambda t=t: scatters[1].slot(t) for t in range(chips - 1)]
+    for number, left in enumerate(range(0, D, 256)):
+        total = dot_tn(rows[:, left : left + 256], both[...])
+        for unit in range(3 * slots):
+            sums_ref[unit, left : left + 256, :] = total[:, unit * HD : (unit + 1) * HD].astype(BF)
+        if number < len(ticks):
+            ticks[number]()
+    scatters[0].finish(grad_a_ref)
+    for number in range(D // 256, len(ticks)):
+        ticks[number]()
+    scatters[1].finish(grad_b_ref)
+    for m in range(MB):
+        for away in range(1, devices):
+            for slot in range(slots):
+
+                @pl.when((me + away) % devices + slot * devices < HEADS)
+                def _():
+                    exchange(m, away, slot).wait_send()
+
+
+def spread_sums(
+    chips,
+    qkv_ref, shared_ref, mixed_ref, mix_ref, small_ref,
+    attn_out, shared_out, small_out,
+    arrived, summed, held, part, out_low, out_arrived, result, pair, line,
+    first_send, first_recv, local_sem, second_send, second_recv, out_send, out_recv, third_send, third_recv,
+    *sems,
+):
+    devices = 2 * chips
+    group, me = lax.axis_index("seq"), lax.axis_index("exp")
+    core = me % 2
+    groups = 4
+    rows = D // devices
+    kinds = groups - 1
+    far = D + LANES
+
+    def row_block(device):
+        return pl.ds(pl.multiple_of(device * rows, 32), rows)
+
+    scatter = Scatter(
+        chips,
+        lambda to: part.at[row_block(2 * to + 1 - core)],
+        lambda to: part.at[row_block(2 * to + core)],
+        pair, line, sems,
+    )
+
+    def unit(owner, k):
+        return shared_ref.at[owner] if k == 1 else qkv_ref.at[owner + kinds * (k // 2)]
+
+    def lives(k, device):
+        return device + (k // 2) * devices < HEADS
+
+    def seq_copy(source, target, send, recv, away):
+        return pltpu.make_async_remote_copy(
+            src_ref=source, dst_ref=target, send_sem=send, recv_sem=recv,
+            device_id={"seq": (group + away) % groups}, device_id_type=MESH,
+        )
+
+    def first(away, k):
+        owner = (group + away) % groups
+        return seq_copy(
+            unit(owner, k), arrived.at[away - 1, k], first_send.at[away - 1, k],
+            first_recv.at[away - 1, k], away,
+        )
+
+    def first_in(away, k):
+        block = arrived.at[away - 1, k]
+        return seq_copy(
+            block, block, first_send.at[away - 1, k], first_recv.at[away - 1, k], away
+        )
+
+    def column_block(device, k):
+        return pl.ds(pl.multiple_of((k * devices + device) * HD, HD), HD)
+
+    def second(away, k):
+        other = (me + away) % devices
+        return pltpu.make_async_remote_copy(
+            src_ref=summed.at[k, row_block(other)],
+            dst_ref=held.at[0, :, column_block(me, k)],
+            send_sem=second_send.at[away, k],
+            recv_sem=second_recv.at[away, k],
+            device_id={"exp": other},
+            device_id_type=MESH,
+        )
+
+    def second_in(away, k):
+        block = held.at[0, :, column_block((me + devices - away) % devices, k)]
+        return pltpu.make_async_remote_copy(
+            src_ref=block,
+            dst_ref=block,
+            send_sem=second_send.at[away, k],
+            recv_sem=second_recv.at[away, k],
+            device_id={"exp": (me + away) % devices},
+            device_id_type=MESH,
+        )
+
+    def second_own(k):
+        return pltpu.make_async_copy(
+            summed.at[k, row_block(me)], held.at[0, :, column_block(me, k)], local_sem.at[k]
+        )
+
+    def third(away, short):
+        if short:
+            source, target = held.at[0, :, :far], held.at[away, :, :far]
+        else:
+            source, target = held.at[0], held.at[away]
+        return seq_copy(source, target, third_send.at[away], third_recv.at[away], away)
+
+    def to_last(source_group):
+        return pltpu.make_async_remote_copy(
+            src_ref=out_low,
+            dst_ref=out_arrived.at[source_group],
+            send_sem=out_send,
+            recv_sem=out_recv.at[source_group],
+            device_id={"seq": kinds},
+            device_id_type=MESH,
+        )
+
+    meet_all(("seq", "exp"))
+    for k in range(3):
+        for away in range(1, groups):
+
+            @pl.when(jnp.logical_and((group + away) % groups < kinds, lives(k, me)))
+            def _():
+                first(away, k).start()
+
+    for left in range(0, D, 256):
+        part[left : left + 256, :D] = dot_tn(mixed_ref[:, left : left + 256], mix_ref[...]).astype(BF)
+    part[:, D:] = small_ref[...].astype(BF)
+    scatter.start()
+    scatter.slot(0)
+
+    @pl.when(group < kinds)
+    def _():
+        for k in range(3):
+
+            @pl.when(lives(k, me))
+            def _():
+                for away in range(1, groups):
+                    first_in(away, k).wait_recv()
+                total = unit(group, k)[...].astype(F32)
+                for away in range(1, groups):
+                    total += arrived[away - 1, k].astype(F32)
+                summed[k] = total.astype(BF)
+                for away in range(1, devices):
+                    second(away, k).start()
+                second_own(k).start()
+
+    for turn_ in range(1, chips - 1):
+        scatter.slot(turn_)
+
+    @pl.when(group < kinds)
+    def _():
+        for k in range(3):
+
+            @pl.when(lives(k, me))
+            def _():
+                second_own(k).wait()
+
+            for away in range(1, devices):
+
+                @pl.when(lives(k, (me + devices - away) % devices))
+                def _():
+                    second_in(away, k).wait_recv()
+
+        for away in range(1, groups):
+            third(away, False).start()
+
+    scatter.finish(result)
+    out_low[...] = result[...].astype(BF)
+
+    @pl.when(group < kinds)
+    def _():
+        to_last(group).start()
+
+    @pl.when(group == kinds)
+    def _():
+        total = result[...]
+        for other in range(kinds):
+            pltpu.make_async_remote_copy(
+                src_ref=out_low, dst_ref=out_arrived.at[other], send_sem=out_send,
+                recv_sem=out_recv.at[other], device_id={"seq": other}, device_id_type=MESH,
+            ).wait_recv()
+            total += out_arrived[other].astype(F32)
+        held[0, :, :far] = total.astype(BF)
+        for away in range(1, groups):
+            third(away, True).start()
+
+    for away in range(1, groups):
+        source = (group + groups - away) % groups
+
+        @pl.when(source == kinds)
+        def _():
+            third(away, True).wait_recv()
+
+        @pl.when(source < kinds)
+        def _():
+            third(away, False).wait_recv()
+
+    for kind in range(kinds):
+        index = (group + groups - kind) % groups
+        attn_out[kind, :, : devices * HD] = held[index, :, : devices * HD].astype(F32)
+        attn_out[kind, :, devices * HD :] = held[
+            index, :, 2 * devices * HD : 2 * devices * HD + D - devices * HD
+        ].astype(F32)
+        shared_out[kind] = held[index, :, devices * HD : 2 * devices * HD].astype(F32)
+    index = (group + groups - kinds) % groups
+    attn_out[kinds] = held[index, :, :D].astype(F32)
+    small_out[...] = held[index, :, D:far].astype(F32)
+
+    for k in range(3):
+        for away in range(1, groups):
+
+            @pl.when(jnp.logical_and((group + away) % groups < kinds, lives(k, me)))
+            def _():
+                first(away, k).wait_send()
+
+    @pl.when(group < kinds)
+    def _():
+        for k in range(3):
+
+            @pl.when(lives(k, me))
+            def _():
+                for away in range(1, devices):
+                    second(away, k).wait_send()
+
+        for away in range(1, groups):
+            third(away, False).wait_send()
+        to_last(group).wait_send()
+
+    @pl.when(group == kinds)
+    def _():
+        for away in range(1, groups):
+            third(away, True).wait_send()
+
+
+def taking(us):
+    return pl.CostEstimate(flops=int(us * 1.0e9), bytes_accessed=2**20, transcendentals=0)
 
 
 def like(*shape, dtype=BF):
@@ -775,6 +1175,7 @@
             compiler_params=pltpu.CompilerParams(
                 collective_id=1, has_side_effects=True, vmem_limit_bytes=VMEM_BYTES
             ),
+            cost_estimate=taking(100),
             name="expert_rows",
         )(own, grad, names, router_in, *weights)
 
@@ -800,7 +1201,7 @@
             grid=(EXP_DEV, D // 256),
             out_shape=(like(EXP_DEV, D, FF),) * 3
             + (
-                like(3, D, LANES, dtype=F32),
+                like(3, D, LANES),
                 like(SEQ_DEV, D, dtype=F32),
                 like(SEQ_DEV, D + LANES, dtype=F32),
             ),
@@ -824,6 +1225,7 @@
             compiler_params=pltpu.CompilerParams(
                 collective_id=2, has_side_effects=True, vmem_limit_bytes=VMEM_BYTES
             ),
+            cost_estimate=taking(60),
             name="expert_sums",
         )(*operands)
 
@@ -835,77 +1237,13 @@
     tails = [
         b[:, D : D + experts] + b[:, D + experts : D + 2 * experts] for b in backs
     ]
-    shared_cols = jnp.concatenate([shared_sum[k, :, :share] for k in range(3)], axis=1)
     return (
         (out_sum_a, out_sum_b),
         [b[:, :D] for b in backs],
         tails,
         (gate_sum, up_sum, down_sum),
-        shared_cols,
-    )
-
-
-def experts_plain(two_own, grad_all, ids_all, expert_at, router_rows, routed, shared, share):
-    me = lax.axis_index("exp")
-    used = EXP_DEV * FF + share
-    padded = -(-used // LANES) * LANES
-    length = grad_all.shape[1]
-
-    def joined(weight, extra):
-        own = lax.dynamic_slice(extra, (0, me * share), (D, share))
-        blank = jnp.zeros((D, padded - used), BF)
-        return jnp.concatenate([weight[i] for i in range(EXP_DEV)] + [own, blank], axis=1)
-
-    gate_all, up_all, down_all = [joined(r, s) for r, s in zip(routed, shared)]
-    column = jnp.arange(padded)
-    all_rows, kept, outs, backs, tails = [], [], [], [], []
-    for micro_batch in range(MB):
-        two_all = gather_exp(two_own[micro_batch])
-        all_rows.append(two_all)
-        logits = dot(two_all, router_rows)
-        named = jnp.any(ids_all[micro_batch][:, :, None] == expert_at[None, None, :], axis=1)
-        gates = named_softmax(logits, named)
-        own_gates = lax.dynamic_slice(gates, (0, me * EXP_DEV), (length, EXP_DEV))
-        weight = jnp.where(
-            column[None, :] < FF,
-            own_gates[:, :1],
-            jnp.where(column[None, :] < 2 * FF, own_gates[:, 1:], 1.0),
-        )
-        gate_part = dot(two_all, gate_all)
-        up_part = dot(two_all, up_all)
-        down_part = dot(grad_all[micro_batch], down_all)
-        sigmoid = jax.nn.sigmoid(gate_part)
-        act = gate_part * sigmoid
-        hidden = act * up_part
-        products = hidden * down_part
-        own_grads = jnp.stack(
-            [jnp.sum(products[:, i * FF : (i + 1) * FF], axis=1) for i in range(EXP_DEV)], axis=1
-        )
-        hidden_low = (weight * hidden).astype(BF)
-        weighted = weight * down_part
-        d_gate = (weighted * up_part * (sigmoid + act * (1.0 - sigmoid))).astype(BF)
-        d_up = (weighted * act).astype(BF)
-        kept.append((hidden_low, d_gate, d_up))
-        outs.append(scatter_exp(dot_nt(hidden_low, down_all)))
-        backs.append(scatter_exp(dot_nt(d_gate, gate_all) + dot_nt(d_up, up_all)))
-        gate_grads = lax.all_gather(own_grads, "exp", axis=1, tiled=True)
-        tails.append(
-            lax.dynamic_slice(
-                gate_grads, (me * SEQ_DEV, 0), (SEQ_DEV, gate_grads.shape[1])
-            )
-        )
-    two_both = jnp.concatenate(all_rows)
-    hidden_low, d_gate, d_up = [jnp.concatenate([k[i] for k in kept]) for i in range(3)]
-    sums = (
-        dot_tn(two_both, d_gate),
-        dot_tn(two_both, d_up),
-        dot_tn(grad_all.reshape(MB * length, D), hidden_low),
-    )
-    routed_sums = [
-        jnp.stack([t[:, i * FF : (i + 1) * FF] for i in range(EXP_DEV)]).astype(BF) for t in sums
-    ]
-    shared_cols = jnp.concatenate([t[:, EXP_DEV * FF : used] for t in sums], axis=1)
-    return outs, backs, tails, routed_sums, shared_cols
+        shared_sum,
+    )
 
 
 def named_softmax(logits, named):
@@ -914,7 +1252,7 @@
     return powers / jnp.sum(powers, axis=-1, keepdims=True)
 
 
-def on_device(
+def on_device_plain(
     tokens,
     cotangent,
     expert_ids,
@@ -942,6 +1280,8 @@
     slots = -(-HEADS // devices)
     wide = slots * HD
     share = FF // devices
+    used = EXP_DEV * FF + share
+    padded = -(-used // LANES) * LANES
 
     head_of = [jnp.minimum(me + slot * devices, HEADS - 1) for slot in range(slots)]
     slot_live = jnp.concatenate(
@@ -965,6 +1305,7 @@
     cos_table, sin_table = angle_tables(jnp.arange(length).astype(F32))
     sin_table = jnp.where(jnp.arange(HD) < HD // 2, -sin_table, sin_table)
     params = pltpu.CompilerParams(vmem_limit_bytes=VMEM_BYTES)
+
     forward = pl.pallas_call(
         functools.partial(attend_forward, slots),
         out_shape=(
@@ -993,13 +1334,21 @@
         name="attend_backward",
     )
 
+    def joined(routed, shared):
+        own = lax.dynamic_slice(shared, (0, me * share), (D, share))
+        blank = jnp.zeros((D, padded - used), BF)
+        return jnp.concatenate([routed[i] for i in range(EXP_DEV)] + [own, blank], axis=1)
+
+    gate_all = joined(routed_gate, shared_gate)
+    up_all = joined(routed_up, shared_up)
+    down_all = joined(routed_down, shared_down)
+
     expert_at = jnp.sum(
         (owner_table[:, None] == jnp.arange(experts)[None, :]) * jnp.arange(experts)[:, None],
         axis=0,
     )
     router_rows = jnp.take(w_router, expert_at, axis=1)
     ids_all = lax.all_gather(expert_ids[:, 0], "exp", axis=1, tiled=True)
-    grad_all = lax.all_gather(cotangent[:, 0], "exp", axis=1, tiled=True)
 
     first = []
     for micro_batch in range(MB):
@@ -1016,27 +1365,63 @@
         rows_in = tokens[micro_batch, 0].astype(F32)
         hidden_one = rows_in + dot(own_mixed, w_out)
         two_low = norm_rows(hidden_one, gain_two).astype(BF)
-        logits = dot(two_low, router_rows)
-        named = jnp.any(
-            expert_ids[micro_batch, 0][:, :, None] == expert_at[None, None, :], axis=1
-        )
-        gates = named_softmax(logits, named)
-        first.append((normed, qkv, mixed, lse, rows_in, hidden_one, two_low, gates))
-
-    experts_of = experts_on_lines if devices <= 8 else experts_plain
-    outs, backs, tails, routed_sums, shared_cols = experts_of(
-        jnp.stack([f[6] for f in first]),
-        grad_all,
-        ids_all,
-        expert_at,
-        router_rows,
-        (routed_gate, routed_up, routed_down),
-        (shared_gate, shared_up, shared_down),
-        share,
-    )
-
-    def routed_sum(parts):
-        return lax.psum_scatter(parts, "seq", scatter_dimension=1, tiled=True).astype(F32)
+        two_all = gather_exp(two_low)
+        grad_all = gather_exp(cotangent[micro_batch, 0])
+        first.append(
+            (normed, qkv, mixed, lse, rows_in, hidden_one, two_all, grad_all)
+        )
+
+    column = jnp.arange(padded)
+    second = []
+    for micro_batch in range(MB):
+        two_all, grad_all = first[micro_batch][6:]
+        logits = dot(two_all, router_rows)
+        named = jnp.any(ids_all[micro_batch][:, :, None] == expert_at[None, None, :], axis=1)
+        chosen = jnp.where(named, logits, -jnp.inf)
+        powers = jnp.where(named, jnp.exp(chosen - jnp.max(chosen, axis=-1, keepdims=True)), 0.0)
+        gates = powers / jnp.sum(powers, axis=-1, keepdims=True)
+        own_gates = lax.dynamic_slice(gates, (0, me * EXP_DEV), (length, EXP_DEV))
+        weight = jnp.where(
+            column[None, :] < FF,
+            own_gates[:, :1],
+            jnp.where(column[None, :] < 2 * FF, own_gates[:, 1:], 1.0),
+        )
+        gate_part = dot(two_all, gate_all)
+        up_part = dot(two_all, up_all)
+        down_part = dot(grad_all, down_all)
+        sigmoid = jax.nn.sigmoid(gate_part)
+        act = gate_part * sigmoid
+        hidden = act * up_part
+        products = hidden * down_part
+        own_grads = jnp.stack(
+            [jnp.sum(products[:, i * FF : (i + 1) * FF], axis=1) for i in range(EXP_DEV)], axis=1
+        )
+        hidden_low = (weight * hidden).astype(BF)
+        weighted = weight * down_part
+        d_gate = (weighted * up_part * (sigmoid + act * (1.0 - sigmoid))).astype(BF)
+        d_up = (weighted * act).astype(BF)
+        out_part = scatter_exp(dot_nt(hidden_low, down_all))
+        back_part = scatter_exp(dot_nt(d_gate, gate_all) + dot_nt(d_up, up_all))
+        gate_grads = lax.all_gather(own_grads, "exp", axis=1, tiled=True)
+        grad_logits = (
+            gates * (gate_grads - jnp.sum(gates * gate_grads, axis=-1, keepdims=True))
+        ).astype(BF)
+        second.append((hidden_low, d_gate, d_up, out_part, back_part, grad_logits))
+
+    two_both = jnp.concatenate([f[6] for f in first])
+    grad_both = jnp.concatenate([f[7] for f in first])
+    gate_sum = dot_tn(two_both, jnp.concatenate([s[1] for s in second]))
+    up_sum = dot_tn(two_both, jnp.concatenate([s[2] for s in second]))
+    down_sum = dot_tn(grad_both, jnp.concatenate([s[0] for s in second]))
+
+    def routed_sum(total):
+        parts = jnp.stack([total[:, i * FF : (i + 1) * FF] for i in range(EXP_DEV)])
+        return lax.psum_scatter(
+            parts.astype(BF), "seq", scatter_dimension=1, tiled=True
+        ).astype(F32)
+
+    def shared_part(total):
+        return total[:, EXP_DEV * FF : used]
 
     outputs_list = []
     grads_list = []
@@ -1044,14 +1429,15 @@
     qkv_sum = jnp.zeros((D, 3 * wide), F32)
     out_sum = jnp.zeros((wide, D), F32)
     for micro_batch in range(MB):
-        normed, qkv, mixed, lse, rows_in, hidden_one, two_low, gates = first[micro_batch]
-        outputs_list.append((hidden_one + outs[micro_batch]).astype(BF))
-        tail = tails[micro_batch]
-        own_logits = (gates * (tail - jnp.sum(gates * tail, axis=-1, keepdims=True))).astype(BF)
-        grad_two = backs[micro_batch] + dot_nt(own_logits, router_rows)
+        normed, qkv, mixed, lse, rows_in, hidden_one, two_all, _ = first[micro_batch]
+        _, _, _, out_part, back_part, grad_logits = second[micro_batch]
+        outputs_list.append((hidden_one + out_part).astype(BF))
+        own_logits = lax.dynamic_slice(grad_logits, (me * SEQ_DEV, 0), (SEQ_DEV, experts))
+        grad_two = back_part + dot_nt(own_logits, router_rows)
         back, gain_terms = norm_back(hidden_one, gain_two, grad_two)
         grad_hidden = cotangent[micro_batch, 0].astype(F32) + back
-        router_part = dot_tn(two_low, own_logits)
+        own_two = lax.dynamic_slice(two_all, (me * SEQ_DEV, 0), (SEQ_DEV, D))
+        router_part = dot_tn(own_two, own_logits)
         mix_all = gather_exp(grad_hidden.astype(BF))
         out_one, qkv_one, grad_part = backward(
             mix_all, normed, qkv, mixed, lse, cos_table, sin_table, w_qkv, w_out_heads, slot_live[None]
@@ -1079,6 +1465,7 @@
         return lax.all_gather(rows, "seq", axis=0, tiled=True).astype(F32)
 
     piece = rows_out // groups
+    shared_cols = jnp.concatenate([shared_part(t) for t in (gate_sum, up_sum, down_sum)], axis=1)
     shared_rows = to_rows(shared_cols).reshape(devices, piece, 3, share)
     shared_full = to_all(shared_rows.transpose(1, 2, 0, 3).reshape(piece, 3 * FF))
     qkv_rows = to_rows(qkv_sum).reshape(devices, piece, slots, 3, HD)
@@ -1109,7 +1496,221 @@
         shared_full[:, :FF],
         shared_full[:, FF : 2 * FF],
         shared_full[:, 2 * FF :],
-        *(routed_sum(parts) for parts in routed_sums),
+        routed_sum(gate_sum),
+        routed_sum(up_sum),
+        routed_sum(down_sum),
+    )
+
+
+def on_device_lines(
+    tokens,
+    cotangent,
+    expert_ids,
+    owner_table,
+    w_query,
+    w_key,
+    w_value,
+    w_out,
+    gain_one,
+    gain_two,
+    w_router,
+    shared_gate,
+    shared_up,
+    shared_down,
+    routed_gate,
+    routed_up,
+    routed_down,
+):
+    devices = lax.axis_size("exp")
+    groups = lax.axis_size("seq")
+    me = lax.axis_index("exp")
+    chips = devices // 2
+    experts = owner_table.shape[0]
+    length = SEQ_DEV * devices
+    rows_out = D // devices
+    slots = -(-HEADS // devices)
+    wide = slots * HD
+    share = FF // devices
+    own = MB * SEQ_DEV
+
+    head_of = [jnp.minimum(me + slot * devices, HEADS - 1) for slot in range(slots)]
+    w_qkv = jnp.concatenate(
+        [
+            lax.dynamic_slice(weight, (0, head * HD), (D, HD))
+            for head in head_of
+            for weight in (w_query, w_key, w_value)
+        ],
+        axis=1,
+    )
+    cos_table, sin_table = angle_tables(jnp.arange(length).astype(F32))
+    sin_table = jnp.where(jnp.arange(HD) < HD // 2, -sin_table, sin_table)
+    forward = pl.pallas_call(
+        functools.partial(attend_forward, slots),
+        out_shape=(
+            like(length, D),
+            like(length, 3 * wide),
+            like(length, wide),
+            like(slots, length, 1, dtype=F32),
+        ),
+        in_specs=[IN_VMEM] * 5,
+        out_specs=(IN_VMEM,) * 4,
+        compiler_params=pltpu.CompilerParams(vmem_limit_bytes=VMEM_BYTES),
+        cost_estimate=taking(12),
+        name="attend_forward",
+    )
+
+    expert_at = jnp.sum(
+        (owner_table[:, None] == jnp.arange(experts)[None, :]) * jnp.arange(experts)[:, None],
+        axis=0,
+    )
+    router_rows = jnp.take(w_router, expert_at, axis=1)
+    ids_all = lax.all_gather(expert_ids[:, 0], "exp", axis=1, tiled=True)
+    grad_all = lax.all_gather(cotangent[:, 0], "exp", axis=1, tiled=True)
+
+    kept, mixed_rows = [], []
+    for micro_batch in range(MB):
+        rows_all = gather_exp(tokens[micro_batch, 0])
+        normed, qkv, mixed, lse = forward(rows_all, gain_one[None], cos_table, sin_table, w_qkv)
+        kept.append((normed, qkv, mixed, lse))
+        sent = lax.all_to_all(
+            mixed.reshape(devices, SEQ_DEV, wide), "exp", split_axis=0, concat_axis=0, tiled=True
+        )
+        mixed_rows.append(
+            sent.reshape(devices, SEQ_DEV, slots, HD)
+            .transpose(1, 2, 0, 3)
+            .reshape(SEQ_DEV, slots * devices * HD)[:, :D]
+        )
+    normed, qkv, mixed, lse = [jnp.stack([k[i] for k in kept]) for i in range(4)]
+    own_mixed = jnp.concatenate(mixed_rows)
+    rows_in = tokens.reshape(own, D).astype(F32)
+    hidden_one = rows_in + dot(own_mixed, w_out)
+    two_low = norm_rows(hidden_one, gain_two).astype(BF)
+    named = jnp.any(
+        expert_ids.reshape(own, TOP)[:, :, None] == expert_at[None, None, :], axis=1
+    )
+    gates = named_softmax(dot(two_low, router_rows), named)
+
+    outs, backs, tails, routed_sums, shared_sum = experts_on_lines(
+        two_low.reshape(MB, SEQ_DEV, D),
+        grad_all,
+        ids_all,
+        expert_at,
+        router_rows,
+        (routed_gate, routed_up, routed_down),
+        (shared_gate, shared_up, shared_down),
+        share,
+    )
+    routed_full = [
+        lax.psum_scatter(parts, "seq", scatter_dimension=1, tiled=True).astype(F32)
+        for parts in routed_sums
+    ]
+    layer_out = (hidden_one + jnp.concatenate(outs)).astype(BF)
+    tail = jnp.concatenate(tails)
+    grad_logits = (gates * (tail - jnp.sum(gates * tail, axis=-1, keepdims=True))).astype(BF)
+    grad_two = jnp.concatenate(backs) + dot_nt(grad_logits, router_rows)
+    back, gain_two_terms = norm_back(hidden_one, gain_two, grad_two)
+    grad_hidden = cotangent.reshape(own, D).astype(F32) + back
+    grad_mix = grad_hidden.astype(BF)
+    d_mixed = dot_nt(grad_mix, w_out).astype(BF)
+
+    heads_sum, grad_a, grad_b = pl.pallas_call(
+        functools.partial(heads_backward, chips, slots),
+        out_shape=(
+            like(3 * slots, D, HD),
+            like(SEQ_DEV, D, dtype=F32),
+            like(SEQ_DEV, D, dtype=F32),
+        ),
+        in_specs=[IN_VMEM] * 8,
+        out_specs=(IN_VMEM,) * 3,
+        scratch_shapes=[
+            pltpu.VMEM((MB, length, wide), BF),
+            pltpu.VMEM((MB, slots, length, length), BF),
+            pltpu.VMEM((MB, length, 3 * wide), BF),
+            pltpu.VMEM((MB, devices, SEQ_DEV, D), BF),
+            pltpu.VMEM((length, HD), F32),
+            pltpu.VMEM((length, HD), F32),
+            pltpu.VMEM((MB, chips, SEQ_DEV, D), BF),
+            pltpu.VMEM((MB, chips + 1, SEQ_DEV, D), BF),
+            pltpu.SemaphoreType.DMA((MB, slots)),
+            pltpu.SemaphoreType.DMA((MB, devices, slots)),
+            pltpu.SemaphoreType.DMA((MB, devices, slots)),
+        ]
+        + scatter_sems(chips) * MB,
+        compiler_params=pltpu.CompilerParams(
+            collective_id=3, has_side_effects=True, vmem_limit_bytes=VMEM_BYTES
+        ),
+        cost_estimate=taking(70),
+        name="heads_backward",
+    )(
+        d_mixed.reshape(MB, SEQ_DEV, D), qkv, mixed, normed, lse, cos_table, sin_table, w_qkv
+    )
+    grad_normed = jnp.concatenate([grad_a, grad_b])
+    back_one, gain_one_terms = norm_back(rows_in, gain_one, grad_normed)
+    grad_tokens = (grad_hidden + back_one).astype(BF)
+    small = jnp.concatenate(
+        [
+            dot_tn(two_low, grad_logits),
+            jnp.sum(gain_one_terms, axis=0)[:, None],
+            jnp.sum(gain_two_terms, axis=0)[:, None],
+            jnp.zeros((D, LANES - experts - 2), F32),
+        ],
+        axis=1,
+    )
+    far = D + LANES
+    attn, shared_full, small_rows = pl.pallas_call(
+        functools.partial(spread_sums, chips),
+        out_shape=(
+            like(groups, rows_out, D, dtype=F32),
+            like(groups - 1, rows_out, devices * HD, dtype=F32),
+            like(rows_out, LANES, dtype=F32),
+        ),
+        in_specs=[IN_VMEM] * 5,
+        out_specs=(IN_VMEM,) * 3,
+        scratch_shapes=[
+            pltpu.VMEM((groups - 1, 3, D, HD), BF),
+            pltpu.VMEM((3, D, HD), BF),
+            pltpu.VMEM((groups, rows_out, 3 * devices * HD), BF),
+            pltpu.VMEM((D, far), BF),
+            pltpu.VMEM((rows_out, far), BF),
+            pltpu.VMEM((groups - 1, rows_out, far), BF),
+            pltpu.VMEM((rows_out, far), F32),
+            pltpu.VMEM((chips, rows_out, far), BF),
+            pltpu.VMEM((chips + 1, rows_out, far), BF),
+            pltpu.SemaphoreType.DMA((groups - 1, 3)),
+            pltpu.SemaphoreType.DMA((groups - 1, 3)),
+            pltpu.SemaphoreType.DMA((3,)),
+            pltpu.SemaphoreType.DMA((devices, 3)),
+            pltpu.SemaphoreType.DMA((devices, 3)),
+            pltpu.SemaphoreType.DMA,
+            pltpu.SemaphoreType.DMA((groups - 1,)),
+            pltpu.SemaphoreType.DMA((groups,)),
+            pltpu.SemaphoreType.DMA((groups,)),
+        ]
+        + scatter_sems(chips),
+        compiler_params=pltpu.CompilerParams(
+            collective_id=4, has_side_effects=True, vmem_limit_bytes=VMEM_BYTES
+        ),
+        cost_estimate=taking(60),
+        name="spread_sums",
+    )(heads_sum, shared_sum, own_mixed, grad_mix, small)
+    shared_grads = shared_full.reshape(groups - 1, rows_out, devices, HD)[..., :share].reshape(
+        groups - 1, rows_out, FF
+    )
+    whole = (MB, 1, SEQ_DEV, D)
+    return (
+        layer_out.reshape(whole),
+        grad_tokens.reshape(whole),
+        attn[0],
+        attn[1],
+        attn[2],
+        attn[3],
+        small_rows[:, experts],
+        small_rows[:, experts + 1],
+        jnp.take(small_rows[:, :experts], owner_table, axis=1),
+        shared_grads[0],
+        shared_grads[1],
+        shared_grads[2],
+        *routed_full,
     )
 
 
@@ -1117,6 +1718,8 @@
     rows = P(None, "seq", "exp", None)
     placed = (rows,) * 3 + (P(),) * 11 + (P("exp", None, None),) * 3
     wide = P("exp", None)
+    on_lines = mesh.shape["exp"] == 8 and mesh.shape["seq"] == 4
+    on_device = on_device_lines if on_lines else on_device_plain
     return jax.shard_map(
         on_device,
         mesh=mesh,

time: 918 us -> 652 us (0.71)
  waiting for transfers between devices: 454 us -> 38 us
  Pallas kernels: 237 us -> 445 us
  blocking collectives: 66.3 us -> 29.2 us
  starting transfers between devices: 24.6 us -> 14.1 us
    reduce_scatter x6 -> x3, waiting for transfers between devices: 226 us -> 0.01 us  [on_device_lines(): lax.psum_scatter(parts, 'seq', scatter_dimension=1, tiled=True).astype(F32)]
    pallas_call x4, Pallas kernels: 67.8 us -> 279 us  [the longest x1 178 us: on_device_lines(): pl.pallas_call(functools.partial(spread_sums, chips), out_shape=(like(gro...]
    unnamed x18 -> x6, waiting for transfers between devices: 127 us -> 1.92 us
    all_gather x4 -> x2, waiting for transfers between devices: 79.8 us -> 36.1 us  [gather_exp(): return lax.all_gather(array, 'exp', axis=0, tiled=True)]
    all_gather x3 -> x1, blocking collectives: 51 us -> 29.2 us  [on_device_lines(): ids_all = lax.all_gather(expert_ids[:, 0], 'exp', axis=1, tiled=True)]
    all_gather x2 -> x1, waiting for transfers between devices: 16.4 us -> 0.01 us  [on_device_lines(): grad_all = lax.all_gather(cotangent[:, 0], 'exp', axis=1, tiled=True)]
    psum x1 -> x0, blocking collectives: 15.3 us -> none  [on_device(): lax.psum(small, 'seq')]
    all_to_all x4 -> x2, starting transfers between devices: 23.5 us -> 13.9 us  [on_device_lines(): lax.all_to_all(mixed.reshape(devices, SEQ_DEV, wide), 'exp', split_axis=0...]
  transfers between devices with their start and end apart: 19 -> 8, of which waited for: 16 -> 2; matrix products, arithmetic and copies ran while one was open for 10% -> 14% of each run, Pallas kernels for 5% -> 43%
where the time goes in v3:
time: 652 us; the launch traced here: 642 us
  Pallas kernels  445 us (68%)
  local copies, waits for them, and re-layouts  55.1 us (8%)
  other arithmetic  39.1 us (6%)
  waiting for transfers between devices  38 us (6%)
  blocking collectives  29.2 us (4%)
  between operations  14.9 us (2%)
  starting transfers between devices  14.1 us (2%)
    pallas_call x1, Pallas kernels, on_device_lines(): pl.pallas_call(functools.partial(spread_sums, chips), out_shape=(like(gro...  178 us
    pallas_call x1, Pallas kernels, call_rows(): pl.pallas_call(kernel, out_shape=(like(MB, devices, SEQ_DEV, D), like(MB...  106 us
    pallas_call x1, Pallas kernels, on_device_lines(): pl.pallas_call(functools.partial(heads_backward, chips, slots), out_shape...  76 us
    pallas_call x1, Pallas kernels, call_sums(): pl.pallas_call(kernel, grid=(EXP_DEV, D // 256), out_shape=(like(EXP_DEV,...  60.8 us
    all_gather x2, waiting for transfers between devices, gather_exp(): return lax.all_gather(array, 'exp', axis=0, tiled=True)  36.1 us
    all_gather x1, blocking collectives, on_device_lines(): ids_all = lax.all_gather(expert_ids[:, 0], 'exp', axis=1, tiled=True)  29.2 us
    pallas_call x2, Pallas kernels, on_device_lines(): forward(rows_all, gain_one[None], cos_table, sin_table, w_qkv)  24.5 us
    unnamed x99, local copies, waits for them, and re-layouts  17.7 us
  transfers between devices with their start and end apart: 8, of which 2 were waited for; matrix products, arithmetic and copies ran while one was open for 14% of the time, Pallas kernels for 43%

profile of v3, /device:TPU:12, one launch (start us, length us, event | category | flops | bytes accessed | tf_op | source)
XLA Modules:
  0.0 642.2 jit_solution(15975075190146112616)
XLA Ops:
  7.3 2.1 fusion.18
  11.5 1.6 constant_dynamic-slice_fusion
  13.1 0.8 pad.16.refs_3_
  13.9 0.8 pad.17.refs_4_
  14.7 1.2 constant_dynamic-slice_fusion.2
  15.9 0.8 pad.18.refs_5_
  18.1 0.9 copy.110
  19.0 1.7 dynamic-slice_dynamic-update-slice_fusion.5
  20.7 1.7 dynamic-slice_dynamic-update-slice_fusion.4
  22.4 1.7 dynamic-slice_dynamic-update-slice_fusion.3
  24.2 1.7 dynamic-slice_dynamic-update-slice_fusion.2
  25.9 1.8 dynamic-slice_dynamic-update-slice_fusion.1
  27.6 1.8 dynamic-slice_dynamic-update-slice_fusion.w_ref
  29.6 2.9 negate_select_fusion
  32.5 12.1 %all-gather.8.cloned.1.call-done = bf16[1,1,1024,1280]{3,2,1,0:T(8,128)(2,1)} async-done(((bf16[1,1,128,1280]{3,2,1,0:T(8,128)(2,1)}), bf16[1,1,1024,1280]{3,2,1,0:T(8,128)(2,1)}) %all-gather.8.cloned.1.call-update) | async-done | bytes 2621456 | tf_op jit(solution)/shard_map/all_gather | solution.py:61
  44.6 12.2 %attend_forward.2 = (bf16[1024,1280]{1,0:T(8,128)(2,1)}, bf16[1024,768]{1,0:T(8,128)(2,1)}, bf16[1024,256]{1,0:T(8,128)(2,1)}, f32[2,1024,1]{2,1,0:T(8,128)}) custom-call(bf16[1024,1280]{1,0:T(8,128)(2,1)} %bitcast.146, f32[1,1280]{1,0:T(1,128)} %broadcast_in_dim.66.gain_ref, f32[1024,128]{1,0:T(8,128)} %get-tuple-element.164.cos_ref, ...), custom_call_target="tpu_custom_call" | custom-call | flops 12000000000 | bytes 1048576 | tf_op jit(solution)/shard_map/attend_forward/pallas_call | solution.py:1573
  56.9 2.0 copy.103
  58.9 5.2 all-to-all-start
  64.1 24.0 %all-gather.10.cloned.1.call-done = bf16[1,1,1024,1280]{3,2,1,0:T(8,128)(2,1)} async-done(((bf16[1,1,128,1280]{3,2,1,0:T(8,128)(2,1)}), bf16[1,1,1024,1280]{3,2,1,0:T(8,128)(2,1)}) %all-gather.10.cloned.1.call-update) | async-done | bytes 2621456 | tf_op jit(solution)/shard_map/all_gather | solution.py:61
  88.2 12.2 %attend_forward.3 = (bf16[1024,1280]{1,0:T(8,128)(2,1)}, bf16[1024,768]{1,0:T(8,128)(2,1)}, bf16[1024,256]{1,0:T(8,128)(2,1)}, f32[2,1024,1]{2,1,0:T(8,128)}) custom-call(bf16[1024,1280]{1,0:T(8,128)(2,1)} %bitcast.145, f32[1,1280]{1,0:T(1,128)} %broadcast_in_dim.66.gain_ref, f32[1024,128]{1,0:T(8,128)} %get-tuple-element.164.cos_ref, ...), custom_call_target="tpu_custom_call" | custom-call | flops 12000000000 | bytes 1048576 | tf_op jit(solution)/shard_map/attend_forward/pallas_call | solution.py:1573
  100.4 2.1 copy.105
  102.5 8.7 %all-to-all-start.1 = ((bf16[8,128,256]{1,2,0:T(8,128)(2,1)}), bf16[8,128,256]{1,2,0:T(8,128)(2,1)}, u32[]{:S(2)}, u32[]{:S(2)}) async-start(bf16[8,128,256]{1,2,0:T(8,128)(2,1)} %copy.105), calls=%async_computation.1 | async-start | bytes 1048576 | tf_op jit(solution)/shard_map/all_to_all | solution.py:1575
  111.2 1.0 fusion.7
  113.0 29.2 %all-gather.3 = s32[2,1,1024,7]{2,1,3,0:T(1,128)S(1)} all-gather(s32[2,1,128,7]{2,1,3,0:T(1,128)S(1)} %copy-done.32), channel_id=5, replica_groups=mesh['seq'=4,'exp'=8] {'exp'}, dimensions={2}, use_global_device_ids=true | all-gather | bytes 64512 | tf_op jit(solution)/shard_map/all_gather | solution.py:1567
  142.3 2.7 compare_reduce_fusion
  144.9 1.1 convert_element_type.95
  146.0 2.2 copy.104
  148.3 1.2 copy.134
  150.2 2.2 copy.106
  152.4 1.3 copy.133
  153.8 1.1 multiply_reduce_fusion.5
  154.9 1.0 copy-done.3
  156.0 1.0 multiply_convert_fusion
  157.0 106.0 %expert_rows.1 = (bf16[2,8,128,1280]{3,2,1,0:T(8,128)(2,1)}, bf16[2048,1920]{1,0:T(8,128)(2,1)}, bf16[2048,1920]{1,0:T(8,128)(2,1)}, bf16[2048,1920]{1,0:T(8,128...) custom-call(bf16[2,128,1280]{2,1,0:T(8,128)(2,1)} %bitcast.120, ...), custom_call_target="tpu_custom_call" | custom-call | flops 99999997952 | bytes 1048576 | tf_op jit(solution)/shard_map/expert_rows/pallas_call | solution.py:1139
  263.0 60.8 %expert_sums.1 = (bf16[2,1280,896]{2,1,0:T(8,128)(2,1)}, bf16[2,1280,896]{2,1,0:T(8,128)(2,1)}, bf16[2,1280,896]{2,1,0:T(8,128)(2,1)}, bf16[3,1280,128]{2,1,0:T(...) custom-call(bf16[2048,1280]{1,0:T(8,128)(2,1)} %bitcast.147, bf16[2048,1280]{1,0:T(8,128)(2,1)} %bitcast.144, ...), custom_call_target="tpu_custom_call" | custom-call | flops 60000002048 | bytes 1048576 | tf_op jit(solution)/shard_map/expert_sums/pallas_call | solution.py:1199
  324.8 1.3 multiply_reduce_fusion.3
  327.2 1.6 reduce.5
  328.8 1.6 reduce.6
  330.4 2.0 copy.114.lse_ref
  332.3 2.4 pad_maximum_fusion.2.mixed_ref
  334.8 3.6 pad_maximum_fusion.1.qkv_ref
  338.5 2.8 pad_maximum_fusion.normed_ref
  341.7 0.9 pad_maximum_fusion.3.mixed_ref
  342.6 0.9 slice.72
  343.6 2.0 slice.71
  345.6 1.0 slice_add_fusion.1
  346.8 2.5 multiply_reduce_fusion
  349.3 1.0 copy-done.6
  350.8 1.9 convolution_convert_fusion
  352.7 76.0 %heads_backward.1 = (bf16[6,1280,128]{2,1,0:T(8,128)(2,1)}, f32[128,1280]{1,0:T(8,128)}, f32[128,1280]{1,0:T(8,128)}) custom-call(bf16[2,128,1280]{2,1,0:T(8,128)(2,1)} %bitcast.148, bf16[2,1024,768]{2,1,0:T(8,128)(2,1)} %pad_maximum_fusion.1.qkv_ref, bf16[2,1024,256]{2,1,0:T(8,128)(2,1)} %pad_maximum_fusion.2.mixed_ref, ...), custom_call_target="tpu_custom_call" | custom-call | flops 70000001024 | bytes 1048576 | tf_op jit(solution)/shard_map/heads_backward/pallas_call | solution.py:1616
  428.7 1.3 constant_dynamic-update-slice_fusion.1
  432.1 1.3 maximum_maximum_fusion.small_ref
  433.4 178.2 %spread_sums.1 = (f32[4,160,1280]{2,1,0:T(8,128)}, f32[3,160,1024]{2,1,0:T(8,128)}, f32[160,128]{1,0:T(8,128)}) custom-call(bf16[6,1280,128]{2,1,0:T(8,128)(2,1)} %get-tuple-element.63.qkv_ref, bf16[3,1280,128]{2,1,0:T(8,128)(2,1)} %get-tuple-element.64.shared_ref, bf16[256,1280]{1,0:T(8,128)(2,1)} %pad_maximum_fusion.3.mixed_ref, ...), custom_call_target="tpu_custom_call" | custom-call | flops 60000002048 | bytes 1048576 | tf_op jit(solution)/shard_map/spread_sums/pallas_call | solution.py:1660
  611.6 2.0 copy.127
  613.6 1.0 fusion.17
  614.5 2.1 squeeze.49
  616.6 1.0 squeeze.50
  617.7 1.0 squeeze.51
  619.5 0.8 slice_reduce_fusion
  621.0 3.8 slice_bitcast_fusion
  624.8 1.7 fusion.5
  626.6 2.8 convert_element_type.91
  629.4 3.0 convert_element_type.92
  632.3 2.8 convert_element_type.93
  (148 shorter events, 12.2 us)
Async XLA Ops:
  7.2 146.6 %copy-start = (bf16[1280,1280]{1,0:T(8,128)(2,1)S(1)}, bf16[1280,1280]{1,0:T(8,128)(2,1)}, u32[]{:S(2)}) copy-start(bf16[1280,1280]{1,0:T(8,128)(2,1)} %param.24) | copy-start | bytes 9830404
  7.2 3.7 copy-start.30
  7.2 37.4 %all-gather.8.cloned.1.call-start = ((), (), s32[]{:S(2)}) async-start(), calls=%async_computation.8 | async-start | bytes 2949120 | tf_op jit(solution)/shard_map/all_gather | solution.py:61
  9.4 78.8 %all-gather.10.cloned.1.call-start = ((), (), s32[]{:S(2)}) async-start(), calls=%async_computation.9 | async-start | bytes 2949120 | tf_op jit(solution)/shard_map/all_gather | solution.py:61
  10.1 146.9 %all-gather.12.cloned.1.call-start = ((), (), s32[]{:S(2)}) async-start(), calls=%async_computation.10 | async-start | bytes 5898240 | tf_op jit(solution)/shard_map/all_gather | solution.py:1568
  13.0 3.7 copy-start.42
  13.1 4.4 copy-start.2
  16.8 96.2 %copy-start.40 = (s32[16]{0:T(128)}, s32[16]{0:T(128)S(1)}, u32[]{:S(2)}) copy-start(s32[16]{0:T(128)S(1)} %select_reduce_fusion) | copy-start | bytes 196
  58.9 43.6 %all-to-all-start = ((bf16[8,128,256]{1,2,0:T(8,128)(2,1)}), bf16[8,128,256]{1,2,0:T(8,128)(2,1)}, u32[]{:S(2)}, u32[]{:S(2)}) async-start(bf16[8,128,256]{1,2,0:T(8,128)(2,1)} %copy.103), calls=%async_computation | async-start | bytes 1048576 | tf_op jit(solution)/shard_map/all_to_all | solution.py:1575
  102.5 10.5 %copy-start.32 = (s32[2,1,128,7]{2,1,3,0:T(1,128)S(1)}, s32[2,1,128,7]{2,1,3,0:T(1,128)}, u32[]{:S(2)}) copy-start(s32[2,1,128,7]{2,1,3,0:T(1,128)} %param.19) | copy-start | bytes 21508
  102.5 47.7 %all-to-all-start.1 = ((bf16[8,128,256]{1,2,0:T(8,128)(2,1)}), bf16[8,128,256]{1,2,0:T(8,128)(2,1)}, u32[]{:S(2)}, u32[]{:S(2)}) async-start(bf16[8,128,256]{1,2,0:T(8,128)(2,1)} %copy.105), calls=%async_computation.1 | async-start | bytes 1048576 | tf_op jit(solution)/shard_map/all_to_all | solution.py:1575
  111.2 515.4 %reduce-scatter.4.cloned.1.call-start = ((), (), s32[]{:S(2)}) async-start(), calls=%async_computation.5 | async-start | bytes 5734400 | tf_op jit(solution)/shard_map/reduce_scatter | solution.py:1604
  111.2 34.8 %copy-start.36 = (pred[16]{0:T(512)(128)(4,1)}, pred[16]{0:T(512)(128)(4,1)S(1)}, u32[]{:S(2)}) copy-start(pred[16]{0:T(512)(128)(4,1)S(1)} %compare_and_fusion.1) | copy-start | bytes 52
  152.4 1.3 copy-start.8
  152.4 1.3 copy-start.18
  153.7 1.2 copy-start.20
  153.8 2.2 copy-start.28
  154.9 1.1 copy-start.3
  154.9 1.1 copy-start.34
  323.9 305.5 %reduce-scatter.6.cloned.1.call-start = ((), (), s32[]{:S(2)}) async-start(), calls=%async_computation.6 | async-start | bytes 5734400 | tf_op jit(solution)/shard_map/reduce_scatter | solution.py:1604
  323.9 0.7 copy-start.33
  324.0 0.8 copy-start.41
  324.0 2.2 copy-start.43
  324.5 307.8 %reduce-scatter.8.cloned.1.call-start = ((), (), s32[]{:S(2)}) async-start(), calls=%async_computation.7 | async-start | bytes 5734400 | tf_op jit(solution)/shard_map/reduce_scatter | solution.py:1604
  332.3 2.4 copy-start.17
  334.8 3.6 copy-start.15
  334.8 3.7 copy-start.16
  338.5 2.8 copy-start.12
  338.5 2.8 copy-start.14
  338.5 2.8 copy-start.37
  338.5 3.2 copy-start.19
  338.5 3.2 copy-start.21
  341.3 1.3 copy-start.22
  342.6 4.1 copy-start.29
  342.6 4.2 copy-start.35
  346.8 3.6 copy-start.4
  346.8 3.6 copy-start.10
  349.3 1.1 copy-start.6
  350.8 1.9 copy-start.26
  428.7 1.3 copy-start.27
  428.7 1.5 copy-start.9
  428.7 1.5 copy-start.31
  430.7 1.1 copy-start.13
  616.6 2.1 copy-start.23
  617.7 2.6 copy-start.39
  621.0 3.8 copy-start.5
  621.0 3.8 copy-start.7
  621.0 3.8 copy-start.11
  621.0 3.8 copy-start.24
  621.0 3.8 copy-start.25
  621.0 3.8 copy-start.38
  629.4 5.8 copy-start.1
Sparse Core Ops, SparseCore 0:
  10.3 34.3 all-gather.7
  46.8 41.2 all-gather.9
  89.8 65.4 all-gather.11
  324.0 55.8 reduce-scatter.3
  382.9 55.9 reduce-scatter.5
  441.8 107.4 reduce-scatter.7

commit v4 on v3

--- a/solution.py
+++ b/solution.py
@@ -3,6 +3,7 @@
 
 import jax
 import jax.numpy as jnp
+import numpy as np
 from jax import lax
 from jax.experimental import pallas as pl
 from jax.experimental.pallas import tpu as pltpu
@@ -43,6 +44,15 @@
     angles = positions[:, None] * frequency[None, :]
     angles = jnp.concatenate([angles, angles], axis=-1)
     return (jnp.cos(angles), jnp.sin(angles))
+
+
+def turn_tables(length):
+    angles = np.arange(length)[:, None] * 10000.0 ** (-2.0 * np.arange(HD // 2) / HD)
+    cos, sin = np.cos(angles), np.sin(angles)
+    return (
+        jnp.asarray(np.concatenate([cos, cos], axis=1), F32),
+        jnp.asarray(np.concatenate([-sin, sin], axis=1), F32),
+    )
 
 
 def dot(a, b):
@@ -449,9 +459,9 @@
 
 def expert_rows(
     chips, experts,
-    own_ref, grad_ref, named_ref, router_ref, routed_refs, shared_refs,
-    rows_ref, hidden_ref, d_gate_ref, d_up_ref, out_b_ref, back_b_ref, out_a_ref, back_a_ref,
-    weights, rows, grads, stage, out, back, pairs, lines, weight_sem, local_sem, grad_sem, stage_sem, keep_sem,
+    own_ref, grad_own_ref, grad_ref, named_ref, router_ref, routed_refs, shared_refs,
+    rows_ref, grads_ref, hidden_ref, d_gate_ref, d_up_ref, out_ref, back_b_ref, back_a_ref,
+    weights, rows, grads, stage, out, back, pair, line, weight_sem, local_sem, stage_sem, keep_sem,
     *sems,
 ):
     chip, core = place()
@@ -459,16 +469,13 @@
     blocks = chips
     size = 2 * SEQ_DEV
     gathers = [Gather(chips, own_ref.at[m], rows.at[m], sems[6 * m : 6 * m + 6]) for m in range(MB)]
-    parts = (out, back)
-    scatters = [
-        Scatter(
-            chips,
-            lambda to, k=k: parts[k].at[0, 2 * to + 1 - core],
-            lambda to, k=k: parts[k].at[0, 2 * to + core],
-            pairs[k], lines[k], sems[12 + 6 * k : 18 + 6 * k],
-        )
-        for k in range(2)
-    ]
+    grad_gather = Gather(chips, grad_own_ref.at[1], grads.at[1], sems[18:24])
+    scatter = Scatter(
+        chips,
+        lambda to: back.at[0, 2 * to + 1 - core],
+        lambda to: back.at[0, 2 * to + core],
+        pair, line, sems[12:18],
+    )
     loads = []
     for k in range(3):
         for e in range(EXP_DEV):
@@ -484,14 +491,6 @@
             )
         )
 
-    def grad_load(step):
-        block = block_order(chip, step % blocks, chips)
-        start = pl.multiple_of(block * size, size)
-        return pltpu.make_async_copy(
-            grad_ref.at[step // blocks, pl.ds(start, size), :], grads.at[step % 2],
-            grad_sem.at[step % 2],
-        )
-
     def stage_out(step, k):
         block = block_order(chip, step % blocks, chips)
         start = pl.multiple_of((step // blocks * blocks + block) * size, size)
@@ -500,19 +499,26 @@
             stage.at[step % 2, k], target.at[pl.ds(start, size), :], stage_sem.at[step % 2, k]
         )
 
-    def keep_out(step, k):
+    def out_copy(step):
         block = block_order(chip, step % blocks, chips)
-        target = (out_b_ref, back_b_ref)[k]
         return pltpu.make_async_copy(
-            parts[k].at[1, pl.ds(2 * block, 2)], target.at[pl.ds(2 * block, 2)],
-            keep_sem.at[k, step % blocks],
-        )
-
-    grad_load(0).start()
+            out.at[step % 2], out_ref.at[step // blocks, pl.ds(2 * block, 2)], keep_sem.at[0, step % 2]
+        )
+
+    def back_copy(step):
+        block = block_order(chip, step % blocks, chips)
+        return pltpu.make_async_copy(
+            back.at[1, pl.ds(2 * block, 2)], back_b_ref.at[pl.ds(2 * block, 2)],
+            keep_sem.at[1, step % blocks],
+        )
+
     for load in loads:
         load.start()
     own_copies = [
         pltpu.make_async_copy(own_ref.at[m], rows.at[m, me], local_sem.at[m]) for m in range(MB)
+    ] + [
+        pltpu.make_async_copy(grad_ref, grads.at[0], local_sem.at[2]),
+        pltpu.make_async_copy(grad_own_ref.at[1], grads.at[1, me], local_sem.at[3]),
     ]
     for copy in own_copies:
         copy.start()
@@ -534,32 +540,33 @@
         for m in range(MB):
             for hop in range(1, chips):
                 at(step, m * blocks + hop, lambda m=m, hop=hop: gathers[m].hop(hop))
+        for hop in range(1, chips):
+            at(step, blocks + hop, lambda hop=hop: grad_gather.hop(hop))
         at(step, 1, gathers[1].start)
-        at(step, blocks, lambda: [s.start() for s in scatters])
-        for turn in range(chips - 1):
-            at(step, blocks + 1 + turn, lambda turn=turn: scatters[1].slot(turn))
+        at(step, 2, grad_gather.start)
+        at(step, blocks, scatter.start)
         for m in range(MB):
 
             @pl.when(micro_batch == m)
             def _():
                 gathers[m].take_pair(block - chip)
 
-        grad_load(step).wait()
-
-        @pl.when(step + 1 < MB * blocks)
+        @pl.when(micro_batch == 1)
         def _():
-            grad_load(step + 1).start()
+            grad_gather.take_pair(block - chip)
 
         @pl.when(step >= 2)
         def _():
             for k in range(3):
                 stage_out(step - 2, k).wait()
+            out_copy(step - 2).wait()
 
         slot = step % 2
         normed = rows[micro_batch, pl.ds(2 * block, 2)].reshape(size, D)
-        grad = grads[slot]
+        grad = grads[micro_batch, pl.ds(2 * block, 2)].reshape(size, D)
         logits = dot(normed, router_ref[...])
-        named = named_ref[pl.ds(pl.multiple_of((micro_batch * blocks + block) * size, size), size), :]
+        names = pl.ds(pl.multiple_of(micro_batch * SEQ_DEV, SEQ_DEV), SEQ_DEV)
+        named = named_ref[pl.ds(2 * block, 2), names, :].reshape(size, LANES).astype(F32)
         chosen = jnp.where(named > 0.0, logits, -1e30)
         powers = jnp.where(
             named > 0.0, jnp.exp(chosen - jnp.max(chosen, axis=1, keepdims=True)), 0.0
@@ -603,9 +610,10 @@
         for k in range(3):
             stage_out(step, k).start()
         for turn in range(chips - 1):
-            at(step, blocks + turn, lambda turn=turn: scatters[0].slot(turn))
+            at(step, blocks + turn, lambda turn=turn: scatter.slot(turn))
         result = dot_nt(stage[slot, 0], weights[2]).astype(BF)
-        out[micro_batch, pl.ds(2 * block, 2)] = result.reshape(2, SEQ_DEV, D)
+        out[slot] = result.reshape(2, SEQ_DEV, D)
+        out_copy(step).start()
         result = (dot_nt(stage[slot, 1], weights[0]) + dot_nt(stage[slot, 2], weights[1])).astype(BF)
         back[micro_batch, pl.ds(2 * block, 2), :, :D] = result.reshape(2, SEQ_DEV, D)
         tail = jnp.zeros((size, LANES), F32)
@@ -617,8 +625,7 @@
 
         @pl.when(micro_batch == 1)
         def _():
-            for k in range(2):
-                keep_out(step, k).start()
+            back_copy(step).start()
 
         return carry
 
@@ -626,41 +633,127 @@
     last = MB * blocks
     row_copies = [
         pltpu.make_async_copy(rows.at[m], rows_ref.at[m], local_sem.at[m]) for m in range(MB)
+    ] + [
+        pltpu.make_async_copy(grads.at[m], grads_ref.at[m], local_sem.at[2 + m]) for m in range(MB)
     ]
     for copy in row_copies:
         copy.start()
-    scatters[0].finish(out_a_ref)
-    scatters[1].finish(back_a_ref)
+    scatter.finish(back_a_ref)
     for m in range(MB):
         gathers[m].finish(False)
+    grad_gather.finish(False)
     for copy in row_copies:
         copy.wait()
     for step in (last - 2, last - 1):
         for k in range(3):
             stage_out(step, k).wait()
+        out_copy(step).wait()
     for turn in range(blocks):
-        for k in range(2):
-            keep_out(blocks + turn, k).wait()
+        back_copy(blocks + turn).wait()
+
+
+def seq_all_scratch(rows, width):
+    groups = 4
+    return [
+        pltpu.VMEM((rows, groups * width), BF),
+        pltpu.VMEM((groups - 1, rows, width), BF),
+        pltpu.VMEM((rows, groups * width), BF),
+    ] + [pltpu.SemaphoreType.DMA((groups,))] * 4
+
+
+class SeqAll:
+    def __init__(self, scratch):
+        self.low, self.arrived, self.whole = scratch[:3]
+        self.first_send, self.first_recv, self.last_send, self.last_recv = scratch[3:]
+        self.groups = 4
+        self.width = self.arrived.shape[2]
+        self.group = lax.axis_index("seq")
+
+    def _part(self, ref, device):
+        return ref.at[:, pl.ds(pl.multiple_of(device * self.width, LANES), self.width)]
+
+    def _copy(self, source, target, send, recv, away):
+        return pltpu.make_async_remote_copy(
+            src_ref=source, dst_ref=target, send_sem=send.at[away], recv_sem=recv.at[away],
+            device_id={"seq": (self.group + away) % self.groups}, device_id_type=MESH,
+        )
+
+    def _first(self, away):
+        part = self._part(self.low, (self.group + away) % self.groups)
+        return self._copy(part, self.arrived.at[away - 1], self.first_send, self.first_recv, away)
+
+    def _last(self, away):
+        part = self._part(self.whole, self.group)
+        return self._copy(part, part, self.last_send, self.last_recv, away)
+
+    def start(self):
+        for away in range(1, self.groups):
+            self._first(away).start()
+
+    def middle(self):
+        total = self._part(self.low, self.group)[...].astype(F32)
+        for away in range(1, self.groups):
+            self._first(away).wait_recv()
+            total += self.arrived[away - 1].astype(F32)
+        self._part(self.whole, self.group)[...] = total.astype(BF)
+        for away in range(1, self.groups):
+            self._last(away).start()
+
+    def take(self):
+        for away in range(1, self.groups):
+            part = self._part(self.whole, (self.group + self.groups - away) % self.groups)
+            self._copy(part, part, self.last_send, self.last_recv, away).wait_recv()
+
+    def finish(self):
+        for away in range(1, self.groups):
+            self._first(away).wait_send()
+            self._last(away).wait_send()
+
+
+def packed(padded, devices):
+    share = FF // devices
+    return jnp.concatenate(
+        [padded[:, device * HD : device * HD + share] for device in range(devices)], axis=1
+    )
 
 
 def expert_sums(
     chips,
-    rows_ref, grads_ref, hidden_ref, d_gate_ref, d_up_ref, shared_h_ref, shared_g_ref, shared_u_ref, out_ref, back_ref,
-    gate_ref, up_ref, down_ref, shared_ref, out_b_ref, back_b_ref,
-    mine_out, mine_back, pairs, lines, local_sem, *sems,
+    rows_ref, grads_ref, hidden_ref, d_gate_ref, d_up_ref, shared_h_ref, shared_g_ref, shared_u_ref, back_ref,
+    gate_ref, up_ref, down_ref, back_b_ref, shared_outs, gate_rows_ref, up_rows_ref,
+    mine, pair, line, local_sem, stage, stage_sem, shared, arrived, summed, held, *sems,
 ):
     chip, core = place()
-    step = pl.program_id(0) * (D // 256) + pl.program_id(1)
-    parts, mine = (out_ref, back_ref), (mine_out, mine_back)
-    scatters = [
-        Scatter(
-            chips,
-            lambda to, k=k: parts[k].at[2 * to + 1 - core],
-            lambda to, k=k: mine[k].at[to],
-            pairs[k], lines[k], sems[6 * k : 6 * k + 6],
-        )
-        for k in range(2)
+    devices = 2 * chips
+    half = D // 2
+    matrix, side = pl.program_id(0), pl.program_id(1)
+    step = 2 * matrix + side
+    last = 2 * 3 * EXP_DEV - 1
+    scatter = Scatter(
+        chips,
+        lambda to: back_ref.at[2 * to + 1 - core],
+        lambda to: mine.at[to],
+        pair, line, sems[:6],
+    )
+    spread = Spread(
+        devices, 4, 1,
+        lambda owner, k: shared.at[owner],
+        lambda k, device: device >= 0,
+        lambda device, k: device,
+        arrived, summed, held, devices * HD, sems[6:13],
+    )
+    routed = [
+        SeqSum(source.at[0], target, k % 2 == 0, k, sems[13:])
+        for k, (source, target) in enumerate(((gate_ref, gate_rows_ref), (up_ref, up_rows_ref)))
     ]
+    targets = [(gate_ref, 0), (up_ref, 0), (gate_ref, 1), (up_ref, 1), (down_ref, 0), (down_ref, 1)]
+
+    def write(number):
+        target, e = targets[number // 2]
+        part = pl.ds(number % 2 * half, half)
+        return pltpu.make_async_copy(
+            stage.at[number % 2], target.at[e, part], stage_sem.at[number % 2]
+        )
 
     def at(number, action):
         @pl.when(step == number)
@@ -669,38 +762,64 @@
 
     def begin():
         loads = [
-            pltpu.make_async_copy(
-                parts[k].at[2 * to + core], mine[k].at[to], local_sem.at[k, to]
-            )
-            for k in range(2)
+            pltpu.make_async_copy(back_ref.at[2 * to + core], mine.at[to], local_sem.at[to])
             for to in range(chips)
         ]
         for load in loads:
             load.start()
-        meet(chips)
-        for s in scatters:
-            s.start()
+        meet_all(("seq", "exp"))
+        scatter.start()
         for load in loads:
             load.wait()
 
     at(0, begin)
-    ticks = [(k, turn) for turn in range(chips - 1) for k in range(2)]
-    for number, (k, turn) in enumerate(ticks):
-        at(min(number + 1, 7), lambda k=k, turn=turn: scatters[k].slot(turn))
-    normed, grad = rows_ref[...], grads_ref[...]
-    gate_ref[0] = dot_tn(normed, d_gate_ref[...]).astype(BF)
-    up_ref[0] = dot_tn(normed, d_up_ref[...]).astype(BF)
-    down_ref[0] = dot_tn(grad, hidden_ref[...]).astype(BF)
-
-    @pl.when(pl.program_id(0) == 0)
+    for number in range(2, last + 1):
+        at(number, lambda number=number: write(number - 2).wait())
+    at(2, lambda: scatter.slot(0))
+    at(3, routed[0].start)
+    at(5, routed[1].start)
+    at(4, lambda: scatter.slot(1))
+    at(6, lambda: scatter.slot(2))
+    at(7, spread.middle)
+    slot = step % 2
+
+    @pl.when(jnp.logical_or(matrix == 0, matrix == 2))
     def _():
-        start = pl.ds(pl.multiple_of(pl.program_id(1) * 256, 256), 256)
-        shared_ref[0, start, :] = dot_tn(normed, shared_g_ref[...]).astype(BF)
-        shared_ref[1, start, :] = dot_tn(normed, shared_u_ref[...]).astype(BF)
-        shared_ref[2, start, :] = dot_tn(grad, shared_h_ref[...]).astype(BF)
-
-    at(8, lambda: scatters[0].finish(out_b_ref))
-    at(9, lambda: scatters[1].finish(back_b_ref))
+        stage[slot] = dot_tn(rows_ref[...], d_gate_ref[...]).astype(BF)
+
+    @pl.when(jnp.logical_or(matrix == 1, matrix == 3))
+    def _():
+        stage[slot] = dot_tn(rows_ref[...], d_up_ref[...]).astype(BF)
+
+    @pl.when(matrix >= 4)
+    def _():
+        stage[slot] = dot_tn(grads_ref[...], hidden_ref[...]).astype(BF)
+
+    @pl.when(matrix == 0)
+    def _():
+        part = pl.ds(pl.multiple_of(side * half, half), half)
+        shared[0, part, :] = dot_tn(rows_ref[...], shared_g_ref[...]).astype(BF)
+        shared[1, part, :] = dot_tn(rows_ref[...], shared_u_ref[...]).astype(BF)
+        shared[2, part, :] = dot_tn(grads_ref[...], shared_h_ref[...]).astype(BF)
+
+    for number in range(last + 1):
+        at(number, lambda number=number: write(number).start())
+    at(1, spread.start)
+    at(8, lambda: scatter.finish(back_b_ref))
+    at(9, spread.hand_out)
+    at(9, routed[0].middle)
+
+    @pl.when(step == last)
+    def _():
+        routed[1].middle()
+        write(last - 1).wait()
+        write(last).wait()
+        spread.take()
+        for kind, target in enumerate(shared_outs):
+            target[...] = packed(spread.of_kind(kind)[...].astype(F32), devices)
+        for job in routed:
+            job.finish()
+        spread.finish()
 
 
 def meet_all(axes):
@@ -715,11 +834,438 @@
     pl.semaphore_wait(barrier, count)
 
 
+FIRST_EXTRA, EXTRA_APART = 2, 3
+
+
+def slot_head(slot, device, devices):
+    return device if slot == 0 else devices + (device - FIRST_EXTRA) // EXTRA_APART
+
+
+def slot_lives(slot, device, devices):
+    if slot == 0:
+        return device >= 0
+    past = device - FIRST_EXTRA
+    return jnp.logical_and(
+        jnp.logical_and(past >= 0, past % EXTRA_APART == 0),
+        past < EXTRA_APART * (HEADS - devices),
+    )
+
+
+def spread_sems(devices, groups, units):
+    return [
+        pltpu.SemaphoreType.DMA((groups - 1, units)),
+        pltpu.SemaphoreType.DMA((groups - 1, units)),
+        pltpu.SemaphoreType.DMA((units,)),
+        pltpu.SemaphoreType.DMA((devices, units)),
+        pltpu.SemaphoreType.DMA((devices, units)),
+        pltpu.SemaphoreType.DMA((groups,)),
+        pltpu.SemaphoreType.DMA((groups,)),
+    ]
+
+
+class Spread:
+    def __init__(self, devices, groups, units, unit, lives, column, arrived, summed, held, width, sems):
+        self.devices, self.groups, self.units = devices, groups, units
+        self.unit, self.lives, self.column = unit, lives, column
+        self.arrived, self.summed, self.held, self.width = arrived, summed, held, width
+        self.first_send, self.first_recv, self.local_sem = sems[:3]
+        self.second_send, self.second_recv, self.third_send, self.third_recv = sems[3:]
+        self.kinds = groups - 1
+        self.rows = D // devices
+        self.group, self.me = lax.axis_index("seq"), lax.axis_index("exp")
+
+    def _rows(self, device):
+        return pl.ds(pl.multiple_of(device * self.rows, 32), self.rows)
+
+    def _columns(self, device, k):
+        return pl.ds(pl.multiple_of(self.column(device, k) * HD, HD), HD)
+
+    def _along_seq(self, source, target, send, recv, away):
+        return pltpu.make_async_remote_copy(
+            src_ref=source, dst_ref=target, send_sem=send, recv_sem=recv,
+            device_id={"seq": (self.group + away) % self.groups}, device_id_type=MESH,
+        )
+
+    def _along_exp(self, source, target, away, k):
+        return pltpu.make_async_remote_copy(
+            src_ref=source, dst_ref=target,
+            send_sem=self.second_send.at[away, k], recv_sem=self.second_recv.at[away, k],
+            device_id={"exp": (self.me + away) % self.devices}, device_id_type=MESH,
+        )
+
+    def _first(self, away, k):
+        owner = (self.group + away) % self.groups
+        return self._along_seq(
+            self.unit(owner, k), self.arrived.at[away - 1, k],
+            self.first_send.at[away - 1, k], self.first_recv.at[away - 1, k], away,
+        )
+
+    def _second(self, away, k):
+        other = (self.me + away) % self.devices
+        return self._along_exp(
+            self.summed.at[k, self._rows(other)], self.held.at[0, :, self._columns(self.me, k)], away, k
+        )
+
+    def _own(self, k):
+        return pltpu.make_async_copy(
+            self.summed.at[k, self._rows(self.me)], self.held.at[0, :, self._columns(self.me, k)],
+            self.local_sem.at[k],
+        )
+
+    def _third(self, away):
+        return self._along_seq(
+            self.held.at[0, :, : self.width], self.held.at[away, :, : self.width],
+            self.third_send.at[away], self.third_recv.at[away], away,
+        )
+
+    def _sends_first(self, action):
+        for k in range(self.units):
+            for away in range(1, self.groups):
+
+                @pl.when(
+                    jnp.logical_and(
+                        (self.group + away) % self.groups < self.kinds, self.lives(k, self.me)
+                    )
+                )
+                def _():
+                    action(self._first(away, k))
+
+    def start(self):
+        self._sends_first(lambda copy: copy.start())
+
+    def middle(self):
+        @pl.when(self.group < self.kinds)
+        def _():
+            for k in range(self.units):
+
+                @pl.when(self.lives(k, self.me))
+                def _():
+                    total = self.unit(self.group, k)[...].astype(F32)
+                    for away in range(1, self.groups):
+                        block = self.arrived.at[away - 1, k]
+                        self._along_seq(
+                            block, block, self.first_send.at[away - 1, k],
+                            self.first_recv.at[away - 1, k], away,
+                        ).wait_recv()
+                        total += block[...].astype(F32)
+                    self.summed[k] = total.astype(BF)
+                    for away in range(1, self.devices):
+                        self._second(away, k).start()
+                    self._own(k).start()
+
+    def hand_out(self):
+        @pl.when(self.group < self.kinds)
+        def _():
+            for k in range(self.units):
+
+                @pl.when(self.lives(k, self.me))
+                def _():
+                    self._own(k).wait()
+
+                for away in range(1, self.devices):
+                    source = (self.me + self.devices - away) % self.devices
+
+                    @pl.when(self.lives(k, source))
+                    def _():
+                        block = self.held.at[0, :, self._columns(source, k)]
+                        self._along_exp(block, block, away, k).wait_recv()
+
+            for away in range(1, self.groups):
+                self._third(away).start()
+
+    def take(self):
+        for away in range(1, self.groups):
+
+            @pl.when((self.group + self.groups - away) % self.groups < self.kinds)
+            def _():
+                self._third(away).wait_recv()
+
+    def of_kind(self, kind):
+        return self.held.at[(self.group + self.groups - kind) % self.groups]
+
+    def finish(self):
+        self._sends_first(lambda copy: copy.wait_send())
+
+        @pl.when(self.group < self.kinds)
+        def _():
+            for k in range(self.units):
+
+                @pl.when(self.lives(k, self.me))
+                def _():
+                    for away in range(1, self.devices):
+                        self._second(away, k).wait_send()
+
+            for away in range(1, self.groups):
+                self._third(away).wait_send()
+
+
+def seq_scratch(jobs):
+    rows = D // 4
+    return [
+        pltpu.VMEM((jobs, 2, rows, FF), BF),
+        pltpu.VMEM((jobs, 2, rows, FF), BF),
+        pltpu.VMEM((jobs, rows, FF), BF),
+        pltpu.VMEM((rows, FF), F32),
+        pltpu.SemaphoreType.DMA((jobs, 2)),
+        pltpu.SemaphoreType.DMA((jobs, 2)),
+        pltpu.SemaphoreType.DMA((jobs, 2)),
+        pltpu.SemaphoreType.DMA((jobs,)),
+        pltpu.SemaphoreType.DMA((jobs,)),
+        pltpu.SemaphoreType.DMA((jobs,)),
+    ]
+
+
+class SeqSum:
+    def __init__(self, source, out, x_first, job, scratch):
+        mine, arrived, last, result = scratch[:4]
+        self.source, self.out, self.x_first = source, out, x_first
+        self.mine, self.arrived, self.last = mine.at[job], arrived.at[job], last.at[job]
+        self.result = result
+        self.first_send, self.first_recv, self.load_sem = [sem.at[job] for sem in scratch[4:7]]
+        self.last_send, self.last_recv, self.out_sem = [sem.at[job] for sem in scratch[7:]]
+        group = lax.axis_index("seq")
+        self.x, self.y = group % 2, group // 2
+        self.rows = source.shape[0] // 4
+        self.own = self.y if x_first else self.x
+
+    def _neighbour(self, along_x):
+        return 2 * self.y + 1 - self.x if along_x else 2 * (1 - self.y) + self.x
+
+    def _block(self, i, kept):
+        side = self.x if self.x_first else self.y
+        side = side if kept else 1 - side
+        number = 2 * i + side if self.x_first else 2 * side + i
+        return self.source.at[pl.ds(pl.multiple_of(number * self.rows, 32), self.rows)]
+
+    def _copy(self, source, target, send, recv, along_x):
+        return pltpu.make_async_remote_copy(
+            src_ref=source, dst_ref=target, send_sem=send, recv_sem=recv,
+            device_id={"seq": self._neighbour(along_x)}, device_id_type=MESH,
+        )
+
+    def _first(self, i):
+        return self._copy(
+            self._block(i, False), self.arrived.at[i], self.first_send.at[i],
+            self.first_recv.at[i], self.x_first,
+        )
+
+    def _load(self, i):
+        return pltpu.make_async_copy(self._block(i, True), self.mine.at[i], self.load_sem.at[i])
+
+    def _last(self):
+        return self._copy(
+            self.mine.at[1 - self.own], self.last, self.last_send, self.last_recv,
+            not self.x_first,
+        )
+
+    def _write(self):
+        return pltpu.make_async_copy(self.result, self.out, self.out_sem)
+
+    def start(self):
+        for i in range(2):
+            self._first(i).start()
+            self._load(i).start()
+
+    def middle(self):
+        for i in range(2):
+            self._first(i).wait_recv()
+            self._load(i).wait()
+            self.mine[i] = (self.mine[i].astype(F32) + self.arrived[i].astype(F32)).astype(BF)
+        self._last().start()
+
+    def finish(self):
+        self._last().wait_recv()
+        self.result[...] = self.mine[self.own].astype(F32) + self.last[...].astype(F32)
+        self._write().start()
+        for i in range(2):
+            self._first(i).wait_send()
+        self._last().wait_send()
+        self._write().wait()
+
+
+def heads_forward(
+    chips, slots,
+    tokens_ref, grad_own_ref, named_own_ref, gain_one_ref, gain_two_ref, cos_ref, sin_ref, w_refs, w_out_ref,
+    normed_ref, qkv_ref, mixed_ref, lse_ref, own_mixed_ref, hidden_ref, two_ref, w_all, grad_ref, named_ref,
+    rows, w_sem, local_sem, send_sem, recv_sem, *sems,
+):
+    devices = 2 * chips
+    me = lax.axis_index("exp")
+    chip, _ = place()
+    length = SEQ_DEV * devices
+    size = 2 * SEQ_DEV
+    step = BLOCK
+    gathers = [Gather(chips, tokens_ref.at[m], rows.at[m], sems[6 * m : 6 * m + 6]) for m in range(MB)]
+    later = [
+        Gather(chips, named_own_ref, named_ref, sems[12:18]),
+        Gather(chips, grad_own_ref.at[0], grad_ref, sems[18:24]),
+    ]
+    keeps = [
+        pltpu.make_async_copy(source, target, local_sem.at[number])
+        for number, (source, target) in enumerate(
+            [(tokens_ref.at[m], rows.at[m, me]) for m in range(MB)]
+            + [(named_own_ref, named_ref.at[me]), (grad_own_ref.at[0], grad_ref.at[me])]
+        )
+    ]
+
+    def load(slot, j):
+        head = jnp.clip(slot_head(slot, me, devices), 0, HEADS - 1)
+        unit = 3 * slot + j
+        return pltpu.make_async_copy(
+            w_refs[j].at[:, pl.ds(pl.multiple_of(head * HD, HD), HD)],
+            w_all.at[:, unit * HD : (unit + 1) * HD],
+            w_sem.at[unit],
+        )
+
+    def head_columns(m, device, slot):
+        return own_mixed_ref.at[
+            m, :, pl.ds(pl.multiple_of(slot_head(slot, device, devices) * HD, HD), HD)
+        ]
+
+    def rows_of(m, device, slot):
+        part = pl.ds(pl.multiple_of(device * SEQ_DEV, SEQ_DEV), SEQ_DEV)
+        return mixed_ref.at[m, part, slot * HD : (slot + 1) * HD]
+
+    def give(m, away, slot):
+        other = (me + away) % devices
+        return pltpu.make_async_remote_copy(
+            src_ref=rows_of(m, other, slot),
+            dst_ref=head_columns(m, me, slot),
+            send_sem=send_sem.at[m, away, slot],
+            recv_sem=recv_sem.at[m, away, slot],
+            device_id={"exp": other},
+            device_id_type=MESH,
+        )
+
+    def keep_own(m, slot):
+        return pltpu.make_async_copy(
+            rows_of(m, me, slot), head_columns(m, me, slot), recv_sem.at[m, 0, slot]
+        )
+
+    def take(m, away, slot):
+        block = head_columns(m, (me + devices - away) % devices, slot)
+        return pltpu.make_async_remote_copy(
+            src_ref=block,
+            dst_ref=block,
+            send_sem=send_sem.at[m, away, slot],
+            recv_sem=recv_sem.at[m, away, slot],
+            device_id={"exp": (me + away) % devices},
+            device_id_type=MESH,
+        )
+
+    for copy in keeps:
+        copy.start()
+    for slot in range(slots):
+        for j in range(3):
+            load(slot, j).start()
+    meet_all(("exp",))
+    gathers[0].start()
+    for copy in keeps:
+        copy.wait()
+    for slot in range(slots):
+        for j in range(3):
+            load(slot, j).wait()
+
+    def body(m, carry):
+        def at(number, action):
+            @pl.when(m == number)
+            def _():
+                action()
+
+        for turn_ in range(chips):
+            block = block_order(chip, turn_, chips)
+            for number in range(MB):
+                if turn_ > 0:
+                    at(number, lambda number=number: gathers[number].hop(turn_))
+                at(number, lambda number=number: gathers[number].take_pair(block - chip))
+            if turn_ == chips - 2:
+                at(0, gathers[1].start)
+                at(1, later[0].start)
+            if turn_ == chips - 1:
+                at(1, later[1].start)
+            part = pl.ds(pl.multiple_of(block * size, size), size)
+            tokens = rows[m, pl.ds(2 * block, 2)].reshape(size, D).astype(F32)
+            normed = norm_rows(tokens, gain_one_ref[...]).astype(BF)
+            normed_ref[m, part, :] = normed
+            qkv = dot(normed, w_all[...])
+            for unit in range(3 * slots):
+                values = qkv[:, unit * HD : (unit + 1) * HD]
+                if unit % 3 < 2:
+                    values = turn(values, cos_ref[part, :], sin_ref[part, :])
+                qkv_ref[m, part, unit * HD : (unit + 1) * HD] = values.astype(BF)
+        for slot in range(slots):
+            base = 3 * HD * slot
+            for start in range(0, length, step):
+                stop = start + step
+                scores = visible_scores(
+                    qkv_ref[m, start:stop, base : base + HD],
+                    qkv_ref[m, :stop, base + HD : base + 2 * HD],
+                    start,
+                )
+                largest = jnp.max(scores, axis=-1, keepdims=True)
+                powers = jnp.exp(scores - largest)
+                total = jnp.sum(powers, axis=-1, keepdims=True)
+                attention = (powers * (1.0 / total)).astype(BF)
+                mixed = dot(attention, qkv_ref[m, :stop, base + 2 * HD : base + 3 * HD])
+                mixed_ref[m, start:stop, slot * HD : (slot + 1) * HD] = mixed.astype(BF)
+                lse_ref[m, slot, start:stop, :] = largest + jnp.log(total)
+            for number in range(MB):
+
+                @pl.when(jnp.logical_and(m == number, slot_lives(slot, me, devices)))
+                def _():
+                    for away in range(1, devices):
+                        give(number, away, slot).start()
+                    keep_own(number, slot).start()
+
+            at(1, lambda: later[slot].hop(1)) if slot < 2 else None
+        return carry
+
+    lax.fori_loop(0, MB, body, 0)
+
+    def finish_rows(m):
+        for slot in range(slots):
+
+            @pl.when(slot_lives(slot, me, devices))
+            def _():
+                keep_own(m, slot).wait()
+
+            for away in range(1, devices):
+
+                @pl.when(slot_lives(slot, (me + devices - away) % devices, devices))
+                def _():
+                    take(m, away, slot).wait_recv()
+
+        hidden = tokens_ref[m].astype(F32) + dot(own_mixed_ref[m], w_out_ref[...])
+        hidden_ref[m] = hidden
+        two_ref[m] = norm_rows(hidden, gain_two_ref[...]).astype(BF)
+
+    finish_rows(0)
+    for hop in range(2, chips):
+        later[0].hop(hop)
+    later[1].hop(2)
+    finish_rows(1)
+    for hop in range(3, chips):
+        later[1].hop(hop)
+    for gather in gathers:
+        gather.finish(False)
+    for gather in later:
+        gather.finish(True)
+    for m in range(MB):
+        for slot in range(slots):
+
+            @pl.when(slot_lives(slot, me, devices))
+            def _():
+                for away in range(1, devices):
+                    give(m, away, slot).wait_send()
+
+
 def heads_backward(
     chips, slots,
-    own_ref, qkv_ref, mixed_ref, normed_ref, lse_ref, cos_ref, sin_ref, w_ref,
-    sums_ref, grad_a_ref, grad_b_ref,
-    d_mixed, probs, raw, parts, d_keys, d_values, pairs, lines, local_sem, send_sem, recv_sem, *sems,
+    own_ref, qkv_ref, mixed_ref, lse_ref, cos_ref, sin_ref, w_ref, own_mixed_ref, mix_ref, small_ref,
+    normed_ref, gate_ref, up_ref, down_ref,
+    sums_ref, grad_a_ref, grad_b_ref, w_out_out, small_out, job_outs,
+    d_mixed, probs, raw, parts, d_keys, d_values, pairs, lines,
+    part, weight_pair, weight_line, result, normed, normed_sem, local_sem, send_sem, recv_sem, *sems,
 ):
     devices = 2 * chips
     me = lax.axis_index("exp")
@@ -737,6 +1283,33 @@
         for m in range(MB)
     ]
 
+    routed = [
+        SeqSum(source, target, k % 2 == 0, k, sems[6 * MB + 6 : -7])
+        for k, (source, target) in enumerate(
+            zip((gate_ref.at[1], up_ref.at[1], down_ref.at[0]), job_outs)
+        )
+    ]
+
+    rows = D // devices
+
+    def row_block(device):
+        return pl.ds(pl.multiple_of(device * rows, 32), rows)
+
+    weight = Scatter(
+        chips,
+        lambda to: part.at[row_block(2 * to + 1 - core)],
+        lambda to: part.at[row_block(2 * to + core)],
+        weight_pair, weight_line, sems[6 * MB : 6 * MB + 6],
+    )
+    weight_all = SeqAll(sems[-7:])
+    far = D + LANES
+
+    def load(number):
+        return pltpu.make_async_copy(
+            normed_ref.at[:, :, 256 * number : 256 * (number + 1)], normed.at[number % 2],
+            normed_sem.at[number % 2],
+        )
+
     def block_at(m, device, slot):
         rows = pl.ds(pl.multiple_of(device * SEQ_DEV, SEQ_DEV), SEQ_DEV)
         return d_mixed.at[m, rows, slot * HD : (slot + 1) * HD]
@@ -747,7 +1320,7 @@
     def exchange(m, away, slot):
         other = (me + away) % devices
         return pltpu.make_async_remote_copy(
-            src_ref=columns(m, other + slot * devices),
+            src_ref=columns(m, slot_head(slot, other, devices)),
             dst_ref=block_at(m, me, slot),
             send_sem=send_sem.at[m, away, slot],
             recv_sem=recv_sem.at[m, away, slot],
@@ -768,29 +1341,40 @@
 
     def keep(m, slot):
         return pltpu.make_async_copy(
-            columns(m, me + slot * devices), block_at(m, me, slot), local_sem.at[m, slot]
-        )
-
-    meet_all(("exp",))
+            columns(m, slot_head(slot, me, devices)), block_at(m, me, slot), local_sem.at[m, slot]
+        )
+
+    meet_all(("seq", "exp"))
     for m in range(MB):
         for away in range(1, devices):
             for slot in range(slots):
 
-                @pl.when((me + away) % devices + slot * devices < HEADS)
+                @pl.when(slot_lives(slot, (me + away) % devices, devices))
                 def _():
                     exchange(m, away, slot).start()
 
         for slot in range(slots):
 
-            @pl.when(me + slot * devices < HEADS)
+            @pl.when(slot_lives(slot, me, devices))
             def _():
                 keep(m, slot).start()
 
-            @pl.when(me + slot * devices >= HEADS)
+            @pl.when(jnp.logical_not(slot_lives(slot, me, devices)))
             def _():
                 d_mixed[m, :, slot * HD : (slot + 1) * HD] = jnp.zeros((length, HD), BF)
 
-    def weigh(m, carry):
+    routed[0].start()
+    routed[1].start()
+    for number in range(2):
+        load(number).start()
+    for left in range(0, D, 256):
+        part[left : left + 256, :D] = dot_tn(
+            own_mixed_ref[:, left : left + 256], mix_ref[...]
+        ).astype(BF)
+    part[:, D:] = small_ref[...]
+    weight.start()
+
+    def weigh(m):
         for slot in range(slots):
             base = 3 * HD * slot
             for start in range(0, length, step):
@@ -800,21 +1384,19 @@
                     qkv_ref[m, :stop, base + HD : base + 2 * HD],
                     start,
                 )
-                probs[m, slot, start:stop, :stop] = jnp.exp(
+                probs[slot, start:stop, :stop] = jnp.exp(
                     scores - lse_ref[m, slot, start:stop, :]
                 ).astype(BF)
-        return carry
-
-    lax.fori_loop(0, MB, weigh, 0)
 
     def body(m, carry):
+        weigh(m)
         for number in range(MB):
 
             @pl.when(m == number)
             def _():
                 for slot in range(slots):
 
-                    @pl.when(me + slot * devices < HEADS)
+                    @pl.when(slot_lives(slot, me, devices))
                     def _():
                         keep(number, slot).wait()
                         for away in range(1, devices):
@@ -823,6 +1405,10 @@
         @pl.when(m == 1)
         def _():
             scatters[0].start()
+            for turn_ in range(min(slots, chips - 1), chips - 1):
+                weight.slot(turn_)
+            routed[0].middle()
+            routed[2].start()
 
         for slot in range(slots):
             base = 3 * HD * slot
@@ -836,7 +1422,7 @@
                 d_mix = d_mixed[m, start:stop, slot * HD : (slot + 1) * HD]
                 mixed = mixed_ref[m, start:stop, slot * HD : (slot + 1) * HD]
                 row_term = jnp.sum(d_mix.astype(F32) * mixed.astype(F32), axis=1, keepdims=True)
-                attention = probs[m, slot, start:stop, :stop]
+                attention = probs[slot, start:stop, :stop]
                 d_scores = (attention.astype(F32) * (dot_nt(d_mix, values) - row_term)).astype(BF)
                 turned = turn(dot(d_scores, keys) * factor, cos_ref[start:stop, :], -sin_ref[start:stop, :])
                 raw[m, start:stop, base : base + HD] = turned.astype(BF)
@@ -849,6 +1435,17 @@
             @pl.when(m == 1)
             def _():
                 scatters[0].slot(min(slot, chips - 2))
+                if slot == 0:
+                    routed[1].middle()
+                else:
+                    weight.finish(result)
+                    weight_all.low[:, :far] = result[...].astype(BF)
+                    weight_all.low[:, far:] = jnp.zeros((rows, LANES), BF)
+                    weight_all.start()
+
+            @pl.when(m == 0)
+            def _():
+                weight.slot(min(slot, chips - 2))
 
         for start in range(0, length, step):
             back = dot_nt(raw[m, start : start + step, :], w_ref[...]).astype(BF)
@@ -858,245 +1455,98 @@
 
     lax.fori_loop(0, MB, body, 0)
     scatters[1].start()
+    routed[0].finish()
     for turn_ in range(min(slots, chips - 1), chips - 1):
         scatters[0].slot(turn_)
-    both = raw.reshape(MB * length, 3 * slots * HD)
-    rows = normed_ref.reshape(MB * length, D)
-    ticks = [lambda: scatters[0].finish(grad_a_ref)]
     ticks = [lambda t=t: scatters[1].slot(t) for t in range(chips - 1)]
     for number, left in enumerate(range(0, D, 256)):
-        total = dot_tn(rows[:, left : left + 256], both[...])
+        load(number).wait()
+        total = dot_tn(normed[number % 2, 0], raw[0]) + dot_tn(normed[number % 2, 1], raw[1])
+        if number + 2 < D // 256:
+            load(number + 2).start()
         for unit in range(3 * slots):
             sums_ref[unit, left : left + 256, :] = total[:, unit * HD : (unit + 1) * HD].astype(BF)
         if number < len(ticks):
             ticks[number]()
     scatters[0].finish(grad_a_ref)
+    weight_all.middle()
+    routed[1].finish()
+    routed[2].middle()
     for number in range(D // 256, len(ticks)):
         ticks[number]()
     scatters[1].finish(grad_b_ref)
+    weight_all.take()
+    w_out_out[...] = weight_all.whole[:, :D].astype(F32)
+    small_out[...] = weight_all.whole[:, D:far].astype(F32)
+    weight_all.finish()
+    routed[2].finish()
     for m in range(MB):
         for away in range(1, devices):
             for slot in range(slots):
 
-                @pl.when((me + away) % devices + slot * devices < HEADS)
+                @pl.when(slot_lives(slot, (me + away) % devices, devices))
                 def _():
                     exchange(m, away, slot).wait_send()
 
 
 def spread_sums(
-    chips,
-    qkv_ref, shared_ref, mixed_ref, mix_ref, small_ref,
-    attn_out, shared_out, small_out,
-    arrived, summed, held, part, out_low, out_arrived, result, pair, line,
-    first_send, first_recv, local_sem, second_send, second_recv, out_send, out_recv, third_send, third_recv,
+    chips, slots,
+    qkv_ref, out_ref, hidden_ref, down_ref,
+    query_out, key_out, value_out, layer_ref, routed_out,
+    arrived, summed, held, layer, mine, pair, line, mine_sem,
     *sems,
 ):
     devices = 2 * chips
-    group, me = lax.axis_index("seq"), lax.axis_index("exp")
+    me = lax.axis_index("exp")
     core = me % 2
     groups = 4
-    rows = D // devices
-    kinds = groups - 1
-    far = D + LANES
-
-    def row_block(device):
-        return pl.ds(pl.multiple_of(device * rows, 32), rows)
-
-    scatter = Scatter(
-        chips,
-        lambda to: part.at[row_block(2 * to + 1 - core)],
-        lambda to: part.at[row_block(2 * to + core)],
-        pair, line, sems,
-    )
-
-    def unit(owner, k):
-        return shared_ref.at[owner] if k == 1 else qkv_ref.at[owner + kinds * (k // 2)]
-
-    def lives(k, device):
-        return device + (k // 2) * devices < HEADS
-
-    def seq_copy(source, target, send, recv, away):
-        return pltpu.make_async_remote_copy(
-            src_ref=source, dst_ref=target, send_sem=send, recv_sem=recv,
-            device_id={"seq": (group + away) % groups}, device_id_type=MESH,
-        )
-
-    def first(away, k):
-        owner = (group + away) % groups
-        return seq_copy(
-            unit(owner, k), arrived.at[away - 1, k], first_send.at[away - 1, k],
-            first_recv.at[away - 1, k], away,
-        )
-
-    def first_in(away, k):
-        block = arrived.at[away - 1, k]
-        return seq_copy(
-            block, block, first_send.at[away - 1, k], first_recv.at[away - 1, k], away
-        )
-
-    def column_block(device, k):
-        return pl.ds(pl.multiple_of((k * devices + device) * HD, HD), HD)
-
-    def second(away, k):
-        other = (me + away) % devices
-        return pltpu.make_async_remote_copy(
-            src_ref=summed.at[k, row_block(other)],
-            dst_ref=held.at[0, :, column_block(me, k)],
-            send_sem=second_send.at[away, k],
-            recv_sem=second_recv.at[away, k],
-            device_id={"exp": other},
-            device_id_type=MESH,
-        )
-
-    def second_in(away, k):
-        block = held.at[0, :, column_block((me + devices - away) % devices, k)]
-        return pltpu.make_async_remote_copy(
-            src_ref=block,
-            dst_ref=block,
-            send_sem=second_send.at[away, k],
-            recv_sem=second_recv.at[away, k],
-            device_id={"exp": (me + away) % devices},
-            device_id_type=MESH,
-        )
-
-    def second_own(k):
-        return pltpu.make_async_copy(
-            summed.at[k, row_block(me)], held.at[0, :, column_block(me, k)], local_sem.at[k]
-        )
-
-    def third(away, short):
-        if short:
-            source, target = held.at[0, :, :far], held.at[away, :, :far]
-        else:
-            source, target = held.at[0], held.at[away]
-        return seq_copy(source, target, third_send.at[away], third_recv.at[away], away)
-
-    def to_last(source_group):
-        return pltpu.make_async_remote_copy(
-            src_ref=out_low,
-            dst_ref=out_arrived.at[source_group],
-            send_sem=out_send,
-            recv_sem=out_recv.at[source_group],
-            device_id={"seq": kinds},
-            device_id_type=MESH,
-        )
-
+    outs = [
+        Scatter(
+            chips,
+            lambda to, m=m: out_ref.at[m, 2 * to + 1 - core],
+            lambda to, m=m: mine.at[m, to],
+            pair.at[m], line.at[m], sems[6 * m : 6 * m + 6],
+        )
+        for m in range(MB)
+    ]
+    spread = Spread(
+        devices, groups, slots,
+        lambda owner, k: qkv_ref.at[owner + (groups - 1) * k],
+        lambda k, device: slot_lives(k, device, devices),
+        lambda device, k: slot_head(k, device, devices),
+        arrived, summed, held, D, sems[6 * MB : 6 * MB + 7],
+    )
+    routed = SeqSum(down_ref.at[1], routed_out, False, 0, sems[6 * MB + 7 :])
+    loads = [
+        pltpu.make_async_copy(out_ref.at[m, 2 * to + core], mine.at[m, to], mine_sem.at[m, to])
+        for m in range(MB)
+        for to in range(chips)
+    ]
+    for load in loads:
+        load.start()
     meet_all(("seq", "exp"))
-    for k in range(3):
-        for away in range(1, groups):
-
-            @pl.when(jnp.logical_and((group + away) % groups < kinds, lives(k, me)))
-            def _():
-                first(away, k).start()
-
-    for left in range(0, D, 256):
-        part[left : left + 256, :D] = dot_tn(mixed_ref[:, left : left + 256], mix_ref[...]).astype(BF)
-    part[:, D:] = small_ref[...].astype(BF)
-    scatter.start()
-    scatter.slot(0)
-
-    @pl.when(group < kinds)
-    def _():
-        for k in range(3):
-
-            @pl.when(lives(k, me))
-            def _():
-                for away in range(1, groups):
-                    first_in(away, k).wait_recv()
-                total = unit(group, k)[...].astype(F32)
-                for away in range(1, groups):
-                    total += arrived[away - 1, k].astype(F32)
-                summed[k] = total.astype(BF)
-                for away in range(1, devices):
-                    second(away, k).start()
-                second_own(k).start()
-
+    spread.start()
+    outs[0].start()
+    outs[1].start()
+    for load in loads:
+        load.wait()
+    outs[0].slot(0)
+    spread.middle()
+    routed.start()
+    spread.hand_out()
+    outs[1].slot(0)
     for turn_ in range(1, chips - 1):
-        scatter.slot(turn_)
-
-    @pl.when(group < kinds)
-    def _():
-        for k in range(3):
-
-            @pl.when(lives(k, me))
-            def _():
-                second_own(k).wait()
-
-            for away in range(1, devices):
-
-                @pl.when(lives(k, (me + devices - away) % devices))
-                def _():
-                    second_in(away, k).wait_recv()
-
-        for away in range(1, groups):
-            third(away, False).start()
-
-    scatter.finish(result)
-    out_low[...] = result[...].astype(BF)
-
-    @pl.when(group < kinds)
-    def _():
-        to_last(group).start()
-
-    @pl.when(group == kinds)
-    def _():
-        total = result[...]
-        for other in range(kinds):
-            pltpu.make_async_remote_copy(
-                src_ref=out_low, dst_ref=out_arrived.at[other], send_sem=out_send,
-                recv_sem=out_recv.at[other], device_id={"seq": other}, device_id_type=MESH,
-            ).wait_recv()
-            total += out_arrived[other].astype(F32)
-        held[0, :, :far] = total.astype(BF)
-        for away in range(1, groups):
-            third(away, True).start()
-
-    for away in range(1, groups):
-        source = (group + groups - away) % groups
-
-        @pl.when(source == kinds)
-        def _():
-            third(away, True).wait_recv()
-
-        @pl.when(source < kinds)
-        def _():
-            third(away, False).wait_recv()
-
-    for kind in range(kinds):
-        index = (group + groups - kind) % groups
-        attn_out[kind, :, : devices * HD] = held[index, :, : devices * HD].astype(F32)
-        attn_out[kind, :, devices * HD :] = held[
-            index, :, 2 * devices * HD : 2 * devices * HD + D - devices * HD
-        ].astype(F32)
-        shared_out[kind] = held[index, :, devices * HD : 2 * devices * HD].astype(F32)
-    index = (group + groups - kinds) % groups
-    attn_out[kinds] = held[index, :, :D].astype(F32)
-    small_out[...] = held[index, :, D:far].astype(F32)
-
-    for k in range(3):
-        for away in range(1, groups):
-
-            @pl.when(jnp.logical_and((group + away) % groups < kinds, lives(k, me)))
-            def _():
-                first(away, k).wait_send()
-
-    @pl.when(group < kinds)
-    def _():
-        for k in range(3):
-
-            @pl.when(lives(k, me))
-            def _():
-                for away in range(1, devices):
-                    second(away, k).wait_send()
-
-        for away in range(1, groups):
-            third(away, False).wait_send()
-        to_last(group).wait_send()
-
-    @pl.when(group == kinds)
-    def _():
-        for away in range(1, groups):
-            third(away, True).wait_send()
+        outs[0].slot(turn_)
+        outs[1].slot(turn_)
+    routed.middle()
+    for m in range(MB):
+        outs[m].finish(layer)
+        layer_ref[m] = (layer[...] + hidden_ref[m]).astype(BF)
+    spread.take()
+    for kind, target in enumerate((query_out, key_out, value_out)):
+        target[...] = spread.of_kind(kind)[...].astype(F32)
+    spread.finish()
+    routed.finish()
 
 
 def taking(us):
@@ -1111,7 +1561,7 @@
 ANYWHERE = pl.BlockSpec(memory_space=pl.ANY)
 
 
-def experts_on_lines(two_own, grad_all, ids_all, expert_at, router_rows, routed, shared, share):
+def experts_on_lines(two_own, grad_own, grad_a, named, expert_at, router_rows, routed, shared, share):
     devices = lax.axis_size("exp")
     me = lax.axis_index("exp")
     experts = expert_at.shape[0]
@@ -1122,52 +1572,42 @@
         jnp.pad(lax.dynamic_slice(w, (0, me * share), (D, share)), ((0, 0), (0, LANES - share)))
         for w in shared
     ]
-    spare = jnp.full((LANES - experts,), -1, jnp.int32)
-    columns = jnp.concatenate([expert_at.astype(jnp.int32), spare])
-    named = jnp.any(ids_all[..., None] == columns, axis=2).astype(F32).reshape(MB * length, LANES)
     router = jnp.pad(router_rows, ((0, 0), (0, LANES - experts)))
     block_back = (devices, SEQ_DEV, D + LANES)
-    block_out = (devices, SEQ_DEV, D)
-    sems = [gather_sems(chips) for _ in range(MB)] + [scatter_sems(chips) for _ in range(2)]
-
-    def call_rows(own, grad, names, router_in, *weights):
-        def kernel(own_ref, grad_ref, named_ref, router_ref, *refs):
+    sems = [gather_sems(chips)] * MB + [scatter_sems(chips), gather_sems(chips)]
+
+    def call_rows(*operands):
+        def kernel(own_ref, grad_own_ref, grad_ref, named_ref, router_ref, *refs):
             expert_rows(
-                chips, experts, own_ref, grad_ref, named_ref, router_ref, refs[:3], refs[3:6], *refs[6:]
+                chips, experts, own_ref, grad_own_ref, grad_ref, named_ref, router_ref,
+                refs[:3], refs[3:6], *refs[6:],
             )
 
         return pl.pallas_call(
             kernel,
             out_shape=(
                 like(MB, devices, SEQ_DEV, D),
+                like(MB, devices, SEQ_DEV, D),
                 like(MB * length, wide),
                 like(MB * length, wide),
                 like(MB * length, wide),
-                like(*block_out),
+                like(MB, devices, SEQ_DEV, D),
                 like(*block_back),
-                like(SEQ_DEV, D, dtype=F32),
                 like(SEQ_DEV, D + LANES, dtype=F32),
             ),
-            in_specs=[IN_VMEM, ANYWHERE, IN_VMEM, IN_VMEM] + [ANYWHERE] * 6,
-            out_specs=(ANYWHERE,) * 6 + (IN_VMEM,) * 2,
+            in_specs=[IN_VMEM, ANYWHERE, ANYWHERE, IN_VMEM, IN_VMEM] + [ANYWHERE] * 6,
+            out_specs=(ANYWHERE,) * 7 + (IN_VMEM,),
             scratch_shapes=[
                 pltpu.VMEM((3, D, wide), BF),
                 pltpu.VMEM((MB, devices, SEQ_DEV, D), BF),
-                pltpu.VMEM((2, 2 * SEQ_DEV, D), BF),
+                pltpu.VMEM((MB, devices, SEQ_DEV, D), BF),
                 pltpu.VMEM((2, 3, 2 * SEQ_DEV, wide), BF),
-                pltpu.VMEM((MB, *block_out), BF),
+                pltpu.VMEM((2, 2, SEQ_DEV, D), BF),
                 pltpu.VMEM((MB, *block_back), BF),
-                (
-                    pltpu.VMEM((chips, SEQ_DEV, D), BF),
-                    pltpu.VMEM((chips, SEQ_DEV, D + LANES), BF),
-                ),
-                (
-                    pltpu.VMEM((chips + 1, SEQ_DEV, D), BF),
-                    pltpu.VMEM((chips + 1, SEQ_DEV, D + LANES), BF),
-                ),
+                pltpu.VMEM((chips, SEQ_DEV, D + LANES), BF),
+                pltpu.VMEM((chips + 1, SEQ_DEV, D + LANES), BF),
                 pltpu.SemaphoreType.DMA((3, EXP_DEV + 1)),
-                pltpu.SemaphoreType.DMA((MB,)),
-                pltpu.SemaphoreType.DMA((2,)),
+                pltpu.SemaphoreType.DMA((4,)),
                 pltpu.SemaphoreType.DMA((2, 3)),
                 pltpu.SemaphoreType.DMA((2, chips)),
             ]
@@ -1177,51 +1617,68 @@
             ),
             cost_estimate=taking(100),
             name="expert_rows",
-        )(own, grad, names, router_in, *weights)
-
-    rows, hidden, d_gate, d_up, out_b, back_b, out_sum_a, back_sum_a = call_rows(
-        two_own, grad_all, named, router, *routed, *own_shared
+        )(*operands)
+
+    rows, grads, hidden, d_gate, d_up, out_parts, back_b, back_sum_a = call_rows(
+        two_own, grad_own, grad_a, named, router, *routed, *own_shared
     )
     flat = MB * length
+
 
     def call_sums(*operands):
         def kernel(*refs):
-            expert_sums(chips, *refs)
-
-        by_rows = pl.BlockSpec((flat, 256), lambda e, d: (0, d))
-        by_expert = pl.BlockSpec((flat, FF), lambda e, d: (0, e))
-        last = pl.BlockSpec((flat, LANES), lambda e, d: (0, EXP_DEV * FF // LANES))
-        routed_out = pl.BlockSpec((1, 256, FF), lambda e, d: (e, d, 0))
+            expert_sums(chips, *refs[:13], refs[13:16], *refs[16:])
+
+        half = D // 2
+        by_rows = pl.BlockSpec((flat, half), lambda k, d: (0, d))
+        by_grads = pl.BlockSpec((flat, half), lambda k, d: (0, d))
+
+        def for_gate(k, d):
+            return (0, (k + 2) // 4)
+
+        def for_up(k, d):
+            return (0, k // 3)
+
+        def for_down(k, d):
+            return (0, k // 5)
+
+        last = pl.BlockSpec(
+            (flat, LANES), lambda k, d: (0, EXP_DEV * FF // LANES), pipeline_mode=pl.Buffered(1)
+        )
 
         def whole(*shape):
-            return pl.BlockSpec(shape, lambda e, d: (0,) * len(shape))
+            return pl.BlockSpec(shape, lambda k, d: (0,) * len(shape))
 
         return pl.pallas_call(
             kernel,
-            grid=(EXP_DEV, D // 256),
+            grid=(3 * EXP_DEV, 2),
             out_shape=(like(EXP_DEV, D, FF),) * 3
-            + (
-                like(3, D, LANES),
-                like(SEQ_DEV, D, dtype=F32),
-                like(SEQ_DEV, D + LANES, dtype=F32),
-            ),
-            in_specs=[by_rows] * 2 + [by_expert] * 3 + [last] * 3 + [ANYWHERE] * 2,
-            out_specs=(routed_out,) * 3
-            + (whole(3, D, LANES), whole(SEQ_DEV, D), whole(SEQ_DEV, D + LANES)),
+            + (like(SEQ_DEV, D + LANES, dtype=F32),)
+            + (like(D // devices, FF, dtype=F32),) * 3
+            + (like(D // 4, FF, dtype=F32),) * 2,
+            in_specs=[by_rows, by_grads]
+            + [pl.BlockSpec((flat, FF), use) for use in (for_down, for_gate, for_up)]
+            + [last] * 3
+            + [ANYWHERE],
+            out_specs=(ANYWHERE,) * 3
+            + (whole(SEQ_DEV, D + LANES),)
+            + (whole(D // devices, FF),) * 3
+            + (ANYWHERE,) * 2,
             scratch_shapes=[
-                pltpu.VMEM((chips, SEQ_DEV, D), BF),
                 pltpu.VMEM((chips, SEQ_DEV, D + LANES), BF),
-                (
-                    pltpu.VMEM((chips, SEQ_DEV, D), BF),
-                    pltpu.VMEM((chips, SEQ_DEV, D + LANES), BF),
-                ),
-                (
-                    pltpu.VMEM((chips + 1, SEQ_DEV, D), BF),
-                    pltpu.VMEM((chips + 1, SEQ_DEV, D + LANES), BF),
-                ),
-                pltpu.SemaphoreType.DMA((2, chips)),
+                pltpu.VMEM((chips, SEQ_DEV, D + LANES), BF),
+                pltpu.VMEM((chips + 1, SEQ_DEV, D + LANES), BF),
+                pltpu.SemaphoreType.DMA((chips,)),
+                pltpu.VMEM((2, half, FF), BF),
+                pltpu.SemaphoreType.DMA((2,)),
+                pltpu.VMEM((3, D, HD), BF),
+                pltpu.VMEM((3, 1, D, HD), BF),
+                pltpu.VMEM((1, D, HD), BF),
+                pltpu.VMEM((4, D // devices, devices * HD), BF),
             ]
-            + scatter_sems(chips) * 2,
+            + scatter_sems(chips)
+            + spread_sems(devices, 4, 1)
+            + seq_scratch(2),
             compiler_params=pltpu.CompilerParams(
                 collective_id=2, has_side_effects=True, vmem_limit_bytes=VMEM_BYTES
             ),
@@ -1229,20 +1686,20 @@
             name="expert_sums",
         )(*operands)
 
-    gate_sum, up_sum, down_sum, shared_sum, out_sum_b, back_sum_b = call_sums(
-        rows.reshape(flat, D), grad_all.reshape(flat, D), hidden, d_gate, d_up, hidden, d_gate, d_up,
-        out_b, back_b,
+    gate_sum, up_sum, down_sum, back_sum_b, *shared_grads, gate_rows, up_rows = call_sums(
+        rows.reshape(flat, D), grads.reshape(flat, D), hidden, d_gate, d_up, hidden, d_gate, d_up, back_b
     )
     backs = (back_sum_a, back_sum_b)
     tails = [
         b[:, D : D + experts] + b[:, D + experts : D + 2 * experts] for b in backs
     ]
     return (
-        (out_sum_a, out_sum_b),
+        out_parts,
         [b[:, :D] for b in backs],
         tails,
+        (gate_rows, up_rows),
         (gate_sum, up_sum, down_sum),
-        shared_sum,
+        shared_grads,
     )
 
 
@@ -1533,78 +1990,74 @@
     share = FF // devices
     own = MB * SEQ_DEV
 
-    head_of = [jnp.minimum(me + slot * devices, HEADS - 1) for slot in range(slots)]
-    w_qkv = jnp.concatenate(
-        [
-            lax.dynamic_slice(weight, (0, head * HD), (D, HD))
-            for head in head_of
-            for weight in (w_query, w_key, w_value)
-        ],
-        axis=1,
-    )
-    cos_table, sin_table = angle_tables(jnp.arange(length).astype(F32))
-    sin_table = jnp.where(jnp.arange(HD) < HD // 2, -sin_table, sin_table)
-    forward = pl.pallas_call(
-        functools.partial(attend_forward, slots),
-        out_shape=(
-            like(length, D),
-            like(length, 3 * wide),
-            like(length, wide),
-            like(slots, length, 1, dtype=F32),
-        ),
-        in_specs=[IN_VMEM] * 5,
-        out_specs=(IN_VMEM,) * 4,
-        compiler_params=pltpu.CompilerParams(vmem_limit_bytes=VMEM_BYTES),
-        cost_estimate=taking(12),
-        name="attend_forward",
-    )
+    cos_table, sin_table = turn_tables(length)
 
     expert_at = jnp.sum(
         (owner_table[:, None] == jnp.arange(experts)[None, :]) * jnp.arange(experts)[:, None],
         axis=0,
     )
     router_rows = jnp.take(w_router, expert_at, axis=1)
-    ids_all = lax.all_gather(expert_ids[:, 0], "exp", axis=1, tiled=True)
-    grad_all = lax.all_gather(cotangent[:, 0], "exp", axis=1, tiled=True)
-
-    kept, mixed_rows = [], []
-    for micro_batch in range(MB):
-        rows_all = gather_exp(tokens[micro_batch, 0])
-        normed, qkv, mixed, lse = forward(rows_all, gain_one[None], cos_table, sin_table, w_qkv)
-        kept.append((normed, qkv, mixed, lse))
-        sent = lax.all_to_all(
-            mixed.reshape(devices, SEQ_DEV, wide), "exp", split_axis=0, concat_axis=0, tiled=True
-        )
-        mixed_rows.append(
-            sent.reshape(devices, SEQ_DEV, slots, HD)
-            .transpose(1, 2, 0, 3)
-            .reshape(SEQ_DEV, slots * devices * HD)[:, :D]
-        )
-    normed, qkv, mixed, lse = [jnp.stack([k[i] for k in kept]) for i in range(4)]
-    own_mixed = jnp.concatenate(mixed_rows)
+    names = jnp.concatenate([expert_at, jnp.full((LANES - experts,), -1, jnp.int32)])
+    named_own = jnp.any(expert_ids.reshape(own, TOP)[:, :, None] == names, axis=1).astype(BF)
+    tokens_own = tokens.reshape(MB, SEQ_DEV, D)
+    grad_own = cotangent.reshape(MB, SEQ_DEV, D)
+
+    def call_forward(*operands):
+        def kernel(*refs):
+            heads_forward(chips, slots, *refs[:7], refs[7:10], *refs[10:])
+
+        return pl.pallas_call(
+            kernel,
+            out_shape=(
+                like(MB, length, D),
+                like(MB, length, 3 * wide),
+                like(MB, length, wide),
+                like(MB, slots, length, 1, dtype=F32),
+                like(MB, SEQ_DEV, D),
+                like(MB, SEQ_DEV, D, dtype=F32),
+                like(MB, SEQ_DEV, D),
+                like(D, 3 * wide),
+                like(devices, SEQ_DEV, D),
+                like(devices, own, LANES),
+            ),
+            in_specs=[IN_VMEM, ANYWHERE] + [IN_VMEM] * 5 + [ANYWHERE] * 3 + [IN_VMEM],
+            out_specs=(IN_VMEM,) * 8 + (ANYWHERE, IN_VMEM),
+            scratch_shapes=[
+                pltpu.VMEM((MB, devices, SEQ_DEV, D), BF),
+                pltpu.SemaphoreType.DMA((3 * slots,)),
+                pltpu.SemaphoreType.DMA((4,)),
+                pltpu.SemaphoreType.DMA((MB, devices, slots)),
+                pltpu.SemaphoreType.DMA((MB, devices, slots)),
+            ]
+            + gather_sems(chips) * 4,
+            compiler_params=pltpu.CompilerParams(
+                collective_id=5, has_side_effects=True, vmem_limit_bytes=VMEM_BYTES
+            ),
+            cost_estimate=taking(70),
+            name="heads_forward",
+        )(*operands)
+
+    normed, qkv, mixed, lse, own_mixed, hidden_one, two_low, w_qkv, grad_a, named_all = call_forward(
+        tokens_own, grad_own, named_own, gain_one[None], gain_two[None], cos_table, sin_table,
+        w_query, w_key, w_value, w_out,
+    )
     rows_in = tokens.reshape(own, D).astype(F32)
-    hidden_one = rows_in + dot(own_mixed, w_out)
-    two_low = norm_rows(hidden_one, gain_two).astype(BF)
-    named = jnp.any(
-        expert_ids.reshape(own, TOP)[:, :, None] == expert_at[None, None, :], axis=1
-    )
-    gates = named_softmax(dot(two_low, router_rows), named)
-
-    outs, backs, tails, routed_sums, shared_sum = experts_on_lines(
+    hidden_rows = hidden_one
+    own_mixed, hidden_one = own_mixed.reshape(own, D), hidden_one.reshape(own, D)
+    two_low = two_low.reshape(own, D)
+    gates = named_softmax(dot(two_low, router_rows), named_own[:, :experts] > 0)
+
+    out_parts, backs, tails, done, routed_sums, shared_grads = experts_on_lines(
         two_low.reshape(MB, SEQ_DEV, D),
-        grad_all,
-        ids_all,
+        grad_own,
+        grad_a,
+        named_all.reshape(devices, MB * SEQ_DEV, LANES),
         expert_at,
         router_rows,
         (routed_gate, routed_up, routed_down),
         (shared_gate, shared_up, shared_down),
         share,
     )
-    routed_full = [
-        lax.psum_scatter(parts, "seq", scatter_dimension=1, tiled=True).astype(F32)
-        for parts in routed_sums
-    ]
-    layer_out = (hidden_one + jnp.concatenate(outs)).astype(BF)
     tail = jnp.concatenate(tails)
     grad_logits = (gates * (tail - jnp.sum(gates * tail, axis=-1, keepdims=True))).astype(BF)
     grad_two = jnp.concatenate(backs) + dot_nt(grad_logits, router_rows)
@@ -1613,89 +2066,97 @@
     grad_mix = grad_hidden.astype(BF)
     d_mixed = dot_nt(grad_mix, w_out).astype(BF)
 
-    heads_sum, grad_a, grad_b = pl.pallas_call(
-        functools.partial(heads_backward, chips, slots),
+    quarter = like(D // groups, FF, dtype=F32)
+    far = D + LANES
+    small = jnp.concatenate(
+        [
+            dot_tn(two_low, grad_logits),
+            jnp.sum(gain_two_terms, axis=0)[:, None],
+            jnp.zeros((D, LANES - experts - 1), F32),
+        ],
+        axis=1,
+    ).astype(BF)
+
+    def backward_kernel(*refs):
+        heads_backward(chips, slots, *refs[:19], refs[19:22], *refs[22:])
+
+    heads_sum, normed_a, normed_b, w_out_rows, small_rows, gate_two, up_two, down_one = pl.pallas_call(
+        backward_kernel,
         out_shape=(
             like(3 * slots, D, HD),
             like(SEQ_DEV, D, dtype=F32),
             like(SEQ_DEV, D, dtype=F32),
-        ),
-        in_specs=[IN_VMEM] * 8,
-        out_specs=(IN_VMEM,) * 3,
+            like(rows_out, D, dtype=F32),
+            like(rows_out, LANES, dtype=F32),
+        )
+        + (quarter,) * 3,
+        in_specs=[IN_VMEM] * 10 + [ANYWHERE] * 4,
+        out_specs=(IN_VMEM,) * 5 + (ANYWHERE,) * 3,
         scratch_shapes=[
             pltpu.VMEM((MB, length, wide), BF),
-            pltpu.VMEM((MB, slots, length, length), BF),
+            pltpu.VMEM((slots, length, length), BF),
             pltpu.VMEM((MB, length, 3 * wide), BF),
             pltpu.VMEM((MB, devices, SEQ_DEV, D), BF),
             pltpu.VMEM((length, HD), F32),
             pltpu.VMEM((length, HD), F32),
             pltpu.VMEM((MB, chips, SEQ_DEV, D), BF),
             pltpu.VMEM((MB, chips + 1, SEQ_DEV, D), BF),
+            pltpu.VMEM((D, far), BF),
+            pltpu.VMEM((chips, rows_out, far), BF),
+            pltpu.VMEM((chips + 1, rows_out, far), BF),
+            pltpu.VMEM((rows_out, far), F32),
+            pltpu.VMEM((2, MB, length, 256), BF),
+            pltpu.SemaphoreType.DMA((2,)),
             pltpu.SemaphoreType.DMA((MB, slots)),
             pltpu.SemaphoreType.DMA((MB, devices, slots)),
             pltpu.SemaphoreType.DMA((MB, devices, slots)),
         ]
-        + scatter_sems(chips) * MB,
+        + scatter_sems(chips) * (MB + 1)
+        + seq_scratch(3)
+        + seq_all_scratch(rows_out, (far + LANES) // groups),
         compiler_params=pltpu.CompilerParams(
             collective_id=3, has_side_effects=True, vmem_limit_bytes=VMEM_BYTES
         ),
         cost_estimate=taking(70),
         name="heads_backward",
     )(
-        d_mixed.reshape(MB, SEQ_DEV, D), qkv, mixed, normed, lse, cos_table, sin_table, w_qkv
-    )
-    grad_normed = jnp.concatenate([grad_a, grad_b])
-    back_one, gain_one_terms = norm_back(rows_in, gain_one, grad_normed)
+        d_mixed.reshape(MB, SEQ_DEV, D), qkv, mixed, lse, cos_table, sin_table, w_qkv, own_mixed,
+        grad_mix, small, normed, *routed_sums,
+    )
+    grad_normed = jnp.concatenate([normed_a, normed_b])
+    back_one, _ = norm_back(rows_in, gain_one, grad_normed)
     grad_tokens = (grad_hidden + back_one).astype(BF)
-    small = jnp.concatenate(
-        [
-            dot_tn(two_low, grad_logits),
-            jnp.sum(gain_one_terms, axis=0)[:, None],
-            jnp.sum(gain_two_terms, axis=0)[:, None],
-            jnp.zeros((D, LANES - experts - 2), F32),
-        ],
-        axis=1,
-    )
-    far = D + LANES
-    attn, shared_full, small_rows = pl.pallas_call(
-        functools.partial(spread_sums, chips),
-        out_shape=(
-            like(groups, rows_out, D, dtype=F32),
-            like(groups - 1, rows_out, devices * HD, dtype=F32),
-            like(rows_out, LANES, dtype=F32),
-        ),
-        in_specs=[IN_VMEM] * 5,
-        out_specs=(IN_VMEM,) * 3,
+    *attn, layer_out, down_two = pl.pallas_call(
+        functools.partial(spread_sums, chips, slots),
+        out_shape=(like(rows_out, D, dtype=F32),) * 3 + (like(MB, SEQ_DEV, D), quarter),
+        in_specs=[IN_VMEM, ANYWHERE, IN_VMEM, ANYWHERE],
+        out_specs=(IN_VMEM,) * 4 + (ANYWHERE,),
         scratch_shapes=[
-            pltpu.VMEM((groups - 1, 3, D, HD), BF),
-            pltpu.VMEM((3, D, HD), BF),
-            pltpu.VMEM((groups, rows_out, 3 * devices * HD), BF),
-            pltpu.VMEM((D, far), BF),
-            pltpu.VMEM((rows_out, far), BF),
-            pltpu.VMEM((groups - 1, rows_out, far), BF),
-            pltpu.VMEM((rows_out, far), F32),
-            pltpu.VMEM((chips, rows_out, far), BF),
-            pltpu.VMEM((chips + 1, rows_out, far), BF),
-            pltpu.SemaphoreType.DMA((groups - 1, 3)),
-            pltpu.SemaphoreType.DMA((groups - 1, 3)),
-            pltpu.SemaphoreType.DMA((3,)),
-            pltpu.SemaphoreType.DMA((devices, 3)),
-            pltpu.SemaphoreType.DMA((devices, 3)),
-            pltpu.SemaphoreType.DMA,
-            pltpu.SemaphoreType.DMA((groups - 1,)),
-            pltpu.SemaphoreType.DMA((groups,)),
-            pltpu.SemaphoreType.DMA((groups,)),
+            pltpu.VMEM((groups - 1, slots, D, HD), BF),
+            pltpu.VMEM((slots, D, HD), BF),
+            pltpu.VMEM((groups, rows_out, D), BF),
+            pltpu.VMEM((SEQ_DEV, D), F32),
+            pltpu.VMEM((MB, chips, SEQ_DEV, D), BF),
+            pltpu.VMEM((MB, chips, SEQ_DEV, D), BF),
+            pltpu.VMEM((MB, chips + 1, SEQ_DEV, D), BF),
+            pltpu.SemaphoreType.DMA((MB, chips)),
         ]
-        + scatter_sems(chips),
+        + scatter_sems(chips) * MB
+        + spread_sems(devices, groups, slots)
+        + seq_scratch(1),
         compiler_params=pltpu.CompilerParams(
             collective_id=4, has_side_effects=True, vmem_limit_bytes=VMEM_BYTES
         ),
-        cost_estimate=taking(60),
+        cost_estimate=taking(80),
         name="spread_sums",
-    )(heads_sum, shared_sum, own_mixed, grad_mix, small)
-    shared_grads = shared_full.reshape(groups - 1, rows_out, devices, HD)[..., :share].reshape(
-        groups - 1, rows_out, FF
-    )
+    )(heads_sum, out_parts, hidden_rows, routed_sums[2])
+    gain_rows = lax.dynamic_slice(gain_one, (me * rows_out,), (rows_out,))
+    gain_one_grad = sum(
+        jnp.sum(
+            lax.dynamic_slice(weight, (me * rows_out, 0), (rows_out, D)).astype(F32) * grad, axis=1
+        )
+        for weight, grad in zip((w_query, w_key, w_value), attn)
+    ) / gain_rows
     whole = (MB, 1, SEQ_DEV, D)
     return (
         layer_out.reshape(whole),
@@ -1703,14 +2164,16 @@
         attn[0],
         attn[1],
         attn[2],
-        attn[3],
+        w_out_rows,
+        gain_one_grad,
         small_rows[:, experts],
-        small_rows[:, experts + 1],
         jnp.take(small_rows[:, :experts], owner_table, axis=1),
         shared_grads[0],
         shared_grads[1],
         shared_grads[2],
-        *routed_full,
+        jnp.stack([done[0], gate_two]),
+        jnp.stack([done[1], up_two]),
+        jnp.stack([down_one, down_two]),
     )
 
 

time: 652 us -> 543 us (0.83)
  Pallas kernels: 445 us -> 483 us
  waiting for transfers between devices: 38 us -> 0 us
  local copies, waits for them, and re-layouts: 55.1 us -> 25.9 us
  blocking collectives: 29.2 us -> 0 us
  other arithmetic: 39.1 us -> 19.5 us
  starting transfers between devices: 14.1 us -> 0 us
  between operations: 14.9 us -> 1.34 us
    pallas_call x6 -> x5, Pallas kernels: 445 us -> 483 us  [the longest x1 112 us: on_device_lines(): pl.pallas_call(backward_kernel, out_shape=(like(3 * slots, D, HD), like(S...]
    all_gather x3 -> x0, waiting for transfers between devices: 36.1 us -> none  [the longest x2 36.1 us: gather_exp(): return lax.all_gather(array, 'exp', axis=0, tiled=True)]
    all_gather x1 -> x0, blocking collectives: 29.2 us -> none  [on_device_lines(): ids_all = lax.all_gather(expert_ids[:, 0], 'exp', axis=1, tiled=True)]
    all_to_all x2 -> x0, starting transfers between devices: 13.9 us -> none  [on_device_lines(): lax.all_to_all(mixed.reshape(devices, SEQ_DEV, wide), 'exp', split_axis=0...]
    convert_element_type x7 -> x1, other arithmetic: 10.7 us -> 0.65 us  [on_device_lines(): jnp.any(expert_ids.reshape(own, TOP)[:, :, None] == names, axis=1)]
    squeeze x4 -> x0, local copies, waits for them, and re-layouts: 7.97 us -> none  [the longest x1 3.79 us: on_device_lines(): attn[3]]
    unnamed x99 -> x97, local copies, waits for them, and re-layouts: 17.7 us -> 14.2 us
  transfers between devices with their start and end apart: 8 -> 0, of which waited for: 2 -> 0; matrix products, arithmetic and copies ran while one was open for 14% -> 0% of each run, Pallas kernels for 43% -> 0%
where the time goes in v4:
time: 543 us; the launch traced here: 533 us
  Pallas kernels  483 us (89%)
  local copies, waits for them, and re-layouts  25.9 us (5%)
  other arithmetic  19.5 us (4%)
    pallas_call x1, Pallas kernels, on_device_lines(): pl.pallas_call(backward_kernel, out_shape=(like(3 * slots, D, HD), like(S...  112 us
    pallas_call x1, Pallas kernels, call_rows(): pl.pallas_call(kernel, out_shape=(like(MB, devices, SEQ_DEV, D), like(MB,...  108 us
    pallas_call x1, Pallas kernels, call_forward(): pl.pallas_call(kernel, out_shape=(like(MB, length, D), like(MB, length, 3...  94.5 us
    pallas_call x1, Pallas kernels, call_sums(): pl.pallas_call(kernel, grid=(3 * EXP_DEV, 2), out_shape=(like(EXP_DEV, D,...  92.2 us
    pallas_call x1, Pallas kernels, on_device_lines(): pl.pallas_call(functools.partial(spread_sums, chips, slots), out_shape=(l...  76.2 us
    unnamed x97, local copies, waits for them, and re-layouts  14.2 us

profile of v4, /device:TPU:12, one launch (start us, length us, event | category | flops | bytes accessed | tf_op | source)
XLA Modules:
  0.0 533.0 jit_solution(15037232733027776136)
XLA Ops:
  0.7 0.9 select_reduce_fusion
  1.6 0.7 copy.89
  2.3 0.3 compare_reduce_fusion
  2.6 0.6 convert_element_type.50.refs_2_
  3.2 1.3 broadcast_in_dim.56.refs_3_
  4.5 1.3 broadcast_in_dim.57.refs_4_
  5.8 94.5 %heads_forward.1 = (bf16[2,1024,1280]{2,1,0:T(8,128)(2,1)}, bf16[2,1024,768]{2,1,0:T(8,128)(2,1)}, bf16[2,1024,256]{2,1,0:T(8,128)(2,1)}, f32[2,2,1024,1]{3,2,1,...) custom-call(bf16[2,128,1280]{2,1,0:T(8,128)(2,1)} %bitcast.82, ...), custom_call_target="tpu_custom_call" | custom-call | flops 70000001024 | bytes 1048576 | tf_op jit(solution)/shard_map/heads_forward/pallas_call | solution.py:2009
  100.3 1.6 constant_dynamic-slice_fusion
  101.9 0.8 pad.17.refs_4_
  102.7 0.8 pad.18.refs_5_
  103.5 0.6 pad_clamp_fusion
  104.1 0.6 gather_fusion
  104.7 0.2 copy.76
  104.9 0.6 compare_and_fusion
  105.5 0.8 pad.15.router_ref
  106.3 0.2 constant_dynamic-slice_fusion.2
  106.5 0.8 pad.16.refs_3_
  107.3 107.9 %expert_rows.1 = (bf16[2,8,128,1280]{3,2,1,0:T(8,128)(2,1)}, bf16[2,8,128,1280]{3,2,1,0:T(8,128)(2,1)}, bf16[2048,1920]{1,0:T(8,128)(2,1)}, bf16[2048,1920]{1,0:...) custom-call(bf16[2,128,1280]{2,1,0:T(8,128)(2,1)} %get-tuple-element, ...), custom_call_target="tpu_custom_call" | custom-call | flops 99999997952 | bytes 1048576 | tf_op jit(solution)/shard_map/expert_rows/pallas_call | solution.py:1586
  215.2 92.2 %expert_sums.1 = (bf16[2,1280,896]{2,1,0:T(8,128)(2,1)}, bf16[2,1280,896]{2,1,0:T(8,128)(2,1)}, bf16[2,1280,896]{2,1,0:T(8,128)(2,1)}, f32[128,1408]{1,0:T(8,128...) custom-call(bf16[2048,1280]{1,0:T(8,128)(2,1)} %bitcast.96, ...), custom_call_target="tpu_custom_call" | custom-call | flops 60000002048 | bytes 1048576 | tf_op jit(solution)/shard_map/expert_sums/pallas_call | solution.py:1652
  307.4 1.0 slice_add_fusion
  308.5 0.4 fusion.15
  308.9 0.2 fusion.9
  309.1 0.2 multiply_reduce_fusion.8
  309.3 0.4 convolution_convert_fusion.1
  309.7 0.2 copy.78
  310.0 1.2 slice.28
  311.3 0.2 copy-done.3
  311.5 0.2 multiply_reduce_fusion.4
  311.7 0.3 copy-done.30
  312.0 0.7 multiply_reduce_fusion.2
  312.7 0.2 broadcast_in_dim.67
  313.0 0.9 maximum_maximum_fusion.refs_9_
  313.9 0.3 copy-done.13
  314.2 0.4 fusion.14.refs_8_
  314.6 1.5 copy-done.41
  316.1 1.9 convolution_convert_fusion
  318.0 112.4 %heads_backward.1 = (bf16[6,1280,128]{2,1,0:T(8,128)(2,1)}, f32[128,1280]{1,0:T(8,128)}, f32[128,1280]{1,0:T(8,128)}, f32[160,1280]{1,0:T(8,128)}, f32[160,128]{...) custom-call(bf16[2,128,1280]{2,1,0:T(8,128)(2,1)} %bitcast.101, ...), custom_call_target="tpu_custom_call" | custom-call | flops 70000001024 | bytes 1048576 | tf_op jit(solution)/shard_map/heads_backward/pallas_call | solution.py:2083
  430.4 76.2 %spread_sums.1 = (f32[160,1280]{1,0:T(8,128)}, f32[160,1280]{1,0:T(8,128)}, f32[160,1280]{1,0:T(8,128)}, bf16[2,128,1280]{2,1,0:T(8,128)(2,1)}, f32[320,896]{1,0:T(8,128)}) custom-call(bf16[6,1280,128]{2,1,0:T(8,128)(2,1)} %get-tuple-element.76.qkv_ref, bf16[2,8,128,1280]{3,2,1,0:T(8,128)(2,1)} %get-tuple-element.77.out_ref, ...), custom_call_target="tpu_custom_call" | custom-call | flops 80000000000 | bytes 1048576 | tf_op jit(solution)/shard_map/spread_sums/pallas_call | solution.py:2129
  506.6 2.9 pad_maximum_fusion.2
  509.6 1.5 pad_maximum_fusion.1
  511.1 0.1 copy-done.15
  511.3 0.7 copy-done.17
  512.0 1.7 pad_maximum_fusion
  513.7 1.3 multiply_reduce_fusion.5
  515.0 1.2 multiply_reduce_fusion.6
  516.3 1.2 multiply_reduce_fusion.7
  517.5 0.6 dynamic-slice_divide_fusion
  518.3 1.0 copy-done.7
  519.3 0.2 multiply_reduce_fusion.1
  519.5 0.3 multiply_reduce_fusion
  519.9 0.8 copy-done.4
  520.6 0.4 copy-done.6
  521.0 1.6 fusion.4
  522.7 0.7 gather_fusion.1
  523.4 0.7 select_bitcast_fusion
  524.1 0.7 slice_reduce_fusion
  524.8 2.0 copy.99
  526.8 0.9 copy.100
  527.7 0.9 copy.101
  528.6 0.9 copy.102
  529.5 0.9 copy.103
  530.4 0.8 copy.104
  531.2 0.8 copy.105
  532.0 0.8 copy.106
  (93 shorter events, 0.6 us)
Async XLA Ops:
  0.6 105.7 %copy-start = (bf16[1280,896]{1,0:T(8,128)(2,1)S(1)}, bf16[1280,896]{1,0:T(8,128)(2,1)}, u32[]{:S(2)}) copy-start(bf16[1280,896]{1,0:T(8,128)(2,1)} %param.30) | copy-start | bytes 6881284
  100.3 3.2 copy-start.40
  100.3 3.8 copy-start.2
  104.9 2.4 copy-start.11
  105.5 0.8 copy-start.37
  215.1 93.2 %copy-start.21 = (f32[128,1408]{1,0:T(8,128)S(1)}, f32[128,1408]{1,0:T(8,128)}, u32[]{:S(2)}) copy-start(f32[128,1408]{1,0:T(8,128)} %get-tuple-element.59) | copy-start | bytes 2162692
  215.1 93.3 %copy-start.12 = (bf16[16,1280]{0,1:T(8,128)(2,1)S(1)}, bf16[16,1280]{0,1:T(8,128)(2,1)}, u32[]{:S(2)}) copy-start(bf16[16,1280]{0,1:T(8,128)(2,1)} %copy-done.11) | copy-start | bytes 122884
  215.2 93.3 %copy-start.20 = (bf16[256,128]{1,0:T(8,128)(2,1)S(1)}, bf16[256,128]{1,0:T(8,128)(2,1)}, u32[]{:S(2)}) copy-start(bf16[256,128]{1,0:T(8,128)(2,1)} %convert_element_type.50.refs_2_) | copy-start | bytes 196612
  215.2 93.3 %copy-start.38 = (pred[16]{0:T(512)(128)(4,1)S(1)}, pred[16]{0:T(512)(128)(4,1)}, u32[]{:S(2)}) copy-start(pred[16]{0:T(512)(128)(4,1)} %copy-done.37) | copy-start | bytes 52
  215.2 93.3 %copy-start.42 = (bf16[2,128,1280]{2,1,0:T(8,128)(2,1)S(1)}, bf16[2,128,1280]{2,1,0:T(8,128)(2,1)}, u32[]{:S(2)}) copy-start(bf16[2,128,1280]{2,1,0:T(8,128)(2,1)} %get-tuple-element.56.own_ref) | copy-start | bytes 1966084
  310.0 1.5 copy-start.3
  311.2 0.8 copy-start.30
  312.0 2.0 copy-start.33
  312.7 1.3 copy-start.5
  312.7 1.5 copy-start.13
  313.9 0.7 copy-start.35
  314.2 1.9 copy-start.41
  316.1 1.9 copy-start.23
  430.4 76.2 %copy-start.19 = (f32[320,896]{1,0:T(8,128)S(1)}, f32[320,896]{1,0:T(8,128)}, u32[]{:S(2)}) copy-start(f32[320,896]{1,0:T(8,128)} %get-tuple-element.93) | copy-start | bytes 3440644
  506.6 3.0 copy-start.16
  506.6 3.0 copy-start.18
  509.6 1.7 copy-start.15
  509.6 2.4 copy-start.17
  512.0 1.7 copy-start.8
  513.7 1.3 copy-start.9
  513.7 2.6 copy-start.10
  515.0 2.5 copy-start.32
  515.0 3.2 copy-start.25
  516.3 2.0 copy-start.24
  518.2 1.1 copy-start.7
  518.2 1.6 copy-start.14
  519.2 1.4 copy-start.4
  519.2 1.8 copy-start.6
  519.2 1.8 copy-start.31
  519.2 1.8 copy-start.34
  519.3 1.8 copy-start.36
  521.0 1.6 copy-start.29
  521.0 2.4 copy-start.39
  527.7 1.8 copy-start.22
  528.6 1.8 copy-start.28
  529.5 1.7 copy-start.27
  530.4 1.6 copy-start.26
  530.4 2.4 copy-start.1

commit v5 on v4

--- a/solution.py
+++ b/solution.py
@@ -19,7 +19,7 @@
 SEQ_DEV = 128
 LANES = 128
 BLOCK = 256
-VMEM_BYTES = 60 * 2**20
+VMEM_BYTES = 62 * 2**20
 
 eps = 1e-06
 BF = jnp.bfloat16
@@ -459,7 +459,7 @@
 
 def expert_rows(
     chips, experts,
-    own_ref, grad_own_ref, grad_ref, named_ref, router_ref, routed_refs, shared_refs,
+    own_ref, grad_own_ref, grad_ref, named_ref, router_ref, owner_ref, routed_refs, shared_refs,
     rows_ref, grads_ref, hidden_ref, d_gate_ref, d_up_ref, out_ref, back_b_ref, back_a_ref,
     weights, rows, grads, stage, out, back, pair, line, weight_sem, local_sem, stage_sem, keep_sem,
     *sems,
@@ -485,11 +485,18 @@
                     weight_sem.at[k, e],
                 )
             )
-        loads.append(
-            pltpu.make_async_copy(
-                shared_refs[k], weights.at[k, :, EXP_DEV * FF :], weight_sem.at[k, EXP_DEV]
-            )
-        )
+
+    def shared_load(k):
+        columns = pl.ds(pl.multiple_of(me * HD, HD), HD)
+        return pltpu.make_async_copy(
+            shared_refs[k].at[:, columns], weights.at[k, :, EXP_DEV * FF :], weight_sem.at[k, EXP_DEV]
+        )
+
+    def shared_loads(action):
+        @pl.when(me < FF // HD)
+        def _():
+            for k in range(3):
+                action(shared_load(k))
 
     def stage_out(step, k):
         block = block_order(chip, step % blocks, chips)
@@ -514,6 +521,13 @@
 
     for load in loads:
         load.start()
+    shared_loads(lambda copy: copy.start())
+
+    @pl.when(me >= FF // HD)
+    def _():
+        for k in range(3):
+            weights[k, :, EXP_DEV * FF :] = jnp.zeros((D, HD), BF)
+
     own_copies = [
         pltpu.make_async_copy(own_ref.at[m], rows.at[m, me], local_sem.at[m]) for m in range(MB)
     ] + [
@@ -528,6 +542,7 @@
         copy.wait()
     for load in loads:
         load.wait()
+    shared_loads(lambda copy: copy.wait())
 
     def at(step, number, action):
         @pl.when(step == number)
@@ -572,9 +587,8 @@
             named > 0.0, jnp.exp(chosen - jnp.max(chosen, axis=1, keepdims=True)), 0.0
         )
         gates = powers / jnp.sum(powers, axis=1, keepdims=True)
-        lane = lax.broadcasted_iota(jnp.int32, (size, LANES), 1)
         own = [
-            jnp.sum(jnp.where(lane == EXP_DEV * me + e, gates, 0.0), axis=1, keepdims=True)
+            jnp.sum(jnp.where(owner_ref[...] == EXP_DEV * me + e, gates, 0.0), axis=1, keepdims=True)
             for e in range(EXP_DEV)
         ]
         gate_grads = [jnp.zeros((size, 1), F32) for _ in range(EXP_DEV)]
@@ -616,11 +630,13 @@
         out_copy(step).start()
         result = (dot_nt(stage[slot, 1], weights[0]) + dot_nt(stage[slot, 2], weights[1])).astype(BF)
         back[micro_batch, pl.ds(2 * block, 2), :, :D] = result.reshape(2, SEQ_DEV, D)
-        tail = jnp.zeros((size, LANES), F32)
+        high_tail, low_tail = jnp.zeros((size, LANES), F32), jnp.zeros((size, LANES), F32)
         for e in range(EXP_DEV):
+            ours = owner_ref[...] == EXP_DEV * me + e
             high = gate_grads[e].astype(BF).astype(F32)
-            tail = jnp.where(lane == EXP_DEV * me + e, high, tail)
-            tail = jnp.where(lane == experts + EXP_DEV * me + e, gate_grads[e] - high, tail)
+            high_tail = jnp.where(ours, high, high_tail)
+            low_tail = jnp.where(ours, gate_grads[e] - high, low_tail)
+        tail = high_tail + pltpu.roll(low_tail, experts, 1)
         back[micro_batch, pl.ds(2 * block, 2), :, D:] = tail.astype(BF).reshape(2, SEQ_DEV, LANES)
 
         @pl.when(micro_batch == 1)
@@ -710,18 +726,11 @@
             self._last(away).wait_send()
 
 
-def packed(padded, devices):
-    share = FF // devices
-    return jnp.concatenate(
-        [padded[:, device * HD : device * HD + share] for device in range(devices)], axis=1
-    )
-
-
 def expert_sums(
     chips,
-    rows_ref, grads_ref, hidden_ref, d_gate_ref, d_up_ref, shared_h_ref, shared_g_ref, shared_u_ref, back_ref,
-    gate_ref, up_ref, down_ref, back_b_ref, shared_outs, gate_rows_ref, up_rows_ref,
-    mine, pair, line, local_sem, stage, stage_sem, shared, arrived, summed, held, *sems,
+    rows_ref, grads_ref, hidden_ref, d_gate_ref, d_up_ref, shared_h_ref, shared_g_ref, shared_u_ref, back_ref, out_ref, hidden_one_ref,
+    gate_ref, up_ref, down_ref, back_b_ref, layer_ref, shared_outs, gate_rows_ref,
+    mine, pair, line, out_mine, out_pair, out_line, layer, local_sem, stage, stage_sem, shared, arrived, summed, held, *sems,
 ):
     chip, core = place()
     devices = 2 * chips
@@ -738,15 +747,24 @@
     spread = Spread(
         devices, 4, 1,
         lambda owner, k: shared.at[owner],
-        lambda k, device: device >= 0,
+        lambda k, device: device < FF // HD,
         lambda device, k: device,
-        arrived, summed, held, devices * HD, sems[6:13],
-    )
+        arrived, summed, held, FF, sems[6:13],
+    )
+    results = [
+        Scatter(
+            chips,
+            lambda to, m=m: out_ref.at[m, 2 * to + 1 - core],
+            lambda to, m=m: out_mine.at[m, to],
+            out_pair.at[m], out_line.at[m], sems[13 + 6 * m : 19 + 6 * m],
+        )
+        for m in range(MB)
+    ]
     routed = [
-        SeqSum(source.at[0], target, k % 2 == 0, k, sems[13:])
-        for k, (source, target) in enumerate(((gate_ref, gate_rows_ref), (up_ref, up_rows_ref)))
+        SeqSum(gate_ref.at[e], gate_rows_ref.at[e], e == 0, e, sems[13 + 6 * MB :])
+        for e in range(EXP_DEV)
     ]
-    targets = [(gate_ref, 0), (up_ref, 0), (gate_ref, 1), (up_ref, 1), (down_ref, 0), (down_ref, 1)]
+    targets = [(ref, e) for ref in (gate_ref, up_ref, down_ref) for e in range(EXP_DEV)]
 
     def write(number):
         target, e = targets[number // 2]
@@ -762,8 +780,12 @@
 
     def begin():
         loads = [
-            pltpu.make_async_copy(back_ref.at[2 * to + core], mine.at[to], local_sem.at[to])
+            pltpu.make_async_copy(source, target, local_sem.at[number, to])
             for to in range(chips)
+            for number, (source, target) in enumerate(
+                [(back_ref.at[2 * to + core], mine.at[to])]
+                + [(out_ref.at[m, 2 * to + core], out_mine.at[m, to]) for m in range(MB)]
+            )
         ]
         for load in loads:
             load.start()
@@ -781,17 +803,24 @@
     at(4, lambda: scatter.slot(1))
     at(6, lambda: scatter.slot(2))
     at(7, spread.middle)
+    at(4, results[0].start)
+    at(5, results[1].start)
+    at(7, lambda: results[0].slot(0))
+    at(8, lambda: results[1].slot(0))
+    at(9, lambda: results[0].slot(1))
+    at(10, lambda: results[1].slot(1))
+    at(11, lambda: results[0].slot(2))
     slot = step % 2
 
-    @pl.when(jnp.logical_or(matrix == 0, matrix == 2))
+    @pl.when(matrix < EXP_DEV)
     def _():
         stage[slot] = dot_tn(rows_ref[...], d_gate_ref[...]).astype(BF)
 
-    @pl.when(jnp.logical_or(matrix == 1, matrix == 3))
+    @pl.when(jnp.logical_and(matrix >= EXP_DEV, matrix < 2 * EXP_DEV))
     def _():
         stage[slot] = dot_tn(rows_ref[...], d_up_ref[...]).astype(BF)
 
-    @pl.when(matrix >= 4)
+    @pl.when(matrix >= 2 * EXP_DEV)
     def _():
         stage[slot] = dot_tn(grads_ref[...], hidden_ref[...]).astype(BF)
 
@@ -812,11 +841,16 @@
     @pl.when(step == last)
     def _():
         routed[1].middle()
+        results[1].slot(2)
+        results[0].finish(layer)
+        layer_ref[0] = (layer[...] + hidden_one_ref[0]).astype(BF)
         write(last - 1).wait()
         write(last).wait()
         spread.take()
         for kind, target in enumerate(shared_outs):
-            target[...] = packed(spread.of_kind(kind)[...].astype(F32), devices)
+            target[...] = spread.of_kind(kind)[...]
+        results[1].finish(layer)
+        layer_ref[1] = (layer[...] + hidden_one_ref[1]).astype(BF)
         for job in routed:
             job.finish()
         spread.finish()
@@ -1005,7 +1039,7 @@
         pltpu.VMEM((jobs, 2, rows, FF), BF),
         pltpu.VMEM((jobs, 2, rows, FF), BF),
         pltpu.VMEM((jobs, rows, FF), BF),
-        pltpu.VMEM((rows, FF), F32),
+        pltpu.VMEM((rows, FF), BF),
         pltpu.SemaphoreType.DMA((jobs, 2)),
         pltpu.SemaphoreType.DMA((jobs, 2)),
         pltpu.SemaphoreType.DMA((jobs, 2)),
@@ -1075,7 +1109,8 @@
 
     def finish(self):
         self._last().wait_recv()
-        self.result[...] = self.mine[self.own].astype(F32) + self.last[...].astype(F32)
+        total = self.mine[self.own].astype(F32) + self.last[...].astype(F32)
+        self.result[...] = total.astype(BF)
         self._write().start()
         for i in range(2):
             self._first(i).wait_send()
@@ -1083,10 +1118,83 @@
         self._write().wait()
 
 
+def far_sum_scratch(jobs):
+    rows = D // 4
+    return [
+        pltpu.VMEM((2, rows, FF), BF),
+        pltpu.VMEM((2, rows, FF), BF),
+        pltpu.VMEM((rows, FF), BF),
+        pltpu.SemaphoreType.DMA((jobs, 2)),
+        pltpu.SemaphoreType.DMA((jobs, 2)),
+        pltpu.SemaphoreType.DMA((jobs, 2)),
+        pltpu.SemaphoreType.DMA((jobs,)),
+        pltpu.SemaphoreType.DMA((jobs,)),
+        pltpu.SemaphoreType.DMA((jobs,)),
+        pltpu.SemaphoreType.DMA((jobs, 2)),
+    ]
+
+
+class FarSeqSum(SeqSum):
+    def __init__(self, source, out, x_first, job, slots, scratch):
+        mine, arrived, last = slots
+        self.ours, self.theirs, result = scratch[:3]
+        self.more_sem = scratch[9].at[job]
+        super().__init__(source, out, x_first, job, [mine, arrived, last, result] + list(scratch[3:9]))
+
+    def _fetch(self, i):
+        return pltpu.make_async_copy(self.arrived.at[i], self.theirs.at[i], self.more_sem.at[i])
+
+    def _load(self, i):
+        return pltpu.make_async_copy(self._block(i, True), self.ours.at[i], self.load_sem.at[i])
+
+    def _store(self, i):
+        return pltpu.make_async_copy(self.ours.at[i], self.mine.at[i], self.load_sem.at[i])
+
+    def start(self):
+        for i in range(2):
+            self._first(i).start()
+
+    def middle(self):
+        for i in range(2):
+            self._load(i).start()
+        for i in range(2):
+            self._first(i).wait_recv()
+            self._fetch(i).start()
+        for i in range(2):
+            self._load(i).wait()
+            self._fetch(i).wait()
+            self.ours[i] = (self.ours[i].astype(F32) + self.theirs[i].astype(F32)).astype(BF)
+            self._store(i).start()
+        for i in range(2):
+            self._store(i).wait()
+        self._last().start()
+
+    def finish(self):
+        ours = pltpu.make_async_copy(self.mine.at[self.own], self.ours.at[0], self.load_sem.at[0])
+        ours.start()
+        self._last().wait_recv()
+        theirs = pltpu.make_async_copy(self.last, self.theirs.at[0], self.more_sem.at[0])
+        theirs.start()
+        ours.wait()
+        theirs.wait()
+        total = self.ours[0].astype(F32) + self.theirs[0].astype(F32)
+        self.result[...] = total.astype(BF)
+        self._write().start()
+        for i in range(2):
+            self._first(i).wait_send()
+        self._last().wait_send()
+        self._write().wait()
+
+
+def softmax_low(scores):
+    powers = jnp.exp(scores - jnp.max(scores, axis=-1, keepdims=True))
+    return (powers * (1.0 / jnp.sum(powers, axis=-1, keepdims=True))).astype(BF)
+
+
 def heads_forward(
     chips, slots,
-    tokens_ref, grad_own_ref, named_own_ref, gain_one_ref, gain_two_ref, cos_ref, sin_ref, w_refs, w_out_ref,
-    normed_ref, qkv_ref, mixed_ref, lse_ref, own_mixed_ref, hidden_ref, two_ref, w_all, grad_ref, named_ref,
+    tokens_ref, grad_own_ref, named_own_ref, gain_ref, cos_ref, sin_ref, w_refs, w_out_ref,
+    normed_ref, qkv_ref, mixed_ref, own_mixed_ref, hidden_ref, two_ref, w_all, grad_ref, named_ref,
     rows, w_sem, local_sem, send_sem, recv_sem, *sems,
 ):
     devices = 2 * chips
@@ -1185,7 +1293,7 @@
                 at(1, later[1].start)
             part = pl.ds(pl.multiple_of(block * size, size), size)
             tokens = rows[m, pl.ds(2 * block, 2)].reshape(size, D).astype(F32)
-            normed = norm_rows(tokens, gain_one_ref[...]).astype(BF)
+            normed = norm_rows(tokens, gain_ref[0:1, :]).astype(BF)
             normed_ref[m, part, :] = normed
             qkv = dot(normed, w_all[...])
             for unit in range(3 * slots):
@@ -1202,13 +1310,9 @@
                     qkv_ref[m, :stop, base + HD : base + 2 * HD],
                     start,
                 )
-                largest = jnp.max(scores, axis=-1, keepdims=True)
-                powers = jnp.exp(scores - largest)
-                total = jnp.sum(powers, axis=-1, keepdims=True)
-                attention = (powers * (1.0 / total)).astype(BF)
+                attention = softmax_low(scores)
                 mixed = dot(attention, qkv_ref[m, :stop, base + 2 * HD : base + 3 * HD])
                 mixed_ref[m, start:stop, slot * HD : (slot + 1) * HD] = mixed.astype(BF)
-                lse_ref[m, slot, start:stop, :] = largest + jnp.log(total)
             for number in range(MB):
 
                 @pl.when(jnp.logical_and(m == number, slot_lives(slot, me, devices)))
@@ -1237,7 +1341,7 @@
 
         hidden = tokens_ref[m].astype(F32) + dot(own_mixed_ref[m], w_out_ref[...])
         hidden_ref[m] = hidden
-        two_ref[m] = norm_rows(hidden, gain_two_ref[...]).astype(BF)
+        two_ref[m] = norm_rows(hidden, gain_ref[1:2, :]).astype(BF)
 
     finish_rows(0)
     for hop in range(2, chips):
@@ -1261,10 +1365,10 @@
 
 def heads_backward(
     chips, slots,
-    own_ref, qkv_ref, mixed_ref, lse_ref, cos_ref, sin_ref, w_ref, own_mixed_ref, mix_ref, small_ref,
-    normed_ref, gate_ref, up_ref, down_ref,
-    sums_ref, grad_a_ref, grad_b_ref, w_out_out, small_out, job_outs,
-    d_mixed, probs, raw, parts, d_keys, d_values, pairs, lines,
+    own_ref, qkv_ref, mixed_ref, cos_ref, sin_ref, w_ref, own_mixed_ref, mix_ref, small_ref,
+    normed_ref, up_ref, down_ref,
+    grad_a_ref, grad_b_ref, weight_outs, w_out_out, small_out, up_out, down_out, job_slots,
+    sums_ref, arrived, summed, held, d_mixed, probs, raw, parts, d_keys, d_values, pairs, lines,
     part, weight_pair, weight_line, result, normed, normed_sem, local_sem, send_sem, recv_sem, *sems,
 ):
     devices = 2 * chips
@@ -1283,13 +1387,21 @@
         for m in range(MB)
     ]
 
+    spread = Spread(
+        devices, 4, slots,
+        lambda owner, k: sums_ref.at[owner + 3 * k],
+        lambda k, device: slot_lives(k, device, devices),
+        lambda device, k: slot_head(k, device, devices),
+        arrived, summed, held, D, sems[6 * MB + 6 : 6 * MB + 13],
+    )
     routed = [
-        SeqSum(source, target, k % 2 == 0, k, sems[6 * MB + 6 : -7])
+        FarSeqSum(source, target, k % 2 == 0, k, job_slots, sems[6 * MB + 13 : -7])
         for k, (source, target) in enumerate(
-            zip((gate_ref.at[1], up_ref.at[1], down_ref.at[0]), job_outs)
+            (ref.at[e], out.at[e])
+            for ref, out in ((up_ref, up_out), (down_ref, down_out))
+            for e in range(EXP_DEV)
         )
     ]
-
     rows = D // devices
 
     def row_block(device):
@@ -1384,9 +1496,7 @@
                     qkv_ref[m, :stop, base + HD : base + 2 * HD],
                     start,
                 )
-                probs[slot, start:stop, :stop] = jnp.exp(
-                    scores - lse_ref[m, slot, start:stop, :]
-                ).astype(BF)
+                probs[start // step][slot] = softmax_low(scores)
 
     def body(m, carry):
         weigh(m)
@@ -1408,7 +1518,6 @@
             for turn_ in range(min(slots, chips - 1), chips - 1):
                 weight.slot(turn_)
             routed[0].middle()
-            routed[2].start()
 
         for slot in range(slots):
             base = 3 * HD * slot
@@ -1422,7 +1531,7 @@
                 d_mix = d_mixed[m, start:stop, slot * HD : (slot + 1) * HD]
                 mixed = mixed_ref[m, start:stop, slot * HD : (slot + 1) * HD]
                 row_term = jnp.sum(d_mix.astype(F32) * mixed.astype(F32), axis=1, keepdims=True)
-                attention = probs[slot, start:stop, :stop]
+                attention = probs[start // step][slot]
                 d_scores = (attention.astype(F32) * (dot_nt(d_mix, values) - row_term)).astype(BF)
                 turned = turn(dot(d_scores, keys) * factor, cos_ref[start:stop, :], -sin_ref[start:stop, :])
                 raw[m, start:stop, base : base + HD] = turned.astype(BF)
@@ -1455,7 +1564,6 @@
 
     lax.fori_loop(0, MB, body, 0)
     scatters[1].start()
-    routed[0].finish()
     for turn_ in range(min(slots, chips - 1), chips - 1):
         scatters[0].slot(turn_)
     ticks = [lambda t=t: scatters[1].slot(t) for t in range(chips - 1)]
@@ -1466,20 +1574,32 @@
             load(number + 2).start()
         for unit in range(3 * slots):
             sums_ref[unit, left : left + 256, :] = total[:, unit * HD : (unit + 1) * HD].astype(BF)
-        if number < len(ticks):
-            ticks[number]()
+        if number == 1:
+            ticks[0]()
+    spread.start()
+    routed[2].start()
+    routed[3].start()
+    ticks[1]()
+    weight_all.middle()
     scatters[0].finish(grad_a_ref)
-    weight_all.middle()
+    routed[0].finish()
+    ticks[2]()
     routed[1].finish()
-    routed[2].middle()
-    for number in range(D // 256, len(ticks)):
-        ticks[number]()
+    spread.middle()
     scatters[1].finish(grad_b_ref)
     weight_all.take()
-    w_out_out[...] = weight_all.whole[:, :D].astype(F32)
-    small_out[...] = weight_all.whole[:, D:far].astype(F32)
+    w_out_out[...] = weight_all.whole[:, :D]
+    small_out[...] = weight_all.whole[:, D:far]
+    spread.hand_out()
+    routed[2].middle()
+    routed[3].middle()
+    spread.take()
+    for kind, target in enumerate(weight_outs):
+        target[...] = spread.of_kind(kind)[...]
+    routed[2].finish()
+    routed[3].finish()
     weight_all.finish()
-    routed[2].finish()
+    spread.finish()
     for m in range(MB):
         for away in range(1, devices):
             for slot in range(slots):
@@ -1489,64 +1609,71 @@
                     exchange(m, away, slot).wait_send()
 
 
-def spread_sums(
-    chips, slots,
-    qkv_ref, out_ref, hidden_ref, down_ref,
-    query_out, key_out, value_out, layer_ref, routed_out,
-    arrived, summed, held, layer, mine, pair, line, mine_sem,
-    *sems,
+def middle_rows(
+    back_a_ref, back_b_ref, named_ref, hidden_ref, grad_ref, two_ref, router_ref, gain_ref, w_out_ref,
+    grad_hidden_ref, mix_ref, d_mixed_ref, small_ref,
+    experts,
 ):
-    devices = 2 * chips
-    me = lax.axis_index("exp")
-    core = me % 2
-    groups = 4
-    outs = [
-        Scatter(
-            chips,
-            lambda to, m=m: out_ref.at[m, 2 * to + 1 - core],
-            lambda to, m=m: mine.at[m, to],
-            pair.at[m], line.at[m], sems[6 * m : 6 * m + 6],
-        )
-        for m in range(MB)
+    size = SEQ_DEV
+    lane = lax.broadcasted_iota(jnp.int32, (MB * size, LANES), 1)
+    named = named_ref[...].astype(F32)
+    logits = jnp.where(named > 0.0, dot(two_ref[...], router_ref[...]), -1e30)
+    powers = jnp.where(named > 0.0, jnp.exp(logits - jnp.max(logits, axis=1, keepdims=True)), 0.0)
+    gates = powers / jnp.sum(powers, axis=1, keepdims=True)
+    tail = jnp.concatenate([back_a_ref[:, D:], back_b_ref[:, D:]], axis=0)
+    tail = jnp.where(lane < experts, tail + pltpu.roll(tail, LANES - experts, 1), 0.0)
+    grad_logits = gates * (tail - jnp.sum(gates * tail, axis=1, keepdims=True))
+    grad_logits = grad_logits.astype(BF)
+    grad_two = jnp.concatenate([back_a_ref[:, :D], back_b_ref[:, :D]], axis=0)
+    grad_two += dot_nt(grad_logits, router_ref[...])
+    back, terms = norm_back(hidden_ref[...], gain_ref[1:2, :], grad_two)
+    grad_hidden = grad_ref[...].astype(F32) + back
+    grad_hidden_ref[...] = grad_hidden
+    mix_ref[...] = grad_hidden.astype(BF)
+    d_mixed_ref[...] = dot_nt(mix_ref[...], w_out_ref[...]).astype(BF)
+    high = terms.astype(BF)
+    low = (terms - high.astype(F32)).astype(BF)
+    chosen = jnp.where(lane == experts, 1.0, 0.0).astype(BF)
+    total = dot_tn(two_ref[...], grad_logits) + dot_tn(high, chosen) + dot_tn(low, chosen)
+    small_ref[...] = total.astype(BF)
+
+
+def last_rows(
+    tokens_ref, normed_a_ref, normed_b_ref, grad_hidden_ref, gain_ref, gain_rows_ref, weight_lows, small_ref, layer_ref,
+    far_lows, w_refs,
+    grad_tokens_ref, weight_outs, router_ref, gain_one_ref, gain_two_ref, layer_out, far_outs,
+    w_rows, w_sem,
+    experts,
+):
+    rows = D // lax.axis_size("exp")
+    start = pl.ds(pl.multiple_of(lax.axis_index("exp") * rows, 32), rows)
+    loads = [
+        pltpu.make_async_copy(w_refs[k].at[start], w_rows.at[k], w_sem.at[k]) for k in range(3)
     ]
-    spread = Spread(
-        devices, groups, slots,
-        lambda owner, k: qkv_ref.at[owner + (groups - 1) * k],
-        lambda k, device: slot_lives(k, device, devices),
-        lambda device, k: slot_head(k, device, devices),
-        arrived, summed, held, D, sems[6 * MB : 6 * MB + 7],
-    )
-    routed = SeqSum(down_ref.at[1], routed_out, False, 0, sems[6 * MB + 7 :])
-    loads = [
-        pltpu.make_async_copy(out_ref.at[m, 2 * to + core], mine.at[m, to], mine_sem.at[m, to])
-        for m in range(MB)
-        for to in range(chips)
-    ]
-    for load in loads:
-        load.start()
-    meet_all(("seq", "exp"))
-    spread.start()
-    outs[0].start()
-    outs[1].start()
-    for load in loads:
-        load.wait()
-    outs[0].slot(0)
-    spread.middle()
-    routed.start()
-    spread.hand_out()
-    outs[1].slot(0)
-    for turn_ in range(1, chips - 1):
-        outs[0].slot(turn_)
-        outs[1].slot(turn_)
-    routed.middle()
-    for m in range(MB):
-        outs[m].finish(layer)
-        layer_ref[m] = (layer[...] + hidden_ref[m]).astype(BF)
-    spread.take()
-    for kind, target in enumerate((query_out, key_out, value_out)):
-        target[...] = spread.of_kind(kind)[...].astype(F32)
-    spread.finish()
-    routed.finish()
+    for copy in loads:
+        copy.start()
+    for low, out in zip(far_lows, far_outs):
+        out[...] = low[...].astype(F32)
+    layer_out[...] = layer_ref[...]
+    for m, normed_ref in enumerate((normed_a_ref, normed_b_ref)):
+        part = slice(m * SEQ_DEV, (m + 1) * SEQ_DEV)
+        back, _ = norm_back(tokens_ref[part, :].astype(F32), gain_ref[0:1, :], normed_ref[...])
+        grad_tokens_ref[part, :] = (grad_hidden_ref[part, :] + back).astype(BF)
+    product = jnp.zeros((rows, D), F32)
+    for k, (low, out) in enumerate(zip(weight_lows, weight_outs)):
+        grad = low[...].astype(F32)
+        out[...] = grad
+        if k < 3:
+            loads[k].wait()
+            product += w_rows[k].astype(F32) * grad
+    ones = jnp.ones((8, D), BF)
+    high = product.astype(BF)
+    low = (product - high.astype(F32)).astype(BF)
+    gain_one_ref[...] = (dot_nt(ones, high) + dot_nt(ones, low))[0:1, :] / gain_rows_ref[...]
+    small = small_ref[...]
+    router_ref[...] = small[:, :experts].astype(F32)
+    column = lax.broadcasted_iota(jnp.int32, (8, LANES), 1)
+    gain_two_ref[...] = dot_nt(jnp.where(column == experts, 1.0, 0.0).astype(BF), small)[0:1, :]
 
 
 def taking(us):
@@ -1561,25 +1688,18 @@
 ANYWHERE = pl.BlockSpec(memory_space=pl.ANY)
 
 
-def experts_on_lines(two_own, grad_own, grad_a, named, expert_at, router_rows, routed, shared, share):
+def experts_on_lines(two_own, hidden_one, grad_own, grad_a, named, experts, router, owners, routed, shared):
     devices = lax.axis_size("exp")
-    me = lax.axis_index("exp")
-    experts = expert_at.shape[0]
     chips = devices // 2
     length = SEQ_DEV * devices
     wide = EXP_DEV * FF + LANES
-    own_shared = [
-        jnp.pad(lax.dynamic_slice(w, (0, me * share), (D, share)), ((0, 0), (0, LANES - share)))
-        for w in shared
-    ]
-    router = jnp.pad(router_rows, ((0, 0), (0, LANES - experts)))
     block_back = (devices, SEQ_DEV, D + LANES)
     sems = [gather_sems(chips)] * MB + [scatter_sems(chips), gather_sems(chips)]
 
     def call_rows(*operands):
-        def kernel(own_ref, grad_own_ref, grad_ref, named_ref, router_ref, *refs):
+        def kernel(own_ref, grad_own_ref, grad_ref, named_ref, router_ref, owner_ref, *refs):
             expert_rows(
-                chips, experts, own_ref, grad_own_ref, grad_ref, named_ref, router_ref,
+                chips, experts, own_ref, grad_own_ref, grad_ref, named_ref, router_ref, owner_ref,
                 refs[:3], refs[3:6], *refs[6:],
             )
 
@@ -1595,7 +1715,7 @@
                 like(*block_back),
                 like(SEQ_DEV, D + LANES, dtype=F32),
             ),
-            in_specs=[IN_VMEM, ANYWHERE, ANYWHERE, IN_VMEM, IN_VMEM] + [ANYWHERE] * 6,
+            in_specs=[IN_VMEM, ANYWHERE, ANYWHERE] + [IN_VMEM] * 3 + [ANYWHERE] * 6,
             out_specs=(ANYWHERE,) * 7 + (IN_VMEM,),
             scratch_shapes=[
                 pltpu.VMEM((3, D, wide), BF),
@@ -1620,21 +1740,21 @@
         )(*operands)
 
     rows, grads, hidden, d_gate, d_up, out_parts, back_b, back_sum_a = call_rows(
-        two_own, grad_own, grad_a, named, router, *routed, *own_shared
+        two_own, grad_own, grad_a, named, router, owners, *routed, *shared
     )
     flat = MB * length
 
 
     def call_sums(*operands):
         def kernel(*refs):
-            expert_sums(chips, *refs[:13], refs[13:16], *refs[16:])
+            expert_sums(chips, *refs[:16], refs[16:19], *refs[19:])
 
         half = D // 2
         by_rows = pl.BlockSpec((flat, half), lambda k, d: (0, d))
         by_grads = pl.BlockSpec((flat, half), lambda k, d: (0, d))
 
         def for_gate(k, d):
-            return (0, (k + 2) // 4)
+            return (0, (k + 4) // 5)
 
         def for_up(k, d):
             return (0, k // 3)
@@ -1653,31 +1773,38 @@
             kernel,
             grid=(3 * EXP_DEV, 2),
             out_shape=(like(EXP_DEV, D, FF),) * 3
-            + (like(SEQ_DEV, D + LANES, dtype=F32),)
-            + (like(D // devices, FF, dtype=F32),) * 3
-            + (like(D // 4, FF, dtype=F32),) * 2,
+            + (like(SEQ_DEV, D + LANES, dtype=F32), like(MB, SEQ_DEV, D))
+            + (like(D // devices, FF),) * 3
+            + (like(EXP_DEV, D // 4, FF),),
             in_specs=[by_rows, by_grads]
-            + [pl.BlockSpec((flat, FF), use) for use in (for_down, for_gate, for_up)]
+            + [pl.BlockSpec((flat, FF), for_down, pipeline_mode=pl.Buffered(1))]
+            + [pl.BlockSpec((flat, FF), use) for use in (for_gate, for_up)]
             + [last] * 3
-            + [ANYWHERE],
+            + [ANYWHERE] * 2
+            + [pl.BlockSpec((MB, SEQ_DEV, D), lambda k, d: (0, 0, 0), pipeline_mode=pl.Buffered(1))],
             out_specs=(ANYWHERE,) * 3
-            + (whole(SEQ_DEV, D + LANES),)
+            + (whole(SEQ_DEV, D + LANES), whole(MB, SEQ_DEV, D))
             + (whole(D // devices, FF),) * 3
-            + (ANYWHERE,) * 2,
+            + (ANYWHERE,),
             scratch_shapes=[
                 pltpu.VMEM((chips, SEQ_DEV, D + LANES), BF),
                 pltpu.VMEM((chips, SEQ_DEV, D + LANES), BF),
                 pltpu.VMEM((chips + 1, SEQ_DEV, D + LANES), BF),
-                pltpu.SemaphoreType.DMA((chips,)),
+                pltpu.VMEM((MB, chips, SEQ_DEV, D), BF),
+                pltpu.VMEM((MB, chips, SEQ_DEV, D), BF),
+                pltpu.VMEM((MB, chips + 1, SEQ_DEV, D), BF),
+                pltpu.VMEM((SEQ_DEV, D), F32),
+                pltpu.SemaphoreType.DMA((1 + MB, chips)),
                 pltpu.VMEM((2, half, FF), BF),
                 pltpu.SemaphoreType.DMA((2,)),
                 pltpu.VMEM((3, D, HD), BF),
                 pltpu.VMEM((3, 1, D, HD), BF),
                 pltpu.VMEM((1, D, HD), BF),
-                pltpu.VMEM((4, D // devices, devices * HD), BF),
+                pltpu.VMEM((4, D // devices, FF), BF),
             ]
             + scatter_sems(chips)
             + spread_sems(devices, 4, 1)
+            + scatter_sems(chips) * MB
             + seq_scratch(2),
             compiler_params=pltpu.CompilerParams(
                 collective_id=2, has_side_effects=True, vmem_limit_bytes=VMEM_BYTES
@@ -1686,18 +1813,15 @@
             name="expert_sums",
         )(*operands)
 
-    gate_sum, up_sum, down_sum, back_sum_b, *shared_grads, gate_rows, up_rows = call_sums(
-        rows.reshape(flat, D), grads.reshape(flat, D), hidden, d_gate, d_up, hidden, d_gate, d_up, back_b
+    gate_sum, up_sum, down_sum, back_sum_b, layer_out, *shared_grads, gate_rows = call_sums(
+        rows.reshape(flat, D), grads.reshape(flat, D), hidden, d_gate, d_up, hidden, d_gate, d_up, back_b,
+        out_parts, hidden_one,
     )
     backs = (back_sum_a, back_sum_b)
-    tails = [
-        b[:, D : D + experts] + b[:, D + experts : D + 2 * experts] for b in backs
-    ]
     return (
-        out_parts,
-        [b[:, :D] for b in backs],
-        tails,
-        (gate_rows, up_rows),
+        layer_out,
+        backs,
+        gate_rows,
         (gate_sum, up_sum, down_sum),
         shared_grads,
     )
@@ -1987,24 +2111,22 @@
     rows_out = D // devices
     slots = -(-HEADS // devices)
     wide = slots * HD
-    share = FF // devices
     own = MB * SEQ_DEV
 
     cos_table, sin_table = turn_tables(length)
 
-    expert_at = jnp.sum(
-        (owner_table[:, None] == jnp.arange(experts)[None, :]) * jnp.arange(experts)[:, None],
-        axis=0,
-    )
-    router_rows = jnp.take(w_router, expert_at, axis=1)
-    names = jnp.concatenate([expert_at, jnp.full((LANES - experts,), -1, jnp.int32)])
-    named_own = jnp.any(expert_ids.reshape(own, TOP)[:, :, None] == names, axis=1).astype(BF)
+    router = jnp.pad(w_router, ((0, 0), (0, LANES - experts)))
+    owners = jnp.pad(owner_table, (0, LANES - experts), constant_values=-1)[None]
+    gains = jnp.stack([gain_one, gain_two])
+    named_own = jnp.any(
+        expert_ids.reshape(own, TOP)[:, :, None] == jnp.arange(LANES)[None, None, :], axis=1
+    ).astype(BF)
     tokens_own = tokens.reshape(MB, SEQ_DEV, D)
     grad_own = cotangent.reshape(MB, SEQ_DEV, D)
 
     def call_forward(*operands):
         def kernel(*refs):
-            heads_forward(chips, slots, *refs[:7], refs[7:10], *refs[10:])
+            heads_forward(chips, slots, *refs[:6], refs[6:9], *refs[9:])
 
         return pl.pallas_call(
             kernel,
@@ -2012,7 +2134,6 @@
                 like(MB, length, D),
                 like(MB, length, 3 * wide),
                 like(MB, length, wide),
-                like(MB, slots, length, 1, dtype=F32),
                 like(MB, SEQ_DEV, D),
                 like(MB, SEQ_DEV, D, dtype=F32),
                 like(MB, SEQ_DEV, D),
@@ -2020,8 +2141,8 @@
                 like(devices, SEQ_DEV, D),
                 like(devices, own, LANES),
             ),
-            in_specs=[IN_VMEM, ANYWHERE] + [IN_VMEM] * 5 + [ANYWHERE] * 3 + [IN_VMEM],
-            out_specs=(IN_VMEM,) * 8 + (ANYWHERE, IN_VMEM),
+            in_specs=[IN_VMEM, ANYWHERE] + [IN_VMEM] * 4 + [ANYWHERE] * 3 + [IN_VMEM],
+            out_specs=(IN_VMEM,) * 7 + (ANYWHERE, IN_VMEM),
             scratch_shapes=[
                 pltpu.VMEM((MB, devices, SEQ_DEV, D), BF),
                 pltpu.SemaphoreType.DMA((3 * slots,)),
@@ -2037,64 +2158,72 @@
             name="heads_forward",
         )(*operands)
 
-    normed, qkv, mixed, lse, own_mixed, hidden_one, two_low, w_qkv, grad_a, named_all = call_forward(
-        tokens_own, grad_own, named_own, gain_one[None], gain_two[None], cos_table, sin_table,
+    normed, qkv, mixed, own_mixed, hidden_one, two_low, w_qkv, grad_a, named_all = call_forward(
+        tokens_own, grad_own, named_own, gains, cos_table, sin_table,
         w_query, w_key, w_value, w_out,
     )
-    rows_in = tokens.reshape(own, D).astype(F32)
     hidden_rows = hidden_one
     own_mixed, hidden_one = own_mixed.reshape(own, D), hidden_one.reshape(own, D)
     two_low = two_low.reshape(own, D)
-    gates = named_softmax(dot(two_low, router_rows), named_own[:, :experts] > 0)
-
-    out_parts, backs, tails, done, routed_sums, shared_grads = experts_on_lines(
+
+    layer_out, backs, gate_full, routed_sums, shared_lows = experts_on_lines(
         two_low.reshape(MB, SEQ_DEV, D),
+        hidden_rows,
         grad_own,
         grad_a,
         named_all.reshape(devices, MB * SEQ_DEV, LANES),
-        expert_at,
-        router_rows,
+        experts,
+        router,
+        owners,
         (routed_gate, routed_up, routed_down),
         (shared_gate, shared_up, shared_down),
-        share,
-    )
-    tail = jnp.concatenate(tails)
-    grad_logits = (gates * (tail - jnp.sum(gates * tail, axis=-1, keepdims=True))).astype(BF)
-    grad_two = jnp.concatenate(backs) + dot_nt(grad_logits, router_rows)
-    back, gain_two_terms = norm_back(hidden_one, gain_two, grad_two)
-    grad_hidden = cotangent.reshape(own, D).astype(F32) + back
-    grad_mix = grad_hidden.astype(BF)
-    d_mixed = dot_nt(grad_mix, w_out).astype(BF)
-
-    quarter = like(D // groups, FF, dtype=F32)
+    )
+    def call_middle(*operands):
+        def kernel(*refs):
+            middle_rows(*refs, experts)
+
+        return pl.pallas_call(
+            kernel,
+            out_shape=(like(own, D, dtype=F32), like(own, D), like(own, D), like(D, LANES)),
+            in_specs=[IN_VMEM] * 9,
+            out_specs=(IN_VMEM,) * 4,
+            compiler_params=pltpu.CompilerParams(vmem_limit_bytes=VMEM_BYTES),
+            cost_estimate=taking(5),
+            name="middle_rows",
+        )(*operands)
+
+    grad_hidden, grad_mix, d_mixed, small = call_middle(
+        *backs, named_own, hidden_one, cotangent.reshape(own, D), two_low, router, gains, w_out
+    )
+    quarter = like(EXP_DEV, D // groups, FF)
     far = D + LANES
-    small = jnp.concatenate(
-        [
-            dot_tn(two_low, grad_logits),
-            jnp.sum(gain_two_terms, axis=0)[:, None],
-            jnp.zeros((D, LANES - experts - 1), F32),
-        ],
-        axis=1,
-    ).astype(BF)
+    jobs = 4
+    slot_shape = (jobs, 2, D // groups, FF)
 
     def backward_kernel(*refs):
-        heads_backward(chips, slots, *refs[:19], refs[19:22], *refs[22:])
-
-    heads_sum, normed_a, normed_b, w_out_rows, small_rows, gate_two, up_two, down_one = pl.pallas_call(
+        heads_backward(
+            chips, slots, *refs[:14], refs[14:17], *refs[17:21], refs[21:24], *refs[24:29],
+            refs[29 : 29 + length // BLOCK], *refs[29 + length // BLOCK :],
+        )
+
+    normed_a, normed_b, *backward_out = pl.pallas_call(
         backward_kernel,
-        out_shape=(
-            like(3 * slots, D, HD),
-            like(SEQ_DEV, D, dtype=F32),
-            like(SEQ_DEV, D, dtype=F32),
-            like(rows_out, D, dtype=F32),
-            like(rows_out, LANES, dtype=F32),
-        )
-        + (quarter,) * 3,
-        in_specs=[IN_VMEM] * 10 + [ANYWHERE] * 4,
-        out_specs=(IN_VMEM,) * 5 + (ANYWHERE,) * 3,
+        out_shape=(like(SEQ_DEV, D, dtype=F32),) * 2
+        + (like(rows_out, D),) * 4
+        + (like(rows_out, LANES),)
+        + (quarter,) * 2
+        + (like(*slot_shape), like(*slot_shape), like(jobs, D // groups, FF)),
+        in_specs=[IN_VMEM] * 9 + [ANYWHERE] * 3,
+        out_specs=(IN_VMEM,) * 7 + (ANYWHERE,) * 5,
         scratch_shapes=[
+            pltpu.VMEM((3 * slots, D, HD), BF),
+            pltpu.VMEM((groups - 1, slots, D, HD), BF),
+            pltpu.VMEM((slots, D, HD), BF),
+            pltpu.VMEM((groups, rows_out, D), BF),
             pltpu.VMEM((MB, length, wide), BF),
-            pltpu.VMEM((slots, length, length), BF),
+        ]
+        + [pltpu.VMEM((slots, BLOCK, stop), BF) for stop in range(BLOCK, length + 1, BLOCK)]
+        + [
             pltpu.VMEM((MB, length, 3 * wide), BF),
             pltpu.VMEM((MB, devices, SEQ_DEV, D), BF),
             pltpu.VMEM((length, HD), F32),
@@ -2112,68 +2241,62 @@
             pltpu.SemaphoreType.DMA((MB, devices, slots)),
         ]
         + scatter_sems(chips) * (MB + 1)
-        + seq_scratch(3)
+        + spread_sems(devices, groups, slots)
+        + far_sum_scratch(jobs)
         + seq_all_scratch(rows_out, (far + LANES) // groups),
         compiler_params=pltpu.CompilerParams(
             collective_id=3, has_side_effects=True, vmem_limit_bytes=VMEM_BYTES
         ),
-        cost_estimate=taking(70),
+        cost_estimate=taking(140),
         name="heads_backward",
     )(
-        d_mixed.reshape(MB, SEQ_DEV, D), qkv, mixed, lse, cos_table, sin_table, w_qkv, own_mixed,
-        grad_mix, small, normed, *routed_sums,
-    )
-    grad_normed = jnp.concatenate([normed_a, normed_b])
-    back_one, _ = norm_back(rows_in, gain_one, grad_normed)
-    grad_tokens = (grad_hidden + back_one).astype(BF)
-    *attn, layer_out, down_two = pl.pallas_call(
-        functools.partial(spread_sums, chips, slots),
-        out_shape=(like(rows_out, D, dtype=F32),) * 3 + (like(MB, SEQ_DEV, D), quarter),
-        in_specs=[IN_VMEM, ANYWHERE, IN_VMEM, ANYWHERE],
-        out_specs=(IN_VMEM,) * 4 + (ANYWHERE,),
-        scratch_shapes=[
-            pltpu.VMEM((groups - 1, slots, D, HD), BF),
-            pltpu.VMEM((slots, D, HD), BF),
-            pltpu.VMEM((groups, rows_out, D), BF),
-            pltpu.VMEM((SEQ_DEV, D), F32),
-            pltpu.VMEM((MB, chips, SEQ_DEV, D), BF),
-            pltpu.VMEM((MB, chips, SEQ_DEV, D), BF),
-            pltpu.VMEM((MB, chips + 1, SEQ_DEV, D), BF),
-            pltpu.SemaphoreType.DMA((MB, chips)),
-        ]
-        + scatter_sems(chips) * MB
-        + spread_sems(devices, groups, slots)
-        + seq_scratch(1),
-        compiler_params=pltpu.CompilerParams(
-            collective_id=4, has_side_effects=True, vmem_limit_bytes=VMEM_BYTES
-        ),
-        cost_estimate=taking(80),
-        name="spread_sums",
-    )(heads_sum, out_parts, hidden_rows, routed_sums[2])
-    gain_rows = lax.dynamic_slice(gain_one, (me * rows_out,), (rows_out,))
-    gain_one_grad = sum(
-        jnp.sum(
-            lax.dynamic_slice(weight, (me * rows_out, 0), (rows_out, D)).astype(F32) * grad, axis=1
-        )
-        for weight, grad in zip((w_query, w_key, w_value), attn)
-    ) / gain_rows
+        d_mixed.reshape(MB, SEQ_DEV, D), qkv, mixed, cos_table, sin_table, w_qkv, own_mixed,
+        grad_mix, small, normed, *routed_sums[1:],
+    )
+    gain_rows = lax.dynamic_slice(gain_one, (me * rows_out,), (rows_out,))[None]
+
+    def call_last(*operands):
+        def kernel(*refs):
+            last_rows(
+                *refs[:6], refs[6:10], *refs[10:12], refs[12:18], refs[18:21], refs[21], refs[22:26],
+                *refs[26:30], refs[30:36], *refs[36:], experts,
+            )
+
+        full = like(EXP_DEV, D // groups, FF, dtype=F32)
+        return pl.pallas_call(
+            kernel,
+            out_shape=(like(own, D),)
+            + (like(rows_out, D, dtype=F32),) * 4
+            + (like(rows_out, experts, dtype=F32),)
+            + (like(1, rows_out, dtype=F32),) * 2
+            + (like(MB, SEQ_DEV, D),)
+            + (like(rows_out, FF, dtype=F32),) * 3
+            + (full,) * 3,
+            in_specs=[IN_VMEM] * 18 + [ANYWHERE] * 3,
+            out_specs=(IN_VMEM,) * 15,
+            scratch_shapes=[pltpu.VMEM((3, rows_out, D), BF), pltpu.SemaphoreType.DMA((3,))],
+            compiler_params=pltpu.CompilerParams(vmem_limit_bytes=VMEM_BYTES),
+            cost_estimate=taking(6),
+            name="last_rows",
+        )(*operands)
+
+    last_out = call_last(
+        tokens.reshape(own, D), normed_a, normed_b, grad_hidden, gains, gain_rows,
+        *backward_out[:5], layer_out, *shared_lows, gate_full, *backward_out[5:7],
+        w_query, w_key, w_value,
+    )
+    grad_tokens, attn, router_grad = last_out[0], last_out[1:5], last_out[5]
+    gain_one_grad, gain_two_grad, layer_out = last_out[6:9]
+    far_grads = last_out[9:]
     whole = (MB, 1, SEQ_DEV, D)
     return (
         layer_out.reshape(whole),
         grad_tokens.reshape(whole),
-        attn[0],
-        attn[1],
-        attn[2],
-        w_out_rows,
-        gain_one_grad,
-        small_rows[:, experts],
-        jnp.take(small_rows[:, :experts], owner_table, axis=1),
-        shared_grads[0],
-        shared_grads[1],
-        shared_grads[2],
-        jnp.stack([done[0], gate_two]),
-        jnp.stack([done[1], up_two]),
-        jnp.stack([down_one, down_two]),
+        *attn,
+        gain_one_grad[0],
+        gain_two_grad[0],
+        router_grad,
+        *far_grads,
     )
 
 

time: 543 us -> 499 us (0.919)
  local copies, waits for them, and re-layouts: 25.9 us -> 6.52 us
  other arithmetic: 19.5 us -> 1.56 us
    unnamed x97 -> x8, local copies, waits for them, and re-layouts: 14.2 us -> 2.49 us
    pallas_call x2 -> x3, Pallas kernels: 189 us -> 179 us  [the longest x1 161 us: on_device_lines(): pl.pallas_call(backward_kernel, out_shape=(like(SEQ_DEV, D, dtype=F32),)...]
    pallas_call x1, Pallas kernels: 92.2 us -> 101 us  [call_sums(): pl.pallas_call(kernel, grid=(3 * EXP_DEV, 2), out_shape=(like(EXP_DEV, D,...]
    reduce_sum x9 -> x0, other arithmetic: 5.8 us -> none  [the longest x3 3.75 us: on_device_lines(): jnp.sum(lax.dynamic_slice(weight, (me * rows_out, 0), (rows_out, D)).asty...]
    another operation x3 -> x1, other arithmetic: 6.15 us -> 0.61 us  [on_device_lines(): gains = jnp.stack([gain_one, gain_two])]
where the time goes in v5:
time: 499 us; the launch traced here: 491 us
  Pallas kernels  482 us (97%)
  local copies, waits for them, and re-layouts  6.52 us (1%)
    pallas_call x1, Pallas kernels, on_device_lines(): pl.pallas_call(backward_kernel, out_shape=(like(SEQ_DEV, D, dtype=F32),)...  161 us
    pallas_call x1, Pallas kernels, call_rows(): pl.pallas_call(kernel, out_shape=(like(MB, devices, SEQ_DEV, D), like(MB,...  108 us
    pallas_call x1, Pallas kernels, call_sums(): pl.pallas_call(kernel, grid=(3 * EXP_DEV, 2), out_shape=(like(EXP_DEV, D,...  101 us
    pallas_call x1, Pallas kernels, call_forward(): pl.pallas_call(kernel, out_shape=(like(MB, length, D), like(MB, length, 3...  93.9 us
    pallas_call x1, Pallas kernels, call_last(): pl.pallas_call(kernel, out_shape=(like(own, D),) + (like(rows_out, D, dty...  10.6 us

profile of v5, /device:TPU:12, one launch (start us, length us, event | category | flops | bytes accessed | tf_op | source)
XLA Modules:
  0.0 490.9 jit_solution(17564496818187124558)
XLA Ops:
  0.6 0.7 copy.53
  1.3 0.3 fusion
  1.7 0.6 convert_element_type.5.refs_2_
  2.3 0.7 stack.10
  3.0 0.7 stack.9
  3.7 0.6 pad_maximum_fusion.refs_3_.refs_7_.refs_4_
  4.3 0.0 copy-start
  4.3 0.0 copy-start.1
  4.3 93.9 %heads_forward.1 = (bf16[2,1024,1280]{2,1,0:T(8,128)(2,1)}, bf16[2,1024,768]{2,1,0:T(8,128)(2,1)}, bf16[2,1024,256]{2,1,0:T(8,128)(2,1)}, bf16[2,128,1280]{2,1,0...) custom-call(bf16[2,128,1280]{2,1,0:T(8,128)(2,1)} %bitcast.36, ...), custom_call_target="tpu_custom_call" | custom-call | flops 70000001024 | bytes 1048576 | tf_op jit(solution)/shard_map/heads_forward/pallas_call | solution.py:2131
  98.2 0.0 copy-done
  98.2 0.2 copy.45
  98.4 0.8 pad.8.router_ref.refs_6_
  99.2 0.0 copy-done.1
  99.2 0.5 pad_bitcast_fusion.owner_ref
  99.7 108.3 %expert_rows.1 = (bf16[2,8,128,1280]{3,2,1,0:T(8,128)(2,1)}, bf16[2,8,128,1280]{3,2,1,0:T(8,128)(2,1)}, bf16[2048,1920]{1,0:T(8,128)(2,1)}, bf16[2048,1920]{1,0:...) custom-call(bf16[2,128,1280]{2,1,0:T(8,128)(2,1)} %get-tuple-element, ...), custom_call_target="tpu_custom_call" | custom-call | flops 99999997952 | bytes 1048576 | tf_op jit(solution)/shard_map/expert_rows/pallas_call | solution.py:1706
  208.0 100.7 %expert_sums.1 = (bf16[2,1280,896]{2,1,0:T(8,128)(2,1)}, bf16[2,1280,896]{2,1,0:T(8,128)(2,1)}, bf16[2,1280,896]{2,1,0:T(8,128)(2,1)}, f32[128,1408]{1,0:T(8,128...) custom-call(bf16[2048,1280]{1,0:T(8,128)(2,1)} %bitcast.38, ...), custom_call_target="tpu_custom_call" | custom-call | flops 60000002048 | bytes 1048576 | tf_op jit(solution)/shard_map/expert_sums/pallas_call | solution.py:1772
  308.7 6.8 %middle_rows.1 = (f32[256,1280]{1,0:T(8,128)}, bf16[256,1280]{1,0:T(8,128)(2,1)}, bf16[256,1280]{1,0:T(8,128)(2,1)}, bf16[1280,128]{1,0:T(8,128)(2,1)}) custom-call(f32[128,1408]{1,0:T(8,128)} %get-tuple-element.71.refs_0_, f32[128,1408]{1,0:T(8,128)} %get-tuple-element.80.refs_1_, bf16[256,128]{1,0:T(8,128)(2,1)} %convert_element_type.5.refs_2_, ...), custom_call_target="tpu_custom_call" | custom-call | flops 5000000000 | bytes 1048576 | tf_op jit(solution)/shard_map/middle_rows/pallas_call | solution.py:2185
  315.6 161.5 %heads_backward.1 = (f32[128,1280]{1,0:T(8,128)}, f32[128,1280]{1,0:T(8,128)}, bf16[160,1280]{1,0:T(8,128)(2,1)}, bf16[160,1280]{1,0:T(8,128)(2,1)}, bf16[160,12...) custom-call(bf16[2,128,1280]{2,1,0:T(8,128)(2,1)} %bitcast.45, ...), custom_call_target="tpu_custom_call" | custom-call | flops 140000002048 | bytes 1048576 | tf_op jit(solution)/shard_map/heads_backward/pallas_call | solution.py:2209
  477.1 1.3 dynamic_slice.3
  478.4 10.6 %last_rows.1 = (bf16[256,1280]{1,0:T(8,128)(2,1)}, f32[160,1280]{1,0:T(8,128)}, f32[160,1280]{1,0:T(8,128)}, f32[160,1280]{1,0:T(8,128)}, f32[160,1280]{1,0:T(8,...) custom-call(bf16[256,1280]{1,0:T(8,128)(2,1)} %bitcast.37, ...), custom_call_target="tpu_custom_call" | custom-call | flops 6000000000 | bytes 1048576 | tf_op jit(solution)/shard_map/last_rows/pallas_call | solution.py:2266
  488.9 1.6 copy.48
  (1 shorter events, 0.0 us)
Async XLA Ops:
  4.3 93.9 %copy-start = (bf16[1280,16]{0,1:T(8,128)(2,1)S(1)}, bf16[1280,16]{0,1:T(8,128)(2,1)}, u32[]{:S(2)}) copy-start(bf16[1280,16]{0,1:T(8,128)(2,1)} %param.29) | copy-start | bytes 122884
  4.3 94.9 %copy-start.1 = (s32[16]{0:T(128)S(1)}, s32[16]{0:T(128)}, u32[]{:S(2)}) copy-start(s32[16]{0:T(128)} %param.22) | copy-start | bytes 196

commit v6 on v5

--- a/solution.py
+++ b/solution.py
@@ -549,6 +549,12 @@
         def _():
             action()
 
+    row_copies = [
+        pltpu.make_async_copy(source.at[m], target.at[m], keep_sem.at[2 + k, m])
+        for m in range(MB)
+        for k, (source, target) in enumerate(((rows, rows_ref), (grads, grads_ref)))
+    ]
+
     def body(step, carry):
         micro_batch = step // blocks
         block = block_order(chip, step % blocks, chips)
@@ -560,6 +566,7 @@
         at(step, 1, gathers[1].start)
         at(step, 2, grad_gather.start)
         at(step, blocks, scatter.start)
+        at(step, blocks, lambda: [copy.start() for copy in row_copies[:2]])
         for m in range(MB):
 
             @pl.when(micro_batch == m)
@@ -576,6 +583,7 @@
                 stage_out(step - 2, k).wait()
             out_copy(step - 2).wait()
 
+        at(step, 2 * blocks - 1, lambda: [copy.start() for copy in row_copies[2:]])
         slot = step % 2
         normed = rows[micro_batch, pl.ds(2 * block, 2)].reshape(size, D)
         grad = grads[micro_batch, pl.ds(2 * block, 2)].reshape(size, D)
@@ -598,7 +606,7 @@
             gate_part = dot(normed, weights[0, :, left:right])
             up_part = dot(normed, weights[1, :, left:right])
             down_part = dot(grad, weights[2, :, left:right])
-            sigmoid = 1.0 / (1.0 + jnp.exp(-gate_part))
+            sigmoid = 0.5 * jnp.tanh(0.5 * gate_part) + 0.5
             act = gate_part * sigmoid
             hidden = act * up_part
             product = hidden * down_part
@@ -647,13 +655,6 @@
 
     lax.fori_loop(0, MB * blocks, body, 0)
     last = MB * blocks
-    row_copies = [
-        pltpu.make_async_copy(rows.at[m], rows_ref.at[m], local_sem.at[m]) for m in range(MB)
-    ] + [
-        pltpu.make_async_copy(grads.at[m], grads_ref.at[m], local_sem.at[2 + m]) for m in range(MB)
-    ]
-    for copy in row_copies:
-        copy.start()
     scatter.finish(back_a_ref)
     for m in range(MB):
         gathers[m].finish(False)
@@ -751,17 +752,14 @@
         lambda device, k: device,
         arrived, summed, held, FF, sems[6:13],
     )
-    results = [
-        Scatter(
-            chips,
-            lambda to, m=m: out_ref.at[m, 2 * to + 1 - core],
-            lambda to, m=m: out_mine.at[m, to],
-            out_pair.at[m], out_line.at[m], sems[13 + 6 * m : 19 + 6 * m],
-        )
-        for m in range(MB)
-    ]
+    results = Scatter(
+        chips,
+        lambda to: out_ref.at[0, 2 * to + 1 - core],
+        lambda to: out_mine.at[to],
+        out_pair, out_line, sems[13:19],
+    )
     routed = [
-        SeqSum(gate_ref.at[e], gate_rows_ref.at[e], e == 0, e, sems[13 + 6 * MB :])
+        SeqSum(gate_ref.at[e], gate_rows_ref.at[e], e == 0, e, sems[19:])
         for e in range(EXP_DEV)
     ]
     targets = [(ref, e) for ref in (gate_ref, up_ref, down_ref) for e in range(EXP_DEV)]
@@ -783,8 +781,10 @@
             pltpu.make_async_copy(source, target, local_sem.at[number, to])
             for to in range(chips)
             for number, (source, target) in enumerate(
-                [(back_ref.at[2 * to + core], mine.at[to])]
-                + [(out_ref.at[m, 2 * to + core], out_mine.at[m, to]) for m in range(MB)]
+                (
+                    (back_ref.at[2 * to + core], mine.at[to]),
+                    (out_ref.at[0, 2 * to + core], out_mine.at[to]),
+                )
             )
         ]
         for load in loads:
@@ -795,21 +795,18 @@
             load.wait()
 
     at(0, begin)
-    for number in range(2, last + 1):
-        at(number, lambda number=number: write(number - 2).wait())
+    for number in range(2, last + 1, 2):
+        at(number, lambda number=number: [write(number - 2).wait(), write(number - 1).wait()])
     at(2, lambda: scatter.slot(0))
-    at(3, routed[0].start)
-    at(5, routed[1].start)
+    at(2, routed[0].start)
+    at(4, routed[1].start)
     at(4, lambda: scatter.slot(1))
     at(6, lambda: scatter.slot(2))
     at(7, spread.middle)
-    at(4, results[0].start)
-    at(5, results[1].start)
-    at(7, lambda: results[0].slot(0))
-    at(8, lambda: results[1].slot(0))
-    at(9, lambda: results[0].slot(1))
-    at(10, lambda: results[1].slot(1))
-    at(11, lambda: results[0].slot(2))
+    at(4, results.start)
+    at(7, lambda: results.slot(0))
+    at(9, lambda: results.slot(1))
+    at(10, lambda: results.slot(2))
     slot = step % 2
 
     @pl.when(matrix < EXP_DEV)
@@ -841,16 +838,13 @@
     @pl.when(step == last)
     def _():
         routed[1].middle()
-        results[1].slot(2)
-        results[0].finish(layer)
-        layer_ref[0] = (layer[...] + hidden_one_ref[0]).astype(BF)
+        results.finish(layer)
+        layer_ref[...] = (layer[...] + hidden_one_ref[...]).astype(BF)
         write(last - 1).wait()
         write(last).wait()
         spread.take()
         for kind, target in enumerate(shared_outs):
             target[...] = spread.of_kind(kind)[...]
-        results[1].finish(layer)
-        layer_ref[1] = (layer[...] + hidden_one_ref[1]).astype(BF)
         for job in routed:
             job.finish()
         spread.finish()
@@ -1365,11 +1359,11 @@
 
 def heads_backward(
     chips, slots,
-    own_ref, qkv_ref, mixed_ref, cos_ref, sin_ref, w_ref, own_mixed_ref, mix_ref, small_ref,
-    normed_ref, up_ref, down_ref,
-    grad_a_ref, grad_b_ref, weight_outs, w_out_out, small_out, up_out, down_out, job_slots,
-    sums_ref, arrived, summed, held, d_mixed, probs, raw, parts, d_keys, d_values, pairs, lines,
-    part, weight_pair, weight_line, result, normed, normed_sem, local_sem, send_sem, recv_sem, *sems,
+    own_ref, qkv_ref, mixed_ref, cos_ref, sin_ref, w_ref, own_mixed_ref, mix_ref, small_ref, hidden_ref,
+    normed_ref, up_ref, down_ref, out_ref,
+    grad_a_ref, grad_b_ref, weight_outs, w_out_out, small_out, layer_ref, up_out, down_out, job_slots,
+    sums_ref, arrived, summed, held, mine, pair, line, layer, d_mixed, probs, raw, parts, d_keys, d_values, pairs, lines,
+    part, weight_pair, weight_line, result, normed, normed_sem, mine_sem, local_sem, send_sem, recv_sem, *sems,
 ):
     devices = 2 * chips
     me = lax.axis_index("exp")
@@ -1394,8 +1388,18 @@
         lambda device, k: slot_head(k, device, devices),
         arrived, summed, held, D, sems[6 * MB + 6 : 6 * MB + 13],
     )
+    results = Scatter(
+        chips,
+        lambda to: out_ref.at[1, 2 * to + 1 - core],
+        lambda to: mine.at[to],
+        pair, line, sems[6 * MB + 13 : 6 * MB + 19],
+    )
+    result_loads = [
+        pltpu.make_async_copy(out_ref.at[1, 2 * to + core], mine.at[to], mine_sem.at[to])
+        for to in range(chips)
+    ]
     routed = [
-        FarSeqSum(source, target, k % 2 == 0, k, job_slots, sems[6 * MB + 13 : -7])
+        FarSeqSum(source, target, k % 2 == 0, k, job_slots, sems[6 * MB + 19 : -7])
         for k, (source, target) in enumerate(
             (ref.at[e], out.at[e])
             for ref, out in ((up_ref, up_out), (down_ref, down_out))
@@ -1475,10 +1479,12 @@
             def _():
                 d_mixed[m, :, slot * HD : (slot + 1) * HD] = jnp.zeros((length, HD), BF)
 
-    routed[0].start()
-    routed[1].start()
+    for job in routed:
+        job.start()
     for number in range(2):
         load(number).start()
+    for copy in result_loads:
+        copy.start()
     for left in range(0, D, 256):
         part[left : left + 256, :D] = dot_tn(
             own_mixed_ref[:, left : left + 256], mix_ref[...]
@@ -1577,27 +1583,33 @@
         if number == 1:
             ticks[0]()
     spread.start()
-    routed[2].start()
-    routed[3].start()
+    results.start()
     ticks[1]()
+    scatters[0].finish(grad_a_ref)
     weight_all.middle()
-    scatters[0].finish(grad_a_ref)
     routed[0].finish()
+    for copy in result_loads:
+        copy.wait()
     ticks[2]()
     routed[1].finish()
     spread.middle()
+    results.slot(0)
+    routed[2].middle()
+    spread.hand_out()
+    routed[3].middle()
+    results.slot(1)
     scatters[1].finish(grad_b_ref)
     weight_all.take()
     w_out_out[...] = weight_all.whole[:, :D]
     small_out[...] = weight_all.whole[:, D:far]
-    spread.hand_out()
-    routed[2].middle()
-    routed[3].middle()
+    results.slot(2)
+    routed[2].finish()
     spread.take()
     for kind, target in enumerate(weight_outs):
         target[...] = spread.of_kind(kind)[...]
-    routed[2].finish()
     routed[3].finish()
+    results.finish(layer)
+    layer_ref[...] = (layer[...] + hidden_ref[...]).astype(BF)
     weight_all.finish()
     spread.finish()
     for m in range(MB):
@@ -1639,9 +1651,9 @@
 
 
 def last_rows(
-    tokens_ref, normed_a_ref, normed_b_ref, grad_hidden_ref, gain_ref, gain_rows_ref, weight_lows, small_ref, layer_ref,
-    far_lows, w_refs,
-    grad_tokens_ref, weight_outs, router_ref, gain_one_ref, gain_two_ref, layer_out, far_outs,
+    tokens_ref, normed_a_ref, normed_b_ref, grad_hidden_ref, gain_ref, gain_rows_ref, weight_lows, small_ref, layer_refs,
+    shared_lows, gate_ref, up_ref, down_ref, w_refs,
+    grad_tokens_ref, weight_outs, router_ref, gain_one_ref, gain_two_ref, layer_out, shared_outs, gate_out, up_out, down_out,
     w_rows, w_sem,
     experts,
 ):
@@ -1652,9 +1664,13 @@
     ]
     for copy in loads:
         copy.start()
-    for low, out in zip(far_lows, far_outs):
+    for low, out in zip(shared_lows, shared_outs):
         out[...] = low[...].astype(F32)
-    layer_out[...] = layer_ref[...]
+    gate_out[...] = gate_ref[...].astype(F32)
+    down_out[...] = down_ref[...].astype(F32)
+    up_out[...] = up_ref[...].astype(F32)
+    for m in range(MB):
+        layer_out[m] = layer_refs[m][...]
     for m, normed_ref in enumerate((normed_a_ref, normed_b_ref)):
         part = slice(m * SEQ_DEV, (m + 1) * SEQ_DEV)
         back, _ = norm_back(tokens_ref[part, :].astype(F32), gain_ref[0:1, :], normed_ref[...])
@@ -1729,7 +1745,7 @@
                 pltpu.SemaphoreType.DMA((3, EXP_DEV + 1)),
                 pltpu.SemaphoreType.DMA((4,)),
                 pltpu.SemaphoreType.DMA((2, 3)),
-                pltpu.SemaphoreType.DMA((2, chips)),
+                pltpu.SemaphoreType.DMA((4, chips)),
             ]
             + [sem for group in sems for sem in group],
             compiler_params=pltpu.CompilerParams(
@@ -1773,7 +1789,7 @@
             kernel,
             grid=(3 * EXP_DEV, 2),
             out_shape=(like(EXP_DEV, D, FF),) * 3
-            + (like(SEQ_DEV, D + LANES, dtype=F32), like(MB, SEQ_DEV, D))
+            + (like(SEQ_DEV, D + LANES, dtype=F32), like(SEQ_DEV, D))
             + (like(D // devices, FF),) * 3
             + (like(EXP_DEV, D // 4, FF),),
             in_specs=[by_rows, by_grads]
@@ -1781,20 +1797,20 @@
             + [pl.BlockSpec((flat, FF), use) for use in (for_gate, for_up)]
             + [last] * 3
             + [ANYWHERE] * 2
-            + [pl.BlockSpec((MB, SEQ_DEV, D), lambda k, d: (0, 0, 0), pipeline_mode=pl.Buffered(1))],
+            + [pl.BlockSpec((SEQ_DEV, D), lambda k, d: (0, 0), pipeline_mode=pl.Buffered(1))],
             out_specs=(ANYWHERE,) * 3
-            + (whole(SEQ_DEV, D + LANES), whole(MB, SEQ_DEV, D))
+            + (whole(SEQ_DEV, D + LANES), whole(SEQ_DEV, D))
             + (whole(D // devices, FF),) * 3
             + (ANYWHERE,),
             scratch_shapes=[
                 pltpu.VMEM((chips, SEQ_DEV, D + LANES), BF),
                 pltpu.VMEM((chips, SEQ_DEV, D + LANES), BF),
                 pltpu.VMEM((chips + 1, SEQ_DEV, D + LANES), BF),
-                pltpu.VMEM((MB, chips, SEQ_DEV, D), BF),
-                pltpu.VMEM((MB, chips, SEQ_DEV, D), BF),
-                pltpu.VMEM((MB, chips + 1, SEQ_DEV, D), BF),
+                pltpu.VMEM((chips, SEQ_DEV, D), BF),
+                pltpu.VMEM((chips, SEQ_DEV, D), BF),
+                pltpu.VMEM((chips + 1, SEQ_DEV, D), BF),
                 pltpu.VMEM((SEQ_DEV, D), F32),
-                pltpu.SemaphoreType.DMA((1 + MB, chips)),
+                pltpu.SemaphoreType.DMA((2, chips)),
                 pltpu.VMEM((2, half, FF), BF),
                 pltpu.SemaphoreType.DMA((2,)),
                 pltpu.VMEM((3, D, HD), BF),
@@ -1804,7 +1820,7 @@
             ]
             + scatter_sems(chips)
             + spread_sems(devices, 4, 1)
-            + scatter_sems(chips) * MB
+            + scatter_sems(chips)
             + seq_scratch(2),
             compiler_params=pltpu.CompilerParams(
                 collective_id=2, has_side_effects=True, vmem_limit_bytes=VMEM_BYTES
@@ -1813,13 +1829,14 @@
             name="expert_sums",
         )(*operands)
 
-    gate_sum, up_sum, down_sum, back_sum_b, layer_out, *shared_grads, gate_rows = call_sums(
+    gate_sum, up_sum, down_sum, back_sum_b, layer_a, *shared_grads, gate_rows = call_sums(
         rows.reshape(flat, D), grads.reshape(flat, D), hidden, d_gate, d_up, hidden, d_gate, d_up, back_b,
-        out_parts, hidden_one,
+        out_parts, hidden_one[0],
     )
     backs = (back_sum_a, back_sum_b)
     return (
-        layer_out,
+        layer_a,
+        out_parts,
         backs,
         gate_rows,
         (gate_sum, up_sum, down_sum),
@@ -2166,7 +2183,7 @@
     own_mixed, hidden_one = own_mixed.reshape(own, D), hidden_one.reshape(own, D)
     two_low = two_low.reshape(own, D)
 
-    layer_out, backs, gate_full, routed_sums, shared_lows = experts_on_lines(
+    layer_a, out_parts, backs, gate_full, routed_sums, shared_lows = experts_on_lines(
         two_low.reshape(MB, SEQ_DEV, D),
         hidden_rows,
         grad_own,
@@ -2202,24 +2219,27 @@
 
     def backward_kernel(*refs):
         heads_backward(
-            chips, slots, *refs[:14], refs[14:17], *refs[17:21], refs[21:24], *refs[24:29],
-            refs[29 : 29 + length // BLOCK], *refs[29 + length // BLOCK :],
+            chips, slots, *refs[:16], refs[16:19], *refs[19:24], refs[24:27], *refs[27:36],
+            refs[36 : 36 + length // BLOCK], *refs[36 + length // BLOCK :],
         )
 
     normed_a, normed_b, *backward_out = pl.pallas_call(
         backward_kernel,
         out_shape=(like(SEQ_DEV, D, dtype=F32),) * 2
         + (like(rows_out, D),) * 4
-        + (like(rows_out, LANES),)
-        + (quarter,) * 2
+        + (like(rows_out, LANES), like(SEQ_DEV, D), quarter, quarter)
         + (like(*slot_shape), like(*slot_shape), like(jobs, D // groups, FF)),
-        in_specs=[IN_VMEM] * 9 + [ANYWHERE] * 3,
-        out_specs=(IN_VMEM,) * 7 + (ANYWHERE,) * 5,
+        in_specs=[IN_VMEM] * 10 + [ANYWHERE] * 4,
+        out_specs=(IN_VMEM,) * 8 + (ANYWHERE,) * 5,
         scratch_shapes=[
             pltpu.VMEM((3 * slots, D, HD), BF),
             pltpu.VMEM((groups - 1, slots, D, HD), BF),
             pltpu.VMEM((slots, D, HD), BF),
             pltpu.VMEM((groups, rows_out, D), BF),
+            pltpu.VMEM((chips, SEQ_DEV, D), BF),
+            pltpu.VMEM((chips, SEQ_DEV, D), BF),
+            pltpu.VMEM((chips + 1, SEQ_DEV, D), BF),
+            pltpu.VMEM((SEQ_DEV, D), F32),
             pltpu.VMEM((MB, length, wide), BF),
         ]
         + [pltpu.VMEM((slots, BLOCK, stop), BF) for stop in range(BLOCK, length + 1, BLOCK)]
@@ -2236,12 +2256,14 @@
             pltpu.VMEM((rows_out, far), F32),
             pltpu.VMEM((2, MB, length, 256), BF),
             pltpu.SemaphoreType.DMA((2,)),
+            pltpu.SemaphoreType.DMA((chips,)),
             pltpu.SemaphoreType.DMA((MB, slots)),
             pltpu.SemaphoreType.DMA((MB, devices, slots)),
             pltpu.SemaphoreType.DMA((MB, devices, slots)),
         ]
         + scatter_sems(chips) * (MB + 1)
         + spread_sems(devices, groups, slots)
+        + scatter_sems(chips)
         + far_sum_scratch(jobs)
         + seq_all_scratch(rows_out, (far + LANES) // groups),
         compiler_params=pltpu.CompilerParams(
@@ -2251,15 +2273,15 @@
         name="heads_backward",
     )(
         d_mixed.reshape(MB, SEQ_DEV, D), qkv, mixed, cos_table, sin_table, w_qkv, own_mixed,
-        grad_mix, small, normed, *routed_sums[1:],
+        grad_mix, small, hidden_rows[1], normed, *routed_sums[1:], out_parts,
     )
     gain_rows = lax.dynamic_slice(gain_one, (me * rows_out,), (rows_out,))[None]
 
     def call_last(*operands):
         def kernel(*refs):
             last_rows(
-                *refs[:6], refs[6:10], *refs[10:12], refs[12:18], refs[18:21], refs[21], refs[22:26],
-                *refs[26:30], refs[30:36], *refs[36:], experts,
+                *refs[:6], refs[6:10], refs[10], refs[11:13], refs[13:16], *refs[16:19],
+                refs[19:22], refs[22], refs[23:27], *refs[27:31], refs[31:34], *refs[34:], experts,
             )
 
         full = like(EXP_DEV, D // groups, FF, dtype=F32)
@@ -2272,7 +2294,7 @@
             + (like(MB, SEQ_DEV, D),)
             + (like(rows_out, FF, dtype=F32),) * 3
             + (full,) * 3,
-            in_specs=[IN_VMEM] * 18 + [ANYWHERE] * 3,
+            in_specs=[IN_VMEM] * 19 + [ANYWHERE] * 3,
             out_specs=(IN_VMEM,) * 15,
             scratch_shapes=[pltpu.VMEM((3, rows_out, D), BF), pltpu.SemaphoreType.DMA((3,))],
             compiler_params=pltpu.CompilerParams(vmem_limit_bytes=VMEM_BYTES),
@@ -2282,7 +2304,7 @@
 
     last_out = call_last(
         tokens.reshape(own, D), normed_a, normed_b, grad_hidden, gains, gain_rows,
-        *backward_out[:5], layer_out, *shared_lows, gate_full, *backward_out[5:7],
+        *backward_out[:5], layer_a, backward_out[5], *shared_lows, gate_full, *backward_out[6:8],
         w_query, w_key, w_value,
     )
     grad_tokens, attn, router_grad = last_out[0], last_out[1:5], last_out[5]

time: 499 us -> 476 us (0.954)
  the two profiles are of different devices: /device:TPU:12 before, /device:TPU:0 now
where the time goes in v6:
time: 476 us; the launch traced here: 468 us
  Pallas kernels  458 us (96%)
  local copies, waits for them, and re-layouts  7.66 us (2%)
    pallas_call x1, Pallas kernels, on_device_lines(): pl.pallas_call(backward_kernel, out_shape=(like(SEQ_DEV, D, dtype=F32),)...  148 us
    pallas_call x1, Pallas kernels, call_rows(): pl.pallas_call(kernel, out_shape=(like(MB, devices, SEQ_DEV, D), like(MB,...  102 us
    pallas_call x1, Pallas kernels, call_forward(): pl.pallas_call(kernel, out_shape=(like(MB, length, D), like(MB, length, 3...  100 us
    pallas_call x1, Pallas kernels, call_sums(): pl.pallas_call(kernel, grid=(3 * EXP_DEV, 2), out_shape=(like(EXP_DEV, D,...  90.6 us
    pallas_call x1, Pallas kernels, call_last(): pl.pallas_call(kernel, out_shape=(like(own, D),) + (like(rows_out, D, dty...  10.6 us

profile of v6, /device:TPU:0, one launch (start us, length us, event | category | flops | bytes accessed | tf_op | source)
XLA Modules:
  0.0 468.3 jit_solution(16512559166313126218)
XLA Ops:
  0.6 0.7 copy.53
  1.3 0.3 fusion
  1.7 0.6 convert_element_type.5.refs_2_
  2.3 0.7 stack.10
  3.0 0.7 stack.9
  3.7 0.6 pad_maximum_fusion.refs_3_.refs_7_.refs_4_
  4.3 0.0 copy-start.1
  4.3 0.0 copy-start.2
  4.3 100.3 %heads_forward.1 = (bf16[2,1024,1280]{2,1,0:T(8,128)(2,1)}, bf16[2,1024,768]{2,1,0:T(8,128)(2,1)}, bf16[2,1024,256]{2,1,0:T(8,128)(2,1)}, bf16[2,128,1280]{2,1,0...) custom-call(bf16[2,128,1280]{2,1,0:T(8,128)(2,1)} %bitcast.41, ...), custom_call_target="tpu_custom_call" | custom-call | flops 70000001024 | bytes 1048576 | tf_op jit(solution)/shard_map/heads_forward/pallas_call | solution.py:2148
  104.6 0.0 copy-done.1
  104.6 0.2 copy.45
  104.9 0.8 pad.8.router_ref.refs_6_
  105.7 0.0 copy-done.2
  105.7 0.5 pad_bitcast_fusion.owner_ref
  106.2 0.0 copy-start
  106.2 101.7 %expert_rows.1 = (bf16[2,8,128,1280]{3,2,1,0:T(8,128)(2,1)}, bf16[2,8,128,1280]{3,2,1,0:T(8,128)(2,1)}, bf16[2048,1920]{1,0:T(8,128)(2,1)}, bf16[2048,1920]{1,0:...) custom-call(bf16[2,128,1280]{2,1,0:T(8,128)(2,1)} %get-tuple-element, ...), custom_call_target="tpu_custom_call" | custom-call | flops 99999997952 | bytes 1048576 | tf_op jit(solution)/shard_map/expert_rows/pallas_call | solution.py:1722
  207.9 0.0 copy-done
  207.9 1.1 slice_bitcast_fusion
  209.0 90.6 %expert_sums.1 = (bf16[2,1280,896]{2,1,0:T(8,128)(2,1)}, bf16[2,1280,896]{2,1,0:T(8,128)(2,1)}, bf16[2,1280,896]{2,1,0:T(8,128)(2,1)}, f32[128,1408]{1,0:T(8,128...) custom-call(bf16[2048,1280]{1,0:T(8,128)(2,1)} %bitcast.43, ...), custom_call_target="tpu_custom_call" | custom-call | flops 60000002048 | bytes 1048576 | tf_op jit(solution)/shard_map/expert_sums/pallas_call | solution.py:1788
  299.6 6.8 %middle_rows.1 = (f32[256,1280]{1,0:T(8,128)}, bf16[256,1280]{1,0:T(8,128)(2,1)}, bf16[256,1280]{1,0:T(8,128)(2,1)}, bf16[1280,128]{1,0:T(8,128)(2,1)}) custom-call(f32[128,1408]{1,0:T(8,128)} %get-tuple-element.72.refs_0_, f32[128,1408]{1,0:T(8,128)} %get-tuple-element.81.refs_1_, bf16[256,128]{1,0:T(8,128)(2,1)} %convert_element_type.5.refs_2_, ...), custom_call_target="tpu_custom_call" | custom-call | flops 5000000000 | bytes 1048576 | tf_op jit(solution)/shard_map/middle_rows/pallas_call | solution.py:2202
  306.5 147.9 %heads_backward.1 = (f32[128,1280]{1,0:T(8,128)}, f32[128,1280]{1,0:T(8,128)}, bf16[160,1280]{1,0:T(8,128)(2,1)}, bf16[160,1280]{1,0:T(8,128)(2,1)}, bf16[160,12...) custom-call(bf16[2,128,1280]{2,1,0:T(8,128)(2,1)} %bitcast.49, ...), custom_call_target="tpu_custom_call" | custom-call | flops 140000002048 | bytes 1048576 | tf_op jit(solution)/shard_map/heads_backward/pallas_call | solution.py:2226
  454.4 1.3 dynamic_slice.3
  455.7 10.6 %last_rows.1 = (bf16[256,1280]{1,0:T(8,128)(2,1)}, f32[160,1280]{1,0:T(8,128)}, f32[160,1280]{1,0:T(8,128)}, f32[160,1280]{1,0:T(8,128)}, f32[160,1280]{1,0:T(8,...) custom-call(bf16[256,1280]{1,0:T(8,128)(2,1)} %bitcast.42, ...), custom_call_target="tpu_custom_call" | custom-call | flops 6000000000 | bytes 1048576 | tf_op jit(solution)/shard_map/last_rows/pallas_call | solution.py:2288
  466.3 1.6 copy.48
  (1 shorter events, 0.0 us)
Async XLA Ops:
  4.3 100.3 %copy-start.1 = (bf16[1280,16]{0,1:T(8,128)(2,1)S(1)}, bf16[1280,16]{0,1:T(8,128)(2,1)}, u32[]{:S(2)}) copy-start(bf16[1280,16]{0,1:T(8,128)(2,1)} %param.29) | copy-start | bytes 122884
  4.3 101.3 %copy-start.2 = (s32[16]{0:T(128)S(1)}, s32[16]{0:T(128)}, u32[]{:S(2)}) copy-start(s32[16]{0:T(128)} %param.22) | copy-start | bytes 196
  106.2 101.7 %copy-start = (f32[2,128,1280]{2,1,0:T(8,128)S(1)}, f32[2,128,1280]{2,1,0:T(8,128)}, u32[]{:S(2)}) copy-start(f32[2,128,1280]{2,1,0:T(8,128)} %get-tuple-element.80) | copy-start | bytes 3932164

commit v7 on v6

--- a/solution.py
+++ b/solution.py
@@ -1277,13 +1277,12 @@
         for turn_ in range(chips):
             block = block_order(chip, turn_, chips)
             for number in range(MB):
-                if turn_ > 0:
+                if turn_ > number:
                     at(number, lambda number=number: gathers[number].hop(turn_))
                 at(number, lambda number=number: gathers[number].take_pair(block - chip))
             if turn_ == chips - 2:
                 at(0, gathers[1].start)
                 at(1, later[0].start)
-            if turn_ == chips - 1:
                 at(1, later[1].start)
             part = pl.ds(pl.multiple_of(block * size, size), size)
             tokens = rows[m, pl.ds(2 * block, 2)].reshape(size, D).astype(F32)
@@ -1315,7 +1314,11 @@
                         give(number, away, slot).start()
                     keep_own(number, slot).start()
 
-            at(1, lambda: later[slot].hop(1)) if slot < 2 else None
+            if slot == 0:
+                at(0, lambda: gathers[1].hop(1))
+                at(1, lambda: [gather.hop(1) for gather in later])
+            else:
+                at(1, lambda: [gather.hop(2) for gather in later])
         return carry
 
     lax.fori_loop(0, MB, body, 0)
@@ -1338,12 +1341,10 @@
         two_ref[m] = norm_rows(hidden, gain_ref[1:2, :]).astype(BF)
 
     finish_rows(0)
-    for hop in range(2, chips):
-        later[0].hop(hop)
-    later[1].hop(2)
     finish_rows(1)
     for hop in range(3, chips):
-        later[1].hop(hop)
+        for gather in later:
+            gather.hop(hop)
     for gather in gathers:
         gather.finish(False)
     for gather in later:
@@ -1521,9 +1522,7 @@
         @pl.when(m == 1)
         def _():
             scatters[0].start()
-            for turn_ in range(min(slots, chips - 1), chips - 1):
-                weight.slot(turn_)
-            routed[0].middle()
+            weight.slot(0)
 
         for slot in range(slots):
             base = 3 * HD * slot
@@ -1550,17 +1549,9 @@
             @pl.when(m == 1)
             def _():
                 scatters[0].slot(min(slot, chips - 2))
-                if slot == 0:
+                if slot == 1:
+                    routed[0].middle()
                     routed[1].middle()
-                else:
-                    weight.finish(result)
-                    weight_all.low[:, :far] = result[...].astype(BF)
-                    weight_all.low[:, far:] = jnp.zeros((rows, LANES), BF)
-                    weight_all.start()
-
-            @pl.when(m == 0)
-            def _():
-                weight.slot(min(slot, chips - 2))
 
         for start in range(0, length, step):
             back = dot_nt(raw[m, start : start + step, :], w_ref[...]).astype(BF)
@@ -1584,30 +1575,36 @@
             ticks[0]()
     spread.start()
     results.start()
+    for turn_ in range(1, chips - 1):
+        weight.slot(turn_)
+    weight.finish(result)
+    weight_all.low[:, :far] = result[...].astype(BF)
+    weight_all.low[:, far:] = jnp.zeros((rows, LANES), BF)
+    weight_all.start()
+    scatters[0].finish(grad_a_ref)
+    routed[2].middle()
+    routed[3].middle()
+    spread.middle()
     ticks[1]()
-    scatters[0].finish(grad_a_ref)
     weight_all.middle()
-    routed[0].finish()
     for copy in result_loads:
         copy.wait()
     ticks[2]()
+    results.slot(0)
+    spread.hand_out()
+    routed[0].finish()
     routed[1].finish()
-    spread.middle()
-    results.slot(0)
-    routed[2].middle()
-    spread.hand_out()
-    routed[3].middle()
     results.slot(1)
     scatters[1].finish(grad_b_ref)
+    results.slot(2)
+    routed[2].finish()
+    routed[3].finish()
     weight_all.take()
     w_out_out[...] = weight_all.whole[:, :D]
     small_out[...] = weight_all.whole[:, D:far]
-    results.slot(2)
-    routed[2].finish()
     spread.take()
     for kind, target in enumerate(weight_outs):
         target[...] = spread.of_kind(kind)[...]
-    routed[3].finish()
     results.finish(layer)
     layer_ref[...] = (layer[...] + hidden_ref[...]).astype(BF)
     weight_all.finish()

time: 476 us -> 467 us (0.981)
  Pallas kernels: 458 us -> 448 us
    pallas_call x1, Pallas kernels: 148 us -> 141 us  [on_device_lines(): pl.pallas_call(backward_kernel, out_shape=(like(SEQ_DEV, D, dtype=F32),)...]
where the time goes in v7:
time: 467 us; the launch traced here: 459 us
  Pallas kernels  448 us (96%)
  local copies, waits for them, and re-layouts  7.66 us (2%)
    pallas_call x1, Pallas kernels, on_device_lines(): pl.pallas_call(backward_kernel, out_shape=(like(SEQ_DEV, D, dtype=F32),)...  141 us
    pallas_call x1, Pallas kernels, call_forward(): pl.pallas_call(kernel, out_shape=(like(MB, length, D), like(MB, length, 3...  101 us
    pallas_call x1, Pallas kernels, call_rows(): pl.pallas_call(kernel, out_shape=(like(MB, devices, SEQ_DEV, D), like(MB,...  100 us
    pallas_call x1, Pallas kernels, call_sums(): pl.pallas_call(kernel, grid=(3 * EXP_DEV, 2), out_shape=(like(EXP_DEV, D,...  89.2 us
    pallas_call x1, Pallas kernels, call_last(): pl.pallas_call(kernel, out_shape=(like(own, D),) + (like(rows_out, D, dty...  10.6 us

profile of v7, /device:TPU:0, one launch (start us, length us, event | category | flops | bytes accessed | tf_op | source)
XLA Modules:
  0.0 458.6 jit_solution(4464793367652894603)
XLA Ops:
  0.6 0.7 copy.53
  1.3 0.3 fusion
  1.7 0.6 convert_element_type.5.refs_2_
  2.3 0.7 stack.10
  3.0 0.7 stack.9
  3.7 0.6 pad_maximum_fusion.refs_3_.refs_7_.refs_4_
  4.3 0.0 copy-start.1
  4.3 0.0 copy-start.2
  4.3 100.6 %heads_forward.1 = (bf16[2,1024,1280]{2,1,0:T(8,128)(2,1)}, bf16[2,1024,768]{2,1,0:T(8,128)(2,1)}, bf16[2,1024,256]{2,1,0:T(8,128)(2,1)}, bf16[2,128,1280]{2,1,0...) custom-call(bf16[2,128,1280]{2,1,0:T(8,128)(2,1)} %bitcast.41, ...), custom_call_target="tpu_custom_call" | custom-call | flops 70000001024 | bytes 1048576 | tf_op jit(solution)/shard_map/heads_forward/pallas_call | solution.py:2145
  104.9 0.0 copy-done.1
  104.9 0.2 copy.45
  105.2 0.8 pad.8.router_ref.refs_6_
  106.0 0.0 copy-done.2
  106.0 0.5 pad_bitcast_fusion.owner_ref
  106.5 0.0 copy-start
  106.5 100.2 %expert_rows.1 = (bf16[2,8,128,1280]{3,2,1,0:T(8,128)(2,1)}, bf16[2,8,128,1280]{3,2,1,0:T(8,128)(2,1)}, bf16[2048,1920]{1,0:T(8,128)(2,1)}, bf16[2048,1920]{1,0:...) custom-call(bf16[2,128,1280]{2,1,0:T(8,128)(2,1)} %get-tuple-element, ...), custom_call_target="tpu_custom_call" | custom-call | flops 99999997952 | bytes 1048576 | tf_op jit(solution)/shard_map/expert_rows/pallas_call | solution.py:1719
  206.7 0.0 copy-done
  206.7 1.1 slice_bitcast_fusion
  207.9 89.2 %expert_sums.1 = (bf16[2,1280,896]{2,1,0:T(8,128)(2,1)}, bf16[2,1280,896]{2,1,0:T(8,128)(2,1)}, bf16[2,1280,896]{2,1,0:T(8,128)(2,1)}, f32[128,1408]{1,0:T(8,128...) custom-call(bf16[2048,1280]{1,0:T(8,128)(2,1)} %bitcast.43, ...), custom_call_target="tpu_custom_call" | custom-call | flops 60000002048 | bytes 1048576 | tf_op jit(solution)/shard_map/expert_sums/pallas_call | solution.py:1785
  297.1 6.8 %middle_rows.1 = (f32[256,1280]{1,0:T(8,128)}, bf16[256,1280]{1,0:T(8,128)(2,1)}, bf16[256,1280]{1,0:T(8,128)(2,1)}, bf16[1280,128]{1,0:T(8,128)(2,1)}) custom-call(f32[128,1408]{1,0:T(8,128)} %get-tuple-element.72.refs_0_, f32[128,1408]{1,0:T(8,128)} %get-tuple-element.81.refs_1_, bf16[256,128]{1,0:T(8,128)(2,1)} %convert_element_type.5.refs_2_, ...), custom_call_target="tpu_custom_call" | custom-call | flops 5000000000 | bytes 1048576 | tf_op jit(solution)/shard_map/middle_rows/pallas_call | solution.py:2199
  303.9 140.8 %heads_backward.1 = (f32[128,1280]{1,0:T(8,128)}, f32[128,1280]{1,0:T(8,128)}, bf16[160,1280]{1,0:T(8,128)(2,1)}, bf16[160,1280]{1,0:T(8,128)(2,1)}, bf16[160,12...) custom-call(bf16[2,128,1280]{2,1,0:T(8,128)(2,1)} %bitcast.49, ...), custom_call_target="tpu_custom_call" | custom-call | flops 140000002048 | bytes 1048576 | tf_op jit(solution)/shard_map/heads_backward/pallas_call | solution.py:2223
  444.7 1.3 dynamic_slice.3
  446.0 10.6 %last_rows.1 = (bf16[256,1280]{1,0:T(8,128)(2,1)}, f32[160,1280]{1,0:T(8,128)}, f32[160,1280]{1,0:T(8,128)}, f32[160,1280]{1,0:T(8,128)}, f32[160,1280]{1,0:T(8,...) custom-call(bf16[256,1280]{1,0:T(8,128)(2,1)} %bitcast.42, ...), custom_call_target="tpu_custom_call" | custom-call | flops 6000000000 | bytes 1048576 | tf_op jit(solution)/shard_map/last_rows/pallas_call | solution.py:2285
  456.6 1.6 copy.48
  (1 shorter events, 0.0 us)
Async XLA Ops:
  4.3 100.6 %copy-start.1 = (bf16[1280,16]{0,1:T(8,128)(2,1)S(1)}, bf16[1280,16]{0,1:T(8,128)(2,1)}, u32[]{:S(2)}) copy-start(bf16[1280,16]{0,1:T(8,128)(2,1)} %param.29) | copy-start | bytes 122884
  4.3 101.6 %copy-start.2 = (s32[16]{0:T(128)S(1)}, s32[16]{0:T(128)}, u32[]{:S(2)}) copy-start(s32[16]{0:T(128)} %param.22) | copy-start | bytes 196
  106.5 100.3 %copy-start = (f32[2,128,1280]{2,1,0:T(8,128)S(1)}, f32[2,128,1280]{2,1,0:T(8,128)}, u32[]{:S(2)}) copy-start(f32[2,128,1280]{2,1,0:T(8,128)} %get-tuple-element.80) | copy-start | bytes 3932164

commit v8 on v7

--- a/solution.py
+++ b/solution.py
@@ -1280,8 +1280,9 @@
                 if turn_ > number:
                     at(number, lambda number=number: gathers[number].hop(turn_))
                 at(number, lambda number=number: gathers[number].take_pair(block - chip))
+            if turn_ == 1:
+                at(0, gathers[1].start)
             if turn_ == chips - 2:
-                at(0, gathers[1].start)
                 at(1, later[0].start)
                 at(1, later[1].start)
             part = pl.ds(pl.multiple_of(block * size, size), size)
@@ -1582,9 +1583,9 @@
     weight_all.low[:, far:] = jnp.zeros((rows, LANES), BF)
     weight_all.start()
     scatters[0].finish(grad_a_ref)
+    spread.middle()
     routed[2].middle()
     routed[3].middle()
-    spread.middle()
     ticks[1]()
     weight_all.middle()
     for copy in result_loads:
@@ -1654,6 +1655,25 @@
     w_rows, w_sem,
     experts,
 ):
+    gate_out[...] = gate_ref[...].astype(F32)
+    up_out[...] = up_ref[...].astype(F32)
+    down_out[...] = down_ref[...].astype(F32)
+
+    @pl.when(pl.program_id(0) == 0)
+    def _():
+        small_outputs(
+            tokens_ref, normed_a_ref, normed_b_ref, grad_hidden_ref, gain_ref, gain_rows_ref, weight_lows, small_ref,
+            layer_refs, shared_lows, w_refs, grad_tokens_ref, weight_outs, router_ref, gain_one_ref, gain_two_ref,
+            layer_out, shared_outs, w_rows, w_sem, experts,
+        )
+
+
+def small_outputs(
+    tokens_ref, normed_a_ref, normed_b_ref, grad_hidden_ref, gain_ref, gain_rows_ref, weight_lows, small_ref, layer_refs,
+    shared_lows, w_refs, grad_tokens_ref, weight_outs, router_ref, gain_one_ref, gain_two_ref, layer_out, shared_outs,
+    w_rows, w_sem,
+    experts,
+):
     rows = D // lax.axis_size("exp")
     start = pl.ds(pl.multiple_of(lax.axis_index("exp") * rows, 32), rows)
     loads = [
@@ -1663,9 +1683,6 @@
         copy.start()
     for low, out in zip(shared_lows, shared_outs):
         out[...] = low[...].astype(F32)
-    gate_out[...] = gate_ref[...].astype(F32)
-    down_out[...] = down_ref[...].astype(F32)
-    up_out[...] = up_ref[...].astype(F32)
     for m in range(MB):
         layer_out[m] = layer_refs[m][...]
     for m, normed_ref in enumerate((normed_a_ref, normed_b_ref)):
@@ -2282,6 +2299,7 @@
             )
 
         full = like(EXP_DEV, D // groups, FF, dtype=F32)
+        by_expert = pl.BlockSpec((1, D // groups, FF), lambda e: (e, 0, 0))
         return pl.pallas_call(
             kernel,
             out_shape=(like(own, D),)
@@ -2291,8 +2309,9 @@
             + (like(MB, SEQ_DEV, D),)
             + (like(rows_out, FF, dtype=F32),) * 3
             + (full,) * 3,
-            in_specs=[IN_VMEM] * 19 + [ANYWHERE] * 3,
-            out_specs=(IN_VMEM,) * 15,
+            grid=(EXP_DEV,),
+            in_specs=[IN_VMEM] * 16 + [by_expert] * 3 + [ANYWHERE] * 3,
+            out_specs=(IN_VMEM,) * 12 + (by_expert,) * 3,
             scratch_shapes=[pltpu.VMEM((3, rows_out, D), BF), pltpu.SemaphoreType.DMA((3,))],
             compiler_params=pltpu.CompilerParams(vmem_limit_bytes=VMEM_BYTES),
             cost_estimate=taking(6),

time: 467 us -> 462 us (0.989)
  the two profiles are of different devices: /device:TPU:0 before, /device:TPU:12 now
where the time goes in v8:
time: 462 us; the launch traced here: 454 us
  Pallas kernels  443 us (96%)
  local copies, waits for them, and re-layouts  7.66 us (2%)
    pallas_call x1, Pallas kernels, on_device_lines(): pl.pallas_call(backward_kernel, out_shape=(like(SEQ_DEV, D, dtype=F32),)...  135 us
    pallas_call x1, Pallas kernels, call_rows(): pl.pallas_call(kernel, out_shape=(like(MB, devices, SEQ_DEV, D), like(MB,...  102 us
    pallas_call x1, Pallas kernels, call_sums(): pl.pallas_call(kernel, grid=(3 * EXP_DEV, 2), out_shape=(like(EXP_DEV, D,...  95 us
    pallas_call x1, Pallas kernels, call_forward(): pl.pallas_call(kernel, out_shape=(like(MB, length, D), like(MB, length, 3...  93.8 us
    pallas_call x1, Pallas kernels, call_last(): pl.pallas_call(kernel, out_shape=(like(own, D),) + (like(rows_out, D, dty...  10.5 us

profile of v8, /device:TPU:12, one launch (start us, length us, event | category | flops | bytes accessed | tf_op | source)
XLA Modules:
  0.0 453.5 jit_solution(9947004140316084471)
XLA Ops:
  0.6 0.7 copy.53
  1.3 0.3 fusion
  1.7 0.6 convert_element_type.5.refs_2_
  2.3 0.7 stack.10
  3.0 0.7 stack.9
  3.7 0.6 pad_maximum_fusion.refs_3_.refs_7_.refs_4_
  4.3 0.0 copy-start.1
  4.3 0.0 copy-start.2
  4.3 93.8 %heads_forward.1 = (bf16[2,1024,1280]{2,1,0:T(8,128)(2,1)}, bf16[2,1024,768]{2,1,0:T(8,128)(2,1)}, bf16[2,1024,256]{2,1,0:T(8,128)(2,1)}, bf16[2,128,1280]{2,1,0...) custom-call(bf16[2,128,1280]{2,1,0:T(8,128)(2,1)} %bitcast.41, ...), custom_call_target="tpu_custom_call" | custom-call | flops 70000001024 | bytes 1048576 | tf_op jit(solution)/shard_map/heads_forward/pallas_call | solution.py:2162
  98.2 0.0 copy-done.1
  98.2 0.2 copy.45
  98.4 0.8 pad.8.router_ref.refs_6_
  99.2 0.0 copy-done.2
  99.2 0.5 pad_bitcast_fusion.owner_ref
  99.7 0.0 copy-start
  99.7 101.8 %expert_rows.1 = (bf16[2,8,128,1280]{3,2,1,0:T(8,128)(2,1)}, bf16[2,8,128,1280]{3,2,1,0:T(8,128)(2,1)}, bf16[2048,1920]{1,0:T(8,128)(2,1)}, bf16[2048,1920]{1,0:...) custom-call(bf16[2,128,1280]{2,1,0:T(8,128)(2,1)} %get-tuple-element, ...), custom_call_target="tpu_custom_call" | custom-call | flops 99999997952 | bytes 1048576 | tf_op jit(solution)/shard_map/expert_rows/pallas_call | solution.py:1736
  201.5 0.0 copy-done
  201.5 1.1 slice_bitcast_fusion
  202.6 95.0 %expert_sums.1 = (bf16[2,1280,896]{2,1,0:T(8,128)(2,1)}, bf16[2,1280,896]{2,1,0:T(8,128)(2,1)}, bf16[2,1280,896]{2,1,0:T(8,128)(2,1)}, f32[128,1408]{1,0:T(8,128...) custom-call(bf16[2048,1280]{1,0:T(8,128)(2,1)} %bitcast.43, ...), custom_call_target="tpu_custom_call" | custom-call | flops 60000002048 | bytes 1048576 | tf_op jit(solution)/shard_map/expert_sums/pallas_call | solution.py:1802
  297.6 6.8 %middle_rows.1 = (f32[256,1280]{1,0:T(8,128)}, bf16[256,1280]{1,0:T(8,128)(2,1)}, bf16[256,1280]{1,0:T(8,128)(2,1)}, bf16[1280,128]{1,0:T(8,128)(2,1)}) custom-call(f32[128,1408]{1,0:T(8,128)} %get-tuple-element.72.refs_0_, f32[128,1408]{1,0:T(8,128)} %get-tuple-element.81.refs_1_, bf16[256,128]{1,0:T(8,128)(2,1)} %convert_element_type.5.refs_2_, ...), custom_call_target="tpu_custom_call" | custom-call | flops 5000000000 | bytes 1048576 | tf_op jit(solution)/shard_map/middle_rows/pallas_call | solution.py:2216
  304.5 135.2 %heads_backward.1 = (f32[128,1280]{1,0:T(8,128)}, f32[128,1280]{1,0:T(8,128)}, bf16[160,1280]{1,0:T(8,128)(2,1)}, bf16[160,1280]{1,0:T(8,128)(2,1)}, bf16[160,12...) custom-call(bf16[2,128,1280]{2,1,0:T(8,128)(2,1)} %bitcast.49, ...), custom_call_target="tpu_custom_call" | custom-call | flops 140000002048 | bytes 1048576 | tf_op jit(solution)/shard_map/heads_backward/pallas_call | solution.py:2240
  439.7 1.3 dynamic_slice.3
  441.0 10.5 %last_rows.1 = (bf16[256,1280]{1,0:T(8,128)(2,1)}, f32[160,1280]{1,0:T(8,128)}, f32[160,1280]{1,0:T(8,128)}, f32[160,1280]{1,0:T(8,128)}, f32[160,1280]{1,0:T(8,...) custom-call(bf16[256,1280]{1,0:T(8,128)(2,1)} %bitcast.42, ...), custom_call_target="tpu_custom_call" | custom-call | flops 6000000000 | bytes 1048576 | tf_op jit(solution)/shard_map/last_rows/pallas_call | solution.py:2303
  451.5 1.6 copy.48
  (1 shorter events, 0.0 us)
Async XLA Ops:
  4.3 93.8 %copy-start.1 = (bf16[1280,16]{0,1:T(8,128)(2,1)S(1)}, bf16[1280,16]{0,1:T(8,128)(2,1)}, u32[]{:S(2)}) copy-start(bf16[1280,16]{0,1:T(8,128)(2,1)} %param.29) | copy-start | bytes 122884
  4.3 94.9 %copy-start.2 = (s32[16]{0:T(128)S(1)}, s32[16]{0:T(128)}, u32[]{:S(2)}) copy-start(s32[16]{0:T(128)} %param.22) | copy-start | bytes 196
  99.7 101.8 %copy-start = (f32[2,128,1280]{2,1,0:T(8,128)S(1)}, f32[2,128,1280]{2,1,0:T(8,128)}, u32[]{:S(2)}) copy-start(f32[2,128,1280]{2,1,0:T(8,128)} %get-tuple-element.80) | copy-start | bytes 3932164
